TPU v7x, 256 devices: a whole 4x4x8 slice. The times are simulated.
256 devices in a mesh: dp: 16 (over y, x_lo, core), seq: 16 (over z, x_hi).
Axes of the slice: x: 4 (x_hi: 2, x_lo: 2; x = x_hi * 2 + x_lo), y: 4, z: 8, core: 2. Of those that a mesh axis runs over, the one named last changes fastest.
Arguments:
- queries: bfloat16 [16, 4096, 384], P('dp', 'seq'), may hold values from -8 to 8
- keys: bfloat16 [16, 4096, 384], P('dp', 'seq'), may hold values from -8 to 8
- values: bfloat16 [16, 4096, 384], P('dp', 'seq'), may hold values from -6 to 6
- out_weight: bfloat16 [384, 768], replicated, may hold values from -0.3125 to 0.3125
- out_grad: bfloat16 [16, 4096, 768], P('dp', 'seq'), may hold values from -6 to 6
- offsets: int32 [3, 6], replicated, may hold values from 0 to 7
- counts: int32 [16], P('dp'), may hold values from 2048 to 4096
Outputs:
- attended: bfloat16 [16, 4096, 768], P('dp', 'seq')
- grad_queries: bfloat16 [16, 4096, 384], P('dp', 'seq')
- grad_keys: bfloat16 [16, 4096, 384], P('dp', 'seq')
- grad_values: bfloat16 [16, 4096, 384], P('dp', 'seq')
- grad_weight: float32 [384, 768], P('seq')
All inputs are finite; a program needn't handle non-finite values.
Results may differ from a plain program's by a relative error of at most 0.027.
Values may be sent and summed in bfloat16 or wider, within the bound.
No kernel may reach another device: no remote copies, remote signals or barrier semaphores. Data moves between devices by JAX's collectives and lax.ppermute only.
A program may use at most 128 MiB of HBM per device.

v0:
```python
import math

import jax
import jax.numpy as jnp
from jax import lax
from jax.sharding import PartitionSpec as P

segment_parts = (16, 4, 2, 1)
dilation_steps = (1, 2, 4, 8)
masked_score = -1e30


def as_sent(shard):

    def short(part):
        return part.astype(jnp.bfloat16) if part.dtype == jnp.float32 else part

    return jax.tree.map(short, shard)


def swapped(block, axis, stride):
    count = lax.axis_size(axis)
    route = []
    for low in range(count):
        high = low | 1 << stride
        if high != low and high < count:
            route += [(low, high), (high, low)]
    return lax.ppermute(block, axis, route)


def select_rows(block, spacing, offset_row):
    shaped = block.reshape(block.shape[0] // spacing, spacing, block.shape[1], block.shape[2])
    picks = jnp.arange(spacing, dtype=jnp.int32)[:, None] == offset_row[None, :]
    return jnp.sum(jnp.where(picks[None, :, :, None], shaped, jnp.zeros_like(shaped)), axis=1)


def place_rows(picked, spacing, offset_row, filler):
    picks = jnp.arange(spacing, dtype=jnp.int32)[:, None] == offset_row[None, :]
    spread = jnp.where(picks[None, :, :, None], picked[:, None, :, :], filler)
    return spread.reshape(picked.shape[0] * spacing, picked.shape[1], picked.shape[2])


def pair_offsets(offsets, pair_index):
    if pair_index == 0:
        return jnp.zeros((offsets.shape[1],), jnp.int32)
    return offsets[pair_index - 1] % dilation_steps[pair_index]


def group_reduce(partial_list, level_list, seq_rank):
    parts = list(partial_list)
    top_level = max(level_list + [0])
    for level in reversed(range(top_level)):
        active = [index for index in range(len(parts)) if level_list[index] > level]
        upper = jnp.right_shift(seq_rank, level) & 1 == 1
        staying_list = []
        leaving_list = []
        for index in active:
            half_rows = parts[index].shape[1] // 2
            lower_half = parts[index][:, :half_rows]
            upper_half = parts[index][:, half_rows:]
            staying_list.append(jnp.where(upper, upper_half, lower_half))
            leaving_list.append(jnp.where(upper, lower_half, upper_half))
        arrived = swapped(as_sent(jnp.concatenate(leaving_list, axis=1)), "seq", level)
        start = 0
        for index, staying in zip(active, staying_list):
            rows_here = staying.shape[1]
            parts[index] = staying + arrived[:, start : start + rows_here]
            start = start + rows_here
    return parts


def per_device(queries, keys, values, out_weight, out_grad, offsets, counts):
    seq_size = lax.axis_size("seq")
    seq_rank = lax.axis_index("seq")
    tok_rows = queries.shape[1]
    feature_width = queries.shape[2]
    head_count = offsets.shape[1]
    head_size = feature_width // head_count
    seq_length = tok_rows * seq_size
    score_scale = 1.0 / math.sqrt(head_size)
    tile_count = counts[0]
    first_row = seq_rank * tok_rows
    query_heads = queries[0].reshape(tok_rows, head_count, head_size)
    key_heads = keys[0].reshape(tok_rows, head_count, head_size)
    value_heads = values[0].reshape(tok_rows, head_count, head_size)
    layouts = []
    local_pairs = []
    for pair_index in range(4):
        spacing = dilation_steps[pair_index]
        segment = seq_length // segment_parts[pair_index]
        group_size = max(segment // tok_rows, 1)
        offset_row = pair_offsets(offsets, pair_index)
        picked = tok_rows // spacing
        query_pos = (
            first_row + jnp.arange(picked, dtype=jnp.int32)[:, None] * spacing + offset_row[None, :]
        )
        group_first = seq_rank // group_size * group_size * tok_rows
        key_pos = (
            group_first
            + jnp.arange(group_size * picked, dtype=jnp.int32)[:, None] * spacing
            + offset_row[None, :]
        )
        key_sel = select_rows(key_heads, spacing, offset_row).reshape(picked, feature_width)
        value_sel = select_rows(value_heads, spacing, offset_row).reshape(picked, feature_width)
        local_pairs.append(jnp.stack([key_sel, value_sel]))
        layouts.append((spacing, segment, group_size, offset_row, picked, query_pos, key_pos))
    level_list = [layouts[pair_index][2].bit_length() - 1 for pair_index in range(4)]
    gathered = list(local_pairs)
    wide_pairs = [pair_index for pair_index in range(4) if layouts[pair_index][2] > 1]
    joined = jnp.concatenate([local_pairs[pair_index] for pair_index in wide_pairs], axis=1)
    everyone = lax.all_gather(joined, "seq", axis=1, tiled=True)
    blocks = everyone.reshape(2, seq_size, joined.shape[1], feature_width)
    column = 0
    for pair_index in wide_pairs:
        group_size = layouts[pair_index][2]
        rows_here = local_pairs[pair_index].shape[1]
        ours = lax.dynamic_slice_in_dim(blocks, seq_rank // group_size * group_size, group_size, 1)
        gathered[pair_index] = ours[:, :, column : column + rows_here].reshape(
            2, group_size * rows_here, feature_width
        )
        column = column + rows_here
    saved = []
    top_list, den_list, num_list = ([], [], [])
    for pair_index in range(4):
        spacing, segment, group_size, offset_row, picked, query_pos, key_pos = layouts[pair_index]
        key_total = group_size * picked
        query_sel = select_rows(query_heads, spacing, offset_row)
        key_all = gathered[pair_index][0].reshape(key_total, head_count, head_size)
        value_all = gathered[pair_index][1].reshape(key_total, head_count, head_size)
        query_t = query_pos.T
        key_t = key_pos.T
        allowed = (key_t[:, None, :] < tile_count) & (
            query_t[:, :, None] // segment == key_t[:, None, :] // segment
        )
        scores = (
            jnp.einsum("qhd,khd->hqk", query_sel, key_all, preferred_element_type=jnp.float32)
            * score_scale
        )
        scores = jnp.where(allowed, scores, masked_score)
        row_max = jnp.max(scores, axis=-1)
        exponent = jnp.where(allowed, jnp.exp(scores - row_max[..., None]), 0.0)
        denominator = jnp.sum(exponent, axis=-1)
        exponent_low = exponent.astype(jnp.bfloat16)
        numerator = jnp.einsum(
            "hqk,khd->qhd", exponent_low, value_all, preferred_element_type=jnp.float32
        )
        top_list.append(place_rows(row_max.T[:, :, None], spacing, offset_row, masked_score))
        den_list.append(place_rows(denominator.T[:, :, None], spacing, offset_row, 0.0))
        num_list.append(place_rows(numerator, spacing, offset_row, 0.0))
        saved.append((query_sel, key_all, value_all, exponent_low))
    top_all = top_list[0]
    for extra in top_list[1:]:
        top_all = jnp.maximum(top_all, extra)
    pair_weights = [jnp.exp(entry - top_all) for entry in top_list]
    den_all = sum((weight_one * den_one for weight_one, den_one in zip(pair_weights, den_list)))
    num_all = sum((weight_one * num_one for weight_one, num_one in zip(pair_weights, num_list)))
    valid = (first_row + jnp.arange(tok_rows, dtype=jnp.int32) < tile_count).astype(jnp.float32)[
        :, None, None
    ]
    norm = valid / (den_all + 1.0 - valid)
    mixed = (num_all * norm).astype(jnp.bfloat16).reshape(tok_rows, feature_width)
    attended = jnp.dot(mixed, out_weight, preferred_element_type=jnp.float32).astype(jnp.bfloat16)
    grad_out = out_grad[0]
    grad_mixed = jnp.einsum(
        "td,wd->tw", grad_out, out_weight, preferred_element_type=jnp.float32
    ).astype(jnp.bfloat16)
    weight_local = jnp.einsum("tw,td->wd", mixed, grad_out, preferred_element_type=jnp.float32)
    grad_heads = grad_mixed.reshape(tok_rows, head_count, head_size)
    delta = jnp.sum(
        grad_heads.astype(jnp.float32)
        * mixed.reshape(tok_rows, head_count, head_size).astype(jnp.float32),
        axis=-1,
        keepdims=True,
    )
    grad_q = jnp.zeros((tok_rows, head_count, head_size), jnp.float32)
    grad_k = jnp.zeros((tok_rows, head_count, head_size), jnp.float32)
    grad_v = jnp.zeros((tok_rows, head_count, head_size), jnp.float32)
    partial_list = []
    for pair_index in range(4):
        spacing, segment, group_size, offset_row, picked, query_pos, key_pos = layouts[pair_index]
        query_sel, key_all, value_all, exponent_low = saved[pair_index]
        factor = select_rows(pair_weights[pair_index] * norm, spacing, offset_row)[:, :, 0].T
        delta_sel = select_rows(delta, spacing, offset_row)[:, :, 0].T
        grad_sel = select_rows(grad_heads, spacing, offset_row)
        prob = exponent_low.astype(jnp.float32) * factor[:, :, None]
        prob_low = prob.astype(jnp.bfloat16)
        value_grad = jnp.einsum(
            "hqk,qhd->khd", prob_low, grad_sel, preferred_element_type=jnp.float32
        )
        dprob = jnp.einsum("qhd,khd->hqk", grad_sel, value_all, preferred_element_type=jnp.float32)
        dscore = (prob * (dprob - delta_sel[:, :, None])).astype(jnp.bfloat16)
        query_grad = (
            jnp.einsum("hqk,khd->qhd", dscore, key_all, preferred_element_type=jnp.float32)
            * score_scale
        )
        key_grad = (
            jnp.einsum("hqk,qhd->khd", dscore, query_sel, preferred_element_type=jnp.float32)
            * score_scale
        )
        key_total = group_size * picked
        partial_list.append(
            jnp.stack(
                [
                    key_grad.reshape(key_total, feature_width),
                    value_grad.reshape(key_total, feature_width),
                ]
            )
        )
        grad_q = grad_q + place_rows(query_grad, spacing, offset_row, 0.0)
    reduced = group_reduce(partial_list, level_list, seq_rank)
    for pair_index in range(4):
        spacing, segment, group_size, offset_row, picked, query_pos, key_pos = layouts[pair_index]
        partials = reduced[pair_index]
        grad_k = grad_k + place_rows(
            partials[0].reshape(picked, head_count, head_size), spacing, offset_row, 0.0
        )
        grad_v = grad_v + place_rows(
            partials[1].reshape(picked, head_count, head_size), spacing, offset_row, 0.0
        )
    weight_total = lax.psum(weight_local.astype(jnp.bfloat16), "dp")
    grad_weight = lax.psum_scatter(weight_total, "seq", scatter_dimension=0, tiled=True).astype(
        jnp.float32
    )
    return (
        attended[None],
        grad_q.reshape(tok_rows, feature_width).astype(jnp.bfloat16)[None],
        grad_k.reshape(tok_rows, feature_width).astype(jnp.bfloat16)[None],
        grad_v.reshape(tok_rows, feature_width).astype(jnp.bfloat16)[None],
        grad_weight,
    )


def solution(mesh):
    placed = (
        P("dp", "seq", None),
        P("dp", "seq", None),
        P("dp", "seq", None),
        P(),
        P("dp", "seq", None),
        P(),
        P("dp"),
    )
    return jax.shard_map(
        per_device,
        mesh=mesh,
        in_specs=placed,
        out_specs=(
            P("dp", "seq", None),
            P("dp", "seq", None),
            P("dp", "seq", None),
            P("dp", "seq", None),
            P("seq", None),
        ),
        check_vma=False,
    )
```

profile of v0, /device:TPU:64, one launch (start us, length us, event | category | flops | bytes accessed | tf_op | source)
XLA Modules:
  0.0 522.5 jit_solution(9575795018851655259)
XLA Ops:
  20.9 3.1 select_reduce_fusion
  24.0 1.6 stack_reshape.41
  25.6 1.6 stack_reshape.40
  28.5 1.6 copy.480
  31.6 3.3 select_reduce_fusion.1
  34.9 1.7 copy.612
  36.5 1.7 copy.611
  38.4 1.9 select_reduce_fusion.2
  71.8 84.3 %all-gather.2.cloned.1.call-done = bf16[2,3584,384]{2,0,1:T(2,128)(2,1)} async-done(((bf16[2,224,384]{2,0,1:T(2,128)(2,1)}), bf16[2,3584,384]{2,0,1:T(2,128)(2,1)}) %all-gather.2.cloned.1.call-update) | async-done | bytes 5505040 | tf_op jit(solution)/shard_map/all_gather | solution.py:111
  156.1 3.3 copy.482
  159.3 2.4 copy-done.1
  170.4 2.1 constant_dynamic-slice_fusion.3
  178.5 1.6 copy.515
  181.5 1.7 broadcast_select_fusion.1
  184.8 1.6 copy.486
  187.7 1.6 broadcast_select_fusion.3
  190.7 1.6 copy.614
  195.0 1.6 broadcast_in_dim.729
  198.2 1.7 copy.510
  201.3 1.9 reshape_squeeze.22
  205.0 2.1 copy.522
  208.0 1.7 copy.506
  209.8 2.0 broadcast_in_dim.740
  211.7 2.2 copy.521
  213.9 2.0 copy.499
  215.9 1.9 reshape_squeeze.21
  217.8 2.1 convolution_bitcast_fusion.2
  219.8 1.9 copy.500
  221.7 2.2 broadcast_in_dim.734
  223.9 2.2 copy.520
  228.0 2.6 multiply_reduce_fusion
  233.1 1.6 copy.572
  234.7 1.6 copy.566
  236.3 1.6 copy.570
  238.0 1.6 copy.565
  239.6 1.6 copy.575
  246.4 2.8 collective-permute-start
  263.0 4.7 collective-permute-done
  272.4 20.9 %collective-permute-done.1 = bf16[2,384,384]{1,2,0:T(8,128)(2,1)S(1)} collective-permute-done((bf16[2,384,384]{1,2,0:T(8,128)(2,1)S(1)}, bf16[2,384,384]{1,2,0:T(8,128)(2,1)S(1)}, u32[]{:S(2)}, u32[]{:S(2)}) %collective-permute-start.1) | collective-permute-done | bytes 589856 | tf_op jit(solution)/shard_map/ppermute | solution.py:28
  295.5 2.3 copy.586
  297.8 2.2 collective-permute-start.2
  300.0 2.0 fusion.10
  302.1 2.0 fusion.11
  305.2 11.3 %collective-permute-done.2 = bf16[2,448,384]{2,1,0:T(8,128)(2,1)S(1)} collective-permute-done((bf16[2,448,384]{2,1,0:T(8,128)(2,1)}, bf16[2,448,384]{2,1,0:T(8,128)(2,1)S(1)}, u32[]{:S(2)}, u32[]{:S(2)}) %collective-permute-start.2) | collective-permute-done | bytes 688160 | tf_op jit(solution)/shard_map/ppermute | solution.py:28
  342.3 2.9 fusion.5
  345.1 101.6 %reduce-scatter.2.cloned.1.call-done = bf16[24,768]{1,0:T(8,128)(2,1)} async-done(((bf16[384,768]{1,0:T(8,128)(2,1)}), bf16[24,768]{1,0:T(8,128)(2,1)}) %reduce-scatter.2.cloned.1.call-update) | async-done | bytes 36880 | tf_op jit(solution)/shard_map/reduce_scatter | solution.py:221
  446.8 53.6 %psum.8 = bf16[24,768]{1,0:T(8,128)(2,1)S(1)} all-reduce(bf16[24,768]{1,0:T(8,128)(2,1)} %reduce-scatter.2.cloned.1.call-done), channel_id=1, replica_groups=mesh['dp'=16,'seq'=16] {'dp'}, use_global_device_ids=true, to_apply=%region_27.28 | all-reduce | flops 18432 | bytes 73728 | tf_op jit(solution)/shard_map/psum | solution.py:220
  512.4 3.0 add_convert_fusion
  (510 shorter events, 143.7 us)
Async XLA Ops:
  7.2 4.6 copy-start.23
  7.2 148.9 %all-gather.2.cloned.1.call-start = ((), (), s32[]{:S(2)}) async-start(), calls=%async_computation.1 | async-start | bytes 5849088 | tf_op jit(solution)/shard_map/all_gather | solution.py:111
  9.6 4.4 copy-start.21
  11.8 4.4 copy-start.22
  19.6 15.3 %copy-start.117 = (s32[6]{0:T(128)}, s32[6]{0:T(128)S(1)}, u32[]{:S(2)}) copy-start(s32[6]{0:T(128)S(1)} %get-tuple-element.58) | copy-start | bytes 76
  19.6 18.6 %copy-start.119 = (s32[6]{0:T(128)}, s32[6]{0:T(128)S(1)}, u32[]{:S(2)}) copy-start(s32[6]{0:T(128)S(1)} %get-tuple-element.56) | copy-start | bytes 76
  20.9 14.0 %copy-start.110 = (pred[8,6]{1,0:T(8,128)(4,1)}, pred[8,6]{1,0:T(8,128)(4,1)S(1)}, u32[]{:S(2)}) copy-start(pred[8,6]{1,0:T(8,128)(4,1)S(1)} %copy.479) | copy-start | bytes 148
  24.0 139.7 %copy-start.66 = (bf16[32,6,64]{2,1,0:T(8,128)(2,1)}, bf16[32,6,64]{2,1,0:T(8,128)(2,1)S(1)}, u32[]{:S(2)}) copy-start(bf16[32,6,64]{2,1,0:T(8,128)(2,1)S(1)} %get-tuple-element.11) | copy-start | bytes 73732
  31.6 8.6 %copy-start.122 = (pred[4,6]{1,0:T(4,128)(4,1)}, pred[4,6]{1,0:T(4,128)(4,1)S(1)}, u32[]{:S(2)}) copy-start(pred[4,6]{1,0:T(4,128)(4,1)S(1)} %copy.476) | copy-start | bytes 76
  44.8 402.0 %reduce-scatter.2.cloned.1.call-start = ((), (), s32[]{:S(2)}) async-start(), calls=%async_computation.2 | async-start | bytes 626688 | tf_op jit(solution)/shard_map/reduce_scatter | solution.py:221
  49.9 7.7 %copy-start.62 = (bf16[64,6,64]{2,1,0:T(8,128)(2,1)S(1)}, bf16[64,6,64]{2,1,0:T(8,128)(2,1)}, u32[]{:S(2)}) copy-start(bf16[64,6,64]{2,1,0:T(8,128)(2,1)} %get-tuple-element.19) | copy-start | bytes 147460
  50.8 9.8 %copy-start.103 = (pred[256,6]{0,1:T(8,128)(4,1)}, pred[256,6]{0,1:T(8,128)(4,1)S(1)}, u32[]{:S(2)}) copy-start(pred[256,6]{0,1:T(8,128)(4,1)S(1)} %copy.615) | copy-start | bytes 4612
  50.8 9.7 %copy-start.46 = (bf16[128,6,64]{2,1,0:T(8,128)(2,1)S(1)}, bf16[128,6,64]{2,1,0:T(8,128)(2,1)}, u32[]{:S(2)}) copy-start(bf16[128,6,64]{2,1,0:T(8,128)(2,1)} %get-tuple-element.15) | copy-start | bytes 294916
  51.0 10.4 %copy-start.104 = (pred[256,6]{0,1:T(8,128)(4,1)}, pred[256,6]{0,1:T(8,128)(4,1)S(1)}, u32[]{:S(2)}) copy-start(pred[256,6]{0,1:T(8,128)(4,1)S(1)} %copy.613) | copy-start | bytes 4612
  52.0 11.5 %copy-start.105 = (pred[256,6]{0,1:T(8,128)(4,1)}, pred[256,6]{0,1:T(8,128)(4,1)S(1)}, u32[]{:S(2)}) copy-start(pred[256,6]{0,1:T(8,128)(4,1)S(1)} %copy.610) | copy-start | bytes 4612
  53.7 13.9 %copy-start.116 = (s32[6]{0:T(128)S(1)}, s32[6]{0:T(128)}, u32[]{:S(2)}) copy-start(s32[6]{0:T(128)} %copy-done.115) | copy-start | bytes 76
  53.7 14.0 %copy-start.118 = (s32[6]{0:T(128)S(1)}, s32[6]{0:T(128)}, u32[]{:S(2)}) copy-start(s32[6]{0:T(128)} %copy-done.117) | copy-start | bytes 76
  53.7 14.7 %copy-start.120 = (s32[6]{0:T(128)S(1)}, s32[6]{0:T(128)}, u32[]{:S(2)}) copy-start(s32[6]{0:T(128)} %copy-done.119) | copy-start | bytes 76
  168.1 4.4 copy-start.18
  168.6 4.1 copy-start.89
  169.0 3.9 copy-start.98
  175.5 21.1 %copy-start.39 = (bf16[1,16,32,384]{3,2,1,0:T(8,128)(2,1)S(1)}, bf16[1,16,32,384]{3,2,1,0:T(8,128)(2,1)}, u32[]{:S(2)}) copy-start(bf16[1,16,32,384]{3,2,1,0:T(8,128)(2,1)} %get-tuple-element.37) | copy-start | bytes 1179652
  228.0 13.1 %copy-start.77 = (f32[6,32]{1,0:T(8,128)S(1)}, f32[6,32]{1,0:T(8,128)}, u32[]{:S(2)}) copy-start(f32[6,32]{1,0:T(8,128)} %copy-done.76) | copy-start | bytes 2308
  228.0 13.1 %copy-start.79 = (f32[6,32]{1,0:T(8,128)S(1)}, f32[6,32]{1,0:T(8,128)}, u32[]{:S(2)}) copy-start(f32[6,32]{1,0:T(8,128)} %copy-done.78) | copy-start | bytes 2308
  241.2 4.0 copy-start.67
  245.2 4.1 copy-start.45
  245.2 4.2 copy-start.44
  245.2 4.3 copy-start.92
  245.2 4.4 copy-start.93
  245.5 5.2 %copy-start.90 = (f32[6,64]{1,0:T(8,128)S(1)}, f32[6,64]{1,0:T(8,128)}, u32[]{:S(2)}) copy-start(f32[6,64]{1,0:T(8,128)} %copy-done.89) | copy-start | bytes 4612
  245.5 5.2 copy-start.94
  245.5 5.2 copy-start.95
  245.5 5.2 copy-start.99
  245.5 5.2 copy-start.112
  245.6 5.2 copy-start.121
  245.6 5.2 copy-start.129
  245.6 5.4 %copy-start.51 = (bf16[64,6,64]{0,2,1:T(8,128)(2,1)S(1)}, bf16[64,6,64]{0,2,1:T(8,128)(2,1)}, u32[]{:S(2)}) copy-start(bf16[64,6,64]{0,2,1:T(8,128)(2,1)} %copy.583) | copy-start | bytes 147460
  246.4 21.3 %collective-permute-start = (bf16[2,256,384]{1,2,0:T(8,128)(2,1)}, bf16[2,256,384]{1,2,0:T(8,128)(2,1)}, u32[]{:S(2)}, u32[]{:S(2)}) collective-permute-start(bf16[2,256,384]{1,2,0:T(8,128)(2,1)} %select_convert_fusion), channel_id=1, source_target_pairs={{0,8},{8,0},{1,9},{9,1},{2,10},{10,2},{3,11},{11,3},{4,12},{12,4},... | collective-permute-start | bytes 1179656 | tf_op jit(solution)/shard_map/ppermute | solution.py:28
  249.4 4.0 copy-start.50
  252.1 4.9 copy-start.48
  261.2 6.5 %copy-start.7 = (f32[6,64,512]{2,1,0:T(8,128)S(1)}, f32[6,64,512]{2,1,0:T(8,128)}, u32[]{:S(2)}) copy-start(f32[6,64,512]{2,1,0:T(8,128)} %copy-done.6) | copy-start | bytes 2359300
  261.2 6.5 %copy-start.9 = (f32[6,64,512]{2,1,0:T(8,128)S(1)}, f32[6,64,512]{2,1,0:T(8,128)}, u32[]{:S(2)}) copy-start(f32[6,64,512]{2,1,0:T(8,128)} %copy-done.8) | copy-start | bytes 2359300
  269.0 24.3 %collective-permute-start.1 = (bf16[2,384,384]{1,2,0:T(8,128)(2,1)S(1)}, bf16[2,384,384]{1,2,0:T(8,128)(2,1)S(1)}, u32[]{:S(2)}, u32[]{:S(2)}) collective-permute-start(bf16[2,384,384]{1,2,0:T(8,128)(2,1)S(1)} %pad_maximum_fusion.4), channel_id=1, source_target_pairs={{0,4},{4,0},{1,5},{5,1},{2,6},{6,2},{3,7},{7,3},{8,12},{12,8},{9,1... | collective-permute-start | bytes 1769480 | tf_op jit(solution)/shard_map/ppermute | solution.py:28
  271.3 22.2 %copy-start.5 = (f32[6,64,512]{2,1,0:T(8,128)S(1)}, f32[6,64,512]{2,1,0:T(8,128)}, u32[]{:S(2)}) copy-start(f32[6,64,512]{2,1,0:T(8,128)} %convolution_multiply_fusion.2) | copy-start | bytes 2359300
  295.5 6.6 %copy-start.11 = (bf16[6,128,512]{2,1,0:T(8,128)(2,1)S(1)}, bf16[6,128,512]{2,1,0:T(8,128)(2,1)}, u32[]{:S(2)}) copy-start(bf16[6,128,512]{2,1,0:T(8,128)(2,1)} %copy-done.10) | copy-start | bytes 2359300
  297.8 18.7 %collective-permute-start.2 = (bf16[2,448,384]{2,1,0:T(8,128)(2,1)}, bf16[2,448,384]{2,1,0:T(8,128)(2,1)S(1)}, u32[]{:S(2)}, u32[]{:S(2)}) collective-permute-start(bf16[2,448,384]{2,1,0:T(8,128)(2,1)} %copy.586), channel_id=1, source_target_pairs={{0,2},{2,0},{1,3},{3,1},{4,6},{6,4},{5,7},{7,5},{8,10},{10,8},{9,1... | collective-permute-start | bytes 2064392 | tf_op jit(solution)/shard_map/ppermute | solution.py:28
  305.2 13.9 %copy-start.15 = (f32[2,256,384]{1,2,0:T(8,128)S(1)}, f32[2,256,384]{1,2,0:T(8,128)}, u32[]{:S(2)}) copy-start(f32[2,256,384]{1,2,0:T(8,128)} %copy-done.14) | copy-start | bytes 2359300
  325.1 175.8 %collective-permute-start.3 = (bf16[2,224,384]{1,2,0:T(8,128)(2,1)}, bf16[2,224,384]{1,2,0:T(8,128)(2,1)}, u32[]{:S(2)}, u32[]{:S(2)}) collective-permute-start(bf16[2,224,384]{1,2,0:T(8,128)(2,1)} %pad_maximum_fusion.6), channel_id=1, source_target_pairs={{0,1},{1,0},{2,3},{3,2},{4,5},{5,4},{6,7},{7,6},{8,9},{9,8},{10,11... | collective-permute-start | bytes 1032200 | tf_op jit(solution)/shard_map/ppermute | solution.py:28
  (92 other events, 178.8 us)
Sparse Core Ops, SparseCore 0:
  44.9 111.1 all-gather.1
  261.3 185.3 reduce-scatter.1
where the time goes:
time: 532 us; the launch traced here: 522 us
  waiting for transfers between devices  223 us (42%)
  local copies, waits for them, and re-layouts  151 us (28%)
  blocking collectives  53.6 us (10%)
  other arithmetic  43.1 us (8%)
  matrix products  29.4 us (6%)
  between operations  16.8 us (3%)
    reduce_scatter x1, waiting for transfers between devices, per_device(): lax.psum_scatter(weight_total, 'seq', scatter_dimension=0, tiled=True)  102 us
    all_gather x1, waiting for transfers between devices, per_device(): everyone = lax.all_gather(joined, 'seq', axis=1, tiled=True)  84.3 us
    psum x1, blocking collectives, per_device(): weight_total = lax.psum(weight_local.astype(jnp.bfloat16), 'dp')  53.6 us
    broadcast_in_dim x73, local copies, waits for them, and re-layouts, place_rows(): spread = jnp.where(picks[None, :, :, None], picked[:, None, :, :], filler)  45.1 us
    ppermute x4, waiting for transfers between devices, swapped(): return lax.ppermute(block, axis, route)  37 us
    unnamed x273, local copies, waits for them, and re-layouts  17.2 us
    another operation x17, local copies, waits for them, and re-layouts, select_rows(): block.reshape(block.shape[0] // spacing, spacing, block.shape[1], block.s...  14.2 us
  transfers between devices with their start and end apart: 6, of which 5 were waited for; matrix products, arithmetic and copies ran while one was open for 15% of the time, Pallas kernels for 0%

commit v1 on v0

v1 whole, which is shorter than its diff:
```python
import jax
import jax.numpy as jnp
from jax import lax
from jax.experimental import pallas as pl
from jax.experimental.pallas import tpu as pltpu
from jax.sharding import PartitionSpec as P

bf16 = jnp.bfloat16
f32 = jnp.float32
low_bias = -1e30


def dot_nn(a, b):
    return lax.dot_general(a, b, (((1,), (0,)), ((), ())), preferred_element_type=f32)


def dot_nt(a, b):
    return lax.dot_general(a, b, (((1,), (1,)), ((), ())), preferred_element_type=f32)


def dot_tn(a, b):
    return lax.dot_general(a, b, (((0,), (0,)), ((), ())), preferred_element_type=f32)


def first_half(rows):
    return lax.broadcasted_iota(jnp.int32, (rows, 128), 1) < 64


def half_of(x, h):
    m = first_half(x.shape[0])
    z = jnp.zeros_like(x)
    return jnp.where(m, x, z) if h == 0 else jnp.where(m, z, x)


def row_order(back):
    a = lax.broadcasted_iota(jnp.int32, (256, 256), 0 if not back else 1)
    b = lax.broadcasted_iota(jnp.int32, (256, 256), 1 if not back else 0)
    return jnp.where(b == (a & 31) * 8 + (a >> 5), 1.0, 0.0).astype(bf16)


class Place:
    def __init__(self, info, offsets, counts):
        self.j = info[0] & 3
        self.base = (info[0] >> 2) * 1024
        self.quarter = info[0] >> 2
        self.chunk = jnp.minimum(info[1], 2)
        self.count = counts[0]
        self.offsets = offsets

    def offs(self, pair):
        r = 2 << pair
        return [self.offsets[pair, 2 * self.chunk + h] & (r - 1) for h in (0, 1)]

    def bias(self, n, step, o, base):
        kk = lax.broadcasted_iota(jnp.int32, (1, n), 1)
        pos = base + ((self.j ^ ((kk >> 5) & 3)) << 8) + (kk & 31) * 8 + o + step * (kk >> 7)
        return jnp.where(pos < self.count, 0.0, low_bias)

    def bias_slot(self, slot):
        kk = lax.broadcasted_iota(jnp.int32, (1, 256), 1)
        pos = self.base + ((self.j ^ slot) << 8) + (kk & 31) * 8 + (kk >> 5)
        return jnp.where(pos < self.count, 0.0, low_bias)

    def valid(self, res):
        rr = lax.broadcasted_iota(jnp.int32, (128, 128), 0)
        pos = self.base + ((self.j ^ (rr >> 5)) << 8) + (rr & 31) * 8 + res
        return jnp.where(pos < self.count, 1.0, 0.0)


def pick(read, pair, oo):
    r = 2 << pair
    m = first_half(128)
    parts = [jnp.where(m, read(oo[0] + r * i), read(oo[1] + r * i)) for i in range(8 // r)]
    return parts[0] if len(parts) == 1 else jnp.concatenate(parts, axis=0)


def put(read, write, val, pair, oo, add):
    r = 2 << pair
    m = first_half(128)
    for i in range(8 // r):
        blk = val[i * 128 : (i + 1) * 128]
        for h in (0, 1):
            mine = m if h == 0 else ~m
            old = read(oo[h] + r * i)
            write(oo[h] + r * i, jnp.where(mine, old + blk if add else blk, old))


def reader(ref, *lead):
    return lambda i: ref[(*lead, i)]


def writer(ref, *lead):
    def w(i, val):
        ref[(*lead, i)] = val

    return w


def slot_rows(ref, slot, *lead):
    return ref[(*lead, slice(None), slice(slot * 32, slot * 32 + 32), slice(None))].reshape(256, 128)


def attend(q2, k2, v2, bias):
    nk = k2.shape[0]
    out, es, ms = None, [], []
    one = jnp.ones((nk, 128), bf16)
    for h in (0, 1):
        s = dot_nt(q2, half_of(k2, h)) + bias[h]
        m = jnp.max(s, axis=1, keepdims=True)
        e = jnp.exp(s - m).astype(bf16)
        o = dot_nn(e, jnp.concatenate([half_of(v2, h), half_of(one, h)], axis=1))
        out = o if out is None else out + o
        es.append(e)
        ms.append(m)
    n = q2.shape[0]
    top = jnp.where(first_half(n), jnp.broadcast_to(ms[0], (n, 128)), jnp.broadcast_to(ms[1], (n, 128)))
    return es, top, out


def back(q2, k2, v2, gf2, fd2, es):
    dq = dk = dv = None
    for h in (0, 1):
        kh, vh = half_of(k2, h), half_of(v2, h)
        e = es[h]
        dp = dot_nt(gf2, vh)
        ds = (e.astype(f32) * (dp - fd2[:, 64 * h : 64 * h + 1])).astype(bf16)
        a, b, c = dot_nn(ds, kh), dot_tn(ds, half_of(q2, h)), dot_tn(e, half_of(gf2, h))
        dq, dk, dv = (a, b, c) if dq is None else (dq + a, dk + b, dv + c)
    return dq, dk, dv


def prep_body(info, q, k, v, og, w, o0, o1, o2, o3, px):
    order = row_order(False)
    px[0] = (dot_nn(order, q[...]) * 0.125).astype(bf16)
    px[1] = dot_nn(order, k[...]).astype(bf16)
    px[2] = dot_nn(order, v[...]).astype(bf16)
    px[3] = dot_nn(order, dot_nt(og[...], w[...]).astype(bf16)).astype(bf16)
    for d, o in enumerate((o0, o1, o2, o3)):
        c = pl.multiple_of(jnp.minimum(info[1] ^ d, 2) * 128, 128)
        for i in range(4):
            o[i] = px[i, :, pl.ds(c, 128)]


def collect_body(info, offsets, counts, m0, m1, m2, m3, x, s4, s8):
    place = Place(info, offsets, counts)
    for slot, m in enumerate((m0, m1, m2, m3)):
        for i in range(4):
            x[i, :, slot * 32 : slot * 32 + 32, :] = m[i].reshape(8, 32, 128)
    o3, o4 = place.offs(1), place.offs(2)
    for i in (0, 1):
        s4[i, 0:256] = pick(reader(x, i + 1), 1, o3)
        last = pick(reader(x, i + 1), 2, o4)
        s4[i, 256:384] = last
        s8[i] = last


def near_body(info, offsets, counts, x, top, num, den, m1, m2, e1, e2):
    place = Place(info, offsets, counts)
    for slot in range(4):
        b = place.bias_slot(slot)
        sl = slice(slot * 32, slot * 32 + 32)
        es, t, o = attend(*[slot_rows(x, slot, i) for i in range(3)], [b, b])
        e1[slot, 0], e1[slot, 1] = es
        t = t.reshape(8, 32, 128)
        top[:, sl, :] = t
        m1[:, sl, :] = t
        num[:, sl, :] = o[:, :128].reshape(8, 32, 128)
        den[:, sl, :] = o[:, 128:].reshape(8, 32, 128)
    oo = place.offs(0)
    q2, k2, v2 = [pick(reader(x, i), 0, oo) for i in range(3)]
    bias = [place.bias(512, 2, oo[h], place.base) for h in (0, 1)]
    es, t, o = attend(q2, k2, v2, bias)
    e2[0], e2[1] = es
    m2[...] = t
    merge(top, num, den, t, o, 0, oo)


def merge(top, num, den, t, o, pair, oo):
    old = pick(reader(top), pair, oo)
    new = jnp.maximum(old, t)
    a, b = jnp.exp(old - new), jnp.exp(t - new)
    n = pick(reader(num), pair, oo) * a + o[:, :128] * b
    d = pick(reader(den), pair, oo) * a + o[:, 128:] * b
    put(reader(top), writer(top), new, pair, oo, False)
    put(reader(num), writer(num), n, pair, oo, False)
    put(reader(den), writer(den), d, pair, oo, False)


def far_body(
    info, offsets, counts, x, r4, r8, r12, top_in, num_in, den_in,
    top, norm, delta, acc, mx0, mx1, mx2, mx3, d4, d8, d12, num, den,
):
    place = Place(info, offsets, counts)
    top[...] = top_in[...]
    num[...] = num_in[...]
    den[...] = den_in[...]
    o3, o4 = place.offs(1), place.offs(2)
    q3, k3, v3 = [pick(reader(x, i), 1, o3) for i in range(3)]
    q4, k4, v4 = [pick(reader(x, i), 2, o4) for i in range(3)]
    k3, v3 = [jnp.concatenate([own, r4[i, 0:256]], axis=0) for i, own in enumerate((k3, v3))]
    k4, v4 = [
        jnp.concatenate([own, r4[i, 256:384], r8[i], r12[i]], axis=0) for i, own in enumerate((k4, v4))
    ]
    at = [(place.quarter ^ i) * 1024 for i in range(4)]
    b3 = [jnp.concatenate([place.bias(256, 4, o3[h], at[i]) for i in (0, 1)], axis=1) for h in (0, 1)]
    b4 = [jnp.concatenate([place.bias(128, 8, o4[h], at[i]) for i in range(4)], axis=1) for h in (0, 1)]
    es3, t3, out3 = attend(q3, k3, v3, b3)
    es4, t4, out4 = attend(q4, k4, v4, b4)
    merge(top, num, den, t3, out3, 1, o3)
    merge(top, num, den, t4, out4, 2, o4)
    ri = lax.broadcasted_iota(jnp.int32, (128, 128), 0) >> 6
    ci = lax.broadcasted_iota(jnp.int32, (128, 128), 1) >> 6
    same = jnp.where(ri == ci, 1.0, 0.0)
    for res in range(8):
        ok = place.valid(res)
        scale = ok / (den[res] + 1.0 - ok)
        norm[res] = scale
        mixed = (num[res] * scale).astype(bf16)
        for slot, mx in enumerate((mx0, mx1, mx2, mx3)):
            mx[res * 32 : res * 32 + 32] = mixed[slot * 32 : slot * 32 + 32]
        prod = x[3, res].astype(f32) * mixed.astype(f32)
        delta[res] = lax.dot_general(
            prod, same, (((1,), (0,)), ((), ())), precision=lax.Precision.HIGHEST, preferred_element_type=f32
        )
    acc[...] = jnp.zeros_like(acc)
    for pair, oo, q2, k2, v2, t, es, parts in (
        (1, o3, q3, k3, v3, t3, es3, ((d4, 0, 256),)),
        (2, o4, q4, k4, v4, t4, es4, ((d4, 256, 128), (d8, 0, 128), (d12, 0, 128))),
    ):
        f2 = jnp.exp(t - pick(reader(top), pair, oo)) * pick(reader(norm), pair, oo)
        gf2 = (pick(reader(x, 3), pair, oo).astype(f32) * f2).astype(bf16)
        fd2 = f2 * pick(reader(delta), pair, oo)
        grads = back(q2, k2, v2, gf2, fd2, es)
        for i in range(3):
            own = grads[i][: q2.shape[0]]
            put(reader(acc, i), writer(acc, i), own, pair, oo, True)
        at_row = q2.shape[0]
        for ref, start, rows in parts:
            for i in (0, 1):
                ref[i, start : start + rows] = grads[i + 1][at_row : at_row + rows].astype(bf16)
            at_row += rows


def near_back_body(info, offsets, counts, x, top, norm, delta, acc_in, m1, m2, e1, e2, acc):
    place = Place(info, offsets, counts)
    for slot in range(4):
        sl = slice(slot * 32, slot * 32 + 32)
        f2 = jnp.exp(slot_rows(m1, slot) - slot_rows(top, slot)) * slot_rows(norm, slot)
        q2, k2, v2, g2 = [slot_rows(x, slot, i) for i in range(4)]
        gf2 = (g2.astype(f32) * f2).astype(bf16)
        fd2 = f2 * slot_rows(delta, slot)
        grads = back(q2, k2, v2, gf2, fd2, [e1[slot, 0], e1[slot, 1]])
        for i in range(3):
            acc[i, :, sl, :] = acc_in[i, :, sl, :] + grads[i].reshape(8, 32, 128)
    oo = place.offs(0)
    q2, k2, v2, g2 = [pick(reader(x, i), 0, oo) for i in range(4)]
    f2 = jnp.exp(m2[...] - pick(reader(top), 0, oo)) * pick(reader(norm), 0, oo)
    gf2 = (g2.astype(f32) * f2).astype(bf16)
    fd2 = f2 * pick(reader(delta), 0, oo)
    grads = back(q2, k2, v2, gf2, fd2, [e2[0], e2[1]])
    for i in range(3):
        put(reader(acc, i), writer(acc, i), grads[i], 0, oo, True)


def finish_body(info, offsets, counts, acc_in, r4, r8, r12, o0, o1, o2, o3, acc):
    place = Place(info, offsets, counts)
    acc[...] = acc_in[...]
    p3, p4 = place.offs(1), place.offs(2)
    for i in (0, 1):
        rd, wr = reader(acc, i + 1), writer(acc, i + 1)
        put(rd, wr, r4[i, 0:256].astype(f32), 1, p3, True)
        far = r4[i, 256:384].astype(f32) + r8[i].astype(f32) + r12[i].astype(f32)
        put(rd, wr, far, 2, p4, True)
    for slot, o in enumerate((o0, o1, o2, o3)):
        o[0] = (slot_rows(acc, slot, 0) * 0.125).astype(bf16)
        o[1] = slot_rows(acc, slot, 1).astype(bf16)
        o[2] = slot_rows(acc, slot, 2).astype(bf16)


def home_body(info, m0, m1, m2, m3, dq, dk, dv, wide):
    order = row_order(True)
    for d, m in enumerate((m0, m1, m2, m3)):
        c = pl.multiple_of((info[1] ^ d) * 128, 128)
        for i in range(3):
            wide[i, :, pl.ds(c, 128)] = m[i]
    for i, o in enumerate((dq, dk, dv)):
        o[...] = dot_nn(order, wide[i, :, 0:384]).astype(bf16)


def project_body(info, m0, m1, m2, m3, og, w, attended, send, keep, wide):
    order = row_order(True)
    for d, m in enumerate((m0, m1, m2, m3)):
        c = pl.multiple_of((info[1] ^ d) * 128, 128)
        wide[:, pl.ds(c, 128)] = m[...]
    mixed = dot_nn(order, wide[:, 0:384]).astype(bf16)
    there = pl.multiple_of((1 - info[2]) * 384, 128)
    here = pl.multiple_of(info[2] * 384, 128)
    send[...] = dot_tn(mixed, og[:, pl.ds(there, 384)]).astype(bf16)
    keep[...] = dot_tn(mixed, og[:, pl.ds(here, 384)])
    attended[...] = dot_nn(mixed, w[...]).astype(bf16)


smem = pl.BlockSpec(memory_space=pltpu.SMEM)
vmem = pl.BlockSpec(memory_space=pltpu.VMEM)


def call(body, scalars, arrays, outs, scratch=(), flops=0):
    shapes = [jax.ShapeDtypeStruct(s, t) for s, t in outs]
    moved = sum(a.size * a.dtype.itemsize for a in arrays) + sum(s.size * s.dtype.itemsize for s in shapes)
    return pl.pallas_call(
        body,
        out_shape=shapes,
        in_specs=[smem] * len(scalars) + [vmem] * len(arrays),
        out_specs=[vmem] * len(shapes),
        scratch_shapes=[pltpu.VMEM(s, t) for s, t in scratch],
        compiler_params=pltpu.CompilerParams(vmem_limit_bytes=48 * 1024 * 1024),
        cost_estimate=pl.CostEstimate(flops=flops, bytes_accessed=moved, transcendentals=0),
    )(*scalars, *arrays)


def routes(seq_step, keep=None):
    pairs = []
    for dp in range(16):
        for s in range(16):
            t = s ^ seq_step
            if keep is not None and (keep(s, t) & 3) ^ (3 * (dp & 1)) == 3:
                continue
            pairs.append((dp * 16 + s, dp * 16 + t))
    return pairs


def shift(block, pairs):
    return lax.ppermute(block, ("dp", "seq"), pairs)


def dp_step(block, step):
    return lax.ppermute(block, "dp", [(i, i ^ step) for i in range(16)])


def seq_step(block, step):
    return lax.ppermute(block, "seq", [(i, i ^ step) for i in range(16)])


def per_device(queries, keys, values, out_weight, out_grad, offsets, counts):
    seq_rank = lax.axis_index("seq").astype(jnp.int32)
    core = lax.axis_index("dp").astype(jnp.int32) & 1
    info = jnp.stack([seq_rank, (seq_rank & 3) ^ (3 * core), core])
    places = [info, offsets, counts]

    chunk = ((4, 256, 128), bf16)
    msgs = call(
        prep_body,
        [info],
        [queries[0], keys[0], values[0], out_grad[0], out_weight],
        [chunk] * 4,
        [((4, 256, 384), bf16)],
    )
    got = [msgs[0]] + [shift(msgs[d], routes(d, lambda s, t: t)) for d in (1, 2, 3)]
    cube = (8, 128, 128)
    x, s4, s8 = call(
        collect_body, places, got, [((4, *cube), bf16), ((2, 384, 128), bf16), ((2, 128, 128), bf16)]
    )
    active = lambda s, t: s
    r4, r8, r12 = [shift(b, routes(d, active)) for b, d in ((s4, 4), (s8, 8), (s8, 12))]
    top, num, den, m1, m2, e1, e2 = call(
        near_body,
        places,
        [x],
        [(cube, f32)] * 4 + [((512, 128), f32), ((4, 2, 256, 256), bf16), ((2, 512, 512), bf16)],
        flops=10**9,
    )
    top, norm, delta, acc, mx0, mx1, mx2, mx3, d4, d8, d12 = call(
        far_body,
        places,
        [x, r4, r8, r12, top, num, den],
        [(cube, f32)] * 3
        + [((3, *cube), f32)]
        + [((256, 128), bf16)] * 4
        + [((2, 384, 128), bf16), ((2, 128, 128), bf16), ((2, 128, 128), bf16)],
        [(cube, f32)] * 2,
        flops=10**9,
    )
    mixed = [mx0] + [shift(b, routes(d, active)) for d, b in ((1, mx1), (2, mx2), (3, mx3))]
    b4, b8, b12 = [shift(b, routes(d, active)) for b, d in ((d4, 4), (d8, 8), (d12, 12))]
    (acc,) = call(
        near_back_body,
        places,
        [x, top, norm, delta, acc, m1, m2, e1, e2],
        [((3, *cube), f32)],
        flops=2 * 10**9,
    )
    attended, send, keep = call(
        project_body,
        [info],
        mixed + [out_grad[0], out_weight],
        [((256, 768), bf16), ((384, 384), bf16), ((384, 384), f32)],
        [((256, 512), bf16)],
        flops=3 * 10**8,
    )
    back_msgs = call(
        finish_body, places, [acc, b4, b8, b12], [((3, 256, 128), bf16)] * 4, [((3, *cube), f32)]
    )
    home = [back_msgs[0]] + [shift(back_msgs[d], routes(d, active)) for d in (1, 2, 3)]
    grads = call(home_body, [info], home, [((256, 384), bf16)] * 3, [((3, 256, 512), bf16)])

    part = keep + dp_step(send, 1)
    rows = part.reshape(16, 24, 384)
    rest = rows
    for bit in (0, 1, 2, 3):
        pairs_view = rest.reshape(rest.shape[0] // 2, 2, 24, 384)
        upper = ((seq_rank >> bit) & 1) == 1
        stay = jnp.where(upper, pairs_view[:, 1], pairs_view[:, 0])
        leave = jnp.where(upper, pairs_view[:, 0], pairs_view[:, 1]).astype(bf16)
        rest = stay + seq_step(leave, 1 << bit).astype(f32)
    total = rest[0]
    for step in (2, 4, 8):
        low = total.astype(bf16)
        total = low.astype(f32) + dp_step(low, step).astype(f32)
    other = dp_step(total, 1)
    grad_weight = jnp.concatenate(
        [jnp.where(core == 0, total, other), jnp.where(core == 0, other, total)], axis=1
    )
    return (attended[None], grads[0][None], grads[1][None], grads[2][None], grad_weight)


def solution(mesh):
    tiles = P("dp", "seq", None)
    return jax.shard_map(
        per_device,
        mesh=mesh,
        in_specs=(tiles, tiles, tiles, P(), tiles, P(), P("dp")),
        out_specs=(tiles, tiles, tiles, tiles, P("seq", None)),
        check_vma=False,
    )
```

time: 532 us -> 160 us (0.30)
  the two profiles are of different devices: /device:TPU:64 before, /device:TPU:32 now
where the time goes in v1:
time: 160 us; the launch traced here: 159 us
  starting transfers between devices  63.6 us (40%)
  waiting for transfers between devices  48.5 us (30%)
  Pallas kernels  22 us (14%)
  local copies, waits for them, and re-layouts  15.6 us (10%)
  other arithmetic  7.84 us (5%)
  between operations  1.62 us (1%)
    ppermute x15, starting transfers between devices, shift(): return lax.ppermute(block, ('dp', 'seq'), pairs)  53.8 us
    ppermute x15, waiting for transfers between devices, shift(): return lax.ppermute(block, ('dp', 'seq'), pairs)  22.4 us
    pallas_call x8, Pallas kernels, call(): pl.pallas_call(body, out_shape=shapes, in_specs=[smem] * len(scalars) + [...  22 us
    ppermute x4, waiting for transfers between devices, seq_step(): return lax.ppermute(block, 'seq', [(i, i ^ step) for i in range(16)])  21 us
    unnamed x48, local copies, waits for them, and re-layouts  15.6 us
    ppermute x5, starting transfers between devices, dp_step(): return lax.ppermute(block, 'dp', [(i, i ^ step) for i in range(16)])  5.51 us
    ppermute x5, waiting for transfers between devices, dp_step(): return lax.ppermute(block, 'dp', [(i, i ^ step) for i in range(16)])  5.09 us
    ppermute x4, starting transfers between devices, seq_step(): return lax.ppermute(block, 'seq', [(i, i ^ step) for i in range(16)])  4.31 us
  transfers between devices with their start and end apart: 24, of which 14 were waited for; matrix products, arithmetic and copies ran while one was open for 0% of the time, Pallas kernels for 8%

profile of v1, /device:TPU:32, one launch (start us, length us, event | category | flops | bytes accessed | tf_op | source)
XLA Modules:
  0.0 159.1 jit_solution(1770534570099551799)
XLA Ops:
  0.7 1.1 copy-done.1
  1.8 1.0 copy-done.3
  3.7 0.9 copy-done.15
  5.6 1.5 shard_map.110
  7.0 1.3 collective-permute-start
  8.3 5.7 %collective-permute-start.1 = (bf16[4,256,128]{2,1,0:T(8,128)(2,1)S(1)}, bf16[4,256,128]{2,1,0:T(8,128)(2,1)S(1)}, u32[]{:S(2)}, u32[]{:S(2)}) collective-permute-start(bf16[4,256,128]{2,1,0:T(8,128)(2,1)S(1)} %get-tuple-element.42), channel_id=1, source_target_pairs={{0,2},{2,0},{3,1},{4,6},{6,4},{7,5},{8,10},{10,8},{11,9},{12,14},{... | collective-permute-start | bytes 786440 | tf_op jit(solution)/shard_map/ppermute | solution.py:333
  14.0 3.0 %collective-permute-start.2 = (bf16[4,256,128]{2,1,0:T(8,128)(2,1)S(1)}, bf16[4,256,128]{2,1,0:T(8,128)(2,1)S(1)}, u32[]{:S(2)}, u32[]{:S(2)}) collective-permute-start(bf16[4,256,128]{2,1,0:T(8,128)(2,1)S(1)} %get-tuple-element.43), channel_id=1, source_target_pairs={{1,2},{2,1},{3,0},{5,6},{6,5},{7,4},{9,10},{10,9},{11,8},{13,14},{... | collective-permute-start | bytes 786440 | tf_op jit(solution)/shard_map/ppermute | solution.py:333
  18.5 2.2 %collective-permute-done.1.m2 = bf16[4,256,128]{2,1,0:T(8,128)(2,1)S(1)} collective-permute-done((bf16[4,256,128]{2,1,0:T(8,128)(2,1)S(1)}, bf16[4,256,128]{2,1,0:T(8,128)(2,1)S(1)}, u32[]{:S(2)}, u32[]{:S(2)}) %collective-permute-start.1) | collective-permute-done | bytes 262176 | tf_op jit(solution)/shard_map/ppermute | solution.py:333
  20.7 4.6 %collective-permute-done.2.m3 = bf16[4,256,128]{2,1,0:T(8,128)(2,1)S(1)} collective-permute-done((bf16[4,256,128]{2,1,0:T(8,128)(2,1)S(1)}, bf16[4,256,128]{2,1,0:T(8,128)(2,1)S(1)}, u32[]{:S(2)}, u32[]{:S(2)}) %collective-permute-start.2) | collective-permute-done | bytes 262176 | tf_op jit(solution)/shard_map/ppermute | solution.py:333
  26.1 5.2 %collective-permute-start.3 = (bf16[2,384,128]{2,1,0:T(8,128)(2,1)S(1)}, bf16[2,384,128]{2,1,0:T(8,128)(2,1)S(1)}, u32[]{:S(2)}, u32[]{:S(2)}) collective-permute-start(bf16[2,384,128]{2,1,0:T(8,128)(2,1)S(1)} %get-tuple-element.45), channel_id=1, source_target_pairs={{0,4},{1,5},{2,6},{4,0},{5,1},{6,2},{8,12},{9,13},{10,14},{12,8},{... | collective-permute-start | bytes 589832 | tf_op jit(solution)/shard_map/ppermute | solution.py:333
  31.2 6.6 %collective-permute-start.4 = (bf16[2,128,128]{2,1,0:T(8,128)(2,1)S(1)}, bf16[2,128,128]{2,1,0:T(8,128)(2,1)S(1)}, u32[]{:S(2)}, u32[]{:S(2)}) collective-permute-start(bf16[2,128,128]{2,1,0:T(8,128)(2,1)S(1)} %get-tuple-element.46), channel_id=1, source_target_pairs={{0,8},{1,9},{2,10},{4,12},{5,13},{6,14},{8,0},{9,1},{10,2},{12,4},... | collective-permute-start | bytes 196616 | tf_op jit(solution)/shard_map/ppermute | solution.py:333
  37.9 1.9 %collective-permute-start.5 = (bf16[2,128,128]{2,1,0:T(8,128)(2,1)S(1)}, bf16[2,128,128]{2,1,0:T(8,128)(2,1)S(1)}, u32[]{:S(2)}, u32[]{:S(2)}) collective-permute-start(bf16[2,128,128]{2,1,0:T(8,128)(2,1)S(1)} %get-tuple-element.46), channel_id=1, source_target_pairs={{0,12},{1,13},{2,14},{4,8},{5,9},{6,10},{8,4},{9,5},{10,6},{12,0},... | collective-permute-start | bytes 196616 | tf_op jit(solution)/shard_map/ppermute | solution.py:333
  39.8 3.3 %shard_map.112 = (f32[8,128,128]{2,1,0:T(8,128)S(1)}, f32[8,128,128]{2,1,0:T(8,128)S(1)}, f32[8,128,128]{2,1,0:T(8,128)S(1)}, f32[8,128,128]{2,1,0:T(8,128)S(1)}...) custom-call(s32[3]{0:T(128)S(1)} %pad_add_fusion.info, ...), custom_call_target="tpu_custom_call" | custom-call | flops 1000000000 | bytes 5505024 | tf_op jit(solution)/shard_map/pallas_call | solution.py:310
  43.9 2.4 %collective-permute-done.5.r12 = bf16[2,128,128]{2,1,0:T(8,128)(2,1)S(1)} collective-permute-done((bf16[2,128,128]{2,1,0:T(8,128)(2,1)S(1)}, bf16[2,128,128]{2,1,0:T(8,128)(2,1)S(1)}, u32[]{:S(2)}, u32[]{:S(2)}) %collective-permute-start.5) | collective-permute-done | bytes 65568 | tf_op jit(solution)/shard_map/ppermute | solution.py:333
  46.3 5.2 %shard_map.113 = (f32[8,128,128]{2,1,0:T(8,128)S(1)}, f32[8,128,128]{2,1,0:T(8,128)S(1)}, f32[8,128,128]{2,1,0:T(8,128)S(1)}, f32[3,8,128,128]{3,2,1,0:T(8,128)}...) custom-call(s32[3]{0:T(128)S(1)} %pad_add_fusion.info, ...), custom_call_target="tpu_custom_call" | custom-call | flops 1000000000 | bytes 6684672 | tf_op jit(solution)/shard_map/pallas_call | solution.py:310
  52.3 1.3 collective-permute-start.6
  53.6 6.6 %collective-permute-start.7 = (bf16[256,128]{1,0:T(8,128)(2,1)S(1)}, bf16[256,128]{1,0:T(8,128)(2,1)S(1)}, u32[]{:S(2)}, u32[]{:S(2)}) collective-permute-start(bf16[256,128]{1,0:T(8,128)(2,1)S(1)} %get-tuple-element.52), channel_id=1, source_target_pairs={{0,2},{1,3},{2,0},{4,6},{5,7},{6,4},{8,10},{9,11},{10,8},{12,14},{... | collective-permute-start | bytes 196616 | tf_op jit(solution)/shard_map/ppermute | solution.py:333
  60.3 1.9 %collective-permute-start.8 = (bf16[256,128]{1,0:T(8,128)(2,1)S(1)}, bf16[256,128]{1,0:T(8,128)(2,1)S(1)}, u32[]{:S(2)}, u32[]{:S(2)}) collective-permute-start(bf16[256,128]{1,0:T(8,128)(2,1)S(1)} %get-tuple-element.53), channel_id=1, source_target_pairs={{0,3},{1,2},{2,1},{4,7},{5,6},{6,5},{8,11},{9,10},{10,9},{12,15},{... | collective-permute-start | bytes 196616 | tf_op jit(solution)/shard_map/ppermute | solution.py:333
  62.5 6.3 %collective-permute-done.8.m3 = bf16[256,128]{1,0:T(8,128)(2,1)S(1)} collective-permute-done((bf16[256,128]{1,0:T(8,128)(2,1)S(1)}, bf16[256,128]{1,0:T(8,128)(2,1)S(1)}, u32[]{:S(2)}, u32[]{:S(2)}) %collective-permute-start.8) | collective-permute-done | bytes 65568 | tf_op jit(solution)/shard_map/ppermute | solution.py:333
  68.8 2.2 %shard_map.114 = (bf16[256,768]{1,0:T(8,128)(2,1)}, bf16[384,384]{1,0:T(8,128)(2,1)}, f32[384,384]{1,0:T(8,128)S(1)}) custom-call(s32[3]{0:T(128)S(1)} %pad_add_fusion.info, bf16[256,128]{1,0:T(8,128)(2,1)S(1)} %get-tuple-element.50.m0, bf16[256,128]{1,0:T(8,128)(2,1)S(1)} %collective-permute-done.6.m1, bf16[256,128]{1,0:T(8,128)(2,1)S(1)} %collective-permute-done.7.m2, ...), custom_call_target="tpu_custom_call" | custom-call | flops 300000000 | bytes 2523136 | tf_op jit(solution)/shard_map/pallas_call | solution.py:310
  71.8 1.9 %collective-permute-done.15 = bf16[384,384]{1,0:T(8,128)(2,1)} collective-permute-done((bf16[384,384]{1,0:T(8,128)(2,1)}, bf16[384,384]{1,0:T(8,128)(2,1)}, u32[]{:S(2)}, u32[]{:S(2)}) %collective-permute-start.15) | collective-permute-done | bytes 294944 | tf_op jit(solution)/shard_map/ppermute | solution.py:337
  73.7 1.2 convert_add_fusion
  76.5 7.7 %collective-permute-done.16 = bf16[8,24,384]{2,1,0:T(8,128)(2,1)} collective-permute-done((bf16[8,24,384]{2,1,0:T(8,128)(2,1)}, bf16[8,24,384]{2,1,0:T(8,128)(2,1)}, u32[]{:S(2)}, u32[]{:S(2)}) %collective-permute-start.16) | collective-permute-done | bytes 147488 | tf_op jit(solution)/shard_map/ppermute | solution.py:341
  84.2 1.2 bitcast_add_fusion
  86.7 4.7 %collective-permute-done.17 = bf16[4,24,384]{2,1,0:T(8,128)(2,1)} collective-permute-done((bf16[4,24,384]{2,1,0:T(8,128)(2,1)}, bf16[4,24,384]{2,1,0:T(8,128)(2,1)}, u32[]{:S(2)}, u32[]{:S(2)}) %collective-permute-start.17) | collective-permute-done | bytes 73760 | tf_op jit(solution)/shard_map/ppermute | solution.py:341
  91.4 1.0 fusion.2
  93.7 1.4 collective-permute-start.18
  95.1 3.7 %collective-permute-done.18 = bf16[2,24,384]{2,1,0:T(8,128)(2,1)} collective-permute-done((bf16[2,24,384]{2,1,0:T(8,128)(2,1)}, bf16[2,24,384]{2,1,0:T(8,128)(2,1)}, u32[]{:S(2)}, u32[]{:S(2)}) %collective-permute-start.18) | collective-permute-done | bytes 36896 | tf_op jit(solution)/shard_map/ppermute | solution.py:341
  98.9 1.0 fusion.6
  99.8 2.9 %collective-permute-start.19 = (bf16[1,24,384]{2,1,0:T(8,128)(2,1)S(1)}, bf16[1,24,384]{2,1,0:T(8,128)(2,1)S(1)}, u32[]{:S(2)}, u32[]{:S(2)}) collective-permute-start(bf16[1,24,384]{2,1,0:T(8,128)(2,1)S(1)} %fusion.9), channel_id=1, source_target_pairs={{0,8},{1,9},{2,10},{3,11},{4,12},{5,13},{6,14},{7,15},{8,0},{9,1},... | collective-permute-start | bytes 55304 | tf_op jit(solution)/shard_map/ppermute | solution.py:341
  102.7 4.9 %collective-permute-done.19 = bf16[1,24,384]{2,1,0:T(8,128)(2,1)S(1)} collective-permute-done((bf16[1,24,384]{2,1,0:T(8,128)(2,1)S(1)}, bf16[1,24,384]{2,1,0:T(8,128)(2,1)S(1)}, u32[]{:S(2)}, u32[]{:S(2)}) %collective-permute-start.19) | collective-permute-done | bytes 18464 | tf_op jit(solution)/shard_map/ppermute | solution.py:341
  108.3 3.2 %collective-permute-done.20 = bf16[24,384]{1,0:T(8,128)(2,1)S(1)} collective-permute-done((bf16[24,384]{1,0:T(8,128)(2,1)S(1)}, bf16[24,384]{1,0:T(8,128)(2,1)S(1)}, u32[]{:S(2)}, u32[]{:S(2)}) %collective-permute-start.20) | collective-permute-done | bytes 18464 | tf_op jit(solution)/shard_map/ppermute | solution.py:337
  111.5 1.8 %collective-permute-start.21 = (bf16[24,384]{1,0:T(8,128)(2,1)S(1)}, bf16[24,384]{1,0:T(8,128)(2,1)S(1)}, u32[]{:S(2)}, u32[]{:S(2)}) collective-permute-start(bf16[24,384]{1,0:T(8,128)(2,1)S(1)} %add_convert_fusion.1), channel_id=1, source_target_pairs={{0,64},{16,80},{32,96},{48,112},{64,0},{80,16},{96,32},{112,48},{1... | collective-permute-start | bytes 55304 | tf_op jit(solution)/shard_map/ppermute | solution.py:337
  113.3 3.3 %collective-permute-start.9 = (bf16[2,384,128]{2,1,0:T(8,128)(2,1)}, bf16[2,384,128]{2,1,0:T(8,128)(2,1)S(1)}, u32[]{:S(2)}, u32[]{:S(2)}) collective-permute-start(bf16[2,384,128]{2,1,0:T(8,128)(2,1)} %copy-done.18), channel_id=1, source_target_pairs={{0,4},{1,5},{2,6},{4,0},{5,1},{6,2},{8,12},{9,13},{10,14},{12,8},{... | collective-permute-start | bytes 589832 | tf_op jit(solution)/shard_map/ppermute | solution.py:333
  116.7 4.7 %collective-permute-start.10 = (bf16[2,128,128]{2,1,0:T(8,128)(2,1)S(1)}, bf16[2,128,128]{2,1,0:T(8,128)(2,1)S(1)}, u32[]{:S(2)}, u32[]{:S(2)}) collective-permute-start(bf16[2,128,128]{2,1,0:T(8,128)(2,1)S(1)} %get-tuple-element.64), channel_id=1, source_target_pairs={{0,8},{1,9},{2,10},{4,12},{5,13},{6,14},{8,0},{9,1},{10,2},{12,4},... | collective-permute-start | bytes 196616 | tf_op jit(solution)/shard_map/ppermute | solution.py:333
  121.4 4.2 %collective-permute-start.11 = (bf16[2,128,128]{2,1,0:T(8,128)(2,1)S(1)}, bf16[2,128,128]{2,1,0:T(8,128)(2,1)S(1)}, u32[]{:S(2)}, u32[]{:S(2)}) collective-permute-start(bf16[2,128,128]{2,1,0:T(8,128)(2,1)S(1)} %get-tuple-element.65), channel_id=1, source_target_pairs={{0,12},{1,13},{2,14},{4,8},{5,9},{6,10},{8,4},{9,5},{10,6},{12,0},... | collective-permute-start | bytes 196616 | tf_op jit(solution)/shard_map/ppermute | solution.py:333
  125.6 3.0 %collective-permute-start.22 = (bf16[24,384]{1,0:T(8,128)(2,1)S(1)}, bf16[24,384]{1,0:T(8,128)(2,1)S(1)}, u32[]{:S(2)}, u32[]{:S(2)}) collective-permute-start(bf16[24,384]{1,0:T(8,128)(2,1)S(1)} %add_convert_fusion), channel_id=1, source_target_pairs={{0,128},{16,144},{32,160},{48,176},{64,192},{80,208},{96,224},{112... | collective-permute-start | bytes 55304 | tf_op jit(solution)/shard_map/ppermute | solution.py:337
  128.6 1.0 copy-done.7
  129.6 1.0 copy-done.9
  130.7 1.0 copy-done.11
  131.7 1.0 copy-done.13
  132.7 6.6 %shard_map.115.acc_in = f32[3,8,128,128]{3,2,1,0:T(8,128)} custom-call(s32[3]{0:T(128)S(1)} %pad_add_fusion.info, s32[3,6]{1,0:T(4,128)S(1)} %copy-done.17, s32[1]{0:T(128)S(6)} %copy.42.counts, bf16[4,8,128,128]{3,2,1,0:T(8,128)(2,1)S(1)} %get-tuple-element.44.x, f32[8,128,128]{2,1,0:T(8,128)S(1)} %copy-done.9, f32[8,128,128]{2,1,0:T(8,128)S(1)} %copy-done.11, ...), custom_call_target="tpu_custom_call" | custom-call | flops 2000000000 | bytes 8650752 | tf_op jit(solution)/shard_map/pallas_call | solution.py:310
  139.3 1.4 copy-done
  141.6 1.3 collective-permute-start.12
  142.9 3.1 %collective-permute-start.13 = (bf16[3,256,128]{2,1,0:T(8,128)(2,1)S(1)}, bf16[3,256,128]{2,1,0:T(8,128)(2,1)S(1)}, u32[]{:S(2)}, u32[]{:S(2)}) collective-permute-start(bf16[3,256,128]{2,1,0:T(8,128)(2,1)S(1)} %get-tuple-element.68), channel_id=1, source_target_pairs={{0,2},{1,3},{2,0},{4,6},{5,7},{6,4},{8,10},{9,11},{10,8},{12,14},{... | collective-permute-start | bytes 589832 | tf_op jit(solution)/shard_map/ppermute | solution.py:333
  146.0 3.7 %collective-permute-start.14 = (bf16[3,256,128]{2,1,0:T(8,128)(2,1)S(1)}, bf16[3,256,128]{2,1,0:T(8,128)(2,1)S(1)}, u32[]{:S(2)}, u32[]{:S(2)}) collective-permute-start(bf16[3,256,128]{2,1,0:T(8,128)(2,1)S(1)} %get-tuple-element.69), channel_id=1, source_target_pairs={{0,3},{1,2},{2,1},{4,7},{5,6},{6,5},{8,11},{9,10},{10,9},{12,15},{... | collective-permute-start | bytes 589832 | tf_op jit(solution)/shard_map/ppermute | solution.py:333
  150.5 5.5 %collective-permute-done.14.m3 = bf16[3,256,128]{2,1,0:T(8,128)(2,1)S(1)} collective-permute-done((bf16[3,256,128]{2,1,0:T(8,128)(2,1)S(1)}, bf16[3,256,128]{2,1,0:T(8,128)(2,1)S(1)}, u32[]{:S(2)}, u32[]{:S(2)}) %collective-permute-start.14) | collective-permute-done | bytes 196640 | tf_op jit(solution)/shard_map/ppermute | solution.py:333
  156.0 1.7 %shard_map.117 = (bf16[256,384]{1,0:T(8,128)(2,1)}, bf16[256,384]{1,0:T(8,128)(2,1)}, bf16[256,384]{1,0:T(8,128)(2,1)}) custom-call(s32[3]{0:T(128)S(1)} %pad_add_fusion.info, bf16[3,256,128]{2,1,0:T(8,128)(2,1)S(1)} %get-tuple-element.66.m0, bf16[3,256,128]{2,1,0:T(8,128)(2,1)S(1)} %collective-permute-done.12.m1, ...), custom_call_target="tpu_custom_call" | custom-call | bytes 1376256 | tf_op jit(solution)/shard_map/pallas_call | solution.py:310
  (71 shorter events, 14.1 us)
Async XLA Ops:
  0.6 24.7 %copy-start.17 = (s32[3,6]{1,0:T(4,128)S(1)}, s32[3,6]{1,0:T(4,128)}, u32[]{:S(2)}) copy-start(s32[3,6]{1,0:T(4,128)} %offsets.9) | copy-start | bytes 220
  0.7 1.1 copy-start.1
  1.8 1.0 copy-start.3
  2.8 0.9 copy-start.14
  3.7 0.9 copy-start.15
  4.6 0.9 copy-start.16
  7.0 11.5 %collective-permute-start = (bf16[4,256,128]{2,1,0:T(8,128)(2,1)S(1)}, bf16[4,256,128]{2,1,0:T(8,128)(2,1)S(1)}, u32[]{:S(2)}, u32[]{:S(2)}) collective-permute-start(bf16[4,256,128]{2,1,0:T(8,128)(2,1)S(1)} %get-tuple-element.41), channel_id=1, source_target_pairs={{0,1},{1,0},{3,2},{4,5},{5,4},{7,6},{8,9},{9,8},{11,10},{12,13},{1... | collective-permute-start | bytes 786440 | tf_op jit(solution)/shard_map/ppermute | solution.py:333
  8.3 12.4 %collective-permute-start.1 = (bf16[4,256,128]{2,1,0:T(8,128)(2,1)S(1)}, bf16[4,256,128]{2,1,0:T(8,128)(2,1)S(1)}, u32[]{:S(2)}, u32[]{:S(2)}) collective-permute-start(bf16[4,256,128]{2,1,0:T(8,128)(2,1)S(1)} %get-tuple-element.42), channel_id=1, source_target_pairs={{0,2},{2,0},{3,1},{4,6},{6,4},{7,5},{8,10},{10,8},{11,9},{12,14},{... | collective-permute-start | bytes 786440 | tf_op jit(solution)/shard_map/ppermute | solution.py:333
  14.0 11.3 %collective-permute-start.2 = (bf16[4,256,128]{2,1,0:T(8,128)(2,1)S(1)}, bf16[4,256,128]{2,1,0:T(8,128)(2,1)S(1)}, u32[]{:S(2)}, u32[]{:S(2)}) collective-permute-start(bf16[4,256,128]{2,1,0:T(8,128)(2,1)S(1)} %get-tuple-element.43), channel_id=1, source_target_pairs={{1,2},{2,1},{3,0},{5,6},{6,5},{7,4},{9,10},{10,9},{11,8},{13,14},{... | collective-permute-start | bytes 786440 | tf_op jit(solution)/shard_map/ppermute | solution.py:333
  26.1 20.3 %collective-permute-start.3 = (bf16[2,384,128]{2,1,0:T(8,128)(2,1)S(1)}, bf16[2,384,128]{2,1,0:T(8,128)(2,1)S(1)}, u32[]{:S(2)}, u32[]{:S(2)}) collective-permute-start(bf16[2,384,128]{2,1,0:T(8,128)(2,1)S(1)} %get-tuple-element.45), channel_id=1, source_target_pairs={{0,4},{1,5},{2,6},{4,0},{5,1},{6,2},{8,12},{9,13},{10,14},{12,8},{... | collective-permute-start | bytes 589832 | tf_op jit(solution)/shard_map/ppermute | solution.py:333
  31.2 12.6 %collective-permute-start.4 = (bf16[2,128,128]{2,1,0:T(8,128)(2,1)S(1)}, bf16[2,128,128]{2,1,0:T(8,128)(2,1)S(1)}, u32[]{:S(2)}, u32[]{:S(2)}) collective-permute-start(bf16[2,128,128]{2,1,0:T(8,128)(2,1)S(1)} %get-tuple-element.46), channel_id=1, source_target_pairs={{0,8},{1,9},{2,10},{4,12},{5,13},{6,14},{8,0},{9,1},{10,2},{12,4},... | collective-permute-start | bytes 196616 | tf_op jit(solution)/shard_map/ppermute | solution.py:333
  37.9 8.4 %collective-permute-start.5 = (bf16[2,128,128]{2,1,0:T(8,128)(2,1)S(1)}, bf16[2,128,128]{2,1,0:T(8,128)(2,1)S(1)}, u32[]{:S(2)}, u32[]{:S(2)}) collective-permute-start(bf16[2,128,128]{2,1,0:T(8,128)(2,1)S(1)} %get-tuple-element.46), channel_id=1, source_target_pairs={{0,12},{1,13},{2,14},{4,8},{5,9},{6,10},{8,4},{9,5},{10,6},{12,0},... | collective-permute-start | bytes 196616 | tf_op jit(solution)/shard_map/ppermute | solution.py:333
  43.1 0.8 copy-start.6
  46.3 22.5 %copy-start.2 = (bf16[384,768]{1,0:T(8,128)(2,1)S(1)}, bf16[384,768]{1,0:T(8,128)(2,1)}, u32[]{:S(2)}) copy-start(bf16[384,768]{1,0:T(8,128)(2,1)} %w.3) | copy-start | bytes 1769476
  46.3 22.5 %copy-start.4 = (bf16[1,256,768]{2,1,0:T(8,128)(2,1)S(1)}, bf16[1,256,768]{2,1,0:T(8,128)(2,1)}, u32[]{:S(2)}) copy-start(bf16[1,256,768]{2,1,0:T(8,128)(2,1)} %param.11) | copy-start | bytes 1179652
  51.5 0.8 copy-start.12
  52.3 18.7 %copy-start.8 = (f32[8,128,128]{2,1,0:T(8,128)}, f32[8,128,128]{2,1,0:T(8,128)S(1)}, u32[]{:S(2)}) copy-start(f32[8,128,128]{2,1,0:T(8,128)S(1)} %get-tuple-element.55.top) | copy-start | bytes 1572868
  52.3 19.5 %copy-start.10 = (f32[8,128,128]{2,1,0:T(8,128)}, f32[8,128,128]{2,1,0:T(8,128)S(1)}, u32[]{:S(2)}) copy-start(f32[8,128,128]{2,1,0:T(8,128)S(1)} %get-tuple-element.56.norm) | copy-start | bytes 1572868
  52.3 19.5 %copy-start.18 = (bf16[2,384,128]{2,1,0:T(8,128)(2,1)}, bf16[2,384,128]{2,1,0:T(8,128)(2,1)S(1)}, u32[]{:S(2)}) copy-start(bf16[2,384,128]{2,1,0:T(8,128)(2,1)S(1)} %get-tuple-element.63) | copy-start | bytes 589828
  52.3 9.9 %collective-permute-start.6 = (bf16[256,128]{1,0:T(8,128)(2,1)S(1)}, bf16[256,128]{1,0:T(8,128)(2,1)S(1)}, u32[]{:S(2)}, u32[]{:S(2)}) collective-permute-start(bf16[256,128]{1,0:T(8,128)(2,1)S(1)} %get-tuple-element.51), channel_id=1, source_target_pairs={{0,1},{1,0},{2,3},{4,5},{5,4},{6,7},{8,9},{9,8},{10,11},{12,13},{1... | collective-permute-start | bytes 196616 | tf_op jit(solution)/shard_map/ppermute | solution.py:333
  53.6 8.9 %collective-permute-start.7 = (bf16[256,128]{1,0:T(8,128)(2,1)S(1)}, bf16[256,128]{1,0:T(8,128)(2,1)S(1)}, u32[]{:S(2)}, u32[]{:S(2)}) collective-permute-start(bf16[256,128]{1,0:T(8,128)(2,1)S(1)} %get-tuple-element.52), channel_id=1, source_target_pairs={{0,2},{1,3},{2,0},{4,6},{5,7},{6,4},{8,10},{9,11},{10,8},{12,14},{... | collective-permute-start | bytes 196616 | tf_op jit(solution)/shard_map/ppermute | solution.py:333
  60.3 8.6 %collective-permute-start.8 = (bf16[256,128]{1,0:T(8,128)(2,1)S(1)}, bf16[256,128]{1,0:T(8,128)(2,1)S(1)}, u32[]{:S(2)}, u32[]{:S(2)}) collective-permute-start(bf16[256,128]{1,0:T(8,128)(2,1)S(1)} %get-tuple-element.53), channel_id=1, source_target_pairs={{0,3},{1,2},{2,1},{4,7},{5,6},{6,5},{8,11},{9,10},{10,9},{12,15},{... | collective-permute-start | bytes 196616 | tf_op jit(solution)/shard_map/ppermute | solution.py:333
  71.0 0.8 copy-start.5
  71.8 1.9 %collective-permute-start.15 = (bf16[384,384]{1,0:T(8,128)(2,1)}, bf16[384,384]{1,0:T(8,128)(2,1)}, u32[]{:S(2)}, u32[]{:S(2)}) collective-permute-start(bf16[384,384]{1,0:T(8,128)(2,1)} %get-tuple-element.74), channel_id=1, source_target_pairs={{0,16},{16,0},{32,48},{48,32},{64,80},{80,64},{96,112},{112,96},{1... | collective-permute-start | bytes 884744 | tf_op jit(solution)/shard_map/ppermute | solution.py:337
  74.9 0.8 copy-start.19
  76.5 7.7 %collective-permute-start.16 = (bf16[8,24,384]{2,1,0:T(8,128)(2,1)}, bf16[8,24,384]{2,1,0:T(8,128)(2,1)}, u32[]{:S(2)}, u32[]{:S(2)}) collective-permute-start(bf16[8,24,384]{2,1,0:T(8,128)(2,1)} %fusion), channel_id=1, source_target_pairs={{0,1},{1,0},{2,3},{3,2},{4,5},{5,4},{6,7},{7,6},{8,9},{9,8},{10,11... | collective-permute-start | bytes 442376 | tf_op jit(solution)/shard_map/ppermute | solution.py:341
  85.3 0.7 copy-start.20
  86.7 4.7 %collective-permute-start.17 = (bf16[4,24,384]{2,1,0:T(8,128)(2,1)}, bf16[4,24,384]{2,1,0:T(8,128)(2,1)}, u32[]{:S(2)}, u32[]{:S(2)}) collective-permute-start(bf16[4,24,384]{2,1,0:T(8,128)(2,1)} %fusion.3), channel_id=1, source_target_pairs={{0,2},{1,3},{2,0},{3,1},{4,6},{5,7},{6,4},{7,5},{8,10},{9,11},{10,... | collective-permute-start | bytes 221192 | tf_op jit(solution)/shard_map/ppermute | solution.py:341
  92.4 0.7 copy-start.21
  93.7 5.2 %collective-permute-start.18 = (bf16[2,24,384]{2,1,0:T(8,128)(2,1)}, bf16[2,24,384]{2,1,0:T(8,128)(2,1)}, u32[]{:S(2)}, u32[]{:S(2)}) collective-permute-start(bf16[2,24,384]{2,1,0:T(8,128)(2,1)} %fusion.7), channel_id=1, source_target_pairs={{0,4},{1,5},{2,6},{3,7},{4,0},{5,1},{6,2},{7,3},{8,12},{9,13},{10,... | collective-permute-start | bytes 110600 | tf_op jit(solution)/shard_map/ppermute | solution.py:341
  99.8 7.8 %collective-permute-start.19 = (bf16[1,24,384]{2,1,0:T(8,128)(2,1)S(1)}, bf16[1,24,384]{2,1,0:T(8,128)(2,1)S(1)}, u32[]{:S(2)}, u32[]{:S(2)}) collective-permute-start(bf16[1,24,384]{2,1,0:T(8,128)(2,1)S(1)} %fusion.9), channel_id=1, source_target_pairs={{0,8},{1,9},{2,10},{3,11},{4,12},{5,13},{6,14},{7,15},{8,0},{9,1},... | collective-permute-start | bytes 55304 | tf_op jit(solution)/shard_map/ppermute | solution.py:341
  107.6 3.8 %collective-permute-start.20 = (bf16[24,384]{1,0:T(8,128)(2,1)S(1)}, bf16[24,384]{1,0:T(8,128)(2,1)S(1)}, u32[]{:S(2)}, u32[]{:S(2)}) collective-permute-start(bf16[24,384]{1,0:T(8,128)(2,1)S(1)} %fusion.10), channel_id=1, source_target_pairs={{0,32},{16,48},{32,0},{48,16},{64,96},{80,112},{96,64},{112,80},{1... | collective-permute-start | bytes 55304 | tf_op jit(solution)/shard_map/ppermute | solution.py:337
  111.5 14.1 %collective-permute-start.21 = (bf16[24,384]{1,0:T(8,128)(2,1)S(1)}, bf16[24,384]{1,0:T(8,128)(2,1)S(1)}, u32[]{:S(2)}, u32[]{:S(2)}) collective-permute-start(bf16[24,384]{1,0:T(8,128)(2,1)S(1)} %add_convert_fusion.1), channel_id=1, source_target_pairs={{0,64},{16,80},{32,96},{48,112},{64,0},{80,16},{96,32},{112,48},{1... | collective-permute-start | bytes 55304 | tf_op jit(solution)/shard_map/ppermute | solution.py:337
  113.3 26.0 %collective-permute-start.9 = (bf16[2,384,128]{2,1,0:T(8,128)(2,1)}, bf16[2,384,128]{2,1,0:T(8,128)(2,1)S(1)}, u32[]{:S(2)}, u32[]{:S(2)}) collective-permute-start(bf16[2,384,128]{2,1,0:T(8,128)(2,1)} %copy-done.18), channel_id=1, source_target_pairs={{0,4},{1,5},{2,6},{4,0},{5,1},{6,2},{8,12},{9,13},{10,14},{12,8},{... | collective-permute-start | bytes 589832 | tf_op jit(solution)/shard_map/ppermute | solution.py:333
  116.7 22.6 %collective-permute-start.10 = (bf16[2,128,128]{2,1,0:T(8,128)(2,1)S(1)}, bf16[2,128,128]{2,1,0:T(8,128)(2,1)S(1)}, u32[]{:S(2)}, u32[]{:S(2)}) collective-permute-start(bf16[2,128,128]{2,1,0:T(8,128)(2,1)S(1)} %get-tuple-element.64), channel_id=1, source_target_pairs={{0,8},{1,9},{2,10},{4,12},{5,13},{6,14},{8,0},{9,1},{10,2},{12,4},... | collective-permute-start | bytes 196616 | tf_op jit(solution)/shard_map/ppermute | solution.py:333
  121.4 17.9 %collective-permute-start.11 = (bf16[2,128,128]{2,1,0:T(8,128)(2,1)S(1)}, bf16[2,128,128]{2,1,0:T(8,128)(2,1)S(1)}, u32[]{:S(2)}, u32[]{:S(2)}) collective-permute-start(bf16[2,128,128]{2,1,0:T(8,128)(2,1)S(1)} %get-tuple-element.65), channel_id=1, source_target_pairs={{0,12},{1,13},{2,14},{4,8},{5,9},{6,10},{8,4},{9,5},{10,6},{12,0},... | collective-permute-start | bytes 196616 | tf_op jit(solution)/shard_map/ppermute | solution.py:333
  125.6 24.2 %copy-start.22 = (bf16[24,384]{1,0:T(8,128)(2,1)}, bf16[24,384]{1,0:T(8,128)(2,1)S(1)}, u32[]{:S(2)}) copy-start(bf16[24,384]{1,0:T(8,128)(2,1)S(1)} %add_convert_fusion) | copy-start | bytes 55300
  125.6 24.1 %collective-permute-start.22 = (bf16[24,384]{1,0:T(8,128)(2,1)S(1)}, bf16[24,384]{1,0:T(8,128)(2,1)S(1)}, u32[]{:S(2)}, u32[]{:S(2)}) collective-permute-start(bf16[24,384]{1,0:T(8,128)(2,1)S(1)} %add_convert_fusion), channel_id=1, source_target_pairs={{0,128},{16,144},{32,160},{48,176},{64,192},{80,208},{96,224},{112... | collective-permute-start | bytes 55304 | tf_op jit(solution)/shard_map/ppermute | solution.py:337
  128.6 1.0 copy-start.7
  129.6 1.0 copy-start.9
  130.7 1.0 copy-start.11
  131.7 1.0 copy-start.13
  139.3 1.4 copy-start
  141.6 8.7 %collective-permute-start.12 = (bf16[3,256,128]{2,1,0:T(8,128)(2,1)S(1)}, bf16[3,256,128]{2,1,0:T(8,128)(2,1)S(1)}, u32[]{:S(2)}, u32[]{:S(2)}) collective-permute-start(bf16[3,256,128]{2,1,0:T(8,128)(2,1)S(1)} %get-tuple-element.67), channel_id=1, source_target_pairs={{0,1},{1,0},{2,3},{4,5},{5,4},{6,7},{8,9},{9,8},{10,11},{12,13},{1... | collective-permute-start | bytes 589832 | tf_op jit(solution)/shard_map/ppermute | solution.py:333
  142.9 7.6 %collective-permute-start.13 = (bf16[3,256,128]{2,1,0:T(8,128)(2,1)S(1)}, bf16[3,256,128]{2,1,0:T(8,128)(2,1)S(1)}, u32[]{:S(2)}, u32[]{:S(2)}) collective-permute-start(bf16[3,256,128]{2,1,0:T(8,128)(2,1)S(1)} %get-tuple-element.68), channel_id=1, source_target_pairs={{0,2},{1,3},{2,0},{4,6},{5,7},{6,4},{8,10},{9,11},{10,8},{12,14},{... | collective-permute-start | bytes 589832 | tf_op jit(solution)/shard_map/ppermute | solution.py:333
  146.0 10.0 %collective-permute-start.14 = (bf16[3,256,128]{2,1,0:T(8,128)(2,1)S(1)}, bf16[3,256,128]{2,1,0:T(8,128)(2,1)S(1)}, u32[]{:S(2)}, u32[]{:S(2)}) collective-permute-start(bf16[3,256,128]{2,1,0:T(8,128)(2,1)S(1)} %get-tuple-element.69), channel_id=1, source_target_pairs={{0,3},{1,2},{2,1},{4,7},{5,6},{6,5},{8,11},{9,10},{10,9},{12,15},{... | collective-permute-start | bytes 589832 | tf_op jit(solution)/shard_map/ppermute | solution.py:333
  149.7 0.6 copy-start.23
  150.4 7.4 %collective-permute-start.23 = (f32[24,384]{1,0:T(8,128)S(1)}, f32[24,384]{1,0:T(8,128)S(1)}, u32[]{:S(2)}, u32[]{:S(2)}) collective-permute-start(f32[24,384]{1,0:T(8,128)S(1)} %convert_add_fusion.1), channel_id=1, source_target_pairs={{0,16},{16,0},{32,48},{48,32},{64,80},{80,64},{96,112},{112,96},{1... | collective-permute-start | bytes 110600 | tf_op jit(solution)/shard_map/ppermute | solution.py:337

commit v2 on v1

v2 whole, which is shorter than its diff:
```python
import jax
import jax.numpy as jnp
from jax import lax
from jax.experimental import pallas as pl
from jax.experimental.pallas import tpu as pltpu
from jax.sharding import PartitionSpec as P

bf16 = jnp.bfloat16
f32 = jnp.float32
low_bias = -1e30


def dot_nn(a, b):
    return lax.dot_general(a, b, (((1,), (0,)), ((), ())), preferred_element_type=f32)


def dot_nt(a, b):
    return lax.dot_general(a, b, (((1,), (1,)), ((), ())), preferred_element_type=f32)


def dot_tn(a, b):
    return lax.dot_general(a, b, (((0,), (0,)), ((), ())), preferred_element_type=f32)


def first_half(rows):
    return lax.broadcasted_iota(jnp.int32, (rows, 128), 1) < 64


def half_of(x, h):
    m = first_half(x.shape[0])
    z = jnp.zeros_like(x)
    return jnp.where(m, x, z) if h == 0 else jnp.where(m, z, x)


def row_order(back):
    a = lax.broadcasted_iota(jnp.int32, (256, 256), 0 if not back else 1)
    b = lax.broadcasted_iota(jnp.int32, (256, 256), 1 if not back else 0)
    return jnp.where(b == (a & 31) * 8 + (a >> 5), 1.0, 0.0).astype(bf16)


class Place:
    def __init__(self, info, offsets, counts):
        self.j = info[0] & 3
        self.base = (info[0] >> 2) * 1024
        self.quarter = info[0] >> 2
        self.chunk = jnp.minimum(info[1], 2)
        self.count = counts[0]
        self.offsets = offsets

    def offs(self, pair):
        r = 2 << pair
        return [self.offsets[pair, 2 * self.chunk + h] & (r - 1) for h in (0, 1)]

    def bias(self, n, step, o, base):
        kk = lax.broadcasted_iota(jnp.int32, (1, n), 1)
        pos = base + ((self.j ^ ((kk >> 5) & 3)) << 8) + (kk & 31) * 8 + o + step * (kk >> 7)
        return jnp.where(pos < self.count, 0.0, low_bias)

    def bias_slot(self, slot):
        kk = lax.broadcasted_iota(jnp.int32, (1, 256), 1)
        pos = self.base + ((self.j ^ slot) << 8) + (kk & 31) * 8 + (kk >> 5)
        return jnp.where(pos < self.count, 0.0, low_bias)

    def valid(self, res):
        rr = lax.broadcasted_iota(jnp.int32, (128, 128), 0)
        pos = self.base + ((self.j ^ (rr >> 5)) << 8) + (rr & 31) * 8 + res
        return jnp.where(pos < self.count, 1.0, 0.0)


def pick(read, pair, oo):
    r = 2 << pair
    m = first_half(128)
    parts = [jnp.where(m, read(oo[0] + r * i), read(oo[1] + r * i)) for i in range(8 // r)]
    return parts[0] if len(parts) == 1 else jnp.concatenate(parts, axis=0)


def put(read, write, val, pair, oo, add):
    r = 2 << pair
    m = first_half(128)
    for i in range(8 // r):
        blk = val[i * 128 : (i + 1) * 128]
        for h in (0, 1):
            mine = m if h == 0 else ~m
            old = read(oo[h] + r * i)
            write(oo[h] + r * i, jnp.where(mine, old + blk if add else blk, old))


def reader(ref, *lead):
    return lambda i: ref[(*lead, i)]


def writer(ref, *lead):
    def w(i, val):
        ref[(*lead, i)] = val

    return w


def slot_rows(ref, slot, *lead):
    return ref[(*lead, slice(None), slice(slot * 32, slot * 32 + 32), slice(None))].reshape(256, 128)


def attend(q2, k2, v2, bias):
    nk = k2.shape[0]
    out, es, ms = None, [], []
    one = jnp.ones((nk, 128), bf16)
    for h in (0, 1):
        s = dot_nt(q2, half_of(k2, h)) + bias[h]
        m = jnp.max(s, axis=1, keepdims=True)
        e = jnp.exp(s - m).astype(bf16)
        o = dot_nn(e, jnp.concatenate([half_of(v2, h), half_of(one, h)], axis=1))
        out = o if out is None else out + o
        es.append(e)
        ms.append(m)
    n = q2.shape[0]
    top = jnp.where(first_half(n), jnp.broadcast_to(ms[0], (n, 128)), jnp.broadcast_to(ms[1], (n, 128)))
    return es, top, out


def back(q2, k2, v2, gf2, fd2, es):
    dq = dk = dv = None
    for h in (0, 1):
        kh, vh = half_of(k2, h), half_of(v2, h)
        e = es[h]
        dp = dot_nt(gf2, vh)
        ds = (e.astype(f32) * (dp - fd2[:, 64 * h : 64 * h + 1])).astype(bf16)
        a, b, c = dot_nn(ds, kh), dot_tn(ds, half_of(q2, h)), dot_tn(e, half_of(gf2, h))
        dq, dk, dv = (a, b, c) if dq is None else (dq + a, dk + b, dv + c)
    return dq, dk, dv


def copies(pairs, sems):
    moves = [pltpu.make_async_copy(src, dst, sems.at[i]) for i, (src, dst) in enumerate(pairs)]
    for m in moves:
        m.start()
    return moves


def prep_body(
    info, q_in, k_in, v_in, og_in, w_in, o0, o1, o2, o3, og_out, px, q, k, v, og, w, sems
):
    moves = copies(((og_in, og), (w_in, w), (q_in, q), (k_in, k), (v_in, v)), sems)
    order = row_order(False)
    moves[0].wait()
    ordered = dot_nn(order, og[...]).astype(bf16)
    og_out[...] = ordered
    moves[1].wait()
    px[1] = dot_nt(ordered, w[...]).astype(bf16)
    moves[2].wait()
    px[0] = (dot_nn(order, q[...]) * 0.125).astype(bf16)
    moves[3].wait()
    px[2] = dot_nn(order, k[...]).astype(bf16)
    moves[4].wait()
    px[3] = dot_nn(order, v[...]).astype(bf16)
    for d, o in enumerate((o0, o1, o2, o3)):
        c = pl.multiple_of(jnp.minimum(info[1] ^ d, 2) * 128, 128)
        for i in range(4):
            o[i] = px[i, :, pl.ds(c, 128)]


def collect_body(info, offsets, counts, m0, m1, m2, m3, qg, kv, s4, s8):
    place = Place(info, offsets, counts)
    for slot, m in enumerate((m0, m1, m2, m3)):
        for i in range(4):
            x = (qg, kv)[i // 2]
            x[i % 2, :, slot * 32 : slot * 32 + 32, :] = m[i].reshape(8, 32, 128)
    o3, o4 = place.offs(1), place.offs(2)
    for i in (0, 1):
        s4[i, 0:256] = pick(reader(kv, i), 1, o3)
        last = pick(reader(kv, i), 2, o4)
        s4[i, 256:384] = last
        s8[i] = last


def near_body(
    info, offsets, counts, qg, kv, top, num, den, m1, m2, e1, e2,
):
    place = Place(info, offsets, counts)
    for slot in range(4):
        b = place.bias_slot(slot)
        sl = slice(slot * 32, slot * 32 + 32)
        es, t, o = attend(slot_rows(qg, slot, 0), slot_rows(kv, slot, 0), slot_rows(kv, slot, 1), [b, b])
        e1[slot, 0], e1[slot, 1] = es
        t = t.reshape(8, 32, 128)
        top[:, sl, :] = t
        m1[:, sl, :] = t
        num[:, sl, :] = o[:, :128].reshape(8, 32, 128)
        den[:, sl, :] = o[:, 128:].reshape(8, 32, 128)
    oo = place.offs(0)
    q2, k2, v2 = [pick(r, 0, oo) for r in (reader(qg, 0), reader(kv, 0), reader(kv, 1))]
    bias = [place.bias(512, 2, oo[h], place.base) for h in (0, 1)]
    es, t, o = attend(q2, k2, v2, bias)
    e2[0], e2[1] = es
    m2[...] = t
    merge(top, num, den, t, o, 0, oo)


def merge(top, num, den, t, o, pair, oo):
    old = pick(reader(top), pair, oo)
    new = jnp.maximum(old, t)
    a, b = jnp.exp(old - new), jnp.exp(t - new)
    n = pick(reader(num), pair, oo) * a + o[:, :128] * b
    d = pick(reader(den), pair, oo) * a + o[:, 128:] * b
    put(reader(top), writer(top), new, pair, oo, False)
    put(reader(num), writer(num), n, pair, oo, False)
    put(reader(den), writer(den), d, pair, oo, False)


def far_keys(place, kv, r4, r8, r12):
    o3, o4 = place.offs(1), place.offs(2)
    k3, v3 = [jnp.concatenate([pick(reader(kv, i), 1, o3), r4[i, 0:256]], axis=0) for i in (0, 1)]
    k4, v4 = [
        jnp.concatenate([pick(reader(kv, i), 2, o4), r4[i, 256:384], r8[i], r12[i]], axis=0) for i in (0, 1)
    ]
    return o3, o4, k3, v3, k4, v4


def far_body(
    info, offsets, counts, kv, qg, r4, r8, r12, top_in, num_in, den_in,
    top, norm, delta, mx0, mx1, mx2, mx3, m3, m4, e3, e4, num, den,
):
    place = Place(info, offsets, counts)
    top[...] = top_in[...]
    num[...] = num_in[...]
    den[...] = den_in[...]
    o3, o4, k3, v3, k4, v4 = far_keys(place, kv, r4, r8, r12)
    at = [(place.quarter ^ i) * 1024 for i in range(4)]
    b3 = [jnp.concatenate([place.bias(256, 4, o3[h], at[i]) for i in (0, 1)], axis=1) for h in (0, 1)]
    b4 = [jnp.concatenate([place.bias(128, 8, o4[h], at[i]) for i in range(4)], axis=1) for h in (0, 1)]
    for pair, oo, k2, v2, b, m, e in ((1, o3, k3, v3, b3, m3, e3), (2, o4, k4, v4, b4, m4, e4)):
        es, t, out = attend(pick(reader(qg, 0), pair, oo), k2, v2, b)
        e[0], e[1] = es
        m[...] = t
        merge(top, num, den, t, out, pair, oo)
    ri = lax.broadcasted_iota(jnp.int32, (128, 128), 0) >> 6
    ci = lax.broadcasted_iota(jnp.int32, (128, 128), 1) >> 6
    same = jnp.where(ri == ci, 1.0, 0.0)
    for res in range(8):
        ok = place.valid(res)
        scale = ok / (den[res] + 1.0 - ok)
        norm[res] = scale
        mixed = (num[res] * scale).astype(bf16)
        for slot, mx in enumerate((mx0, mx1, mx2, mx3)):
            mx[res * 32 : res * 32 + 32] = mixed[slot * 32 : slot * 32 + 32]
        prod = qg[1, res].astype(f32) * mixed.astype(f32)
        delta[res] = lax.dot_general(
            prod, same, (((1,), (0,)), ((), ())), precision=lax.Precision.HIGHEST, preferred_element_type=f32
        )


def pair_back(place, kv, qg, top, norm, delta, t, es, pair, oo, k2, v2):
    f2 = jnp.exp(t - pick(reader(top), pair, oo)) * pick(reader(norm), pair, oo)
    gf2 = (pick(reader(qg, 1), pair, oo).astype(f32) * f2).astype(bf16)
    fd2 = f2 * pick(reader(delta), pair, oo)
    return back(pick(reader(qg, 0), pair, oo), k2, v2, gf2, fd2, es)


def far_back_body(
    info, offsets, counts, kv, qg, r4, r8, r12, top, norm, delta, m3, m4, e3, e4,
    acc, d4, d8, d12,
):
    place = Place(info, offsets, counts)
    o3, o4, k3, v3, k4, v4 = far_keys(place, kv, r4, r8, r12)
    acc[...] = jnp.zeros_like(acc)
    for pair, oo, k2, v2, m, e, parts in (
        (1, o3, k3, v3, m3, e3, ((d4, 0, 256),)),
        (2, o4, k4, v4, m4, e4, ((d4, 256, 128), (d8, 0, 128), (d12, 0, 128))),
    ):
        grads = pair_back(place, kv, qg, top, norm, delta, m[...], [e[0], e[1]], pair, oo, k2, v2)
        at_row = m.shape[0]
        for i in range(3):
            put(reader(acc, i), writer(acc, i), grads[i][:at_row], pair, oo, True)
        for ref, start, rows in parts:
            for i in (0, 1):
                ref[i, start : start + rows] = grads[i + 1][at_row : at_row + rows].astype(bf16)
            at_row += rows


def back_two_body(info, offsets, counts, kv, qg, top, norm, delta, acc_in, m2, e2, acc):
    place = Place(info, offsets, counts)
    acc[...] = acc_in[...]
    oo = place.offs(0)
    k2, v2 = pick(reader(kv, 0), 0, oo), pick(reader(kv, 1), 0, oo)
    grads = pair_back(place, kv, qg, top, norm, delta, m2[...], [e2[0], e2[1]], 0, oo, k2, v2)
    for i in range(3):
        put(reader(acc, i), writer(acc, i), grads[i], 0, oo, True)


def back_one_body(info, offsets, counts, kv, qg, top, norm, delta, acc_in, m1, e1, acc):
    for slot in range(4):
        sl = slice(slot * 32, slot * 32 + 32)
        f2 = jnp.exp(slot_rows(m1, slot) - slot_rows(top, slot)) * slot_rows(norm, slot)
        q2, k2, v2, g2 = [slot_rows(r, slot, i) for r, i in ((qg, 0), (kv, 0), (kv, 1), (qg, 1))]
        gf2 = (g2.astype(f32) * f2).astype(bf16)
        fd2 = f2 * slot_rows(delta, slot)
        grads = back(q2, k2, v2, gf2, fd2, [e1[slot, 0], e1[slot, 1]])
        for i in range(3):
            acc[i, :, sl, :] = acc_in[i, :, sl, :] + grads[i].reshape(8, 32, 128)


def cores_body(keep, got, d4, d8, d12, own, f4, f8, f12):
    for u, (d, f) in enumerate(((None, own), (d4, f4), (d8, f8), (d12, f12))):
        part = keep[4 * u : 4 * u + 4] + got[4 * u : 4 * u + 4].astype(f32)
        if u == 0:
            f[...] = part
        else:
            n = d.shape[1]
            f[0:n] = d[0]
            f[n : 2 * n] = d[1]
            f[2 * n : 2 * n + 288] = part.reshape(288, 128).astype(bf16)


def finish_body(info, offsets, counts, acc_in, r4, r8, r12, part, own, o0, o1, o2, o3, acc):
    place = Place(info, offsets, counts)
    acc[...] = acc_in[...]
    p3, p4 = place.offs(1), place.offs(2)
    for i in (0, 1):
        rd, wr = reader(acc, i + 1), writer(acc, i + 1)
        put(rd, wr, r4[i * 384 : i * 384 + 256].astype(f32), 1, p3, True)
        far = r4[i * 384 + 256 : i * 384 + 384].astype(f32)
        far = far + r8[i * 128 : i * 128 + 128].astype(f32) + r12[i * 128 : i * 128 + 128].astype(f32)
        put(rd, wr, far, 2, p4, True)
    grads = [r[n : n + 288].astype(f32).reshape(4, 72, 128) for r, n in ((r4, 768), (r8, 256), (r12, 256))]
    total = part[...] + grads[0] + (grads[1] + grads[2])
    own[...] = total[0]
    for slot, o in enumerate((o0, o1, o2, o3)):
        o[0:256] = (slot_rows(acc, slot, 0) * 0.125).astype(bf16)
        o[256:512] = slot_rows(acc, slot, 1).astype(bf16)
        o[512:768] = slot_rows(acc, slot, 2).astype(bf16)
        o[768:848] = jnp.concatenate([total[slot], jnp.zeros((8, 128), f32)], axis=0).astype(bf16)


def home_body(info, m0, m1, m2, m3, dq, dk, dv, wide):
    order = row_order(True)
    for d, m in enumerate((m0, m1, m2, m3)):
        c = pl.multiple_of((info[1] ^ d) * 128, 128)
        for i in range(3):
            wide[i, :, pl.ds(c, 128)] = m[256 * i : 256 * i + 256]
    for i, o in enumerate((dq, dk, dv)):
        o[...] = dot_nn(order, wide[i, :, 0:384]).astype(bf16)


def near_sum_body(own, m1, m2, m3, o):
    a, b, c = [m[768:848].astype(f32)[0:72] for m in (m1, m2, m3)]
    o[...] = (own[...] + a + (b + c)).astype(bf16)


def widen(info, msgs, wide):
    for d, m in enumerate(msgs):
        wide[:, pl.ds(pl.multiple_of((info[1] ^ d) * 128, 128), 128)] = m[...]


def project_body(info, m0, m1, m2, m3, og, send, keep, wide, both, away):
    widen(info, (m0, m1, m2, m3), wide)
    both[...] = dot_tn(wide[:, 0:384], og[...])
    for s in range(16):
        for t in range(3):
            at = slice(t * 24, t * 24 + 24)
            there = pl.multiple_of((1 - info[2]) * 384 + t * 128, 128)
            here = pl.multiple_of(info[2] * 384 + t * 128, 128)
            away[s ^ info[0], at] = both[s * 24 : s * 24 + 24, pl.ds(there, 128)]
            keep[s ^ info[0], at] = both[s * 24 : s * 24 + 24, pl.ds(here, 128)]
    send[...] = away[...].astype(bf16)


def attended_body(info, m0, m1, m2, m3, w, o, wide):
    widen(info, (m0, m1, m2, m3), wide)
    mixed = dot_nn(row_order(True), wide[:, 0:384]).astype(bf16)
    o[...] = dot_nn(mixed, w[...]).astype(bf16)


def sum_body(a, b, c, d, o):
    one = a[...].astype(f32) + b[...].astype(f32)
    o[...] = (one + (c[...].astype(f32) + d[...].astype(f32))).astype(o.dtype)


def pair_body(a, b, o):
    o[...] = (a[...].astype(f32) + b[...].astype(f32)).astype(o.dtype)


def join_body(info, a, b, o):
    for t in range(3):
        at = slice(t * 24, t * 24 + 24)
        o[:, pl.ds(pl.multiple_of(info[2] * 384 + t * 128, 128), 128)] = a[at]
        o[:, pl.ds(pl.multiple_of((1 - info[2]) * 384 + t * 128, 128), 128)] = b[at]


smem = pl.BlockSpec(memory_space=pltpu.SMEM)
vmem = pl.BlockSpec(memory_space=pltpu.VMEM)
hbm = pl.BlockSpec(memory_space=pltpu.HBM)


def call(body, scalars, arrays, outs, scratch=(), flops=0, space=vmem, sems=0, limit=12):
    shapes = [jax.ShapeDtypeStruct(s, t) for s, t in outs]
    moved = sum(a.size * a.dtype.itemsize for a in arrays) + sum(s.size * s.dtype.itemsize for s in shapes)
    return pl.pallas_call(
        body,
        out_shape=shapes,
        in_specs=[smem] * len(scalars) + [space] * len(arrays),
        out_specs=[vmem] * len(shapes),
        scratch_shapes=[pltpu.VMEM(s, t) for s, t in scratch] + [pltpu.SemaphoreType.DMA((sems,))] * (sems > 0),
        compiler_params=pltpu.CompilerParams(vmem_limit_bytes=limit * 1024 * 1024),
        cost_estimate=pl.CostEstimate(flops=flops, bytes_accessed=moved, transcendentals=0),
    )(*scalars, *arrays)


def routes(seq_step, keep=None):
    pairs = []
    for dp in range(16):
        for s in range(16):
            t = s ^ seq_step
            if keep is not None and (keep(s, t) & 3) ^ (3 * (dp & 1)) == 3:
                continue
            pairs.append((dp * 16 + s, dp * 16 + t))
    return pairs


def shift(block, pairs):
    return lax.ppermute(block, ("dp", "seq"), pairs)


def dp_step(block, step):
    return lax.ppermute(block, "dp", [(i, i ^ step) for i in range(16)])


def seq_step(block, step):
    return lax.ppermute(block, "seq", [(i, i ^ step) for i in range(16)])


def per_device(queries, keys, values, out_weight, out_grad, offsets, counts):
    seq_rank = lax.axis_index("seq").astype(jnp.int32)
    core = lax.axis_index("dp").astype(jnp.int32) & 1
    info = jnp.stack([seq_rank, (seq_rank & 3) ^ (3 * core), core])
    places = [info, offsets, counts]

    chunk = ((4, 256, 128), bf16)
    third = ((256, 384), bf16)
    cube = (8, 128, 128)
    block = (72, 128)
    active = lambda s, t: s

    *msgs, og = call(
        prep_body,
        [info],
        [queries[0], keys[0], values[0], out_grad[0], out_weight],
        [chunk] * 4 + [((256, 768), bf16)],
        [((4, 256, 384), bf16), third, third, third, ((256, 768), bf16), ((384, 768), bf16)],
        space=hbm,
        sems=5,
        limit=60,
    )
    got = [msgs[0]] + [shift(msgs[d], routes(d, lambda s, t: t)) for d in (1, 2, 3)]
    qg, kv, s4, s8 = call(
        collect_body,
        places,
        got,
        [((2, *cube), bf16)] * 2 + [((2, 384, 128), bf16), ((2, 128, 128), bf16)],
    )
    r4 = shift(s4, routes(4, active))
    top, num, den, m1, m2, e1, e2 = call(
        near_body,
        places,
        [qg, kv],
        [(cube, f32)] * 4 + [((512, 128), f32), ((4, 2, 256, 256), bf16), ((2, 512, 512), bf16)],
        flops=10**9,
    )
    s8, top = lax.optimization_barrier((s8, top))
    r8, r12 = [shift(s8, routes(d, active)) for d in (8, 12)]
    top, norm, delta, mx0, mx1, mx2, mx3, m3, m4, e3, e4 = call(
        far_body,
        places,
        [kv, qg, r4, r8, r12, top, num, den],
        [(cube, f32)] * 3
        + [((256, 128), bf16)] * 4
        + [((256, 128), f32), ((128, 128), f32), ((2, 256, 512), bf16), ((2, 128, 512), bf16)],
        [(cube, f32)] * 2,
        flops=10**9,
    )
    mixed = [mx0] + [shift(b, routes(d, active)) for d, b in ((1, mx1), (2, mx2), (3, mx3))]
    state = [kv, qg, top, norm, delta]
    acc, d4, d8, d12 = call(
        far_back_body,
        places,
        [kv, qg, r4, r8, r12, top, norm, delta, m3, m4, e3, e4],
        [((3, *cube), f32), ((2, 384, 128), bf16), ((2, 128, 128), bf16), ((2, 128, 128), bf16)],
        flops=10**9,
    )
    acc, *mixed = lax.optimization_barrier([acc] + mixed)
    send, keep = call(
        project_body,
        [info],
        mixed + [og],
        [((16, *block), bf16), ((16, *block), f32)],
        [((256, 512), bf16), ((384, 768), f32), ((16, *block), f32)],
        flops=3 * 10**8,
    )
    arrived = dp_step(send, 1)
    acc, keep = lax.optimization_barrier((acc, keep))
    (acc,) = call(back_two_body, places, state + [acc, m2, e2], [((3, *cube), f32)], flops=10**9)
    acc, keep = lax.optimization_barrier((acc, keep))
    part, f4, f8, f12 = call(
        cores_body,
        [],
        [keep, arrived, d4, d8, d12],
        [((4, *block), f32), ((1056, 128), bf16), ((544, 128), bf16), ((544, 128), bf16)],
    )
    f4, f8, f12 = [shift(b, routes(d)) for d, b in ((4, f4), (8, f8), (12, f12))]
    acc, part, *mixed = lax.optimization_barrier([acc, part] + mixed)
    (attended,) = call(
        attended_body, [info], mixed + [out_weight], [((256, 768), bf16)], [((256, 512), bf16)], flops=3 * 10**8
    )
    (acc,) = call(back_one_body, places, state + [acc, m1, e1], [((3, *cube), f32)], flops=10**9)
    own, *outs = call(
        finish_body,
        places,
        [acc, f4, f8, f12, part],
        [(block, f32)] + [((848, 128), bf16)] * 4,
        [((3, *cube), f32)],
    )
    home = [outs[0]] + [shift(outs[d], routes(d)) for d in (1, 2, 3)]
    (own,) = call(near_sum_body, [], [own] + home[1:], [(block, bf16)])
    arrived = dp_step(own, 2)
    home = lax.optimization_barrier([own] + home)[1:]
    grads = call(home_body, [info], home, [third] * 3, [((3, 256, 512), bf16)])
    (own,) = call(pair_body, [], [own, arrived], [(block, bf16)])
    rest = [dp_step(own, d) for d in (4, 8, 12)]
    (own,) = call(sum_body, [], [own] + rest, [(block, f32)])
    (grad_weight,) = call(join_body, [info], [own, dp_step(own, 1)], [((24, 768), f32)])
    return (attended[None], grads[0][None], grads[1][None], grads[2][None], grad_weight)


def solution(mesh):
    tiles = P("dp", "seq", None)
    return jax.shard_map(
        per_device,
        mesh=mesh,
        in_specs=(tiles, tiles, tiles, P(), tiles, P(), P("dp")),
        out_specs=(tiles, tiles, tiles, tiles, P("seq", None)),
        check_vma=False,
    )
```

time: 160 us -> 126 us (0.79)
  the two profiles are of different devices: /device:TPU:32 before, /device:TPU:1 now
where the time goes in v2:
time: 126 us; the launch traced here: 125 us
  waiting for transfers between devices  57.1 us (45%)
  starting transfers between devices  40.1 us (32%)
  Pallas kernels  25.2 us (20%)
  between operations  1.52 us (1%)
    ppermute x15, waiting for transfers between devices, shift(): return lax.ppermute(block, ('dp', 'seq'), pairs)  51.3 us
    ppermute x15, starting transfers between devices, shift(): return lax.ppermute(block, ('dp', 'seq'), pairs)  27.5 us
    pallas_call x16, Pallas kernels, call(): pl.pallas_call(body, out_shape=shapes, in_specs=[smem] * len(scalars) + [...  25.2 us
    ppermute x6, starting transfers between devices, dp_step(): return lax.ppermute(block, 'dp', [(i, i ^ step) for i in range(16)])  12.6 us
    ppermute x6, waiting for transfers between devices, dp_step(): return lax.ppermute(block, 'dp', [(i, i ^ step) for i in range(16)])  5.76 us
  transfers between devices with their start and end apart: 21, of which 13 were waited for; matrix products, arithmetic and copies ran while one was open for 0% of the time, Pallas kernels for 11%

profile of v2, /device:TPU:1, one launch (start us, length us, event | category | flops | bytes accessed | tf_op | source)
XLA Modules:
  0.0 125.4 jit_solution(18267708657940959265)
XLA Ops:
  0.6 0.6 pad_add_fusion.info
  1.2 4.3 %shard_map.110 = (bf16[4,256,128]{2,1,0:T(8,128)(2,1)}, bf16[4,256,128]{2,1,0:T(8,128)(2,1)}, bf16[4,256,128]{2,1,0:T(8,128)(2,1)}, bf16[4,256,128]{2,1,0:T(8,128)(2,1)}, bf16[256,768]{1,0:T(8,128)(2,1)}) custom-call(s32[3]{0:T(128)} %pad_add_fusion.info, bf16[256,384]{1,0:T(8,128)(2,1)} %bitcast.13, bf16[256,384]{1,0:T(8,128)(2,1)} %bitcast.14, ...), custom_call_target="tpu_custom_call" | custom-call | bytes 3014656 | tf_op jit(solution)/shard_map/pallas_call | solution.py:396
  5.5 5.5 %collective-permute-start = (bf16[4,256,128]{2,1,0:T(8,128)(2,1)}, bf16[4,256,128]{2,1,0:T(8,128)(2,1)S(1)}, u32[]{:S(2)}, u32[]{:S(2)}) collective-permute-start(bf16[4,256,128]{2,1,0:T(8,128)(2,1)} %get-tuple-element.72), channel_id=1, source_target_pairs={{0,1},{1,0},{3,2},{4,5},{5,4},{7,6},{8,9},{9,8},{11,10},{12,13},{1... | collective-permute-start | bytes 786440 | tf_op jit(solution)/shard_map/ppermute | solution.py:419
  11.0 3.5 %collective-permute-start.1 = (bf16[4,256,128]{2,1,0:T(8,128)(2,1)}, bf16[4,256,128]{2,1,0:T(8,128)(2,1)S(1)}, u32[]{:S(2)}, u32[]{:S(2)}) collective-permute-start(bf16[4,256,128]{2,1,0:T(8,128)(2,1)} %get-tuple-element.73), channel_id=1, source_target_pairs={{0,2},{2,0},{3,1},{4,6},{6,4},{7,5},{8,10},{10,8},{11,9},{12,14},{... | collective-permute-start | bytes 786440 | tf_op jit(solution)/shard_map/ppermute | solution.py:419
  14.6 1.9 %collective-permute-start.2 = (bf16[4,256,128]{2,1,0:T(8,128)(2,1)}, bf16[4,256,128]{2,1,0:T(8,128)(2,1)S(1)}, u32[]{:S(2)}, u32[]{:S(2)}) collective-permute-start(bf16[4,256,128]{2,1,0:T(8,128)(2,1)} %get-tuple-element.74), channel_id=1, source_target_pairs={{1,2},{2,1},{3,0},{5,6},{6,5},{7,4},{9,10},{10,9},{11,8},{13,14},{... | collective-permute-start | bytes 786440 | tf_op jit(solution)/shard_map/ppermute | solution.py:419
  17.1 3.4 %collective-permute-done.1.m2 = bf16[4,256,128]{2,1,0:T(8,128)(2,1)S(1)} collective-permute-done((bf16[4,256,128]{2,1,0:T(8,128)(2,1)}, bf16[4,256,128]{2,1,0:T(8,128)(2,1)S(1)}, u32[]{:S(2)}, u32[]{:S(2)}) %collective-permute-start.1) | collective-permute-done | bytes 262176 | tf_op jit(solution)/shard_map/ppermute | solution.py:419
  20.5 2.8 %collective-permute-done.2.m3 = bf16[4,256,128]{2,1,0:T(8,128)(2,1)S(1)} collective-permute-done((bf16[4,256,128]{2,1,0:T(8,128)(2,1)}, bf16[4,256,128]{2,1,0:T(8,128)(2,1)S(1)}, u32[]{:S(2)}, u32[]{:S(2)}) %collective-permute-start.2) | collective-permute-done | bytes 262176 | tf_op jit(solution)/shard_map/ppermute | solution.py:419
  23.3 0.9 copy-done.1
  24.3 0.7 shard_map.111
  25.0 0.7 collective-permute-start.3
  25.7 3.3 %shard_map.112 = (f32[8,128,128]{2,1,0:T(8,128)S(1)}, f32[8,128,128]{2,1,0:T(8,128)S(1)}, f32[8,128,128]{2,1,0:T(8,128)S(1)}, f32[8,128,128]{2,1,0:T(8,128)S(1)}...) custom-call(s32[3]{0:T(128)S(1)} %copy-done.2, ...), custom_call_target="tpu_custom_call" | custom-call | flops 1000000000 | bytes 5505024 | tf_op jit(solution)/shard_map/pallas_call | solution.py:396
  28.9 0.7 collective-permute-start.5
  29.6 0.7 collective-permute-start.4
  30.3 2.5 %shard_map.113 = (f32[8,128,128]{2,1,0:T(8,128)S(1)}, f32[8,128,128]{2,1,0:T(8,128)S(1)}, f32[8,128,128]{2,1,0:T(8,128)S(1)}, bf16[256,128]{1,0:T(8,128)(2,1)S(1...) custom-call(s32[3]{0:T(128)S(1)} %copy-done.2, ...), custom_call_target="tpu_custom_call" | custom-call | flops 1000000000 | bytes 5767168 | tf_op jit(solution)/shard_map/pallas_call | solution.py:396
  32.8 1.3 %collective-permute-start.6 = (bf16[256,128]{1,0:T(8,128)(2,1)S(1)}, bf16[256,128]{1,0:T(8,128)(2,1)S(1)}, u32[]{:S(2)}, u32[]{:S(2)}) collective-permute-start(bf16[256,128]{1,0:T(8,128)(2,1)S(1)} %get-tuple-element.93), channel_id=1, source_target_pairs={{0,1},{1,0},{2,3},{4,5},{5,4},{6,7},{8,9},{9,8},{10,11},{12,13},{1... | collective-permute-start | bytes 196616 | tf_op jit(solution)/shard_map/ppermute | solution.py:419
  34.1 1.3 %collective-permute-start.7 = (bf16[256,128]{1,0:T(8,128)(2,1)S(1)}, bf16[256,128]{1,0:T(8,128)(2,1)S(1)}, u32[]{:S(2)}, u32[]{:S(2)}) collective-permute-start(bf16[256,128]{1,0:T(8,128)(2,1)S(1)} %get-tuple-element.94), channel_id=1, source_target_pairs={{0,2},{1,3},{2,0},{4,6},{5,7},{6,4},{8,10},{9,11},{10,8},{12,14},{... | collective-permute-start | bytes 196616 | tf_op jit(solution)/shard_map/ppermute | solution.py:419
  35.4 1.3 %collective-permute-start.8 = (bf16[256,128]{1,0:T(8,128)(2,1)S(1)}, bf16[256,128]{1,0:T(8,128)(2,1)S(1)}, u32[]{:S(2)}, u32[]{:S(2)}) collective-permute-start(bf16[256,128]{1,0:T(8,128)(2,1)S(1)} %get-tuple-element.95), channel_id=1, source_target_pairs={{0,3},{1,2},{2,1},{4,7},{5,6},{6,5},{8,11},{9,10},{10,9},{12,15},{... | collective-permute-start | bytes 196616 | tf_op jit(solution)/shard_map/ppermute | solution.py:419
  36.7 2.3 %shard_map.114 = (f32[3,8,128,128]{3,2,1,0:T(8,128)S(1)}, bf16[2,384,128]{2,1,0:T(8,128)(2,1)S(1)}, bf16[2,128,128]{2,1,0:T(8,128)(2,1)S(1)}, bf16[2,128,128]{2,1,0:T(8,128)(2,1)S(1)}) custom-call(s32[3]{0:T(128)S(1)} %copy-done.2, s32[3,6]{1,0:T(4,128)S(1)} %copy-done.3, s32[1]{0:T(128)S(6)} %copy.12.counts, ...), custom_call_target="tpu_custom_call" | custom-call | flops 1000000000 | bytes 5832704 | tf_op jit(solution)/shard_map/pallas_call | solution.py:396
  39.0 18.5 %collective-permute-done.6.m1 = bf16[256,128]{1,0:T(8,128)(2,1)S(1)} collective-permute-done((bf16[256,128]{1,0:T(8,128)(2,1)S(1)}, bf16[256,128]{1,0:T(8,128)(2,1)S(1)}, u32[]{:S(2)}, u32[]{:S(2)}) %collective-permute-start.6) | collective-permute-done | bytes 65568 | tf_op jit(solution)/shard_map/ppermute | solution.py:419
  57.4 2.1 %collective-permute-done.7.m2 = bf16[256,128]{1,0:T(8,128)(2,1)S(1)} collective-permute-done((bf16[256,128]{1,0:T(8,128)(2,1)S(1)}, bf16[256,128]{1,0:T(8,128)(2,1)S(1)}, u32[]{:S(2)}, u32[]{:S(2)}) %collective-permute-start.7) | collective-permute-done | bytes 65568 | tf_op jit(solution)/shard_map/ppermute | solution.py:419
  59.6 2.4 %collective-permute-done.8.m3 = bf16[256,128]{1,0:T(8,128)(2,1)S(1)} collective-permute-done((bf16[256,128]{1,0:T(8,128)(2,1)S(1)}, bf16[256,128]{1,0:T(8,128)(2,1)S(1)}, u32[]{:S(2)}, u32[]{:S(2)}) %collective-permute-start.8) | collective-permute-done | bytes 65568 | tf_op jit(solution)/shard_map/ppermute | solution.py:419
  61.9 1.1 shard_map.115
  63.0 4.5 %collective-permute-start.9 = (bf16[16,72,128]{2,1,0:T(8,128)(2,1)S(1)}, bf16[16,72,128]{2,1,0:T(8,128)(2,1)S(1)}, u32[]{:S(2)}, u32[]{:S(2)}) collective-permute-start(bf16[16,72,128]{2,1,0:T(8,128)(2,1)S(1)} %get-tuple-element.109), channel_id=1, source_target_pairs={{0,16},{16,0},{32,48},{48,32},{64,80},{80,64},{96,112},{112,96},{1... | collective-permute-start | bytes 884744 | tf_op jit(solution)/shard_map/ppermute | solution.py:423
  67.5 2.8 %shard_map.116.acc_in = f32[3,8,128,128]{3,2,1,0:T(8,128)S(1)} custom-call(s32[3]{0:T(128)S(1)} %copy-done.2, s32[3,6]{1,0:T(4,128)S(1)} %copy-done.3, s32[1]{0:T(128)S(6)} %copy.12.counts, bf16[2,8,128,128]{3,2,1,0:T(8,128)(2,1)S(1)} %get-tuple-element.75.kv, bf16[2,8,128,128]{3,2,1,0:T(8,128)(2,1)S(1)} %get-tuple-element.76.qg, ...), custom_call_target="tpu_custom_call" | custom-call | flops 1000000000 | bytes 7077888 | tf_op jit(solution)/shard_map/pallas_call | solution.py:396
  70.3 0.1 shard_map.117
  70.4 1.1 collective-permute-start.10
  71.5 0.6 collective-permute-start.11
  72.1 4.0 %collective-permute-start.12 = (bf16[544,128]{1,0:T(8,128)(2,1)S(1)}, bf16[544,128]{1,0:T(8,128)(2,1)S(1)}, u32[]{:S(2)}, u32[]{:S(2)}) collective-permute-start(bf16[544,128]{1,0:T(8,128)(2,1)S(1)} %get-tuple-element.123), channel_id=1, source_target_pairs={{0,12},{1,13},{2,14},{3,15},{4,8},{5,9},{6,10},{7,11},{8,4},{9,5},... | collective-permute-start | bytes 417800 | tf_op jit(solution)/shard_map/ppermute | solution.py:419
  76.1 2.5 %shard_map.119.acc_in = f32[3,8,128,128]{3,2,1,0:T(8,128)S(1)} custom-call(s32[3]{0:T(128)S(1)} %copy-done.2, s32[3,6]{1,0:T(4,128)S(1)} %copy-done.3, s32[1]{0:T(128)S(6)} %copy.12.counts, bf16[2,8,128,128]{3,2,1,0:T(8,128)(2,1)S(1)} %get-tuple-element.75.kv, bf16[2,8,128,128]{3,2,1,0:T(8,128)(2,1)S(1)} %get-tuple-element.76.qg, ...), custom_call_target="tpu_custom_call" | custom-call | flops 1000000000 | bytes 7340032 | tf_op jit(solution)/shard_map/pallas_call | solution.py:396
  78.7 6.2 %collective-permute-done.11.r8 = bf16[544,128]{1,0:T(8,128)(2,1)S(1)} collective-permute-done((bf16[544,128]{1,0:T(8,128)(2,1)S(1)}, bf16[544,128]{1,0:T(8,128)(2,1)S(1)}, u32[]{:S(2)}, u32[]{:S(2)}) %collective-permute-start.11) | collective-permute-done | bytes 139296 | tf_op jit(solution)/shard_map/ppermute | solution.py:419
  84.8 6.6 %collective-permute-done.12.r12 = bf16[544,128]{1,0:T(8,128)(2,1)S(1)} collective-permute-done((bf16[544,128]{1,0:T(8,128)(2,1)S(1)}, bf16[544,128]{1,0:T(8,128)(2,1)S(1)}, u32[]{:S(2)}, u32[]{:S(2)}) %collective-permute-start.12) | collective-permute-done | bytes 139296 | tf_op jit(solution)/shard_map/ppermute | solution.py:419
  91.4 0.9 shard_map.120
  92.4 3.7 %collective-permute-start.13 = (bf16[848,128]{1,0:T(8,128)(2,1)S(1)}, bf16[848,128]{1,0:T(8,128)(2,1)S(1)}, u32[]{:S(2)}, u32[]{:S(2)}) collective-permute-start(bf16[848,128]{1,0:T(8,128)(2,1)S(1)} %get-tuple-element.126), channel_id=1, source_target_pairs={{0,1},{1,0},{2,3},{3,2},{4,5},{5,4},{6,7},{7,6},{8,9},{9,8},{10,11... | collective-permute-start | bytes 651272 | tf_op jit(solution)/shard_map/ppermute | solution.py:419
  96.0 1.3 %collective-permute-start.15 = (bf16[848,128]{1,0:T(8,128)(2,1)S(1)}, bf16[848,128]{1,0:T(8,128)(2,1)S(1)}, u32[]{:S(2)}, u32[]{:S(2)}) collective-permute-start(bf16[848,128]{1,0:T(8,128)(2,1)S(1)} %get-tuple-element.128), channel_id=1, source_target_pairs={{0,3},{1,2},{2,1},{3,0},{4,7},{5,6},{6,5},{7,4},{8,11},{9,10},{10,... | collective-permute-start | bytes 651272 | tf_op jit(solution)/shard_map/ppermute | solution.py:419
  97.3 3.7 %collective-permute-done.13.m1 = bf16[848,128]{1,0:T(8,128)(2,1)S(1)} collective-permute-done((bf16[848,128]{1,0:T(8,128)(2,1)S(1)}, bf16[848,128]{1,0:T(8,128)(2,1)S(1)}, u32[]{:S(2)}, u32[]{:S(2)}) %collective-permute-start.13) | collective-permute-done | bytes 217120 | tf_op jit(solution)/shard_map/ppermute | solution.py:419
  101.0 1.2 collective-permute-done.14.m2
  102.1 4.6 %collective-permute-done.15.m3 = bf16[848,128]{1,0:T(8,128)(2,1)S(1)} collective-permute-done((bf16[848,128]{1,0:T(8,128)(2,1)S(1)}, bf16[848,128]{1,0:T(8,128)(2,1)S(1)}, u32[]{:S(2)}, u32[]{:S(2)}) %collective-permute-start.15) | collective-permute-done | bytes 217120 | tf_op jit(solution)/shard_map/ppermute | solution.py:419
  106.7 0.4 collective-permute-start.16
  107.1 2.3 %collective-permute-done.16.b = bf16[72,128]{1,0:T(8,128)(2,1)S(1)} collective-permute-done((bf16[72,128]{1,0:T(8,128)(2,1)S(1)}, bf16[72,128]{1,0:T(8,128)(2,1)S(1)}, u32[]{:S(2)}, u32[]{:S(2)}) %collective-permute-start.16) | collective-permute-done | bytes 18464 | tf_op jit(solution)/shard_map/ppermute | solution.py:423
  109.4 2.8 %collective-permute-start.19 = (bf16[72,128]{1,0:T(8,128)(2,1)S(1)}, bf16[72,128]{1,0:T(8,128)(2,1)S(1)}, u32[]{:S(2)}, u32[]{:S(2)}) collective-permute-start(bf16[72,128]{1,0:T(8,128)(2,1)S(1)} %shard_map.123.a), channel_id=1, source_target_pairs={{0,192},{16,208},{32,224},{48,240},{64,128},{80,144},{96,160},{112... | collective-permute-start | bytes 55304 | tf_op jit(solution)/shard_map/ppermute | solution.py:423
  112.2 0.4 collective-permute-start.18
  112.6 0.3 collective-permute-start.17
  112.9 0.5 collective-permute-done.19.d
  113.4 3.0 %collective-permute-done.18.c = bf16[72,128]{1,0:T(8,128)(2,1)S(1)} collective-permute-done((bf16[72,128]{1,0:T(8,128)(2,1)S(1)}, bf16[72,128]{1,0:T(8,128)(2,1)S(1)}, u32[]{:S(2)}, u32[]{:S(2)}) %collective-permute-start.18) | collective-permute-done | bytes 18464 | tf_op jit(solution)/shard_map/ppermute | solution.py:423
  116.4 4.2 %collective-permute-start.20 = (f32[72,128]{1,0:T(8,128)S(1)}, f32[72,128]{1,0:T(8,128)S(1)}, u32[]{:S(2)}, u32[]{:S(2)}) collective-permute-start(f32[72,128]{1,0:T(8,128)S(1)} %shard_map.124.a), channel_id=1, source_target_pairs={{0,16},{16,0},{32,48},{48,32},{64,80},{80,64},{96,112},{112,96},{1... | collective-permute-start | bytes 110600 | tf_op jit(solution)/shard_map/ppermute | solution.py:423
  120.6 1.9 %shard_map.118 = bf16[256,768]{1,0:T(8,128)(2,1)} custom-call(s32[3]{0:T(128)S(1)} %copy-done.2, bf16[256,128]{1,0:T(8,128)(2,1)S(1)} %get-tuple-element.114.m0, bf16[256,128]{1,0:T(8,128)(2,1)S(1)} %collective-permute-done.6.m1, bf16[256,128]{1,0:T(8,128)(2,1)S(1)} %collective-permute-done.7.m2, bf16[256,128]{1,0:T(8,128)(2,1)S(1)} %collective-permute-done.8.m3, ...), custom_call_target="tpu_custom_call" | custom-call | flops 300000000 | bytes 1245184 | tf_op jit(solution)/shard_map/pallas_call | solution.py:396
  122.5 1.7 %shard_map.122 = (bf16[256,384]{1,0:T(8,128)(2,1)}, bf16[256,384]{1,0:T(8,128)(2,1)}, bf16[256,384]{1,0:T(8,128)(2,1)}) custom-call(s32[3]{0:T(128)S(1)} %copy-done.2, bf16[848,128]{1,0:T(8,128)(2,1)S(1)} %get-tuple-element.130.m0, bf16[848,128]{1,0:T(8,128)(2,1)S(1)} %collective-permute-done.13.m1, bf16[848,128]{1,0:T(8,128)(2,1)S(1)} %collective-permute-done.14.m2, ...), custom_call_target="tpu_custom_call" | custom-call | bytes 1458176 | tf_op jit(solution)/shard_map/pallas_call | solution.py:396
  124.2 1.2 shard_map.125
  (21 shorter events, 0.1 us)
Async XLA Ops:
  0.6 22.7 %copy-start.3 = (s32[3,6]{1,0:T(4,128)S(1)}, s32[3,6]{1,0:T(4,128)}, u32[]{:S(2)}) copy-start(s32[3,6]{1,0:T(4,128)} %offsets.13) | copy-start | bytes 220
  1.2 22.1 %copy-start.2 = (s32[3]{0:T(128)S(1)}, s32[3]{0:T(128)}, u32[]{:S(2)}) copy-start(s32[3]{0:T(128)} %pad_add_fusion.info) | copy-start | bytes 40
  5.5 11.6 %collective-permute-start = (bf16[4,256,128]{2,1,0:T(8,128)(2,1)}, bf16[4,256,128]{2,1,0:T(8,128)(2,1)S(1)}, u32[]{:S(2)}, u32[]{:S(2)}) collective-permute-start(bf16[4,256,128]{2,1,0:T(8,128)(2,1)} %get-tuple-element.72), channel_id=1, source_target_pairs={{0,1},{1,0},{3,2},{4,5},{5,4},{7,6},{8,9},{9,8},{11,10},{12,13},{1... | collective-permute-start | bytes 786440 | tf_op jit(solution)/shard_map/ppermute | solution.py:419
  11.0 9.5 %collective-permute-start.1 = (bf16[4,256,128]{2,1,0:T(8,128)(2,1)}, bf16[4,256,128]{2,1,0:T(8,128)(2,1)S(1)}, u32[]{:S(2)}, u32[]{:S(2)}) collective-permute-start(bf16[4,256,128]{2,1,0:T(8,128)(2,1)} %get-tuple-element.73), channel_id=1, source_target_pairs={{0,2},{2,0},{3,1},{4,6},{6,4},{7,5},{8,10},{10,8},{11,9},{12,14},{... | collective-permute-start | bytes 786440 | tf_op jit(solution)/shard_map/ppermute | solution.py:419
  14.6 8.7 %collective-permute-start.2 = (bf16[4,256,128]{2,1,0:T(8,128)(2,1)}, bf16[4,256,128]{2,1,0:T(8,128)(2,1)S(1)}, u32[]{:S(2)}, u32[]{:S(2)}) collective-permute-start(bf16[4,256,128]{2,1,0:T(8,128)(2,1)} %get-tuple-element.74), channel_id=1, source_target_pairs={{1,2},{2,1},{3,0},{5,6},{6,5},{7,4},{9,10},{10,9},{11,8},{13,14},{... | collective-permute-start | bytes 786440 | tf_op jit(solution)/shard_map/ppermute | solution.py:419
  23.3 1.0 copy-start.1
  25.0 5.3 %collective-permute-start.3 = (bf16[2,384,128]{2,1,0:T(8,128)(2,1)S(1)}, bf16[2,384,128]{2,1,0:T(8,128)(2,1)S(1)}, u32[]{:S(2)}, u32[]{:S(2)}) collective-permute-start(bf16[2,384,128]{2,1,0:T(8,128)(2,1)S(1)} %get-tuple-element.77), channel_id=1, source_target_pairs={{0,4},{1,5},{2,6},{4,0},{5,1},{6,2},{8,12},{9,13},{10,14},{12,8},{... | collective-permute-start | bytes 589832 | tf_op jit(solution)/shard_map/ppermute | solution.py:419
  28.9 1.3 %collective-permute-start.5 = (bf16[2,128,128]{2,1,0:T(8,128)(2,1)S(1)}, bf16[2,128,128]{2,1,0:T(8,128)(2,1)S(1)}, u32[]{:S(2)}, u32[]{:S(2)}) collective-permute-start(bf16[2,128,128]{2,1,0:T(8,128)(2,1)S(1)} %get-tuple-element.80), channel_id=1, source_target_pairs={{0,12},{1,13},{2,14},{4,8},{5,9},{6,10},{8,4},{9,5},{10,6},{12,0},... | collective-permute-start | bytes 196616 | tf_op jit(solution)/shard_map/ppermute | solution.py:419
  29.6 0.7 collective-permute-start.4
  32.8 24.6 %collective-permute-start.6 = (bf16[256,128]{1,0:T(8,128)(2,1)S(1)}, bf16[256,128]{1,0:T(8,128)(2,1)S(1)}, u32[]{:S(2)}, u32[]{:S(2)}) collective-permute-start(bf16[256,128]{1,0:T(8,128)(2,1)S(1)} %get-tuple-element.93), channel_id=1, source_target_pairs={{0,1},{1,0},{2,3},{4,5},{5,4},{6,7},{8,9},{9,8},{10,11},{12,13},{1... | collective-permute-start | bytes 196616 | tf_op jit(solution)/shard_map/ppermute | solution.py:419
  34.1 25.5 %collective-permute-start.7 = (bf16[256,128]{1,0:T(8,128)(2,1)S(1)}, bf16[256,128]{1,0:T(8,128)(2,1)S(1)}, u32[]{:S(2)}, u32[]{:S(2)}) collective-permute-start(bf16[256,128]{1,0:T(8,128)(2,1)S(1)} %get-tuple-element.94), channel_id=1, source_target_pairs={{0,2},{1,3},{2,0},{4,6},{5,7},{6,4},{8,10},{9,11},{10,8},{12,14},{... | collective-permute-start | bytes 196616 | tf_op jit(solution)/shard_map/ppermute | solution.py:419
  35.4 26.5 %collective-permute-start.8 = (bf16[256,128]{1,0:T(8,128)(2,1)S(1)}, bf16[256,128]{1,0:T(8,128)(2,1)S(1)}, u32[]{:S(2)}, u32[]{:S(2)}) collective-permute-start(bf16[256,128]{1,0:T(8,128)(2,1)S(1)} %get-tuple-element.95), channel_id=1, source_target_pairs={{0,3},{1,2},{2,1},{4,7},{5,6},{6,5},{8,11},{9,10},{10,9},{12,15},{... | collective-permute-start | bytes 196616 | tf_op jit(solution)/shard_map/ppermute | solution.py:419
  36.7 25.2 %copy-start.4 = (bf16[256,768]{1,0:T(8,128)(2,1)S(1)}, bf16[256,768]{1,0:T(8,128)(2,1)}, u32[]{:S(2)}) copy-start(bf16[256,768]{1,0:T(8,128)(2,1)} %get-tuple-element.101.og) | copy-start | bytes 1179652
  63.0 7.3 %collective-permute-start.9 = (bf16[16,72,128]{2,1,0:T(8,128)(2,1)S(1)}, bf16[16,72,128]{2,1,0:T(8,128)(2,1)S(1)}, u32[]{:S(2)}, u32[]{:S(2)}) collective-permute-start(bf16[16,72,128]{2,1,0:T(8,128)(2,1)S(1)} %get-tuple-element.109), channel_id=1, source_target_pairs={{0,16},{16,0},{32,48},{48,32},{64,80},{80,64},{96,112},{112,96},{1... | collective-permute-start | bytes 884744 | tf_op jit(solution)/shard_map/ppermute | solution.py:423
  70.4 21.1 %collective-permute-start.10 = (bf16[1056,128]{1,0:T(8,128)(2,1)S(1)}, bf16[1056,128]{1,0:T(8,128)(2,1)S(1)}, u32[]{:S(2)}, u32[]{:S(2)}) collective-permute-start(bf16[1056,128]{1,0:T(8,128)(2,1)S(1)} %get-tuple-element.121), channel_id=1, source_target_pairs={{0,4},{1,5},{2,6},{3,7},{4,0},{5,1},{6,2},{7,3},{8,12},{9,13},{10,... | collective-permute-start | bytes 811016 | tf_op jit(solution)/shard_map/ppermute | solution.py:419
  71.5 13.3 %collective-permute-start.11 = (bf16[544,128]{1,0:T(8,128)(2,1)S(1)}, bf16[544,128]{1,0:T(8,128)(2,1)S(1)}, u32[]{:S(2)}, u32[]{:S(2)}) collective-permute-start(bf16[544,128]{1,0:T(8,128)(2,1)S(1)} %get-tuple-element.122), channel_id=1, source_target_pairs={{0,8},{1,9},{2,10},{3,11},{4,12},{5,13},{6,14},{7,15},{8,0},{9,1},... | collective-permute-start | bytes 417800 | tf_op jit(solution)/shard_map/ppermute | solution.py:419
  72.1 19.3 %collective-permute-start.12 = (bf16[544,128]{1,0:T(8,128)(2,1)S(1)}, bf16[544,128]{1,0:T(8,128)(2,1)S(1)}, u32[]{:S(2)}, u32[]{:S(2)}) collective-permute-start(bf16[544,128]{1,0:T(8,128)(2,1)S(1)} %get-tuple-element.123), channel_id=1, source_target_pairs={{0,12},{1,13},{2,14},{3,15},{4,8},{5,9},{6,10},{7,11},{8,4},{9,5},... | collective-permute-start | bytes 417800 | tf_op jit(solution)/shard_map/ppermute | solution.py:419
  78.7 41.9 %copy-start = (bf16[384,768]{1,0:T(8,128)(2,1)S(1)}, bf16[384,768]{1,0:T(8,128)(2,1)}, u32[]{:S(2)}) copy-start(bf16[384,768]{1,0:T(8,128)(2,1)} %w.1) | copy-start | bytes 1769476
  92.4 8.6 %collective-permute-start.13 = (bf16[848,128]{1,0:T(8,128)(2,1)S(1)}, bf16[848,128]{1,0:T(8,128)(2,1)S(1)}, u32[]{:S(2)}, u32[]{:S(2)}) collective-permute-start(bf16[848,128]{1,0:T(8,128)(2,1)S(1)} %get-tuple-element.126), channel_id=1, source_target_pairs={{0,1},{1,0},{2,3},{3,2},{4,5},{5,4},{6,7},{7,6},{8,9},{9,8},{10,11... | collective-permute-start | bytes 651272 | tf_op jit(solution)/shard_map/ppermute | solution.py:419
  96.0 6.1 %collective-permute-start.14 = (bf16[848,128]{1,0:T(8,128)(2,1)S(1)}, bf16[848,128]{1,0:T(8,128)(2,1)S(1)}, u32[]{:S(2)}, u32[]{:S(2)}) collective-permute-start(bf16[848,128]{1,0:T(8,128)(2,1)S(1)} %get-tuple-element.127), channel_id=1, source_target_pairs={{0,2},{1,3},{2,0},{3,1},{4,6},{5,7},{6,4},{7,5},{8,10},{9,11},{10,... | collective-permute-start | bytes 651272 | tf_op jit(solution)/shard_map/ppermute | solution.py:419
  96.0 10.7 %collective-permute-start.15 = (bf16[848,128]{1,0:T(8,128)(2,1)S(1)}, bf16[848,128]{1,0:T(8,128)(2,1)S(1)}, u32[]{:S(2)}, u32[]{:S(2)}) collective-permute-start(bf16[848,128]{1,0:T(8,128)(2,1)S(1)} %get-tuple-element.128), channel_id=1, source_target_pairs={{0,3},{1,2},{2,1},{3,0},{4,7},{5,6},{6,5},{7,4},{8,11},{9,10},{10,... | collective-permute-start | bytes 651272 | tf_op jit(solution)/shard_map/ppermute | solution.py:419
  106.7 2.7 %collective-permute-start.16 = (bf16[72,128]{1,0:T(8,128)(2,1)S(1)}, bf16[72,128]{1,0:T(8,128)(2,1)S(1)}, u32[]{:S(2)}, u32[]{:S(2)}) collective-permute-start(bf16[72,128]{1,0:T(8,128)(2,1)S(1)} %shard_map.121.a), channel_id=1, source_target_pairs={{0,32},{16,48},{32,0},{48,16},{64,96},{80,112},{96,64},{112,80},{1... | collective-permute-start | bytes 55304 | tf_op jit(solution)/shard_map/ppermute | solution.py:423
  109.4 4.0 %collective-permute-start.19 = (bf16[72,128]{1,0:T(8,128)(2,1)S(1)}, bf16[72,128]{1,0:T(8,128)(2,1)S(1)}, u32[]{:S(2)}, u32[]{:S(2)}) collective-permute-start(bf16[72,128]{1,0:T(8,128)(2,1)S(1)} %shard_map.123.a), channel_id=1, source_target_pairs={{0,192},{16,208},{32,224},{48,240},{64,128},{80,144},{96,160},{112... | collective-permute-start | bytes 55304 | tf_op jit(solution)/shard_map/ppermute | solution.py:423
  112.2 4.1 %collective-permute-start.18 = (bf16[72,128]{1,0:T(8,128)(2,1)S(1)}, bf16[72,128]{1,0:T(8,128)(2,1)S(1)}, u32[]{:S(2)}, u32[]{:S(2)}) collective-permute-start(bf16[72,128]{1,0:T(8,128)(2,1)S(1)} %shard_map.123.a), channel_id=1, source_target_pairs={{0,128},{16,144},{32,160},{48,176},{64,192},{80,208},{96,224},{112... | collective-permute-start | bytes 55304 | tf_op jit(solution)/shard_map/ppermute | solution.py:423
  112.6 3.8 %collective-permute-start.17 = (bf16[72,128]{1,0:T(8,128)(2,1)S(1)}, bf16[72,128]{1,0:T(8,128)(2,1)S(1)}, u32[]{:S(2)}, u32[]{:S(2)}) collective-permute-start(bf16[72,128]{1,0:T(8,128)(2,1)S(1)} %shard_map.123.a), channel_id=1, source_target_pairs={{0,64},{16,80},{32,96},{48,112},{64,0},{80,16},{96,32},{112,48},{1... | collective-permute-start | bytes 55304 | tf_op jit(solution)/shard_map/ppermute | solution.py:423
  116.4 7.8 %collective-permute-start.20 = (f32[72,128]{1,0:T(8,128)S(1)}, f32[72,128]{1,0:T(8,128)S(1)}, u32[]{:S(2)}, u32[]{:S(2)}) collective-permute-start(f32[72,128]{1,0:T(8,128)S(1)} %shard_map.124.a), channel_id=1, source_target_pairs={{0,16},{16,0},{32,48},{48,32},{64,80},{80,64},{96,112},{112,96},{1... | collective-permute-start | bytes 110600 | tf_op jit(solution)/shard_map/ppermute | solution.py:423

commit v3 on v2

--- a/solution.py
+++ b/solution.py
@@ -136,50 +136,55 @@
     return moves
 
 
-def prep_body(
-    info, q_in, k_in, v_in, og_in, w_in, o0, o1, o2, o3, og_out, px, q, k, v, og, w, sems
-):
-    moves = copies(((og_in, og), (w_in, w), (q_in, q), (k_in, k), (v_in, v)), sems)
+def prep_body(info, q_in, k_in, v_in, o0, o1, o2, o3, px, q, k, v, sems):
+    moves = copies(((q_in, q), (k_in, k), (v_in, v)), sems)
     order = row_order(False)
-    moves[0].wait()
-    ordered = dot_nn(order, og[...]).astype(bf16)
-    og_out[...] = ordered
-    moves[1].wait()
-    px[1] = dot_nt(ordered, w[...]).astype(bf16)
-    moves[2].wait()
-    px[0] = (dot_nn(order, q[...]) * 0.125).astype(bf16)
-    moves[3].wait()
-    px[2] = dot_nn(order, k[...]).astype(bf16)
-    moves[4].wait()
-    px[3] = dot_nn(order, v[...]).astype(bf16)
+    for i, src in enumerate((q, k, v)):
+        moves[i].wait()
+        rows = dot_nn(order, src[...])
+        px[i] = (rows * 0.125 if i == 0 else rows).astype(bf16)
     for d, o in enumerate((o0, o1, o2, o3)):
         c = pl.multiple_of(jnp.minimum(info[1] ^ d, 2) * 128, 128)
-        for i in range(4):
+        for i in range(3):
             o[i] = px[i, :, pl.ds(c, 128)]
 
 
-def collect_body(info, offsets, counts, m0, m1, m2, m3, qg, kv, s4, s8):
+def grad_body(info, og, w, m_in, og_out, o0, o1, o2, o3, m_out, gx):
+    m_out[...] = m_in[...]
+    ordered = dot_nn(row_order(False), og[...]).astype(bf16)
+    og_out[...] = ordered
+    gx[...] = dot_nt(ordered, w[...]).astype(bf16)
+    for d, o in enumerate((o0, o1, o2, o3)):
+        o[...] = gx[:, pl.ds(pl.multiple_of(jnp.minimum(info[1] ^ d, 2) * 128, 128), 128)]
+
+
+def collect_body(info, offsets, counts, m0, m1, m2, m3, x, s4, s8):
     place = Place(info, offsets, counts)
     for slot, m in enumerate((m0, m1, m2, m3)):
-        for i in range(4):
-            x = (qg, kv)[i // 2]
-            x[i % 2, :, slot * 32 : slot * 32 + 32, :] = m[i].reshape(8, 32, 128)
+        for i in range(3):
+            x[i, :, slot * 32 : slot * 32 + 32, :] = m[i].reshape(8, 32, 128)
     o3, o4 = place.offs(1), place.offs(2)
     for i in (0, 1):
-        s4[i, 0:256] = pick(reader(kv, i), 1, o3)
-        last = pick(reader(kv, i), 2, o4)
+        s4[i, 0:256] = pick(reader(x, i + 1), 1, o3)
+        last = pick(reader(x, i + 1), 2, o4)
         s4[i, 256:384] = last
         s8[i] = last
 
 
+def relay_body(s8, r4, o):
+    for i in (0, 1):
+        o[i] = s8[i]
+        o[2 + i] = r4[i, 256:384]
+
+
 def near_body(
-    info, offsets, counts, qg, kv, top, num, den, m1, m2, e1, e2,
+    info, offsets, counts, x, top, num, den, m1, m2, e1, e2,
 ):
     place = Place(info, offsets, counts)
     for slot in range(4):
         b = place.bias_slot(slot)
         sl = slice(slot * 32, slot * 32 + 32)
-        es, t, o = attend(slot_rows(qg, slot, 0), slot_rows(kv, slot, 0), slot_rows(kv, slot, 1), [b, b])
+        es, t, o = attend(*[slot_rows(x, slot, i) for i in range(3)], [b, b])
         e1[slot, 0], e1[slot, 1] = es
         t = t.reshape(8, 32, 128)
         top[:, sl, :] = t
@@ -187,7 +192,7 @@
         num[:, sl, :] = o[:, :128].reshape(8, 32, 128)
         den[:, sl, :] = o[:, 128:].reshape(8, 32, 128)
     oo = place.offs(0)
-    q2, k2, v2 = [pick(r, 0, oo) for r in (reader(qg, 0), reader(kv, 0), reader(kv, 1))]
+    q2, k2, v2 = [pick(reader(x, i), 0, oo) for i in range(3)]
     bias = [place.bias(512, 2, oo[h], place.base) for h in (0, 1)]
     es, t, o = attend(q2, k2, v2, bias)
     e2[0], e2[1] = es
@@ -206,67 +211,75 @@
     put(reader(den), writer(den), d, pair, oo, False)
 
 
-def far_keys(place, kv, r4, r8, r12):
+def far_keys(place, x, r4, r12):
     o3, o4 = place.offs(1), place.offs(2)
-    k3, v3 = [jnp.concatenate([pick(reader(kv, i), 1, o3), r4[i, 0:256]], axis=0) for i in (0, 1)]
+    k3, v3 = [jnp.concatenate([pick(reader(x, i + 1), 1, o3), r4[i, 0:256]], axis=0) for i in (0, 1)]
     k4, v4 = [
-        jnp.concatenate([pick(reader(kv, i), 2, o4), r4[i, 256:384], r8[i], r12[i]], axis=0) for i in (0, 1)
+        jnp.concatenate([pick(reader(x, i + 1), 2, o4), r4[i, 256:384], r12[2 + i], r12[i]], axis=0) for i in (0, 1)
     ]
     return o3, o4, k3, v3, k4, v4
 
 
 def far_body(
-    info, offsets, counts, kv, qg, r4, r8, r12, top_in, num_in, den_in,
-    top, norm, delta, mx0, mx1, mx2, mx3, m3, m4, e3, e4, num, den,
+    info, offsets, counts, x, r4, r12, top_in, num_in, den_in, g0, g1, g2, g3,
+    top, norm, mx0, mx1, mx2, mx3, m3, m4, e3, e4, num, den,
 ):
     place = Place(info, offsets, counts)
     top[...] = top_in[...]
     num[...] = num_in[...]
     den[...] = den_in[...]
-    o3, o4, k3, v3, k4, v4 = far_keys(place, kv, r4, r8, r12)
+    o3, o4, k3, v3, k4, v4 = far_keys(place, x, r4, r12)
     at = [(place.quarter ^ i) * 1024 for i in range(4)]
     b3 = [jnp.concatenate([place.bias(256, 4, o3[h], at[i]) for i in (0, 1)], axis=1) for h in (0, 1)]
     b4 = [jnp.concatenate([place.bias(128, 8, o4[h], at[i]) for i in range(4)], axis=1) for h in (0, 1)]
     for pair, oo, k2, v2, b, m, e in ((1, o3, k3, v3, b3, m3, e3), (2, o4, k4, v4, b4, m4, e4)):
-        es, t, out = attend(pick(reader(qg, 0), pair, oo), k2, v2, b)
+        es, t, out = attend(pick(reader(x, 0), pair, oo), k2, v2, b)
         e[0], e[1] = es
         m[...] = t
         merge(top, num, den, t, out, pair, oo)
-    ri = lax.broadcasted_iota(jnp.int32, (128, 128), 0) >> 6
-    ci = lax.broadcasted_iota(jnp.int32, (128, 128), 1) >> 6
-    same = jnp.where(ri == ci, 1.0, 0.0)
+    outs = (mx0, mx1, mx2, mx3)
     for res in range(8):
         ok = place.valid(res)
         scale = ok / (den[res] + 1.0 - ok)
         norm[res] = scale
         mixed = (num[res] * scale).astype(bf16)
-        for slot, mx in enumerate((mx0, mx1, mx2, mx3)):
+        for slot, mx in enumerate(outs):
             mx[res * 32 : res * 32 + 32] = mixed[slot * 32 : slot * 32 + 32]
-        prod = qg[1, res].astype(f32) * mixed.astype(f32)
-        delta[res] = lax.dot_general(
+    for mx, g in zip(outs, (g0, g1, g2, g3)):
+        mx[256:512] = g[...]
+
+
+def pair_back(place, x, g, top, norm, delta, t, es, pair, oo, k2, v2):
+    f2 = jnp.exp(t - pick(reader(top), pair, oo)) * pick(reader(norm), pair, oo)
+    gf2 = (pick(reader(g), pair, oo).astype(f32) * f2).astype(bf16)
+    fd2 = f2 * pick(reader(delta), pair, oo)
+    return back(pick(reader(x, 0), pair, oo), k2, v2, gf2, fd2, es)
+
+
+def far_back_body(
+    info, offsets, counts, x, r4, r12, top, norm, m3, m4, e3, e4, mx0, mx1, mx2, mx3, in0, in1, in2, in3,
+    g, delta, acc, d4, d8, d12,
+):
+    place = Place(info, offsets, counts)
+    ri = lax.broadcasted_iota(jnp.int32, (128, 128), 0) >> 6
+    ci = lax.broadcasted_iota(jnp.int32, (128, 128), 1) >> 6
+    same = jnp.where(ri == ci, 1.0, 0.0)
+    for slot, (mx, got) in enumerate(((mx0, in0), (mx1, in1), (mx2, in2), (mx3, in3))):
+        sl = slice(slot * 32, slot * 32 + 32)
+        rows = got[256:512]
+        g[:, sl, :] = rows.reshape(8, 32, 128)
+        prod = rows.astype(f32) * mx[0:256].astype(f32)
+        sums = lax.dot_general(
             prod, same, (((1,), (0,)), ((), ())), precision=lax.Precision.HIGHEST, preferred_element_type=f32
         )
-
-
-def pair_back(place, kv, qg, top, norm, delta, t, es, pair, oo, k2, v2):
-    f2 = jnp.exp(t - pick(reader(top), pair, oo)) * pick(reader(norm), pair, oo)
-    gf2 = (pick(reader(qg, 1), pair, oo).astype(f32) * f2).astype(bf16)
-    fd2 = f2 * pick(reader(delta), pair, oo)
-    return back(pick(reader(qg, 0), pair, oo), k2, v2, gf2, fd2, es)
-
-
-def far_back_body(
-    info, offsets, counts, kv, qg, r4, r8, r12, top, norm, delta, m3, m4, e3, e4,
-    acc, d4, d8, d12,
-):
-    place = Place(info, offsets, counts)
-    o3, o4, k3, v3, k4, v4 = far_keys(place, kv, r4, r8, r12)
+        delta[:, sl, :] = sums.reshape(8, 32, 128)
+    o3, o4, k3, v3, k4, v4 = far_keys(place, x, r4, r12)
     acc[...] = jnp.zeros_like(acc)
     for pair, oo, k2, v2, m, e, parts in (
         (1, o3, k3, v3, m3, e3, ((d4, 0, 256),)),
         (2, o4, k4, v4, m4, e4, ((d4, 256, 128), (d8, 0, 128), (d12, 0, 128))),
     ):
-        grads = pair_back(place, kv, qg, top, norm, delta, m[...], [e[0], e[1]], pair, oo, k2, v2)
+        grads = pair_back(place, x, g, top, norm, delta, m[...], [e[0], e[1]], pair, oo, k2, v2)
         at_row = m.shape[0]
         for i in range(3):
             put(reader(acc, i), writer(acc, i), grads[i][:at_row], pair, oo, True)
@@ -276,21 +289,22 @@
             at_row += rows
 
 
-def back_two_body(info, offsets, counts, kv, qg, top, norm, delta, acc_in, m2, e2, acc):
+def back_two_body(info, offsets, counts, x, g, top, norm, delta, acc_in, m2, e2, acc):
     place = Place(info, offsets, counts)
     acc[...] = acc_in[...]
     oo = place.offs(0)
-    k2, v2 = pick(reader(kv, 0), 0, oo), pick(reader(kv, 1), 0, oo)
-    grads = pair_back(place, kv, qg, top, norm, delta, m2[...], [e2[0], e2[1]], 0, oo, k2, v2)
+    k2, v2 = pick(reader(x, 1), 0, oo), pick(reader(x, 2), 0, oo)
+    grads = pair_back(place, x, g, top, norm, delta, m2[...], [e2[0], e2[1]], 0, oo, k2, v2)
     for i in range(3):
         put(reader(acc, i), writer(acc, i), grads[i], 0, oo, True)
 
 
-def back_one_body(info, offsets, counts, kv, qg, top, norm, delta, acc_in, m1, e1, acc):
+def back_one_body(info, offsets, counts, x, g, top, norm, delta, acc_in, m1, e1, acc):
     for slot in range(4):
         sl = slice(slot * 32, slot * 32 + 32)
         f2 = jnp.exp(slot_rows(m1, slot) - slot_rows(top, slot)) * slot_rows(norm, slot)
-        q2, k2, v2, g2 = [slot_rows(r, slot, i) for r, i in ((qg, 0), (kv, 0), (kv, 1), (qg, 1))]
+        q2, k2, v2 = [slot_rows(x, slot, i) for i in range(3)]
+        g2 = slot_rows(g, slot)
         gf2 = (g2.astype(f32) * f2).astype(bf16)
         fd2 = f2 * slot_rows(delta, slot)
         grads = back(q2, k2, v2, gf2, fd2, [e1[slot, 0], e1[slot, 1]])
@@ -347,7 +361,7 @@
 
 def widen(info, msgs, wide):
     for d, m in enumerate(msgs):
-        wide[:, pl.ds(pl.multiple_of((info[1] ^ d) * 128, 128), 128)] = m[...]
+        wide[:, pl.ds(pl.multiple_of((info[1] ^ d) * 128, 128), 128)] = m[0:256]
 
 
 def project_body(info, m0, m1, m2, m3, og, send, keep, wide, both, away):
@@ -433,59 +447,59 @@
     info = jnp.stack([seq_rank, (seq_rank & 3) ^ (3 * core), core])
     places = [info, offsets, counts]
 
-    chunk = ((4, 256, 128), bf16)
+    chunk = ((3, 256, 128), bf16)
     third = ((256, 384), bf16)
     cube = (8, 128, 128)
     block = (72, 128)
     active = lambda s, t: s
 
-    *msgs, og = call(
+    msgs = call(
         prep_body,
         [info],
-        [queries[0], keys[0], values[0], out_grad[0], out_weight],
-        [chunk] * 4 + [((256, 768), bf16)],
-        [((4, 256, 384), bf16), third, third, third, ((256, 768), bf16), ((384, 768), bf16)],
+        [queries[0], keys[0], values[0]],
+        [chunk] * 4,
+        [((3, 256, 384), bf16), third, third, third],
         space=hbm,
-        sems=5,
-        limit=60,
-    )
-    got = [msgs[0]] + [shift(msgs[d], routes(d, lambda s, t: t)) for d in (1, 2, 3)]
-    qg, kv, s4, s8 = call(
+        sems=3,
+        limit=57,
+    )
+    got = [shift(msgs[d], routes(d, lambda s, t: t)) for d in (1, 2, 3)]
+    og, g0, g1, g2, g3, own = call(
+        grad_body,
+        [info],
+        [out_grad[0], out_weight, msgs[0]],
+        [((256, 768), bf16)] + [((256, 128), bf16)] * 4 + [chunk],
+        [((256, 384), bf16)],
+        flops=3 * 10**8,
+    )
+    x, s4, s8 = call(
         collect_body,
         places,
-        got,
-        [((2, *cube), bf16)] * 2 + [((2, 384, 128), bf16), ((2, 128, 128), bf16)],
+        [own] + got,
+        [((3, *cube), bf16), ((2, 384, 128), bf16), ((2, 128, 128), bf16)],
     )
     r4 = shift(s4, routes(4, active))
     top, num, den, m1, m2, e1, e2 = call(
         near_body,
         places,
-        [qg, kv],
+        [x],
         [(cube, f32)] * 4 + [((512, 128), f32), ((4, 2, 256, 256), bf16), ((2, 512, 512), bf16)],
         flops=10**9,
     )
-    s8, top = lax.optimization_barrier((s8, top))
-    r8, r12 = [shift(s8, routes(d, active)) for d in (8, 12)]
-    top, norm, delta, mx0, mx1, mx2, mx3, m3, m4, e3, e4 = call(
+    top, r4 = lax.optimization_barrier((top, r4))
+    (s12,) = call(relay_body, [], [s8, r4], [((4, 128, 128), bf16)])
+    r12 = shift(s12, routes(12, active))
+    top, norm, mx0, mx1, mx2, mx3, m3, m4, e3, e4 = call(
         far_body,
         places,
-        [kv, qg, r4, r8, r12, top, num, den],
-        [(cube, f32)] * 3
-        + [((256, 128), bf16)] * 4
+        [x, r4, r12, top, num, den, g0, g1, g2, g3],
+        [(cube, f32)] * 2
+        + [((512, 128), bf16)] * 4
         + [((256, 128), f32), ((128, 128), f32), ((2, 256, 512), bf16), ((2, 128, 512), bf16)],
         [(cube, f32)] * 2,
         flops=10**9,
     )
-    mixed = [mx0] + [shift(b, routes(d, active)) for d, b in ((1, mx1), (2, mx2), (3, mx3))]
-    state = [kv, qg, top, norm, delta]
-    acc, d4, d8, d12 = call(
-        far_back_body,
-        places,
-        [kv, qg, r4, r8, r12, top, norm, delta, m3, m4, e3, e4],
-        [((3, *cube), f32), ((2, 384, 128), bf16), ((2, 128, 128), bf16), ((2, 128, 128), bf16)],
-        flops=10**9,
-    )
-    acc, *mixed = lax.optimization_barrier([acc] + mixed)
+    mixed = [mx0] + [shift(b, routes(d)) for d, b in ((1, mx1), (2, mx2), (3, mx3))]
     send, keep = call(
         project_body,
         [info],
@@ -495,9 +509,16 @@
         flops=3 * 10**8,
     )
     arrived = dp_step(send, 1)
-    acc, keep = lax.optimization_barrier((acc, keep))
-    (acc,) = call(back_two_body, places, state + [acc, m2, e2], [((3, *cube), f32)], flops=10**9)
-    acc, keep = lax.optimization_barrier((acc, keep))
+    keep, *mixed = lax.optimization_barrier([keep] + mixed)
+    g, delta, acc, d4, d8, d12 = call(
+        far_back_body,
+        places,
+        [x, r4, r12, top, norm, m3, m4, e3, e4, mx0, mx1, mx2, mx3] + mixed,
+        [(cube, bf16), (cube, f32), ((3, *cube), f32)]
+        + [((2, 384, 128), bf16), ((2, 128, 128), bf16), ((2, 128, 128), bf16)],
+        flops=10**9,
+    )
+    state = [x, g, top, norm, delta]
     part, f4, f8, f12 = call(
         cores_body,
         [],
@@ -509,6 +530,8 @@
     (attended,) = call(
         attended_body, [info], mixed + [out_weight], [((256, 768), bf16)], [((256, 512), bf16)], flops=3 * 10**8
     )
+    acc, attended = lax.optimization_barrier((acc, attended))
+    (acc,) = call(back_two_body, places, state + [acc, m2, e2], [((3, *cube), f32)], flops=10**9)
     (acc,) = call(back_one_body, places, state + [acc, m1, e1], [((3, *cube), f32)], flops=10**9)
     own, *outs = call(
         finish_body,
@@ -524,6 +547,7 @@
     grads = call(home_body, [info], home, [third] * 3, [((3, 256, 512), bf16)])
     (own,) = call(pair_body, [], [own, arrived], [(block, bf16)])
     rest = [dp_step(own, d) for d in (4, 8, 12)]
+    *grads, own = lax.optimization_barrier([*grads, own])
     (own,) = call(sum_body, [], [own] + rest, [(block, f32)])
     (grad_weight,) = call(join_body, [info], [own, dp_step(own, 1)], [((24, 768), f32)])
     return (attended[None], grads[0][None], grads[1][None], grads[2][None], grad_weight)

time: 126 us -> 115 us (0.913)
  waiting for transfers between devices: 57.1 us -> 28.3 us
  starting transfers between devices: 40.1 us -> 54.9 us
  local copies, waits for them, and re-layouts: 0.97 us -> 3.66 us
    ppermute x15 -> x14, waiting for transfers between devices: 51.3 us -> 23.8 us  [shift(): return lax.ppermute(block, ('dp', 'seq'), pairs)]
    ppermute x15 -> x14, starting transfers between devices: 27.5 us -> 46.2 us  [shift(): return lax.ppermute(block, ('dp', 'seq'), pairs)]
    ppermute x6, starting transfers between devices: 12.6 us -> 8.76 us  [dp_step(): return lax.ppermute(block, 'dp', [(i, i ^ step) for i in range(16)])]
    unnamed x10 -> x14, local copies, waits for them, and re-layouts: 0.97 us -> 3.66 us
    pallas_call x16 -> x18, Pallas kernels: 25.2 us -> 25.3 us  [call(): pl.pallas_call(body, out_shape=shapes, in_specs=[smem] * len(scalars) + [...]
  transfers between devices with their start and end apart: 21 -> 20, of which waited for: 13 -> 10; matrix products, arithmetic and copies ran while one was open for 0% -> 0% of each run, Pallas kernels for 11% -> 14%
where the time goes in v3:
time: 115 us; the launch traced here: 114 us
  starting transfers between devices  54.9 us (48%)
  waiting for transfers between devices  28.3 us (25%)
  Pallas kernels  25.3 us (22%)
  local copies, waits for them, and re-layouts  3.66 us (3%)
  between operations  1.53 us (1%)
    ppermute x14, starting transfers between devices, shift(): return lax.ppermute(block, ('dp', 'seq'), pairs)  46.2 us
    pallas_call x18, Pallas kernels, call(): pl.pallas_call(body, out_shape=shapes, in_specs=[smem] * len(scalars) + [...  25.3 us
    ppermute x14, waiting for transfers between devices, shift(): return lax.ppermute(block, ('dp', 'seq'), pairs)  23.8 us
    ppermute x6, starting transfers between devices, dp_step(): return lax.ppermute(block, 'dp', [(i, i ^ step) for i in range(16)])  8.76 us
    ppermute x6, waiting for transfers between devices, dp_step(): return lax.ppermute(block, 'dp', [(i, i ^ step) for i in range(16)])  4.52 us
    unnamed x14, local copies, waits for them, and re-layouts  3.66 us
  transfers between devices with their start and end apart: 20, of which 10 were waited for; matrix products, arithmetic and copies ran while one was open for 0% of the time, Pallas kernels for 14%

profile of v3, /device:TPU:1, one launch (start us, length us, event | category | flops | bytes accessed | tf_op | source)
XLA Modules:
  0.0 114.4 jit_solution(3811397653986021928)
XLA Ops:
  0.6 0.7 pad_add_fusion.info
  1.3 3.2 %shard_map.110 = (bf16[3,256,128]{2,1,0:T(8,128)(2,1)}, bf16[3,256,128]{2,1,0:T(8,128)(2,1)}, bf16[3,256,128]{2,1,0:T(8,128)(2,1)}, bf16[3,256,128]{2,1,0:T(8,128)(2,1)}) custom-call(s32[3]{0:T(128)} %pad_add_fusion.info, bf16[256,384]{1,0:T(8,128)(2,1)} %bitcast.13, bf16[256,384]{1,0:T(8,128)(2,1)} %bitcast.14, bf16[256,384]{1,0:T(8,128)(2,1)} %bitcast.15), custom_call_target="tpu_custom_call" | custom-call | bytes 1376256 | tf_op jit(solution)/shard_map/pallas_call | solution.py:410
  4.5 5.5 %collective-permute-start = (bf16[3,256,128]{2,1,0:T(8,128)(2,1)}, bf16[3,256,128]{2,1,0:T(8,128)(2,1)S(1)}, u32[]{:S(2)}, u32[]{:S(2)}) collective-permute-start(bf16[3,256,128]{2,1,0:T(8,128)(2,1)} %get-tuple-element.80), channel_id=1, source_target_pairs={{0,1},{1,0},{3,2},{4,5},{5,4},{7,6},{8,9},{9,8},{11,10},{12,13},{1... | collective-permute-start | bytes 589832 | tf_op jit(solution)/shard_map/ppermute | solution.py:433
  10.0 3.5 %collective-permute-start.1 = (bf16[3,256,128]{2,1,0:T(8,128)(2,1)}, bf16[3,256,128]{2,1,0:T(8,128)(2,1)S(1)}, u32[]{:S(2)}, u32[]{:S(2)}) collective-permute-start(bf16[3,256,128]{2,1,0:T(8,128)(2,1)} %get-tuple-element.81), channel_id=1, source_target_pairs={{0,2},{2,0},{3,1},{4,6},{6,4},{7,5},{8,10},{10,8},{11,9},{12,14},{... | collective-permute-start | bytes 589832 | tf_op jit(solution)/shard_map/ppermute | solution.py:433
  13.6 1.9 %collective-permute-start.2 = (bf16[3,256,128]{2,1,0:T(8,128)(2,1)}, bf16[3,256,128]{2,1,0:T(8,128)(2,1)S(1)}, u32[]{:S(2)}, u32[]{:S(2)}) collective-permute-start(bf16[3,256,128]{2,1,0:T(8,128)(2,1)} %get-tuple-element.82), channel_id=1, source_target_pairs={{1,2},{2,1},{3,0},{5,6},{6,5},{7,4},{9,10},{10,9},{11,8},{13,14},{... | collective-permute-start | bytes 589832 | tf_op jit(solution)/shard_map/ppermute | solution.py:433
  16.1 0.0 copy-start
  16.1 1.1 copy-done
  17.1 1.0 copy-done.2
  18.1 0.9 copy-done.3
  19.1 0.7 copy-done.4
  19.7 1.1 shard_map.111
  20.9 0.7 shard_map.112
  21.6 0.7 collective-permute-start.3
  22.2 3.3 %shard_map.113 = (f32[8,128,128]{2,1,0:T(8,128)S(1)}, f32[8,128,128]{2,1,0:T(8,128)S(1)}, f32[8,128,128]{2,1,0:T(8,128)S(1)}, f32[8,128,128]{2,1,0:T(8,128)S(1)}...) custom-call(s32[3]{0:T(128)S(1)} %copy-done.4, ...), custom_call_target="tpu_custom_call" | custom-call | flops 1000000000 | bytes 5242880 | tf_op jit(solution)/shard_map/pallas_call | solution.py:410
  25.6 0.7 collective-permute-start.4
  26.3 2.0 %shard_map.115 = (f32[8,128,128]{2,1,0:T(8,128)S(1)}, f32[8,128,128]{2,1,0:T(8,128)S(1)}, bf16[512,128]{1,0:T(8,128)(2,1)S(1)}, bf16[512,128]{1,0:T(8,128)(2,1)S...) custom-call(s32[3]{0:T(128)S(1)} %copy-done.4, ...), custom_call_target="tpu_custom_call" | custom-call | flops 1000000000 | bytes 5505024 | tf_op jit(solution)/shard_map/pallas_call | solution.py:410
  28.3 19.9 %collective-permute-start.5 = (bf16[512,128]{1,0:T(8,128)(2,1)S(1)}, bf16[512,128]{1,0:T(8,128)(2,1)S(1)}, u32[]{:S(2)}, u32[]{:S(2)}) collective-permute-start(bf16[512,128]{1,0:T(8,128)(2,1)S(1)} %get-tuple-element.102.mx1), channel_id=1, source_target_pairs={{0,1},{1,0},{2,3},{3,2},{4,5},{5,4},{6,7},{7,6},{8,9},{9,8},{10,11... | collective-permute-start | bytes 393224 | tf_op jit(solution)/shard_map/ppermute | solution.py:433
  48.2 3.2 %collective-permute-start.6 = (bf16[512,128]{1,0:T(8,128)(2,1)S(1)}, bf16[512,128]{1,0:T(8,128)(2,1)S(1)}, u32[]{:S(2)}, u32[]{:S(2)}) collective-permute-start(bf16[512,128]{1,0:T(8,128)(2,1)S(1)} %get-tuple-element.103.mx2), channel_id=1, source_target_pairs={{0,2},{1,3},{2,0},{3,1},{4,6},{5,7},{6,4},{7,5},{8,10},{9,11},{10,... | collective-permute-start | bytes 393224 | tf_op jit(solution)/shard_map/ppermute | solution.py:433
  51.4 3.7 %collective-permute-done.6.m2.in2 = bf16[512,128]{1,0:T(8,128)(2,1)S(1)} collective-permute-done((bf16[512,128]{1,0:T(8,128)(2,1)S(1)}, bf16[512,128]{1,0:T(8,128)(2,1)S(1)}, u32[]{:S(2)}, u32[]{:S(2)}) %collective-permute-start.6) | collective-permute-done | bytes 131104 | tf_op jit(solution)/shard_map/ppermute | solution.py:433
  55.1 2.9 %collective-permute-done.7.m3.in3 = bf16[512,128]{1,0:T(8,128)(2,1)S(1)} collective-permute-done((bf16[512,128]{1,0:T(8,128)(2,1)S(1)}, bf16[512,128]{1,0:T(8,128)(2,1)S(1)}, u32[]{:S(2)}, u32[]{:S(2)}) %collective-permute-start.7) | collective-permute-done | bytes 131104 | tf_op jit(solution)/shard_map/ppermute | solution.py:433
  58.0 1.1 shard_map.116
  59.0 0.1 collective-permute-start.8
  59.1 2.8 %shard_map.117 = (bf16[8,128,128]{2,1,0:T(8,128)(2,1)S(1)}, f32[8,128,128]{2,1,0:T(8,128)S(1)}, f32[3,8,128,128]{3,2,1,0:T(8,128)S(1)}, bf16[2,384,128]{2,1,0:T(...) custom-call(s32[3]{0:T(128)S(1)} %copy-done.4, s32[3,6]{1,0:T(4,128)S(1)} %copy-done.6, ...), custom_call_target="tpu_custom_call" | custom-call | flops 1000000000 | bytes 6881280 | tf_op jit(solution)/shard_map/pallas_call | solution.py:410
  62.0 0.1 shard_map.118
  62.1 3.2 %collective-permute-start.9 = (bf16[1056,128]{1,0:T(8,128)(2,1)S(1)}, bf16[1056,128]{1,0:T(8,128)(2,1)S(1)}, u32[]{:S(2)}, u32[]{:S(2)}) collective-permute-start(bf16[1056,128]{1,0:T(8,128)(2,1)S(1)} %get-tuple-element.131), channel_id=1, source_target_pairs={{0,4},{1,5},{2,6},{3,7},{4,0},{5,1},{6,2},{7,3},{8,12},{9,13},{10,... | collective-permute-start | bytes 811016 | tf_op jit(solution)/shard_map/ppermute | solution.py:433
  65.3 2.6 %collective-permute-start.10 = (bf16[544,128]{1,0:T(8,128)(2,1)S(1)}, bf16[544,128]{1,0:T(8,128)(2,1)S(1)}, u32[]{:S(2)}, u32[]{:S(2)}) collective-permute-start(bf16[544,128]{1,0:T(8,128)(2,1)S(1)} %get-tuple-element.132), channel_id=1, source_target_pairs={{0,8},{1,9},{2,10},{3,11},{4,12},{5,13},{6,14},{7,15},{8,0},{9,1},... | collective-permute-start | bytes 417800 | tf_op jit(solution)/shard_map/ppermute | solution.py:433
  67.8 0.8 collective-permute-start.11
  68.7 1.9 %shard_map.119 = bf16[256,768]{1,0:T(8,128)(2,1)} custom-call(s32[3]{0:T(128)S(1)} %copy-done.4, bf16[512,128]{1,0:T(8,128)(2,1)S(1)} %get-tuple-element.119.m0.mx0.in0, bf16[512,128]{1,0:T(8,128)(2,1)S(1)} %collective-permute-done.5.m1.in1, bf16[512,128]{1,0:T(8,128)(2,1)S(1)} %collective-permute-done.6.m2.in2, ...), custom_call_target="tpu_custom_call" | custom-call | flops 300000000 | bytes 1507328 | tf_op jit(solution)/shard_map/pallas_call | solution.py:410
  70.5 2.8 %shard_map.120.acc_in = f32[3,8,128,128]{3,2,1,0:T(8,128)S(1)} custom-call(s32[3]{0:T(128)S(1)} %copy-done.4, s32[3,6]{1,0:T(4,128)S(1)} %copy-done.6, s32[1]{0:T(128)S(6)} %copy.12.counts, bf16[3,8,128,128]{3,2,1,0:T(8,128)(2,1)S(1)} %get-tuple-element.83.x, bf16[8,128,128]{2,1,0:T(8,128)(2,1)S(1)} %get-tuple-element.124.g, ...), custom_call_target="tpu_custom_call" | custom-call | flops 1000000000 | bytes 7077888 | tf_op jit(solution)/shard_map/pallas_call | solution.py:410
  73.4 2.5 %shard_map.121.acc_in = f32[3,8,128,128]{3,2,1,0:T(8,128)S(1)} custom-call(s32[3]{0:T(128)S(1)} %copy-done.4, s32[3,6]{1,0:T(4,128)S(1)} %copy-done.6, s32[1]{0:T(128)S(6)} %copy.12.counts, bf16[3,8,128,128]{3,2,1,0:T(8,128)(2,1)S(1)} %get-tuple-element.83.x, bf16[8,128,128]{2,1,0:T(8,128)(2,1)S(1)} %get-tuple-element.124.g, ...), custom_call_target="tpu_custom_call" | custom-call | flops 1000000000 | bytes 7340032 | tf_op jit(solution)/shard_map/pallas_call | solution.py:410
  75.9 7.1 %collective-permute-done.10.r8 = bf16[544,128]{1,0:T(8,128)(2,1)S(1)} collective-permute-done((bf16[544,128]{1,0:T(8,128)(2,1)S(1)}, bf16[544,128]{1,0:T(8,128)(2,1)S(1)}, u32[]{:S(2)}, u32[]{:S(2)}) %collective-permute-start.10) | collective-permute-done | bytes 139296 | tf_op jit(solution)/shard_map/ppermute | solution.py:433
  83.0 0.9 collective-permute-done.9.r4
  83.9 0.9 shard_map.122
  84.8 2.8 %collective-permute-start.12 = (bf16[848,128]{1,0:T(8,128)(2,1)S(1)}, bf16[848,128]{1,0:T(8,128)(2,1)S(1)}, u32[]{:S(2)}, u32[]{:S(2)}) collective-permute-start(bf16[848,128]{1,0:T(8,128)(2,1)S(1)} %get-tuple-element.136), channel_id=1, source_target_pairs={{0,1},{1,0},{2,3},{3,2},{4,5},{5,4},{6,7},{7,6},{8,9},{9,8},{10,11... | collective-permute-start | bytes 651272 | tf_op jit(solution)/shard_map/ppermute | solution.py:433
  87.6 1.4 %collective-permute-start.14 = (bf16[848,128]{1,0:T(8,128)(2,1)S(1)}, bf16[848,128]{1,0:T(8,128)(2,1)S(1)}, u32[]{:S(2)}, u32[]{:S(2)}) collective-permute-start(bf16[848,128]{1,0:T(8,128)(2,1)S(1)} %get-tuple-element.138), channel_id=1, source_target_pairs={{0,3},{1,2},{2,1},{3,0},{4,7},{5,6},{6,5},{7,4},{8,11},{9,10},{10,... | collective-permute-start | bytes 651272 | tf_op jit(solution)/shard_map/ppermute | solution.py:433
  89.1 3.7 %collective-permute-done.12.m1 = bf16[848,128]{1,0:T(8,128)(2,1)S(1)} collective-permute-done((bf16[848,128]{1,0:T(8,128)(2,1)S(1)}, bf16[848,128]{1,0:T(8,128)(2,1)S(1)}, u32[]{:S(2)}, u32[]{:S(2)}) %collective-permute-start.12) | collective-permute-done | bytes 217120 | tf_op jit(solution)/shard_map/ppermute | solution.py:433
  92.7 1.1 collective-permute-done.13.m2
  93.8 4.4 %collective-permute-done.14.m3 = bf16[848,128]{1,0:T(8,128)(2,1)S(1)} collective-permute-done((bf16[848,128]{1,0:T(8,128)(2,1)S(1)}, bf16[848,128]{1,0:T(8,128)(2,1)S(1)}, u32[]{:S(2)}, u32[]{:S(2)}) %collective-permute-start.14) | collective-permute-done | bytes 217120 | tf_op jit(solution)/shard_map/ppermute | solution.py:433
  98.3 0.8 collective-permute-start.15
  99.0 1.9 %collective-permute-done.15.b = bf16[72,128]{1,0:T(8,128)(2,1)S(1)} collective-permute-done((bf16[72,128]{1,0:T(8,128)(2,1)S(1)}, bf16[72,128]{1,0:T(8,128)(2,1)S(1)}, u32[]{:S(2)}, u32[]{:S(2)}) %collective-permute-start.15) | collective-permute-done | bytes 18464 | tf_op jit(solution)/shard_map/ppermute | solution.py:437
  101.0 2.8 %collective-permute-start.18 = (bf16[72,128]{1,0:T(8,128)(2,1)S(1)}, bf16[72,128]{1,0:T(8,128)(2,1)S(1)}, u32[]{:S(2)}, u32[]{:S(2)}) collective-permute-start(bf16[72,128]{1,0:T(8,128)(2,1)S(1)} %shard_map.125.a), channel_id=1, source_target_pairs={{0,192},{16,208},{32,224},{48,240},{64,128},{80,144},{96,160},{112... | collective-permute-start | bytes 55304 | tf_op jit(solution)/shard_map/ppermute | solution.py:437
  103.7 0.3 collective-permute-start.17
  104.1 0.3 collective-permute-start.16
  104.4 1.7 %shard_map.124 = (bf16[256,384]{1,0:T(8,128)(2,1)}, bf16[256,384]{1,0:T(8,128)(2,1)}, bf16[256,384]{1,0:T(8,128)(2,1)}) custom-call(s32[3]{0:T(128)S(1)} %copy-done.5, bf16[848,128]{1,0:T(8,128)(2,1)S(1)} %get-tuple-element.140.m0, bf16[848,128]{1,0:T(8,128)(2,1)S(1)} %collective-permute-done.12.m1, bf16[848,128]{1,0:T(8,128)(2,1)S(1)} %collective-permute-done.13.m2, ...), custom_call_target="tpu_custom_call" | custom-call | bytes 1458176 | tf_op jit(solution)/shard_map/pallas_call | solution.py:410
  106.1 1.7 %collective-permute-done.17.c = bf16[72,128]{1,0:T(8,128)(2,1)S(1)} collective-permute-done((bf16[72,128]{1,0:T(8,128)(2,1)S(1)}, bf16[72,128]{1,0:T(8,128)(2,1)S(1)}, u32[]{:S(2)}, u32[]{:S(2)}) %collective-permute-start.17) | collective-permute-done | bytes 18464 | tf_op jit(solution)/shard_map/ppermute | solution.py:437
  107.9 4.4 %collective-permute-start.19 = (f32[72,128]{1,0:T(8,128)S(1)}, f32[72,128]{1,0:T(8,128)S(1)}, u32[]{:S(2)}, u32[]{:S(2)}) collective-permute-start(f32[72,128]{1,0:T(8,128)S(1)} %shard_map.126.a), channel_id=1, source_target_pairs={{0,16},{16,0},{32,48},{48,32},{64,80},{80,64},{96,112},{112,96},{1... | collective-permute-start | bytes 110600 | tf_op jit(solution)/shard_map/ppermute | solution.py:437
  112.3 0.9 collective-permute-done.19.b
  113.2 1.2 %shard_map.127 = f32[24,768]{1,0:T(8,128)} custom-call(s32[3]{0:T(128)S(1)} %copy-done.5, f32[72,128]{1,0:T(8,128)S(1)} %shard_map.126.a, f32[72,128]{1,0:T(8,128)S(1)} %collective-permute-done.19.b), custom_call_target="tpu_custom_call" | custom-call | bytes 147456 | tf_op jit(solution)/shard_map/pallas_call | solution.py:410
  (25 shorter events, 0.1 us)
Async XLA Ops:
  0.6 20.2 %copy-start.6 = (s32[3,6]{1,0:T(4,128)S(1)}, s32[3,6]{1,0:T(4,128)}, u32[]{:S(2)}) copy-start(s32[3,6]{1,0:T(4,128)} %offsets.13) | copy-start | bytes 220
  4.5 16.3 %collective-permute-start = (bf16[3,256,128]{2,1,0:T(8,128)(2,1)}, bf16[3,256,128]{2,1,0:T(8,128)(2,1)S(1)}, u32[]{:S(2)}, u32[]{:S(2)}) collective-permute-start(bf16[3,256,128]{2,1,0:T(8,128)(2,1)} %get-tuple-element.80), channel_id=1, source_target_pairs={{0,1},{1,0},{3,2},{4,5},{5,4},{7,6},{8,9},{9,8},{11,10},{12,13},{1... | collective-permute-start | bytes 589832 | tf_op jit(solution)/shard_map/ppermute | solution.py:433
  10.0 10.8 %collective-permute-start.1 = (bf16[3,256,128]{2,1,0:T(8,128)(2,1)}, bf16[3,256,128]{2,1,0:T(8,128)(2,1)S(1)}, u32[]{:S(2)}, u32[]{:S(2)}) collective-permute-start(bf16[3,256,128]{2,1,0:T(8,128)(2,1)} %get-tuple-element.81), channel_id=1, source_target_pairs={{0,2},{2,0},{3,1},{4,6},{6,4},{7,5},{8,10},{10,8},{11,9},{12,14},{... | collective-permute-start | bytes 589832 | tf_op jit(solution)/shard_map/ppermute | solution.py:433
  13.6 7.3 %collective-permute-start.2 = (bf16[3,256,128]{2,1,0:T(8,128)(2,1)}, bf16[3,256,128]{2,1,0:T(8,128)(2,1)S(1)}, u32[]{:S(2)}, u32[]{:S(2)}) collective-permute-start(bf16[3,256,128]{2,1,0:T(8,128)(2,1)} %get-tuple-element.82), channel_id=1, source_target_pairs={{1,2},{2,1},{3,0},{5,6},{6,5},{7,4},{9,10},{10,9},{11,8},{13,14},{... | collective-permute-start | bytes 589832 | tf_op jit(solution)/shard_map/ppermute | solution.py:433
  16.1 1.1 copy-start
  17.1 1.0 copy-start.2
  18.1 0.9 copy-start.3
  19.1 0.7 copy-start.4
  21.6 4.0 %collective-permute-start.3 = (bf16[2,384,128]{2,1,0:T(8,128)(2,1)S(1)}, bf16[2,384,128]{2,1,0:T(8,128)(2,1)S(1)}, u32[]{:S(2)}, u32[]{:S(2)}) collective-permute-start(bf16[2,384,128]{2,1,0:T(8,128)(2,1)S(1)} %get-tuple-element.85), channel_id=1, source_target_pairs={{0,4},{1,5},{2,6},{4,0},{5,1},{6,2},{8,12},{9,13},{10,14},{12,8},{... | collective-permute-start | bytes 589832 | tf_op jit(solution)/shard_map/ppermute | solution.py:433
  25.6 0.7 collective-permute-start.4
  28.3 23.1 %collective-permute-start.5 = (bf16[512,128]{1,0:T(8,128)(2,1)S(1)}, bf16[512,128]{1,0:T(8,128)(2,1)S(1)}, u32[]{:S(2)}, u32[]{:S(2)}) collective-permute-start(bf16[512,128]{1,0:T(8,128)(2,1)S(1)} %get-tuple-element.102.mx1), channel_id=1, source_target_pairs={{0,1},{1,0},{2,3},{3,2},{4,5},{5,4},{6,7},{7,6},{8,9},{9,8},{10,11... | collective-permute-start | bytes 393224 | tf_op jit(solution)/shard_map/ppermute | solution.py:433
  48.2 6.9 %collective-permute-start.6 = (bf16[512,128]{1,0:T(8,128)(2,1)S(1)}, bf16[512,128]{1,0:T(8,128)(2,1)S(1)}, u32[]{:S(2)}, u32[]{:S(2)}) collective-permute-start(bf16[512,128]{1,0:T(8,128)(2,1)S(1)} %get-tuple-element.103.mx2), channel_id=1, source_target_pairs={{0,2},{1,3},{2,0},{3,1},{4,6},{5,7},{6,4},{7,5},{8,10},{9,11},{10,... | collective-permute-start | bytes 393224 | tf_op jit(solution)/shard_map/ppermute | solution.py:433
  51.4 6.6 %collective-permute-start.7 = (bf16[512,128]{1,0:T(8,128)(2,1)S(1)}, bf16[512,128]{1,0:T(8,128)(2,1)S(1)}, u32[]{:S(2)}, u32[]{:S(2)}) collective-permute-start(bf16[512,128]{1,0:T(8,128)(2,1)S(1)} %get-tuple-element.104.mx3), channel_id=1, source_target_pairs={{0,3},{1,2},{2,1},{3,0},{4,7},{5,6},{6,5},{7,4},{8,11},{9,10},{10,... | collective-permute-start | bytes 393224 | tf_op jit(solution)/shard_map/ppermute | solution.py:433
  59.0 3.0 %collective-permute-start.8 = (bf16[16,72,128]{2,1,0:T(8,128)(2,1)S(1)}, bf16[16,72,128]{2,1,0:T(8,128)(2,1)S(1)}, u32[]{:S(2)}, u32[]{:S(2)}) collective-permute-start(bf16[16,72,128]{2,1,0:T(8,128)(2,1)S(1)} %get-tuple-element.113), channel_id=1, source_target_pairs={{0,16},{16,0},{32,48},{48,32},{64,80},{80,64},{96,112},{112,96},{1... | collective-permute-start | bytes 884744 | tf_op jit(solution)/shard_map/ppermute | solution.py:437
  62.0 6.7 %copy-start.1 = (bf16[384,768]{1,0:T(8,128)(2,1)S(1)}, bf16[384,768]{1,0:T(8,128)(2,1)}, u32[]{:S(2)}) copy-start(bf16[384,768]{1,0:T(8,128)(2,1)} %w.3) | copy-start | bytes 1769476
  62.1 21.8 %collective-permute-start.9 = (bf16[1056,128]{1,0:T(8,128)(2,1)S(1)}, bf16[1056,128]{1,0:T(8,128)(2,1)S(1)}, u32[]{:S(2)}, u32[]{:S(2)}) collective-permute-start(bf16[1056,128]{1,0:T(8,128)(2,1)S(1)} %get-tuple-element.131), channel_id=1, source_target_pairs={{0,4},{1,5},{2,6},{3,7},{4,0},{5,1},{6,2},{7,3},{8,12},{9,13},{10,... | collective-permute-start | bytes 811016 | tf_op jit(solution)/shard_map/ppermute | solution.py:433
  65.3 17.7 %collective-permute-start.10 = (bf16[544,128]{1,0:T(8,128)(2,1)S(1)}, bf16[544,128]{1,0:T(8,128)(2,1)S(1)}, u32[]{:S(2)}, u32[]{:S(2)}) collective-permute-start(bf16[544,128]{1,0:T(8,128)(2,1)S(1)} %get-tuple-element.132), channel_id=1, source_target_pairs={{0,8},{1,9},{2,10},{3,11},{4,12},{5,13},{6,14},{7,15},{8,0},{9,1},... | collective-permute-start | bytes 417800 | tf_op jit(solution)/shard_map/ppermute | solution.py:433
  67.8 15.1 %collective-permute-start.11 = (bf16[544,128]{1,0:T(8,128)(2,1)S(1)}, bf16[544,128]{1,0:T(8,128)(2,1)S(1)}, u32[]{:S(2)}, u32[]{:S(2)}) collective-permute-start(bf16[544,128]{1,0:T(8,128)(2,1)S(1)} %get-tuple-element.133), channel_id=1, source_target_pairs={{0,12},{1,13},{2,14},{3,15},{4,8},{5,9},{6,10},{7,11},{8,4},{9,5},... | collective-permute-start | bytes 417800 | tf_op jit(solution)/shard_map/ppermute | solution.py:433
  75.9 28.5 %copy-start.5 = (s32[3]{0:T(128)S(1)}, s32[3]{0:T(128)}, u32[]{:S(2)}) copy-start(s32[3]{0:T(128)} %pad_add_fusion.info) | copy-start | bytes 40
  84.8 7.9 %collective-permute-start.12 = (bf16[848,128]{1,0:T(8,128)(2,1)S(1)}, bf16[848,128]{1,0:T(8,128)(2,1)S(1)}, u32[]{:S(2)}, u32[]{:S(2)}) collective-permute-start(bf16[848,128]{1,0:T(8,128)(2,1)S(1)} %get-tuple-element.136), channel_id=1, source_target_pairs={{0,1},{1,0},{2,3},{3,2},{4,5},{5,4},{6,7},{7,6},{8,9},{9,8},{10,11... | collective-permute-start | bytes 651272 | tf_op jit(solution)/shard_map/ppermute | solution.py:433
  87.6 6.2 %collective-permute-start.13 = (bf16[848,128]{1,0:T(8,128)(2,1)S(1)}, bf16[848,128]{1,0:T(8,128)(2,1)S(1)}, u32[]{:S(2)}, u32[]{:S(2)}) collective-permute-start(bf16[848,128]{1,0:T(8,128)(2,1)S(1)} %get-tuple-element.137), channel_id=1, source_target_pairs={{0,2},{1,3},{2,0},{3,1},{4,6},{5,7},{6,4},{7,5},{8,10},{9,11},{10,... | collective-permute-start | bytes 651272 | tf_op jit(solution)/shard_map/ppermute | solution.py:433
  87.6 10.6 %collective-permute-start.14 = (bf16[848,128]{1,0:T(8,128)(2,1)S(1)}, bf16[848,128]{1,0:T(8,128)(2,1)S(1)}, u32[]{:S(2)}, u32[]{:S(2)}) collective-permute-start(bf16[848,128]{1,0:T(8,128)(2,1)S(1)} %get-tuple-element.138), channel_id=1, source_target_pairs={{0,3},{1,2},{2,1},{3,0},{4,7},{5,6},{6,5},{7,4},{8,11},{9,10},{10,... | collective-permute-start | bytes 651272 | tf_op jit(solution)/shard_map/ppermute | solution.py:433
  98.3 2.7 %collective-permute-start.15 = (bf16[72,128]{1,0:T(8,128)(2,1)S(1)}, bf16[72,128]{1,0:T(8,128)(2,1)S(1)}, u32[]{:S(2)}, u32[]{:S(2)}) collective-permute-start(bf16[72,128]{1,0:T(8,128)(2,1)S(1)} %shard_map.123.a), channel_id=1, source_target_pairs={{0,32},{16,48},{32,0},{48,16},{64,96},{80,112},{96,64},{112,80},{1... | collective-permute-start | bytes 55304 | tf_op jit(solution)/shard_map/ppermute | solution.py:437
  101.0 5.2 %collective-permute-start.18 = (bf16[72,128]{1,0:T(8,128)(2,1)S(1)}, bf16[72,128]{1,0:T(8,128)(2,1)S(1)}, u32[]{:S(2)}, u32[]{:S(2)}) collective-permute-start(bf16[72,128]{1,0:T(8,128)(2,1)S(1)} %shard_map.125.a), channel_id=1, source_target_pairs={{0,192},{16,208},{32,224},{48,240},{64,128},{80,144},{96,160},{112... | collective-permute-start | bytes 55304 | tf_op jit(solution)/shard_map/ppermute | solution.py:437
  103.7 4.1 %collective-permute-start.17 = (bf16[72,128]{1,0:T(8,128)(2,1)S(1)}, bf16[72,128]{1,0:T(8,128)(2,1)S(1)}, u32[]{:S(2)}, u32[]{:S(2)}) collective-permute-start(bf16[72,128]{1,0:T(8,128)(2,1)S(1)} %shard_map.125.a), channel_id=1, source_target_pairs={{0,128},{16,144},{32,160},{48,176},{64,192},{80,208},{96,224},{112... | collective-permute-start | bytes 55304 | tf_op jit(solution)/shard_map/ppermute | solution.py:437
  104.1 3.8 %collective-permute-start.16 = (bf16[72,128]{1,0:T(8,128)(2,1)S(1)}, bf16[72,128]{1,0:T(8,128)(2,1)S(1)}, u32[]{:S(2)}, u32[]{:S(2)}) collective-permute-start(bf16[72,128]{1,0:T(8,128)(2,1)S(1)} %shard_map.125.a), channel_id=1, source_target_pairs={{0,64},{16,80},{32,96},{48,112},{64,0},{80,16},{96,32},{112,48},{1... | collective-permute-start | bytes 55304 | tf_op jit(solution)/shard_map/ppermute | solution.py:437
  107.9 5.3 %collective-permute-start.19 = (f32[72,128]{1,0:T(8,128)S(1)}, f32[72,128]{1,0:T(8,128)S(1)}, u32[]{:S(2)}, u32[]{:S(2)}) collective-permute-start(f32[72,128]{1,0:T(8,128)S(1)} %shard_map.126.a), channel_id=1, source_target_pairs={{0,16},{16,0},{32,48},{48,32},{64,80},{80,64},{96,112},{112,96},{1... | collective-permute-start | bytes 110600 | tf_op jit(solution)/shard_map/ppermute | solution.py:437

commit v4 on v3

--- a/solution.py
+++ b/solution.py
@@ -211,32 +211,48 @@
     put(reader(den), writer(den), d, pair, oo, False)
 
 
-def far_keys(place, x, r4, r12):
-    o3, o4 = place.offs(1), place.offs(2)
-    k3, v3 = [jnp.concatenate([pick(reader(x, i + 1), 1, o3), r4[i, 0:256]], axis=0) for i in (0, 1)]
-    k4, v4 = [
-        jnp.concatenate([pick(reader(x, i + 1), 2, o4), r4[i, 256:384], r12[2 + i], r12[i]], axis=0) for i in (0, 1)
+def keys3(place, x, r4):
+    oo = place.offs(1)
+    return [oo] + [jnp.concatenate([pick(reader(x, i + 1), 1, oo), r4[i, 0:256]], axis=0) for i in (0, 1)]
+
+
+def keys4(place, x, r4, r12):
+    oo = place.offs(2)
+    return [oo] + [
+        jnp.concatenate([pick(reader(x, i + 1), 2, oo), r4[i, 256:384], r12[2 + i], r12[i]], axis=0)
+        for i in (0, 1)
     ]
-    return o3, o4, k3, v3, k4, v4
-
-
-def far_body(
-    info, offsets, counts, x, r4, r12, top_in, num_in, den_in, g0, g1, g2, g3,
-    top, norm, mx0, mx1, mx2, mx3, m3, m4, e3, e4, num, den,
-):
+
+
+def mid_body(info, offsets, counts, x, r4, top_in, num_in, den_in, top, num, den, m3, e3):
     place = Place(info, offsets, counts)
     top[...] = top_in[...]
     num[...] = num_in[...]
     den[...] = den_in[...]
-    o3, o4, k3, v3, k4, v4 = far_keys(place, x, r4, r12)
+    oo, k2, v2 = keys3(place, x, r4)
+    at = [(place.quarter ^ i) * 1024 for i in (0, 1)]
+    bias = [jnp.concatenate([place.bias(256, 4, oo[h], b) for b in at], axis=1) for h in (0, 1)]
+    es, t, out = attend(pick(reader(x, 0), 1, oo), k2, v2, bias)
+    e3[0], e3[1] = es
+    m3[...] = t
+    merge(top, num, den, t, out, 1, oo)
+
+
+def far_body(
+    info, offsets, counts, x, r4, r12, top_in, num_in, den_in, g0, g1, g2, g3,
+    top, norm, mx0, mx1, mx2, mx3, m4, e4, num, den,
+):
+    place = Place(info, offsets, counts)
+    top[...] = top_in[...]
+    num[...] = num_in[...]
+    den[...] = den_in[...]
+    oo, k2, v2 = keys4(place, x, r4, r12)
     at = [(place.quarter ^ i) * 1024 for i in range(4)]
-    b3 = [jnp.concatenate([place.bias(256, 4, o3[h], at[i]) for i in (0, 1)], axis=1) for h in (0, 1)]
-    b4 = [jnp.concatenate([place.bias(128, 8, o4[h], at[i]) for i in range(4)], axis=1) for h in (0, 1)]
-    for pair, oo, k2, v2, b, m, e in ((1, o3, k3, v3, b3, m3, e3), (2, o4, k4, v4, b4, m4, e4)):
-        es, t, out = attend(pick(reader(x, 0), pair, oo), k2, v2, b)
-        e[0], e[1] = es
-        m[...] = t
-        merge(top, num, den, t, out, pair, oo)
+    bias = [jnp.concatenate([place.bias(128, 8, oo[h], b) for b in at], axis=1) for h in (0, 1)]
+    es, t, out = attend(pick(reader(x, 0), 2, oo), k2, v2, bias)
+    e4[0], e4[1] = es
+    m4[...] = t
+    merge(top, num, den, t, out, 2, oo)
     outs = (mx0, mx1, mx2, mx3)
     for res in range(8):
         ok = place.valid(res)
@@ -273,7 +289,8 @@
             prod, same, (((1,), (0,)), ((), ())), precision=lax.Precision.HIGHEST, preferred_element_type=f32
         )
         delta[:, sl, :] = sums.reshape(8, 32, 128)
-    o3, o4, k3, v3, k4, v4 = far_keys(place, x, r4, r12)
+    o3, k3, v3 = keys3(place, x, r4)
+    o4, k4, v4 = keys4(place, x, r4, r12)
     acc[...] = jnp.zeros_like(acc)
     for pair, oo, k2, v2, m, e, parts in (
         (1, o3, k3, v3, m3, e3, ((d4, 0, 256),)),
@@ -324,7 +341,12 @@
             f[2 * n : 2 * n + 288] = part.reshape(288, 128).astype(bf16)
 
 
-def finish_body(info, offsets, counts, acc_in, r4, r8, r12, part, own, o0, o1, o2, o3, acc):
+def far_sum_body(part, f4, f8, f12, low):
+    a, b, c = [r[n : n + 288].astype(f32) for r, n in ((f4, 768), (f8, 256), (f12, 256))]
+    low[...] = (part[...].reshape(288, 128) + a + (b + c)).astype(bf16)
+
+
+def finish_body(info, offsets, counts, acc_in, r4, r8, r12, o0, o1, o2, o3, acc):
     place = Place(info, offsets, counts)
     acc[...] = acc_in[...]
     p3, p4 = place.offs(1), place.offs(2)
@@ -334,14 +356,10 @@
         far = r4[i * 384 + 256 : i * 384 + 384].astype(f32)
         far = far + r8[i * 128 : i * 128 + 128].astype(f32) + r12[i * 128 : i * 128 + 128].astype(f32)
         put(rd, wr, far, 2, p4, True)
-    grads = [r[n : n + 288].astype(f32).reshape(4, 72, 128) for r, n in ((r4, 768), (r8, 256), (r12, 256))]
-    total = part[...] + grads[0] + (grads[1] + grads[2])
-    own[...] = total[0]
     for slot, o in enumerate((o0, o1, o2, o3)):
         o[0:256] = (slot_rows(acc, slot, 0) * 0.125).astype(bf16)
         o[256:512] = slot_rows(acc, slot, 1).astype(bf16)
         o[512:768] = slot_rows(acc, slot, 2).astype(bf16)
-        o[768:848] = jnp.concatenate([total[slot], jnp.zeros((8, 128), f32)], axis=0).astype(bf16)
 
 
 def home_body(info, m0, m1, m2, m3, dq, dk, dv, wide):
@@ -354,9 +372,11 @@
         o[...] = dot_nn(order, wide[i, :, 0:384]).astype(bf16)
 
 
-def near_sum_body(own, m1, m2, m3, o):
-    a, b, c = [m[768:848].astype(f32)[0:72] for m in (m1, m2, m3)]
-    o[...] = (own[...] + a + (b + c)).astype(bf16)
+def halves_body(mine, other, own, s1, s2, s3):
+    a, b = mine[...].astype(f32), other[...].astype(f32)
+    for d, o in enumerate((own, s1, s2, s3)):
+        at = slice(72 * d, 72 * d + 72)
+        o[...] = jnp.concatenate([a[at], b[at]], axis=0).astype(o.dtype)
 
 
 def widen(info, msgs, wide):
@@ -392,11 +412,12 @@
     o[...] = (a[...].astype(f32) + b[...].astype(f32)).astype(o.dtype)
 
 
-def join_body(info, a, b, o):
-    for t in range(3):
-        at = slice(t * 24, t * 24 + 24)
-        o[:, pl.ds(pl.multiple_of(info[2] * 384 + t * 128, 128), 128)] = a[at]
-        o[:, pl.ds(pl.multiple_of((1 - info[2]) * 384 + t * 128, 128), 128)] = b[at]
+def join_body(info, own, a, b, c, o):
+    total = own[...] + a[...].astype(f32) + (b[...].astype(f32) + c[...].astype(f32))
+    for h in (0, 1):
+        for t in range(3):
+            col = pl.multiple_of((info[2] ^ h) * 384 + t * 128, 128)
+            o[:, pl.ds(col, 128)] = total[72 * h + 24 * t : 72 * h + 24 * t + 24]
 
 
 smem = pl.BlockSpec(memory_space=pltpu.SMEM)
@@ -463,7 +484,7 @@
         sems=3,
         limit=57,
     )
-    got = [shift(msgs[d], routes(d, lambda s, t: t)) for d in (1, 2, 3)]
+    got = [shift(msgs[d], routes(d)) for d in (1, 2, 3)]
     og, g0, g1, g2, g3, own = call(
         grad_body,
         [info],
@@ -478,7 +499,7 @@
         [own] + got,
         [((3, *cube), bf16), ((2, 384, 128), bf16), ((2, 128, 128), bf16)],
     )
-    r4 = shift(s4, routes(4, active))
+    r4 = shift(s4, routes(4))
     top, num, den, m1, m2, e1, e2 = call(
         near_body,
         places,
@@ -488,14 +509,20 @@
     )
     top, r4 = lax.optimization_barrier((top, r4))
     (s12,) = call(relay_body, [], [s8, r4], [((4, 128, 128), bf16)])
-    r12 = shift(s12, routes(12, active))
-    top, norm, mx0, mx1, mx2, mx3, m3, m4, e3, e4 = call(
+    r12 = shift(s12, routes(12))
+    top, s12 = lax.optimization_barrier((top, s12))
+    top, num, den, m3, e3 = call(
+        mid_body,
+        places,
+        [x, r4, top, num, den],
+        [(cube, f32)] * 3 + [((256, 128), f32), ((2, 256, 512), bf16)],
+        flops=10**9,
+    )
+    top, norm, mx0, mx1, mx2, mx3, m4, e4 = call(
         far_body,
         places,
         [x, r4, r12, top, num, den, g0, g1, g2, g3],
-        [(cube, f32)] * 2
-        + [((512, 128), bf16)] * 4
-        + [((256, 128), f32), ((128, 128), f32), ((2, 256, 512), bf16), ((2, 128, 512), bf16)],
+        [(cube, f32)] * 2 + [((512, 128), bf16)] * 4 + [((128, 128), f32), ((2, 128, 512), bf16)],
         [(cube, f32)] * 2,
         flops=10**9,
     )
@@ -533,23 +560,24 @@
     acc, attended = lax.optimization_barrier((acc, attended))
     (acc,) = call(back_two_body, places, state + [acc, m2, e2], [((3, *cube), f32)], flops=10**9)
     (acc,) = call(back_one_body, places, state + [acc, m1, e1], [((3, *cube), f32)], flops=10**9)
-    own, *outs = call(
-        finish_body,
-        places,
-        [acc, f4, f8, f12, part],
-        [(block, f32)] + [((848, 128), bf16)] * 4,
-        [((3, *cube), f32)],
-    )
-    home = [outs[0]] + [shift(outs[d], routes(d)) for d in (1, 2, 3)]
-    (own,) = call(near_sum_body, [], [own] + home[1:], [(block, bf16)])
-    arrived = dp_step(own, 2)
-    home = lax.optimization_barrier([own] + home)[1:]
+    (low,) = call(far_sum_body, [], [part, f4, f8, f12], [((288, 128), bf16)])
+    acc, low = lax.optimization_barrier((acc, low))
+    arrived = dp_step(low, 2)
+    outs = call(
+        finish_body, places, [acc, f4, f8, f12], [((768, 128), bf16)] * 4, [((3, *cube), f32)]
+    )
+    first, low = lax.optimization_barrier((outs[0], low))
+    home = [first] + [shift(outs[d], routes(d)) for d in (1, 2, 3)]
+    (low,) = call(pair_body, [], [low, arrived], [((288, 128), bf16)])
+    rest = [dp_step(low, d) for d in (4, 8, 12)]
+    (low,) = call(sum_body, [], [low] + rest, [((288, 128), bf16)])
     grads = call(home_body, [info], home, [third] * 3, [((3, 256, 512), bf16)])
-    (own,) = call(pair_body, [], [own, arrived], [(block, bf16)])
-    rest = [dp_step(own, d) for d in (4, 8, 12)]
+    own, s1, s2, s3 = call(
+        halves_body, [], [low, dp_step(low, 1)], [((144, 128), f32)] + [((144, 128), bf16)] * 3
+    )
+    near = [seq_step(b, d) for d, b in ((1, s1), (2, s2), (3, s3))]
     *grads, own = lax.optimization_barrier([*grads, own])
-    (own,) = call(sum_body, [], [own] + rest, [(block, f32)])
-    (grad_weight,) = call(join_body, [info], [own, dp_step(own, 1)], [((24, 768), f32)])
+    (grad_weight,) = call(join_body, [info], [own] + near, [((24, 768), f32)])
     return (attended[None], grads[0][None], grads[1][None], grads[2][None], grad_weight)
 
 

time: 115 us -> 110 us (0.957)
  starting transfers between devices: 54.9 us -> 43.4 us
  waiting for transfers between devices: 28.3 us -> 33.6 us
  Pallas kernels: 25.3 us -> 26.6 us
    ppermute x14, starting transfers between devices: 46.2 us -> 28.7 us  [shift(): return lax.ppermute(block, ('dp', 'seq'), pairs)]
    ppermute x0 -> x3, starting transfers between devices: none -> 4.24 us  [seq_step(): return lax.ppermute(block, 'seq', [(i, i ^ step) for i in range(16)])]
    ppermute x6, waiting for transfers between devices: 4.52 us -> 7.25 us  [dp_step(): return lax.ppermute(block, 'dp', [(i, i ^ step) for i in range(16)])]
    ppermute x6, starting transfers between devices: 8.76 us -> 10.4 us  [dp_step(): return lax.ppermute(block, 'dp', [(i, i ^ step) for i in range(16)])]
    ppermute x14, waiting for transfers between devices: 23.8 us -> 25.2 us  [shift(): return lax.ppermute(block, ('dp', 'seq'), pairs)]
    pallas_call x18 -> x20, Pallas kernels: 25.3 us -> 26.6 us  [call(): pl.pallas_call(body, out_shape=shapes, in_specs=[smem] * len(scalars) + [...]
  transfers between devices with their start and end apart: 20 -> 23, of which waited for: 10 -> 12; matrix products, arithmetic and copies ran while one was open for 0% -> 0% of each run, Pallas kernels for 14% -> 17%
where the time goes in v4:
time: 110 us; the launch traced here: 109 us
  starting transfers between devices  43.4 us (39%)
  waiting for transfers between devices  33.6 us (31%)
  Pallas kernels  26.6 us (24%)
  local copies, waits for them, and re-layouts  3.62 us (3%)
  between operations  1.47 us (1%)
    ppermute x14, starting transfers between devices, shift(): return lax.ppermute(block, ('dp', 'seq'), pairs)  28.7 us
    pallas_call x20, Pallas kernels, call(): pl.pallas_call(body, out_shape=shapes, in_specs=[smem] * len(scalars) + [...  26.6 us
    ppermute x14, waiting for transfers between devices, shift(): return lax.ppermute(block, ('dp', 'seq'), pairs)  25.2 us
    ppermute x6, starting transfers between devices, dp_step(): return lax.ppermute(block, 'dp', [(i, i ^ step) for i in range(16)])  10.4 us
    ppermute x6, waiting for transfers between devices, dp_step(): return lax.ppermute(block, 'dp', [(i, i ^ step) for i in range(16)])  7.25 us
    ppermute x3, starting transfers between devices, seq_step(): return lax.ppermute(block, 'seq', [(i, i ^ step) for i in range(16)])  4.24 us
    unnamed x14, local copies, waits for them, and re-layouts  3.62 us
  transfers between devices with their start and end apart: 23, of which 12 were waited for; matrix products, arithmetic and copies ran while one was open for 0% of the time, Pallas kernels for 17%

profile of v4, /device:TPU:1, one launch (start us, length us, event | category | flops | bytes accessed | tf_op | source)
XLA Modules:
  0.0 109.2 jit_solution(9064875237859634836)
XLA Ops:
  0.6 0.6 pad_add_fusion.info
  1.3 3.2 %shard_map.110 = (bf16[3,256,128]{2,1,0:T(8,128)(2,1)}, bf16[3,256,128]{2,1,0:T(8,128)(2,1)}, bf16[3,256,128]{2,1,0:T(8,128)(2,1)}, bf16[3,256,128]{2,1,0:T(8,128)(2,1)}) custom-call(s32[3]{0:T(128)} %pad_add_fusion.info, bf16[256,384]{1,0:T(8,128)(2,1)} %bitcast.13, bf16[256,384]{1,0:T(8,128)(2,1)} %bitcast.14, bf16[256,384]{1,0:T(8,128)(2,1)} %bitcast.15), custom_call_target="tpu_custom_call" | custom-call | bytes 1376256 | tf_op jit(solution)/shard_map/pallas_call | solution.py:431
  4.5 3.7 %collective-permute-start = (bf16[3,256,128]{2,1,0:T(8,128)(2,1)}, bf16[3,256,128]{2,1,0:T(8,128)(2,1)S(1)}, u32[]{:S(2)}, u32[]{:S(2)}) collective-permute-start(bf16[3,256,128]{2,1,0:T(8,128)(2,1)} %get-tuple-element.87), channel_id=1, source_target_pairs={{0,1},{1,0},{2,3},{3,2},{4,5},{5,4},{6,7},{7,6},{8,9},{9,8},{10,11... | collective-permute-start | bytes 589832 | tf_op jit(solution)/shard_map/ppermute | solution.py:454
  8.1 1.6 %collective-permute-start.1 = (bf16[3,256,128]{2,1,0:T(8,128)(2,1)}, bf16[3,256,128]{2,1,0:T(8,128)(2,1)S(1)}, u32[]{:S(2)}, u32[]{:S(2)}) collective-permute-start(bf16[3,256,128]{2,1,0:T(8,128)(2,1)} %get-tuple-element.88), channel_id=1, source_target_pairs={{0,2},{1,3},{2,0},{3,1},{4,6},{5,7},{6,4},{7,5},{8,10},{9,11},{10,... | collective-permute-start | bytes 589832 | tf_op jit(solution)/shard_map/ppermute | solution.py:454
  10.4 1.1 copy-done
  11.5 1.0 copy-done.2
  12.5 0.9 copy-done.3
  13.4 0.6 copy-done.4
  14.0 1.1 %shard_map.111 = (bf16[256,768]{1,0:T(8,128)(2,1)S(1)}, bf16[256,128]{1,0:T(8,128)(2,1)S(1)}, bf16[256,128]{1,0:T(8,128)(2,1)S(1)}, bf16[256,128]{1,0:T(8,128)(2...) custom-call(s32[3]{0:T(128)S(1)} %copy-done.4, bf16[256,768]{1,0:T(8,128)(2,1)S(1)} %bitcast.11, ...), custom_call_target="tpu_custom_call" | custom-call | flops 300000000 | bytes 2031616 | tf_op jit(solution)/shard_map/pallas_call | solution.py:431
  15.2 4.1 %collective-permute-done.2.m3 = bf16[3,256,128]{2,1,0:T(8,128)(2,1)S(1)} collective-permute-done((bf16[3,256,128]{2,1,0:T(8,128)(2,1)}, bf16[3,256,128]{2,1,0:T(8,128)(2,1)S(1)}, u32[]{:S(2)}, u32[]{:S(2)}) %collective-permute-start.2) | collective-permute-done | bytes 196640 | tf_op jit(solution)/shard_map/ppermute | solution.py:454
  19.3 0.7 shard_map.112
  20.0 1.9 %collective-permute-start.3 = (bf16[2,384,128]{2,1,0:T(8,128)(2,1)S(1)}, bf16[2,384,128]{2,1,0:T(8,128)(2,1)S(1)}, u32[]{:S(2)}, u32[]{:S(2)}) collective-permute-start(bf16[2,384,128]{2,1,0:T(8,128)(2,1)S(1)} %get-tuple-element.92), channel_id=1, source_target_pairs={{0,4},{1,5},{2,6},{3,7},{4,0},{5,1},{6,2},{7,3},{8,12},{9,13},{10,... | collective-permute-start | bytes 589832 | tf_op jit(solution)/shard_map/ppermute | solution.py:454
  21.9 3.3 %shard_map.113 = (f32[8,128,128]{2,1,0:T(8,128)S(1)}, f32[8,128,128]{2,1,0:T(8,128)S(1)}, f32[8,128,128]{2,1,0:T(8,128)S(1)}, f32[8,128,128]{2,1,0:T(8,128)S(1)}...) custom-call(s32[3]{0:T(128)S(1)} %copy-done.4, ...), custom_call_target="tpu_custom_call" | custom-call | flops 1000000000 | bytes 5242880 | tf_op jit(solution)/shard_map/pallas_call | solution.py:431
  25.2 6.1 %collective-permute-done.3.r4 = bf16[2,384,128]{2,1,0:T(8,128)(2,1)S(1)} collective-permute-done((bf16[2,384,128]{2,1,0:T(8,128)(2,1)S(1)}, bf16[2,384,128]{2,1,0:T(8,128)(2,1)S(1)}, u32[]{:S(2)}, u32[]{:S(2)}) %collective-permute-start.3) | collective-permute-done | bytes 196640 | tf_op jit(solution)/shard_map/ppermute | solution.py:454
  31.3 3.5 %collective-permute-start.4 = (bf16[4,128,128]{2,1,0:T(8,128)(2,1)S(1)}, bf16[4,128,128]{2,1,0:T(8,128)(2,1)S(1)}, u32[]{:S(2)}, u32[]{:S(2)}) collective-permute-start(bf16[4,128,128]{2,1,0:T(8,128)(2,1)S(1)} %shard_map.114), channel_id=1, source_target_pairs={{0,12},{1,13},{2,14},{3,15},{4,8},{5,9},{6,10},{7,11},{8,4},{9,5},... | collective-permute-start | bytes 393224 | tf_op jit(solution)/shard_map/ppermute | solution.py:454
  34.9 1.7 %shard_map.115 = (f32[8,128,128]{2,1,0:T(8,128)S(1)}, f32[8,128,128]{2,1,0:T(8,128)S(1)}, f32[8,128,128]{2,1,0:T(8,128)S(1)}, f32[256,128]{1,0:T(8,128)S(1)}, bf16[2,256,512]{2,1,0:T(8,128)(2,1)S(1)}) custom-call(s32[3]{0:T(128)S(1)} %copy-done.4, s32[3,6]{1,0:T(4,128)S(1)} %copy-done.6, s32[1]{0:T(128)S(6)} %copy.12.counts, ...), custom_call_target="tpu_custom_call" | custom-call | flops 1000000000 | bytes 4784128 | tf_op jit(solution)/shard_map/pallas_call | solution.py:431
  36.6 1.4 %collective-permute-done.4.r12 = bf16[4,128,128]{2,1,0:T(8,128)(2,1)S(1)} collective-permute-done((bf16[4,128,128]{2,1,0:T(8,128)(2,1)S(1)}, bf16[4,128,128]{2,1,0:T(8,128)(2,1)S(1)}, u32[]{:S(2)}, u32[]{:S(2)}) %collective-permute-start.4) | collective-permute-done | bytes 131104 | tf_op jit(solution)/shard_map/ppermute | solution.py:454
  38.0 1.5 %shard_map.116 = (f32[8,128,128]{2,1,0:T(8,128)S(1)}, f32[8,128,128]{2,1,0:T(8,128)S(1)}, bf16[512,128]{1,0:T(8,128)(2,1)S(1)}, bf16[512,128]{1,0:T(8,128)(2,1)S...) custom-call(s32[3]{0:T(128)S(1)} %copy-done.4, ...), custom_call_target="tpu_custom_call" | custom-call | flops 1000000000 | bytes 4849664 | tf_op jit(solution)/shard_map/pallas_call | solution.py:431
  39.5 2.0 %collective-permute-start.5 = (bf16[512,128]{1,0:T(8,128)(2,1)S(1)}, bf16[512,128]{1,0:T(8,128)(2,1)S(1)}, u32[]{:S(2)}, u32[]{:S(2)}) collective-permute-start(bf16[512,128]{1,0:T(8,128)(2,1)S(1)} %get-tuple-element.113.mx1), channel_id=1, source_target_pairs={{0,1},{1,0},{2,3},{3,2},{4,5},{5,4},{6,7},{7,6},{8,9},{9,8},{10,11... | collective-permute-start | bytes 393224 | tf_op jit(solution)/shard_map/ppermute | solution.py:454
  41.5 5.6 %collective-permute-start.6 = (bf16[512,128]{1,0:T(8,128)(2,1)S(1)}, bf16[512,128]{1,0:T(8,128)(2,1)S(1)}, u32[]{:S(2)}, u32[]{:S(2)}) collective-permute-start(bf16[512,128]{1,0:T(8,128)(2,1)S(1)} %get-tuple-element.114.mx2), channel_id=1, source_target_pairs={{0,2},{1,3},{2,0},{3,1},{4,6},{5,7},{6,4},{7,5},{8,10},{9,11},{10,... | collective-permute-start | bytes 393224 | tf_op jit(solution)/shard_map/ppermute | solution.py:454
  47.1 0.5 collective-permute-start.7
  47.5 2.6 %collective-permute-done.6.m2.in2 = bf16[512,128]{1,0:T(8,128)(2,1)S(1)} collective-permute-done((bf16[512,128]{1,0:T(8,128)(2,1)S(1)}, bf16[512,128]{1,0:T(8,128)(2,1)S(1)}, u32[]{:S(2)}, u32[]{:S(2)}) %collective-permute-start.6) | collective-permute-done | bytes 131104 | tf_op jit(solution)/shard_map/ppermute | solution.py:454
  50.2 3.1 %collective-permute-done.7.m3.in3 = bf16[512,128]{1,0:T(8,128)(2,1)S(1)} collective-permute-done((bf16[512,128]{1,0:T(8,128)(2,1)S(1)}, bf16[512,128]{1,0:T(8,128)(2,1)S(1)}, u32[]{:S(2)}, u32[]{:S(2)}) %collective-permute-start.7) | collective-permute-done | bytes 131104 | tf_op jit(solution)/shard_map/ppermute | solution.py:454
  53.3 1.1 shard_map.117
  54.4 2.5 %collective-permute-start.8 = (bf16[16,72,128]{2,1,0:T(8,128)(2,1)S(1)}, bf16[16,72,128]{2,1,0:T(8,128)(2,1)S(1)}, u32[]{:S(2)}, u32[]{:S(2)}) collective-permute-start(bf16[16,72,128]{2,1,0:T(8,128)(2,1)S(1)} %get-tuple-element.124), channel_id=1, source_target_pairs={{0,16},{16,0},{32,48},{48,32},{64,80},{80,64},{96,112},{112,96},{1... | collective-permute-start | bytes 884744 | tf_op jit(solution)/shard_map/ppermute | solution.py:458
  56.8 2.8 %shard_map.118 = (bf16[8,128,128]{2,1,0:T(8,128)(2,1)S(1)}, f32[8,128,128]{2,1,0:T(8,128)S(1)}, f32[3,8,128,128]{3,2,1,0:T(8,128)S(1)}, bf16[2,384,128]{2,1,0:T(...) custom-call(s32[3]{0:T(128)S(1)} %copy-done.4, s32[3,6]{1,0:T(4,128)S(1)} %copy-done.6, ...), custom_call_target="tpu_custom_call" | custom-call | flops 1000000000 | bytes 6881280 | tf_op jit(solution)/shard_map/pallas_call | solution.py:431
  59.8 2.0 %collective-permute-start.9 = (bf16[1056,128]{1,0:T(8,128)(2,1)S(1)}, bf16[1056,128]{1,0:T(8,128)(2,1)S(1)}, u32[]{:S(2)}, u32[]{:S(2)}) collective-permute-start(bf16[1056,128]{1,0:T(8,128)(2,1)S(1)} %get-tuple-element.143), channel_id=1, source_target_pairs={{0,4},{1,5},{2,6},{3,7},{4,0},{5,1},{6,2},{7,3},{8,12},{9,13},{10,... | collective-permute-start | bytes 811016 | tf_op jit(solution)/shard_map/ppermute | solution.py:454
  61.7 2.1 %collective-permute-start.10 = (bf16[544,128]{1,0:T(8,128)(2,1)S(1)}, bf16[544,128]{1,0:T(8,128)(2,1)S(1)}, u32[]{:S(2)}, u32[]{:S(2)}) collective-permute-start(bf16[544,128]{1,0:T(8,128)(2,1)S(1)} %get-tuple-element.144), channel_id=1, source_target_pairs={{0,8},{1,9},{2,10},{3,11},{4,12},{5,13},{6,14},{7,15},{8,0},{9,1},... | collective-permute-start | bytes 417800 | tf_op jit(solution)/shard_map/ppermute | solution.py:454
  63.8 1.7 %collective-permute-start.11 = (bf16[544,128]{1,0:T(8,128)(2,1)S(1)}, bf16[544,128]{1,0:T(8,128)(2,1)S(1)}, u32[]{:S(2)}, u32[]{:S(2)}) collective-permute-start(bf16[544,128]{1,0:T(8,128)(2,1)S(1)} %get-tuple-element.145), channel_id=1, source_target_pairs={{0,12},{1,13},{2,14},{3,15},{4,8},{5,9},{6,10},{7,11},{8,4},{9,5},... | collective-permute-start | bytes 417800 | tf_op jit(solution)/shard_map/ppermute | solution.py:454
  65.5 1.9 %shard_map.120 = bf16[256,768]{1,0:T(8,128)(2,1)} custom-call(s32[3]{0:T(128)S(1)} %copy-done.4, bf16[512,128]{1,0:T(8,128)(2,1)S(1)} %get-tuple-element.130.m0.mx0.in0, bf16[512,128]{1,0:T(8,128)(2,1)S(1)} %collective-permute-done.5.m1.in1, bf16[512,128]{1,0:T(8,128)(2,1)S(1)} %collective-permute-done.6.m2.in2, ...), custom_call_target="tpu_custom_call" | custom-call | flops 300000000 | bytes 1507328 | tf_op jit(solution)/shard_map/pallas_call | solution.py:431
  67.4 2.8 %shard_map.121.acc_in = f32[3,8,128,128]{3,2,1,0:T(8,128)S(1)} custom-call(s32[3]{0:T(128)S(1)} %copy-done.4, s32[3,6]{1,0:T(4,128)S(1)} %copy-done.6, s32[1]{0:T(128)S(6)} %copy.12.counts, bf16[3,8,128,128]{3,2,1,0:T(8,128)(2,1)S(1)} %get-tuple-element.90.x, bf16[8,128,128]{2,1,0:T(8,128)(2,1)S(1)} %get-tuple-element.135.g, ...), custom_call_target="tpu_custom_call" | custom-call | flops 1000000000 | bytes 7077888 | tf_op jit(solution)/shard_map/pallas_call | solution.py:431
  70.2 2.5 %shard_map.122.acc_in = f32[3,8,128,128]{3,2,1,0:T(8,128)S(1)} custom-call(s32[3]{0:T(128)S(1)} %copy-done.4, s32[3,6]{1,0:T(4,128)S(1)} %copy-done.6, s32[1]{0:T(128)S(6)} %copy.12.counts, bf16[3,8,128,128]{3,2,1,0:T(8,128)(2,1)S(1)} %get-tuple-element.90.x, bf16[8,128,128]{2,1,0:T(8,128)(2,1)S(1)} %get-tuple-element.135.g, ...), custom_call_target="tpu_custom_call" | custom-call | flops 1000000000 | bytes 7340032 | tf_op jit(solution)/shard_map/pallas_call | solution.py:431
  72.7 4.6 %collective-permute-done.10.f8.r8 = bf16[544,128]{1,0:T(8,128)(2,1)S(1)} collective-permute-done((bf16[544,128]{1,0:T(8,128)(2,1)S(1)}, bf16[544,128]{1,0:T(8,128)(2,1)S(1)}, u32[]{:S(2)}, u32[]{:S(2)}) %collective-permute-start.10) | collective-permute-done | bytes 139296 | tf_op jit(solution)/shard_map/ppermute | solution.py:454
  77.5 3.1 %collective-permute-done.9.f4.r4 = bf16[1056,128]{1,0:T(8,128)(2,1)S(1)} collective-permute-done((bf16[1056,128]{1,0:T(8,128)(2,1)S(1)}, bf16[1056,128]{1,0:T(8,128)(2,1)S(1)}, u32[]{:S(2)}, u32[]{:S(2)}) %collective-permute-start.9) | collective-permute-done | bytes 270368 | tf_op jit(solution)/shard_map/ppermute | solution.py:454
  80.6 0.4 collective-permute-start.15
  81.0 0.9 shard_map.124
  81.9 2.0 %collective-permute-done.15.b = bf16[288,128]{1,0:T(8,128)(2,1)S(1)} collective-permute-done((bf16[288,128]{1,0:T(8,128)(2,1)S(1)}, bf16[288,128]{1,0:T(8,128)(2,1)S(1)}, u32[]{:S(2)}, u32[]{:S(2)}) %collective-permute-start.15) | collective-permute-done | bytes 73760 | tf_op jit(solution)/shard_map/ppermute | solution.py:458
  84.0 2.8 %collective-permute-start.18 = (bf16[288,128]{1,0:T(8,128)(2,1)S(1)}, bf16[288,128]{1,0:T(8,128)(2,1)S(1)}, u32[]{:S(2)}, u32[]{:S(2)}) collective-permute-start(bf16[288,128]{1,0:T(8,128)(2,1)S(1)} %shard_map.126.a), channel_id=1, source_target_pairs={{0,192},{16,208},{32,224},{48,240},{64,128},{80,144},{96,160},{112... | collective-permute-start | bytes 221192 | tf_op jit(solution)/shard_map/ppermute | solution.py:458
  86.8 1.5 %collective-permute-start.12 = (bf16[768,128]{1,0:T(8,128)(2,1)S(1)}, bf16[768,128]{1,0:T(8,128)(2,1)S(1)}, u32[]{:S(2)}, u32[]{:S(2)}) collective-permute-start(bf16[768,128]{1,0:T(8,128)(2,1)S(1)} %get-tuple-element.150), channel_id=1, source_target_pairs={{0,1},{1,0},{2,3},{3,2},{4,5},{5,4},{6,7},{7,6},{8,9},{9,8},{10,11... | collective-permute-start | bytes 589832 | tf_op jit(solution)/shard_map/ppermute | solution.py:454
  88.3 2.6 %collective-permute-start.14 = (bf16[768,128]{1,0:T(8,128)(2,1)S(1)}, bf16[768,128]{1,0:T(8,128)(2,1)S(1)}, u32[]{:S(2)}, u32[]{:S(2)}) collective-permute-start(bf16[768,128]{1,0:T(8,128)(2,1)S(1)} %get-tuple-element.152), channel_id=1, source_target_pairs={{0,3},{1,2},{2,1},{3,0},{4,7},{5,6},{6,5},{7,4},{8,11},{9,10},{10,... | collective-permute-start | bytes 589832 | tf_op jit(solution)/shard_map/ppermute | solution.py:454
  91.6 4.3 %collective-permute-done.17.c = bf16[288,128]{1,0:T(8,128)(2,1)S(1)} collective-permute-done((bf16[288,128]{1,0:T(8,128)(2,1)S(1)}, bf16[288,128]{1,0:T(8,128)(2,1)S(1)}, u32[]{:S(2)}, u32[]{:S(2)}) %collective-permute-start.17) | collective-permute-done | bytes 73760 | tf_op jit(solution)/shard_map/ppermute | solution.py:458
  96.0 4.0 %collective-permute-start.19 = (bf16[288,128]{1,0:T(8,128)(2,1)S(1)}, bf16[288,128]{1,0:T(8,128)(2,1)S(1)}, u32[]{:S(2)}, u32[]{:S(2)}) collective-permute-start(bf16[288,128]{1,0:T(8,128)(2,1)S(1)} %shard_map.127.mine), channel_id=1, source_target_pairs={{0,16},{16,0},{32,48},{48,32},{64,80},{80,64},{96,112},{112,96},{1... | collective-permute-start | bytes 221192 | tf_op jit(solution)/shard_map/ppermute | solution.py:458
  100.0 0.9 collective-permute-done.19.other
  101.0 1.6 %collective-permute-start.20 = (bf16[144,128]{1,0:T(8,128)(2,1)S(1)}, bf16[144,128]{1,0:T(8,128)(2,1)S(1)}, u32[]{:S(2)}, u32[]{:S(2)}) collective-permute-start(bf16[144,128]{1,0:T(8,128)(2,1)S(1)} %get-tuple-element.162), channel_id=1, source_target_pairs={{0,1},{1,0},{2,3},{3,2},{4,5},{5,4},{6,7},{7,6},{8,9},{9,8},{10,11... | collective-permute-start | bytes 110600 | tf_op jit(solution)/shard_map/ppermute | solution.py:462
  102.6 2.6 %collective-permute-start.22 = (bf16[144,128]{1,0:T(8,128)(2,1)S(1)}, bf16[144,128]{1,0:T(8,128)(2,1)S(1)}, u32[]{:S(2)}, u32[]{:S(2)}) collective-permute-start(bf16[144,128]{1,0:T(8,128)(2,1)S(1)} %get-tuple-element.164), channel_id=1, source_target_pairs={{0,3},{1,2},{2,1},{3,0},{4,7},{5,6},{6,5},{7,4},{8,11},{9,10},{10,... | collective-permute-start | bytes 110600 | tf_op jit(solution)/shard_map/ppermute | solution.py:462
  105.2 1.7 %shard_map.125 = (bf16[256,384]{1,0:T(8,128)(2,1)}, bf16[256,384]{1,0:T(8,128)(2,1)}, bf16[256,384]{1,0:T(8,128)(2,1)}) custom-call(s32[3]{0:T(128)S(1)} %copy-done.5, bf16[768,128]{1,0:T(8,128)(2,1)S(1)} %get-tuple-element.149.m0, bf16[768,128]{1,0:T(8,128)(2,1)S(1)} %collective-permute-done.12.m1, bf16[768,128]{1,0:T(8,128)(2,1)S(1)} %collective-permute-done.13.m2, ...), custom_call_target="tpu_custom_call" | custom-call | bytes 1376256 | tf_op jit(solution)/shard_map/pallas_call | solution.py:431
  106.9 1.1 collective-permute-done.22.c
  108.0 1.2 %shard_map.129 = f32[24,768]{1,0:T(8,128)} custom-call(s32[3]{0:T(128)S(1)} %copy-done.5, f32[144,128]{1,0:T(8,128)S(1)} %get-tuple-element.161.own, bf16[144,128]{1,0:T(8,128)(2,1)S(1)} %collective-permute-done.20.a, bf16[144,128]{1,0:T(8,128)(2,1)S(1)} %collective-permute-done.21.b, bf16[144,128]{1,0:T(8,128)(2,1)S(1)} %collective-permute-done.22.c), custom_call_target="tpu_custom_call" | custom-call | bytes 258048 | tf_op jit(solution)/shard_map/pallas_call | solution.py:431
  (33 shorter events, 1.1 us)
Async XLA Ops:
  0.6 18.7 %copy-start.6 = (s32[3,6]{1,0:T(4,128)S(1)}, s32[3,6]{1,0:T(4,128)}, u32[]{:S(2)}) copy-start(s32[3,6]{1,0:T(4,128)} %offsets.15) | copy-start | bytes 220
  4.5 10.7 %collective-permute-start = (bf16[3,256,128]{2,1,0:T(8,128)(2,1)}, bf16[3,256,128]{2,1,0:T(8,128)(2,1)S(1)}, u32[]{:S(2)}, u32[]{:S(2)}) collective-permute-start(bf16[3,256,128]{2,1,0:T(8,128)(2,1)} %get-tuple-element.87), channel_id=1, source_target_pairs={{0,1},{1,0},{2,3},{3,2},{4,5},{5,4},{6,7},{7,6},{8,9},{9,8},{10,11... | collective-permute-start | bytes 589832 | tf_op jit(solution)/shard_map/ppermute | solution.py:454
  8.1 7.0 %collective-permute-start.1 = (bf16[3,256,128]{2,1,0:T(8,128)(2,1)}, bf16[3,256,128]{2,1,0:T(8,128)(2,1)S(1)}, u32[]{:S(2)}, u32[]{:S(2)}) collective-permute-start(bf16[3,256,128]{2,1,0:T(8,128)(2,1)} %get-tuple-element.88), channel_id=1, source_target_pairs={{0,2},{1,3},{2,0},{3,1},{4,6},{5,7},{6,4},{7,5},{8,10},{9,11},{10,... | collective-permute-start | bytes 589832 | tf_op jit(solution)/shard_map/ppermute | solution.py:454
  9.8 9.5 %collective-permute-start.2 = (bf16[3,256,128]{2,1,0:T(8,128)(2,1)}, bf16[3,256,128]{2,1,0:T(8,128)(2,1)S(1)}, u32[]{:S(2)}, u32[]{:S(2)}) collective-permute-start(bf16[3,256,128]{2,1,0:T(8,128)(2,1)} %get-tuple-element.89), channel_id=1, source_target_pairs={{0,3},{1,2},{2,1},{3,0},{4,7},{5,6},{6,5},{7,4},{8,11},{9,10},{10,... | collective-permute-start | bytes 589832 | tf_op jit(solution)/shard_map/ppermute | solution.py:454
  10.4 1.1 copy-start
  11.5 1.0 copy-start.2
  12.5 0.9 copy-start.3
  13.4 0.6 copy-start.4
  20.0 11.3 %collective-permute-start.3 = (bf16[2,384,128]{2,1,0:T(8,128)(2,1)S(1)}, bf16[2,384,128]{2,1,0:T(8,128)(2,1)S(1)}, u32[]{:S(2)}, u32[]{:S(2)}) collective-permute-start(bf16[2,384,128]{2,1,0:T(8,128)(2,1)S(1)} %get-tuple-element.92), channel_id=1, source_target_pairs={{0,4},{1,5},{2,6},{3,7},{4,0},{5,1},{6,2},{7,3},{8,12},{9,13},{10,... | collective-permute-start | bytes 589832 | tf_op jit(solution)/shard_map/ppermute | solution.py:454
  31.3 6.7 %collective-permute-start.4 = (bf16[4,128,128]{2,1,0:T(8,128)(2,1)S(1)}, bf16[4,128,128]{2,1,0:T(8,128)(2,1)S(1)}, u32[]{:S(2)}, u32[]{:S(2)}) collective-permute-start(bf16[4,128,128]{2,1,0:T(8,128)(2,1)S(1)} %shard_map.114), channel_id=1, source_target_pairs={{0,12},{1,13},{2,14},{3,15},{4,8},{5,9},{6,10},{7,11},{8,4},{9,5},... | collective-permute-start | bytes 393224 | tf_op jit(solution)/shard_map/ppermute | solution.py:454
  39.5 8.1 %collective-permute-start.5 = (bf16[512,128]{1,0:T(8,128)(2,1)S(1)}, bf16[512,128]{1,0:T(8,128)(2,1)S(1)}, u32[]{:S(2)}, u32[]{:S(2)}) collective-permute-start(bf16[512,128]{1,0:T(8,128)(2,1)S(1)} %get-tuple-element.113.mx1), channel_id=1, source_target_pairs={{0,1},{1,0},{2,3},{3,2},{4,5},{5,4},{6,7},{7,6},{8,9},{9,8},{10,11... | collective-permute-start | bytes 393224 | tf_op jit(solution)/shard_map/ppermute | solution.py:454
  41.5 8.7 %collective-permute-start.6 = (bf16[512,128]{1,0:T(8,128)(2,1)S(1)}, bf16[512,128]{1,0:T(8,128)(2,1)S(1)}, u32[]{:S(2)}, u32[]{:S(2)}) collective-permute-start(bf16[512,128]{1,0:T(8,128)(2,1)S(1)} %get-tuple-element.114.mx2), channel_id=1, source_target_pairs={{0,2},{1,3},{2,0},{3,1},{4,6},{5,7},{6,4},{7,5},{8,10},{9,11},{10,... | collective-permute-start | bytes 393224 | tf_op jit(solution)/shard_map/ppermute | solution.py:454
  47.1 6.2 %collective-permute-start.7 = (bf16[512,128]{1,0:T(8,128)(2,1)S(1)}, bf16[512,128]{1,0:T(8,128)(2,1)S(1)}, u32[]{:S(2)}, u32[]{:S(2)}) collective-permute-start(bf16[512,128]{1,0:T(8,128)(2,1)S(1)} %get-tuple-element.115.mx3), channel_id=1, source_target_pairs={{0,3},{1,2},{2,1},{3,0},{4,7},{5,6},{6,5},{7,4},{8,11},{9,10},{10,... | collective-permute-start | bytes 393224 | tf_op jit(solution)/shard_map/ppermute | solution.py:454
  54.4 5.3 %collective-permute-start.8 = (bf16[16,72,128]{2,1,0:T(8,128)(2,1)S(1)}, bf16[16,72,128]{2,1,0:T(8,128)(2,1)S(1)}, u32[]{:S(2)}, u32[]{:S(2)}) collective-permute-start(bf16[16,72,128]{2,1,0:T(8,128)(2,1)S(1)} %get-tuple-element.124), channel_id=1, source_target_pairs={{0,16},{16,0},{32,48},{48,32},{64,80},{80,64},{96,112},{112,96},{1... | collective-permute-start | bytes 884744 | tf_op jit(solution)/shard_map/ppermute | solution.py:458
  59.7 5.8 %copy-start.1 = (bf16[384,768]{1,0:T(8,128)(2,1)S(1)}, bf16[384,768]{1,0:T(8,128)(2,1)}, u32[]{:S(2)}) copy-start(bf16[384,768]{1,0:T(8,128)(2,1)} %w.3) | copy-start | bytes 1769476
  59.8 20.8 %collective-permute-start.9 = (bf16[1056,128]{1,0:T(8,128)(2,1)S(1)}, bf16[1056,128]{1,0:T(8,128)(2,1)S(1)}, u32[]{:S(2)}, u32[]{:S(2)}) collective-permute-start(bf16[1056,128]{1,0:T(8,128)(2,1)S(1)} %get-tuple-element.143), channel_id=1, source_target_pairs={{0,4},{1,5},{2,6},{3,7},{4,0},{5,1},{6,2},{7,3},{8,12},{9,13},{10,... | collective-permute-start | bytes 811016 | tf_op jit(solution)/shard_map/ppermute | solution.py:454
  61.7 15.6 %collective-permute-start.10 = (bf16[544,128]{1,0:T(8,128)(2,1)S(1)}, bf16[544,128]{1,0:T(8,128)(2,1)S(1)}, u32[]{:S(2)}, u32[]{:S(2)}) collective-permute-start(bf16[544,128]{1,0:T(8,128)(2,1)S(1)} %get-tuple-element.144), channel_id=1, source_target_pairs={{0,8},{1,9},{2,10},{3,11},{4,12},{5,13},{6,14},{7,15},{8,0},{9,1},... | collective-permute-start | bytes 417800 | tf_op jit(solution)/shard_map/ppermute | solution.py:454
  63.8 13.7 %collective-permute-start.11 = (bf16[544,128]{1,0:T(8,128)(2,1)S(1)}, bf16[544,128]{1,0:T(8,128)(2,1)S(1)}, u32[]{:S(2)}, u32[]{:S(2)}) collective-permute-start(bf16[544,128]{1,0:T(8,128)(2,1)S(1)} %get-tuple-element.145), channel_id=1, source_target_pairs={{0,12},{1,13},{2,14},{3,15},{4,8},{5,9},{6,10},{7,11},{8,4},{9,5},... | collective-permute-start | bytes 417800 | tf_op jit(solution)/shard_map/ppermute | solution.py:454
  80.6 24.6 %copy-start.5 = (s32[3]{0:T(128)S(1)}, s32[3]{0:T(128)}, u32[]{:S(2)}) copy-start(s32[3]{0:T(128)} %pad_add_fusion.info) | copy-start | bytes 40
  80.6 3.3 %collective-permute-start.15 = (bf16[288,128]{1,0:T(8,128)(2,1)S(1)}, bf16[288,128]{1,0:T(8,128)(2,1)S(1)}, u32[]{:S(2)}, u32[]{:S(2)}) collective-permute-start(bf16[288,128]{1,0:T(8,128)(2,1)S(1)} %shard_map.123.a), channel_id=1, source_target_pairs={{0,32},{16,48},{32,0},{48,16},{64,96},{80,112},{96,64},{112,80},{1... | collective-permute-start | bytes 221192 | tf_op jit(solution)/shard_map/ppermute | solution.py:458
  84.0 7.3 %collective-permute-start.18 = (bf16[288,128]{1,0:T(8,128)(2,1)S(1)}, bf16[288,128]{1,0:T(8,128)(2,1)S(1)}, u32[]{:S(2)}, u32[]{:S(2)}) collective-permute-start(bf16[288,128]{1,0:T(8,128)(2,1)S(1)} %shard_map.126.a), channel_id=1, source_target_pairs={{0,192},{16,208},{32,224},{48,240},{64,128},{80,144},{96,160},{112... | collective-permute-start | bytes 221192 | tf_op jit(solution)/shard_map/ppermute | solution.py:458
  86.8 15.8 %collective-permute-start.12 = (bf16[768,128]{1,0:T(8,128)(2,1)S(1)}, bf16[768,128]{1,0:T(8,128)(2,1)S(1)}, u32[]{:S(2)}, u32[]{:S(2)}) collective-permute-start(bf16[768,128]{1,0:T(8,128)(2,1)S(1)} %get-tuple-element.150), channel_id=1, source_target_pairs={{0,1},{1,0},{2,3},{3,2},{4,5},{5,4},{6,7},{7,6},{8,9},{9,8},{10,11... | collective-permute-start | bytes 589832 | tf_op jit(solution)/shard_map/ppermute | solution.py:454
  88.3 16.9 %collective-permute-start.13 = (bf16[768,128]{1,0:T(8,128)(2,1)S(1)}, bf16[768,128]{1,0:T(8,128)(2,1)S(1)}, u32[]{:S(2)}, u32[]{:S(2)}) collective-permute-start(bf16[768,128]{1,0:T(8,128)(2,1)S(1)} %get-tuple-element.151), channel_id=1, source_target_pairs={{0,2},{1,3},{2,0},{3,1},{4,6},{5,7},{6,4},{7,5},{8,10},{9,11},{10,... | collective-permute-start | bytes 589832 | tf_op jit(solution)/shard_map/ppermute | solution.py:454
  88.3 16.9 %collective-permute-start.14 = (bf16[768,128]{1,0:T(8,128)(2,1)S(1)}, bf16[768,128]{1,0:T(8,128)(2,1)S(1)}, u32[]{:S(2)}, u32[]{:S(2)}) collective-permute-start(bf16[768,128]{1,0:T(8,128)(2,1)S(1)} %get-tuple-element.152), channel_id=1, source_target_pairs={{0,3},{1,2},{2,1},{3,0},{4,7},{5,6},{6,5},{7,4},{8,11},{9,10},{10,... | collective-permute-start | bytes 589832 | tf_op jit(solution)/shard_map/ppermute | solution.py:454
  90.9 5.0 %collective-permute-start.17 = (bf16[288,128]{1,0:T(8,128)(2,1)S(1)}, bf16[288,128]{1,0:T(8,128)(2,1)S(1)}, u32[]{:S(2)}, u32[]{:S(2)}) collective-permute-start(bf16[288,128]{1,0:T(8,128)(2,1)S(1)} %shard_map.126.a), channel_id=1, source_target_pairs={{0,128},{16,144},{32,160},{48,176},{64,192},{80,208},{96,224},{112... | collective-permute-start | bytes 221192 | tf_op jit(solution)/shard_map/ppermute | solution.py:458
  91.3 4.7 %collective-permute-start.16 = (bf16[288,128]{1,0:T(8,128)(2,1)S(1)}, bf16[288,128]{1,0:T(8,128)(2,1)S(1)}, u32[]{:S(2)}, u32[]{:S(2)}) collective-permute-start(bf16[288,128]{1,0:T(8,128)(2,1)S(1)} %shard_map.126.a), channel_id=1, source_target_pairs={{0,64},{16,80},{32,96},{48,112},{64,0},{80,16},{96,32},{112,48},{1... | collective-permute-start | bytes 221192 | tf_op jit(solution)/shard_map/ppermute | solution.py:458
  96.0 4.9 %collective-permute-start.19 = (bf16[288,128]{1,0:T(8,128)(2,1)S(1)}, bf16[288,128]{1,0:T(8,128)(2,1)S(1)}, u32[]{:S(2)}, u32[]{:S(2)}) collective-permute-start(bf16[288,128]{1,0:T(8,128)(2,1)S(1)} %shard_map.127.mine), channel_id=1, source_target_pairs={{0,16},{16,0},{32,48},{48,32},{64,80},{80,64},{96,112},{112,96},{1... | collective-permute-start | bytes 221192 | tf_op jit(solution)/shard_map/ppermute | solution.py:458
  101.0 6.0 %collective-permute-start.20 = (bf16[144,128]{1,0:T(8,128)(2,1)S(1)}, bf16[144,128]{1,0:T(8,128)(2,1)S(1)}, u32[]{:S(2)}, u32[]{:S(2)}) collective-permute-start(bf16[144,128]{1,0:T(8,128)(2,1)S(1)} %get-tuple-element.162), channel_id=1, source_target_pairs={{0,1},{1,0},{2,3},{3,2},{4,5},{5,4},{6,7},{7,6},{8,9},{9,8},{10,11... | collective-permute-start | bytes 110600 | tf_op jit(solution)/shard_map/ppermute | solution.py:462
  102.6 4.4 %collective-permute-start.21 = (bf16[144,128]{1,0:T(8,128)(2,1)S(1)}, bf16[144,128]{1,0:T(8,128)(2,1)S(1)}, u32[]{:S(2)}, u32[]{:S(2)}) collective-permute-start(bf16[144,128]{1,0:T(8,128)(2,1)S(1)} %get-tuple-element.163), channel_id=1, source_target_pairs={{0,2},{1,3},{2,0},{3,1},{4,6},{5,7},{6,4},{7,5},{8,10},{9,11},{10,... | collective-permute-start | bytes 110600 | tf_op jit(solution)/shard_map/ppermute | solution.py:462
  102.6 5.5 %collective-permute-start.22 = (bf16[144,128]{1,0:T(8,128)(2,1)S(1)}, bf16[144,128]{1,0:T(8,128)(2,1)S(1)}, u32[]{:S(2)}, u32[]{:S(2)}) collective-permute-start(bf16[144,128]{1,0:T(8,128)(2,1)S(1)} %get-tuple-element.164), channel_id=1, source_target_pairs={{0,3},{1,2},{2,1},{3,0},{4,7},{5,6},{6,5},{7,4},{8,11},{9,10},{10,... | collective-permute-start | bytes 110600 | tf_op jit(solution)/shard_map/ppermute | solution.py:462

commit v5 on v4

--- a/solution.py
+++ b/solution.py
@@ -118,15 +118,18 @@
 
 
 def back(q2, k2, v2, gf2, fd2, es):
-    dq = dk = dv = None
+    low = gf2.astype(bf16)
+    qt, gt = q2.astype(f32).T.astype(bf16), gf2.T.astype(bf16)
+    dq, dks, dvs = None, [], []
     for h in (0, 1):
-        kh, vh = half_of(k2, h), half_of(v2, h)
-        e = es[h]
-        dp = dot_nt(gf2, vh)
+        e, at = es[h], slice(64 * h, 64 * h + 64)
+        dp = dot_nt(low, half_of(v2, h))
         ds = (e.astype(f32) * (dp - fd2[:, 64 * h : 64 * h + 1])).astype(bf16)
-        a, b, c = dot_nn(ds, kh), dot_tn(ds, half_of(q2, h)), dot_tn(e, half_of(gf2, h))
-        dq, dk, dv = (a, b, c) if dq is None else (dq + a, dk + b, dv + c)
-    return dq, dk, dv
+        a = dot_nn(ds, half_of(k2, h))
+        dq = a if dq is None else dq + a
+        dks.append(dot_nn(qt[at], ds))
+        dvs.append(dot_nn(gt[at], e))
+    return dq, jnp.concatenate(dks, axis=0).T, jnp.concatenate(dvs, axis=0).T
 
 
 def copies(pairs, sems):
@@ -136,15 +139,16 @@
     return moves
 
 
-def prep_body(info, q_in, k_in, v_in, o0, o1, o2, o3, px, q, k, v, sems):
+def prep_body(q_in, k_in, v_in, o0, o1, o2, o3, px, q, k, v, sems):
     moves = copies(((q_in, q), (k_in, k), (v_in, v)), sems)
+    chunk = (lax.axis_index("seq") & 3) ^ (3 * (lax.axis_index("dp") & 1))
     order = row_order(False)
     for i, src in enumerate((q, k, v)):
         moves[i].wait()
         rows = dot_nn(order, src[...])
         px[i] = (rows * 0.125 if i == 0 else rows).astype(bf16)
     for d, o in enumerate((o0, o1, o2, o3)):
-        c = pl.multiple_of(jnp.minimum(info[1] ^ d, 2) * 128, 128)
+        c = pl.multiple_of(jnp.minimum(chunk ^ d, 2) * 128, 128)
         for i in range(3):
             o[i] = px[i, :, pl.ds(c, 128)]
 
@@ -267,7 +271,7 @@
 
 def pair_back(place, x, g, top, norm, delta, t, es, pair, oo, k2, v2):
     f2 = jnp.exp(t - pick(reader(top), pair, oo)) * pick(reader(norm), pair, oo)
-    gf2 = (pick(reader(g), pair, oo).astype(f32) * f2).astype(bf16)
+    gf2 = pick(reader(g), pair, oo).astype(f32) * f2
     fd2 = f2 * pick(reader(delta), pair, oo)
     return back(pick(reader(x, 0), pair, oo), k2, v2, gf2, fd2, es)
 
@@ -322,28 +326,24 @@
         f2 = jnp.exp(slot_rows(m1, slot) - slot_rows(top, slot)) * slot_rows(norm, slot)
         q2, k2, v2 = [slot_rows(x, slot, i) for i in range(3)]
         g2 = slot_rows(g, slot)
-        gf2 = (g2.astype(f32) * f2).astype(bf16)
+        gf2 = g2.astype(f32) * f2
         fd2 = f2 * slot_rows(delta, slot)
         grads = back(q2, k2, v2, gf2, fd2, [e1[slot, 0], e1[slot, 1]])
         for i in range(3):
             acc[i, :, sl, :] = acc_in[i, :, sl, :] + grads[i].reshape(8, 32, 128)
 
 
-def cores_body(keep, got, d4, d8, d12, own, f4, f8, f12):
-    for u, (d, f) in enumerate(((None, own), (d4, f4), (d8, f8), (d12, f12))):
-        part = keep[4 * u : 4 * u + 4] + got[4 * u : 4 * u + 4].astype(f32)
-        if u == 0:
-            f[...] = part
-        else:
-            n = d.shape[1]
-            f[0:n] = d[0]
-            f[n : 2 * n] = d[1]
-            f[2 * n : 2 * n + 288] = part.reshape(288, 128).astype(bf16)
-
-
-def far_sum_body(part, f4, f8, f12, low):
-    a, b, c = [r[n : n + 288].astype(f32) for r, n in ((f4, 768), (f8, 256), (f12, 256))]
-    low[...] = (part[...].reshape(288, 128) + a + (b + c)).astype(bf16)
+def cores_body(keep, got, own, s1, s2, s3):
+    for d, o in enumerate((own, s1, s2, s3)):
+        parts = [keep[4 * u + d] + got[4 * u + d].astype(f32) for u in range(4)]
+        o[...] = jnp.concatenate(parts, axis=0).astype(o.dtype)
+
+
+def quarters_body(a, b, c, d, own, s4, s8, s12):
+    one = a[...].astype(f32) + b[...].astype(f32)
+    total = one + (c[...].astype(f32) + d[...].astype(f32))
+    for u, o in enumerate((own, s4, s8, s12)):
+        o[...] = total[72 * u : 72 * u + 72].astype(o.dtype)
 
 
 def finish_body(info, offsets, counts, acc_in, r4, r8, r12, o0, o1, o2, o3, acc):
@@ -352,9 +352,8 @@
     p3, p4 = place.offs(1), place.offs(2)
     for i in (0, 1):
         rd, wr = reader(acc, i + 1), writer(acc, i + 1)
-        put(rd, wr, r4[i * 384 : i * 384 + 256].astype(f32), 1, p3, True)
-        far = r4[i * 384 + 256 : i * 384 + 384].astype(f32)
-        far = far + r8[i * 128 : i * 128 + 128].astype(f32) + r12[i * 128 : i * 128 + 128].astype(f32)
+        put(rd, wr, r4[i, 0:256].astype(f32), 1, p3, True)
+        far = r4[i, 256:384].astype(f32) + r8[i].astype(f32) + r12[i].astype(f32)
         put(rd, wr, far, 2, p4, True)
     for slot, o in enumerate((o0, o1, o2, o3)):
         o[0:256] = (slot_rows(acc, slot, 0) * 0.125).astype(bf16)
@@ -370,13 +369,6 @@
             wide[i, :, pl.ds(c, 128)] = m[256 * i : 256 * i + 256]
     for i, o in enumerate((dq, dk, dv)):
         o[...] = dot_nn(order, wide[i, :, 0:384]).astype(bf16)
-
-
-def halves_body(mine, other, own, s1, s2, s3):
-    a, b = mine[...].astype(f32), other[...].astype(f32)
-    for d, o in enumerate((own, s1, s2, s3)):
-        at = slice(72 * d, 72 * d + 72)
-        o[...] = jnp.concatenate([a[at], b[at]], axis=0).astype(o.dtype)
 
 
 def widen(info, msgs, wide):
@@ -412,12 +404,11 @@
     o[...] = (a[...].astype(f32) + b[...].astype(f32)).astype(o.dtype)
 
 
-def join_body(info, own, a, b, c, o):
-    total = own[...] + a[...].astype(f32) + (b[...].astype(f32) + c[...].astype(f32))
-    for h in (0, 1):
+def join_body(info, a, b, o):
+    for h, m in enumerate((a, b)):
         for t in range(3):
             col = pl.multiple_of((info[2] ^ h) * 384 + t * 128, 128)
-            o[:, pl.ds(col, 128)] = total[72 * h + 24 * t : 72 * h + 24 * t + 24]
+            o[:, pl.ds(col, 128)] = m[24 * t : 24 * t + 24]
 
 
 smem = pl.BlockSpec(memory_space=pltpu.SMEM)
@@ -435,7 +426,7 @@
         out_specs=[vmem] * len(shapes),
         scratch_shapes=[pltpu.VMEM(s, t) for s, t in scratch] + [pltpu.SemaphoreType.DMA((sems,))] * (sems > 0),
         compiler_params=pltpu.CompilerParams(vmem_limit_bytes=limit * 1024 * 1024),
-        cost_estimate=pl.CostEstimate(flops=flops, bytes_accessed=moved, transcendentals=0),
+        cost_estimate=pl.CostEstimate(flops=1000, bytes_accessed=1000, transcendentals=0),
     )(*scalars, *arrays)
 
 
@@ -476,7 +467,7 @@
 
     msgs = call(
         prep_body,
-        [info],
+        [],
         [queries[0], keys[0], values[0]],
         [chunk] * 4,
         [((3, 256, 384), bf16), third, third, third],
@@ -546,38 +537,36 @@
         flops=10**9,
     )
     state = [x, g, top, norm, delta]
-    part, f4, f8, f12 = call(
-        cores_body,
-        [],
-        [keep, arrived, d4, d8, d12],
-        [((4, *block), f32), ((1056, 128), bf16), ((544, 128), bf16), ((544, 128), bf16)],
-    )
-    f4, f8, f12 = [shift(b, routes(d)) for d, b in ((4, f4), (8, f8), (12, f12))]
-    acc, part, *mixed = lax.optimization_barrier([acc, part] + mixed)
+    flat = ((288, 128), bf16)
+    own, s1, s2, s3 = call(cores_body, [], [keep, arrived], [((288, 128), f32)] + [flat] * 3)
+    near = [seq_step(b, d) for d, b in ((1, s1), (2, s2), (3, s3))]
+    d4, d8, d12, own = lax.optimization_barrier((d4, d8, d12, own))
+    far = [shift(b, routes(d)) for d, b in ((4, d4), (8, d8), (12, d12))]
+    (low,) = call(sum_body, [], [own] + near, [flat])
+    acc, low = lax.optimization_barrier((acc, low))
+    arrived = dp_step(low, 2)
+    (acc,) = call(back_two_body, places, state + [acc, m2, e2], [((3, *cube), f32)], flops=10**9)
+    acc, low = lax.optimization_barrier((acc, low))
+    (low,) = call(pair_body, [], [low, arrived], [flat])
+    rest = [dp_step(low, d) for d in (4, 8, 12)]
+    acc, low = lax.optimization_barrier((acc, low))
+    (acc,) = call(back_one_body, places, state + [acc, m1, e1], [((3, *cube), f32)], flops=10**9)
+    acc, low = lax.optimization_barrier((acc, low))
+    own, s4, s8, s12 = call(quarters_body, [], [low] + rest, [(block, f32)] + [(block, bf16)] * 3)
+    acc, own = lax.optimization_barrier((acc, own))
+    outs = call(finish_body, places, [acc] + far, [((768, 128), bf16)] * 4, [((3, *cube), f32)])
+    home = [outs[0]] + [shift(outs[d], routes(d)) for d in (1, 2, 3)]
+    quarters = [seq_step(b, d) for d, b in ((4, s4), (8, s8), (12, s12))]
+    first, *mixed = lax.optimization_barrier([outs[0]] + mixed)
     (attended,) = call(
         attended_body, [info], mixed + [out_weight], [((256, 768), bf16)], [((256, 512), bf16)], flops=3 * 10**8
     )
-    acc, attended = lax.optimization_barrier((acc, attended))
-    (acc,) = call(back_two_body, places, state + [acc, m2, e2], [((3, *cube), f32)], flops=10**9)
-    (acc,) = call(back_one_body, places, state + [acc, m1, e1], [((3, *cube), f32)], flops=10**9)
-    (low,) = call(far_sum_body, [], [part, f4, f8, f12], [((288, 128), bf16)])
-    acc, low = lax.optimization_barrier((acc, low))
-    arrived = dp_step(low, 2)
-    outs = call(
-        finish_body, places, [acc, f4, f8, f12], [((768, 128), bf16)] * 4, [((3, *cube), f32)]
-    )
-    first, low = lax.optimization_barrier((outs[0], low))
-    home = [first] + [shift(outs[d], routes(d)) for d in (1, 2, 3)]
-    (low,) = call(pair_body, [], [low, arrived], [((288, 128), bf16)])
-    rest = [dp_step(low, d) for d in (4, 8, 12)]
-    (low,) = call(sum_body, [], [low] + rest, [((288, 128), bf16)])
-    grads = call(home_body, [info], home, [third] * 3, [((3, 256, 512), bf16)])
-    own, s1, s2, s3 = call(
-        halves_body, [], [low, dp_step(low, 1)], [((144, 128), f32)] + [((144, 128), bf16)] * 3
-    )
-    near = [seq_step(b, d) for d, b in ((1, s1), (2, s2), (3, s3))]
+    first, attended = lax.optimization_barrier((first, attended))
+    grads = call(home_body, [info], [first] + home[1:], [third] * 3, [((3, 256, 512), bf16)])
     *grads, own = lax.optimization_barrier([*grads, own])
-    (grad_weight,) = call(join_body, [info], [own] + near, [((24, 768), f32)])
+    (own,) = call(sum_body, [], [own] + quarters, [(block, f32)])
+    other = dp_step(own, 1)
+    (grad_weight,) = call(join_body, [info], [own, other], [((24, 768), f32)])
     return (attended[None], grads[0][None], grads[1][None], grads[2][None], grad_weight)
 
 

time: 110 us -> 105 us (0.955)
  waiting for transfers between devices: 33.6 us -> 23.3 us
  starting transfers between devices: 43.4 us -> 51.6 us
  Pallas kernels: 26.6 us -> 25.2 us
    ppermute x14, waiting for transfers between devices: 25.2 us -> 19.2 us  [shift(): return lax.ppermute(block, ('dp', 'seq'), pairs)]
    ppermute x3 -> x6, starting transfers between devices: 4.24 us -> 9.9 us  [seq_step(): return lax.ppermute(block, 'seq', [(i, i ^ step) for i in range(16)])]
    ppermute x6, waiting for transfers between devices: 7.25 us -> 2.08 us  [dp_step(): return lax.ppermute(block, 'dp', [(i, i ^ step) for i in range(16)])]
    ppermute x6, starting transfers between devices: 10.4 us -> 12.5 us  [dp_step(): return lax.ppermute(block, 'dp', [(i, i ^ step) for i in range(16)])]
    pallas_call x20, Pallas kernels: 26.6 us -> 25.2 us  [call(): pl.pallas_call(body, out_shape=shapes, in_specs=[smem] * len(scalars) + [...]
    unnamed x14 -> x10, local copies, waits for them, and re-layouts: 3.62 us -> 3 us
  transfers between devices with their start and end apart: 23 -> 26, of which waited for: 12 -> 10; matrix products, arithmetic and copies ran while one was open for 0% -> 0% of each run, Pallas kernels for 17% -> 16%
where the time goes in v5:
time: 105 us
  starting transfers between devices  51.6 us (49%)
  Pallas kernels  25.2 us (24%)
  waiting for transfers between devices  23.3 us (22%)
  local copies, waits for them, and re-layouts  3 us (3%)
  between operations  1.48 us (1%)
    ppermute x14, starting transfers between devices, shift(): return lax.ppermute(block, ('dp', 'seq'), pairs)  29.1 us
    pallas_call x20, Pallas kernels, call(): pl.pallas_call(body, out_shape=shapes, in_specs=[smem] * len(scalars) + [...  25.2 us
    ppermute x14, waiting for transfers between devices, shift(): return lax.ppermute(block, ('dp', 'seq'), pairs)  19.2 us
    ppermute x6, starting transfers between devices, dp_step(): return lax.ppermute(block, 'dp', [(i, i ^ step) for i in range(16)])  12.5 us
    ppermute x6, starting transfers between devices, seq_step(): return lax.ppermute(block, 'seq', [(i, i ^ step) for i in range(16)])  9.9 us
    unnamed x10, local copies, waits for them, and re-layouts  3 us
  transfers between devices with their start and end apart: 26, of which 10 were waited for; matrix products, arithmetic and copies ran while one was open for 0% of the time, Pallas kernels for 16%

profile of v5, /device:TPU:1, one launch (start us, length us, event | category | flops | bytes accessed | tf_op | source)
XLA Modules:
  0.0 104.6 jit_solution(15074879455771445007)
XLA Ops:
  0.6 2.5 %shard_map.110 = (bf16[3,256,128]{2,1,0:T(8,128)(2,1)}, bf16[3,256,128]{2,1,0:T(8,128)(2,1)}, bf16[3,256,128]{2,1,0:T(8,128)(2,1)}, bf16[3,256,128]{2,1,0:T(8,128)(2,1)}) custom-call(bf16[256,384]{1,0:T(8,128)(2,1)} %bitcast.13, bf16[256,384]{1,0:T(8,128)(2,1)} %bitcast.14, bf16[256,384]{1,0:T(8,128)(2,1)} %bitcast.15), custom_call_target="tpu_custom_call" | custom-call | flops 1000 | bytes 1000 | tf_op jit(solution)/shard_map/pallas_call | solution.py:422
  3.2 3.7 %collective-permute-start = (bf16[3,256,128]{2,1,0:T(8,128)(2,1)}, bf16[3,256,128]{2,1,0:T(8,128)(2,1)S(1)}, u32[]{:S(2)}, u32[]{:S(2)}) collective-permute-start(bf16[3,256,128]{2,1,0:T(8,128)(2,1)} %get-tuple-element.96), channel_id=1, source_target_pairs={{0,1},{1,0},{2,3},{3,2},{4,5},{5,4},{6,7},{7,6},{8,9},{9,8},{10,11... | collective-permute-start | bytes 589832 | tf_op jit(solution)/shard_map/ppermute | solution.py:445
  6.8 1.6 %collective-permute-start.1 = (bf16[3,256,128]{2,1,0:T(8,128)(2,1)}, bf16[3,256,128]{2,1,0:T(8,128)(2,1)S(1)}, u32[]{:S(2)}, u32[]{:S(2)}) collective-permute-start(bf16[3,256,128]{2,1,0:T(8,128)(2,1)} %get-tuple-element.97), channel_id=1, source_target_pairs={{0,2},{1,3},{2,0},{3,1},{4,6},{5,7},{6,4},{7,5},{8,10},{9,11},{10,... | collective-permute-start | bytes 589832 | tf_op jit(solution)/shard_map/ppermute | solution.py:445
  8.6 1.1 %copy-done = bf16[384,768]{1,0:T(8,128)(2,1)S(1)} copy-done((bf16[384,768]{1,0:T(8,128)(2,1)S(1)}, bf16[384,768]{1,0:T(8,128)(2,1)}, u32[]{:S(2)}) %copy-start) | copy-done | bytes 589848
  9.6 1.0 copy-done.2
  10.6 0.9 copy-done.3
  11.6 1.1 %shard_map.111 = (bf16[256,768]{1,0:T(8,128)(2,1)S(1)}, bf16[256,128]{1,0:T(8,128)(2,1)S(1)}, bf16[256,128]{1,0:T(8,128)(2,1)S(1)}, bf16[256,128]{1,0:T(8,128)(2...) custom-call(s32[3]{0:T(128)S(1)} %pad_add_fusion.info, bf16[256,768]{1,0:T(8,128)(2,1)S(1)} %bitcast.11, ...), custom_call_target="tpu_custom_call" | custom-call | flops 1000 | bytes 1000 | tf_op jit(solution)/shard_map/pallas_call | solution.py:422
  13.3 4.7 %collective-permute-done.2.m3 = bf16[3,256,128]{2,1,0:T(8,128)(2,1)S(1)} collective-permute-done((bf16[3,256,128]{2,1,0:T(8,128)(2,1)}, bf16[3,256,128]{2,1,0:T(8,128)(2,1)S(1)}, u32[]{:S(2)}, u32[]{:S(2)}) %collective-permute-start.2) | collective-permute-done | bytes 196640 | tf_op jit(solution)/shard_map/ppermute | solution.py:445
  18.0 0.7 shard_map.112
  18.7 1.9 %collective-permute-start.3 = (bf16[2,384,128]{2,1,0:T(8,128)(2,1)S(1)}, bf16[2,384,128]{2,1,0:T(8,128)(2,1)S(1)}, u32[]{:S(2)}, u32[]{:S(2)}) collective-permute-start(bf16[2,384,128]{2,1,0:T(8,128)(2,1)S(1)} %get-tuple-element.101), channel_id=1, source_target_pairs={{0,4},{1,5},{2,6},{3,7},{4,0},{5,1},{6,2},{7,3},{8,12},{9,13},{10,... | collective-permute-start | bytes 589832 | tf_op jit(solution)/shard_map/ppermute | solution.py:445
  20.6 3.3 %shard_map.113 = (f32[8,128,128]{2,1,0:T(8,128)S(1)}, f32[8,128,128]{2,1,0:T(8,128)S(1)}, f32[8,128,128]{2,1,0:T(8,128)S(1)}, f32[8,128,128]{2,1,0:T(8,128)S(1)}...) custom-call(s32[3]{0:T(128)S(1)} %pad_add_fusion.info, ...), custom_call_target="tpu_custom_call" | custom-call | flops 1000 | bytes 1000 | tf_op jit(solution)/shard_map/pallas_call | solution.py:422
  23.9 6.1 %collective-permute-done.3.r4 = bf16[2,384,128]{2,1,0:T(8,128)(2,1)S(1)} collective-permute-done((bf16[2,384,128]{2,1,0:T(8,128)(2,1)S(1)}, bf16[2,384,128]{2,1,0:T(8,128)(2,1)S(1)}, u32[]{:S(2)}, u32[]{:S(2)}) %collective-permute-start.3) | collective-permute-done | bytes 196640 | tf_op jit(solution)/shard_map/ppermute | solution.py:445
  30.0 3.6 %collective-permute-start.4 = (bf16[4,128,128]{2,1,0:T(8,128)(2,1)S(1)}, bf16[4,128,128]{2,1,0:T(8,128)(2,1)S(1)}, u32[]{:S(2)}, u32[]{:S(2)}) collective-permute-start(bf16[4,128,128]{2,1,0:T(8,128)(2,1)S(1)} %shard_map.114), channel_id=1, source_target_pairs={{0,12},{1,13},{2,14},{3,15},{4,8},{5,9},{6,10},{7,11},{8,4},{9,5},... | collective-permute-start | bytes 393224 | tf_op jit(solution)/shard_map/ppermute | solution.py:445
  33.6 1.7 %shard_map.115 = (f32[8,128,128]{2,1,0:T(8,128)S(1)}, f32[8,128,128]{2,1,0:T(8,128)S(1)}, f32[8,128,128]{2,1,0:T(8,128)S(1)}, f32[256,128]{1,0:T(8,128)S(1)}, bf16[2,256,512]{2,1,0:T(8,128)(2,1)S(1)}) custom-call(s32[3]{0:T(128)S(1)} %pad_add_fusion.info, s32[3,6]{1,0:T(4,128)S(1)} %copy-done.4, s32[1]{0:T(128)S(6)} %copy.12.counts, ...), custom_call_target="tpu_custom_call" | custom-call | flops 1000 | bytes 1000 | tf_op jit(solution)/shard_map/pallas_call | solution.py:422
  35.3 1.4 %collective-permute-done.4.r12 = bf16[4,128,128]{2,1,0:T(8,128)(2,1)S(1)} collective-permute-done((bf16[4,128,128]{2,1,0:T(8,128)(2,1)S(1)}, bf16[4,128,128]{2,1,0:T(8,128)(2,1)S(1)}, u32[]{:S(2)}, u32[]{:S(2)}) %collective-permute-start.4) | collective-permute-done | bytes 131104 | tf_op jit(solution)/shard_map/ppermute | solution.py:445
  36.7 1.5 %shard_map.116 = (f32[8,128,128]{2,1,0:T(8,128)S(1)}, f32[8,128,128]{2,1,0:T(8,128)S(1)}, bf16[512,128]{1,0:T(8,128)(2,1)S(1)}, bf16[512,128]{1,0:T(8,128)(2,1)S...) custom-call(s32[3]{0:T(128)S(1)} %pad_add_fusion.info, ...), custom_call_target="tpu_custom_call" | custom-call | flops 1000 | bytes 1000 | tf_op jit(solution)/shard_map/pallas_call | solution.py:422
  38.2 2.0 %collective-permute-start.5 = (bf16[512,128]{1,0:T(8,128)(2,1)S(1)}, bf16[512,128]{1,0:T(8,128)(2,1)S(1)}, u32[]{:S(2)}, u32[]{:S(2)}) collective-permute-start(bf16[512,128]{1,0:T(8,128)(2,1)S(1)} %get-tuple-element.122.mx1), channel_id=1, source_target_pairs={{0,1},{1,0},{2,3},{3,2},{4,5},{5,4},{6,7},{7,6},{8,9},{9,8},{10,11... | collective-permute-start | bytes 393224 | tf_op jit(solution)/shard_map/ppermute | solution.py:445
  40.2 5.6 %collective-permute-start.6 = (bf16[512,128]{1,0:T(8,128)(2,1)S(1)}, bf16[512,128]{1,0:T(8,128)(2,1)S(1)}, u32[]{:S(2)}, u32[]{:S(2)}) collective-permute-start(bf16[512,128]{1,0:T(8,128)(2,1)S(1)} %get-tuple-element.123.mx2), channel_id=1, source_target_pairs={{0,2},{1,3},{2,0},{3,1},{4,6},{5,7},{6,4},{7,5},{8,10},{9,11},{10,... | collective-permute-start | bytes 393224 | tf_op jit(solution)/shard_map/ppermute | solution.py:445
  45.8 0.5 collective-permute-start.7
  46.2 2.6 %collective-permute-done.6.m2.in2 = bf16[512,128]{1,0:T(8,128)(2,1)S(1)} collective-permute-done((bf16[512,128]{1,0:T(8,128)(2,1)S(1)}, bf16[512,128]{1,0:T(8,128)(2,1)S(1)}, u32[]{:S(2)}, u32[]{:S(2)}) %collective-permute-start.6) | collective-permute-done | bytes 131104 | tf_op jit(solution)/shard_map/ppermute | solution.py:445
  48.9 3.1 %collective-permute-done.7.m3.in3 = bf16[512,128]{1,0:T(8,128)(2,1)S(1)} collective-permute-done((bf16[512,128]{1,0:T(8,128)(2,1)S(1)}, bf16[512,128]{1,0:T(8,128)(2,1)S(1)}, u32[]{:S(2)}, u32[]{:S(2)}) %collective-permute-start.7) | collective-permute-done | bytes 131104 | tf_op jit(solution)/shard_map/ppermute | solution.py:445
  52.0 1.1 %shard_map.117 = (bf16[16,72,128]{2,1,0:T(8,128)(2,1)S(1)}, f32[16,72,128]{2,1,0:T(8,128)S(1)}) custom-call(s32[3]{0:T(128)S(1)} %pad_add_fusion.info, bf16[512,128]{1,0:T(8,128)(2,1)S(1)} %get-tuple-element.163.m0.mx0.in0, bf16[512,128]{1,0:T(8,128)(2,1)S(1)} %collective-permute-done.5.m1.in1, bf16[512,128]{1,0:T(8,128)(2,1)S(1)} %collective-permute-done.6.m2.in2, ...), custom_call_target="tpu_custom_call" | custom-call | flops 1000 | bytes 1000 | tf_op jit(solution)/shard_map/pallas_call | solution.py:422
  53.1 2.3 %collective-permute-start.8 = (bf16[16,72,128]{2,1,0:T(8,128)(2,1)S(1)}, bf16[16,72,128]{2,1,0:T(8,128)(2,1)S(1)}, u32[]{:S(2)}, u32[]{:S(2)}) collective-permute-start(bf16[16,72,128]{2,1,0:T(8,128)(2,1)S(1)} %get-tuple-element.138), channel_id=1, source_target_pairs={{0,16},{16,0},{32,48},{48,32},{64,80},{80,64},{96,112},{112,96},{1... | collective-permute-start | bytes 884744 | tf_op jit(solution)/shard_map/ppermute | solution.py:449
  55.4 1.2 %collective-permute-done.8.got = bf16[16,72,128]{2,1,0:T(8,128)(2,1)S(1)} collective-permute-done((bf16[16,72,128]{2,1,0:T(8,128)(2,1)S(1)}, bf16[16,72,128]{2,1,0:T(8,128)(2,1)S(1)}, u32[]{:S(2)}, u32[]{:S(2)}) %collective-permute-start.8) | collective-permute-done | bytes 294944 | tf_op jit(solution)/shard_map/ppermute | solution.py:449
  56.6 1.6 %collective-permute-start.9 = (bf16[288,128]{1,0:T(8,128)(2,1)S(1)}, bf16[288,128]{1,0:T(8,128)(2,1)S(1)}, u32[]{:S(2)}, u32[]{:S(2)}) collective-permute-start(bf16[288,128]{1,0:T(8,128)(2,1)S(1)} %get-tuple-element.141), channel_id=1, source_target_pairs={{0,1},{1,0},{2,3},{3,2},{4,5},{5,4},{6,7},{7,6},{8,9},{9,8},{10,11... | collective-permute-start | bytes 221192 | tf_op jit(solution)/shard_map/ppermute | solution.py:453
  58.2 1.5 %collective-permute-start.10 = (bf16[288,128]{1,0:T(8,128)(2,1)S(1)}, bf16[288,128]{1,0:T(8,128)(2,1)S(1)}, u32[]{:S(2)}, u32[]{:S(2)}) collective-permute-start(bf16[288,128]{1,0:T(8,128)(2,1)S(1)} %get-tuple-element.142), channel_id=1, source_target_pairs={{0,2},{1,3},{2,0},{3,1},{4,6},{5,7},{6,4},{7,5},{8,10},{9,11},{10,... | collective-permute-start | bytes 221192 | tf_op jit(solution)/shard_map/ppermute | solution.py:453
  59.7 1.2 %collective-permute-start.11 = (bf16[288,128]{1,0:T(8,128)(2,1)S(1)}, bf16[288,128]{1,0:T(8,128)(2,1)S(1)}, u32[]{:S(2)}, u32[]{:S(2)}) collective-permute-start(bf16[288,128]{1,0:T(8,128)(2,1)S(1)} %get-tuple-element.143), channel_id=1, source_target_pairs={{0,3},{1,2},{2,1},{3,0},{4,7},{5,6},{6,5},{7,4},{8,11},{9,10},{10,... | collective-permute-start | bytes 221192 | tf_op jit(solution)/shard_map/ppermute | solution.py:453
  60.9 2.8 %shard_map.118 = (bf16[8,128,128]{2,1,0:T(8,128)(2,1)S(1)}, f32[8,128,128]{2,1,0:T(8,128)S(1)}, f32[3,8,128,128]{3,2,1,0:T(8,128)S(1)}, bf16[2,384,128]{2,1,0:T(...) custom-call(s32[3]{0:T(128)S(1)} %pad_add_fusion.info, s32[3,6]{1,0:T(4,128)S(1)} %copy-done.4, ...), custom_call_target="tpu_custom_call" | custom-call | flops 1000 | bytes 1000 | tf_op jit(solution)/shard_map/pallas_call | solution.py:422
  63.7 1.6 %collective-permute-done.11.d = bf16[288,128]{1,0:T(8,128)(2,1)S(1)} collective-permute-done((bf16[288,128]{1,0:T(8,128)(2,1)S(1)}, bf16[288,128]{1,0:T(8,128)(2,1)S(1)}, u32[]{:S(2)}, u32[]{:S(2)}) %collective-permute-start.11) | collective-permute-done | bytes 73760 | tf_op jit(solution)/shard_map/ppermute | solution.py:453
  65.7 1.1 %collective-permute-start.16 = (bf16[2,384,128]{2,1,0:T(8,128)(2,1)S(1)}, bf16[2,384,128]{2,1,0:T(8,128)(2,1)S(1)}, u32[]{:S(2)}, u32[]{:S(2)}) collective-permute-start(bf16[2,384,128]{2,1,0:T(8,128)(2,1)S(1)} %get-tuple-element.158), channel_id=1, source_target_pairs={{0,4},{1,5},{2,6},{3,7},{4,0},{5,1},{6,2},{7,3},{8,12},{9,13},{10,... | collective-permute-start | bytes 589832 | tf_op jit(solution)/shard_map/ppermute | solution.py:445
  66.8 2.3 %shard_map.121.acc_in = f32[3,8,128,128]{3,2,1,0:T(8,128)S(1)} custom-call(s32[3]{0:T(128)S(1)} %pad_add_fusion.info, s32[3,6]{1,0:T(4,128)S(1)} %copy-done.4, s32[1]{0:T(128)S(6)} %copy.12.counts, bf16[3,8,128,128]{3,2,1,0:T(8,128)(2,1)S(1)} %get-tuple-element.99.x, bf16[8,128,128]{2,1,0:T(8,128)(2,1)S(1)} %get-tuple-element.131.g, ...), custom_call_target="tpu_custom_call" | custom-call | flops 1000 | bytes 1000 | tf_op jit(solution)/shard_map/pallas_call | solution.py:422
  69.2 2.8 %collective-permute-start.15 = (bf16[288,128]{1,0:T(8,128)(2,1)S(1)}, bf16[288,128]{1,0:T(8,128)(2,1)S(1)}, u32[]{:S(2)}, u32[]{:S(2)}) collective-permute-start(bf16[288,128]{1,0:T(8,128)(2,1)S(1)} %shard_map.122.a), channel_id=1, source_target_pairs={{0,192},{16,208},{32,224},{48,240},{64,128},{80,144},{96,160},{112... | collective-permute-start | bytes 221192 | tf_op jit(solution)/shard_map/ppermute | solution.py:449
  72.7 2.7 %collective-permute-start.17 = (bf16[2,128,128]{2,1,0:T(8,128)(2,1)S(1)}, bf16[2,128,128]{2,1,0:T(8,128)(2,1)S(1)}, u32[]{:S(2)}, u32[]{:S(2)}) collective-permute-start(bf16[2,128,128]{2,1,0:T(8,128)(2,1)S(1)} %get-tuple-element.159), channel_id=1, source_target_pairs={{0,8},{1,9},{2,10},{3,11},{4,12},{5,13},{6,14},{7,15},{8,0},{9,1},... | collective-permute-start | bytes 196616 | tf_op jit(solution)/shard_map/ppermute | solution.py:445
  75.3 2.0 %collective-permute-start.18 = (bf16[2,128,128]{2,1,0:T(8,128)(2,1)S(1)}, bf16[2,128,128]{2,1,0:T(8,128)(2,1)S(1)}, u32[]{:S(2)}, u32[]{:S(2)}) collective-permute-start(bf16[2,128,128]{2,1,0:T(8,128)(2,1)S(1)} %get-tuple-element.160), channel_id=1, source_target_pairs={{0,12},{1,13},{2,14},{3,15},{4,8},{5,9},{6,10},{7,11},{8,4},{9,5},... | collective-permute-start | bytes 196616 | tf_op jit(solution)/shard_map/ppermute | solution.py:445
  77.3 2.3 %shard_map.123.acc_in = f32[3,8,128,128]{3,2,1,0:T(8,128)S(1)} custom-call(s32[3]{0:T(128)S(1)} %pad_add_fusion.info, s32[3,6]{1,0:T(4,128)S(1)} %copy-done.4, s32[1]{0:T(128)S(6)} %copy.12.counts, bf16[3,8,128,128]{3,2,1,0:T(8,128)(2,1)S(1)} %get-tuple-element.99.x, bf16[8,128,128]{2,1,0:T(8,128)(2,1)S(1)} %get-tuple-element.131.g, ...), custom_call_target="tpu_custom_call" | custom-call | flops 1000 | bytes 1000 | tf_op jit(solution)/shard_map/pallas_call | solution.py:422
  79.7 1.3 %collective-permute-done.18.r12 = bf16[2,128,128]{2,1,0:T(8,128)(2,1)S(1)} collective-permute-done((bf16[2,128,128]{2,1,0:T(8,128)(2,1)S(1)}, bf16[2,128,128]{2,1,0:T(8,128)(2,1)S(1)}, u32[]{:S(2)}, u32[]{:S(2)}) %collective-permute-start.18) | collective-permute-done | bytes 65568 | tf_op jit(solution)/shard_map/ppermute | solution.py:445
  81.0 0.9 shard_map.125
  81.9 2.1 %collective-permute-start.19 = (bf16[768,128]{1,0:T(8,128)(2,1)S(1)}, bf16[768,128]{1,0:T(8,128)(2,1)S(1)}, u32[]{:S(2)}, u32[]{:S(2)}) collective-permute-start(bf16[768,128]{1,0:T(8,128)(2,1)S(1)} %get-tuple-element.169), channel_id=1, source_target_pairs={{0,1},{1,0},{2,3},{3,2},{4,5},{5,4},{6,7},{7,6},{8,9},{9,8},{10,11... | collective-permute-start | bytes 589832 | tf_op jit(solution)/shard_map/ppermute | solution.py:445
  84.0 1.8 %collective-permute-start.20 = (bf16[768,128]{1,0:T(8,128)(2,1)S(1)}, bf16[768,128]{1,0:T(8,128)(2,1)S(1)}, u32[]{:S(2)}, u32[]{:S(2)}) collective-permute-start(bf16[768,128]{1,0:T(8,128)(2,1)S(1)} %get-tuple-element.170), channel_id=1, source_target_pairs={{0,2},{1,3},{2,0},{3,1},{4,6},{5,7},{6,4},{7,5},{8,10},{9,11},{10,... | collective-permute-start | bytes 589832 | tf_op jit(solution)/shard_map/ppermute | solution.py:445
  85.8 0.7 collective-permute-start.21
  86.5 1.9 %collective-permute-start.22 = (bf16[72,128]{1,0:T(8,128)(2,1)S(1)}, bf16[72,128]{1,0:T(8,128)(2,1)S(1)}, u32[]{:S(2)}, u32[]{:S(2)}) collective-permute-start(bf16[72,128]{1,0:T(8,128)(2,1)S(1)} %get-tuple-element.180), channel_id=1, source_target_pairs={{0,4},{1,5},{2,6},{3,7},{4,0},{5,1},{6,2},{7,3},{8,12},{9,13},{10,... | collective-permute-start | bytes 55304 | tf_op jit(solution)/shard_map/ppermute | solution.py:453
  88.4 2.4 %collective-permute-start.23 = (bf16[72,128]{1,0:T(8,128)(2,1)S(1)}, bf16[72,128]{1,0:T(8,128)(2,1)S(1)}, u32[]{:S(2)}, u32[]{:S(2)}) collective-permute-start(bf16[72,128]{1,0:T(8,128)(2,1)S(1)} %get-tuple-element.181), channel_id=1, source_target_pairs={{0,8},{1,9},{2,10},{3,11},{4,12},{5,13},{6,14},{7,15},{8,0},{9,1},... | collective-permute-start | bytes 55304 | tf_op jit(solution)/shard_map/ppermute | solution.py:453
  90.9 1.3 %collective-permute-start.24 = (bf16[72,128]{1,0:T(8,128)(2,1)S(1)}, bf16[72,128]{1,0:T(8,128)(2,1)S(1)}, u32[]{:S(2)}, u32[]{:S(2)}) collective-permute-start(bf16[72,128]{1,0:T(8,128)(2,1)S(1)} %get-tuple-element.182), channel_id=1, source_target_pairs={{0,12},{1,13},{2,14},{3,15},{4,8},{5,9},{6,10},{7,11},{8,4},{9,5},... | collective-permute-start | bytes 55304 | tf_op jit(solution)/shard_map/ppermute | solution.py:453
  92.2 1.9 %shard_map.126 = bf16[256,768]{1,0:T(8,128)(2,1)} custom-call(s32[3]{0:T(128)S(1)} %pad_add_fusion.info, bf16[512,128]{1,0:T(8,128)(2,1)S(1)} %get-tuple-element.163.m0.mx0.in0, bf16[512,128]{1,0:T(8,128)(2,1)S(1)} %collective-permute-done.5.m1.in1, bf16[512,128]{1,0:T(8,128)(2,1)S(1)} %collective-permute-done.6.m2.in2, ...), custom_call_target="tpu_custom_call" | custom-call | flops 1000 | bytes 1000 | tf_op jit(solution)/shard_map/pallas_call | solution.py:422
  94.1 1.7 %shard_map.127 = (bf16[256,384]{1,0:T(8,128)(2,1)}, bf16[256,384]{1,0:T(8,128)(2,1)}, bf16[256,384]{1,0:T(8,128)(2,1)}) custom-call(s32[3]{0:T(128)S(1)} %pad_add_fusion.info, bf16[768,128]{1,0:T(8,128)(2,1)S(1)} %get-tuple-element.168.m0, bf16[768,128]{1,0:T(8,128)(2,1)S(1)} %collective-permute-done.19.m1, bf16[768,128]{1,0:T(8,128)(2,1)S(1)} %collective-permute-done.20.m2, ...), custom_call_target="tpu_custom_call" | custom-call | flops 1000 | bytes 1000 | tf_op jit(solution)/shard_map/pallas_call | solution.py:422
  96.2 6.4 %collective-permute-start.25 = (f32[72,128]{1,0:T(8,128)S(1)}, f32[72,128]{1,0:T(8,128)S(1)}, u32[]{:S(2)}, u32[]{:S(2)}) collective-permute-start(f32[72,128]{1,0:T(8,128)S(1)} %shard_map.128.a), channel_id=1, source_target_pairs={{0,16},{16,0},{32,48},{48,32},{64,80},{80,64},{96,112},{112,96},{1... | collective-permute-start | bytes 110600 | tf_op jit(solution)/shard_map/ppermute | solution.py:449
  102.5 0.9 collective-permute-done.25.b
  103.4 1.2 %shard_map.129 = f32[24,768]{1,0:T(8,128)} custom-call(s32[3]{0:T(128)S(1)} %pad_add_fusion.info, f32[72,128]{1,0:T(8,128)S(1)} %shard_map.128.a, f32[72,128]{1,0:T(8,128)S(1)} %collective-permute-done.25.b), custom_call_target="tpu_custom_call" | custom-call | flops 1000 | bytes 1000 | tf_op jit(solution)/shard_map/pallas_call | solution.py:422
  (35 shorter events, 1.7 us)
Async XLA Ops:
  0.6 17.4 %copy-start.4 = (s32[3,6]{1,0:T(4,128)S(1)}, s32[3,6]{1,0:T(4,128)}, u32[]{:S(2)}) copy-start(s32[3,6]{1,0:T(4,128)} %offsets.15) | copy-start | bytes 220
  3.2 10.1 %collective-permute-start = (bf16[3,256,128]{2,1,0:T(8,128)(2,1)}, bf16[3,256,128]{2,1,0:T(8,128)(2,1)S(1)}, u32[]{:S(2)}, u32[]{:S(2)}) collective-permute-start(bf16[3,256,128]{2,1,0:T(8,128)(2,1)} %get-tuple-element.96), channel_id=1, source_target_pairs={{0,1},{1,0},{2,3},{3,2},{4,5},{5,4},{6,7},{7,6},{8,9},{9,8},{10,11... | collective-permute-start | bytes 589832 | tf_op jit(solution)/shard_map/ppermute | solution.py:445
  6.8 6.5 %collective-permute-start.1 = (bf16[3,256,128]{2,1,0:T(8,128)(2,1)}, bf16[3,256,128]{2,1,0:T(8,128)(2,1)S(1)}, u32[]{:S(2)}, u32[]{:S(2)}) collective-permute-start(bf16[3,256,128]{2,1,0:T(8,128)(2,1)} %get-tuple-element.97), channel_id=1, source_target_pairs={{0,2},{1,3},{2,0},{3,1},{4,6},{5,7},{6,4},{7,5},{8,10},{9,11},{10,... | collective-permute-start | bytes 589832 | tf_op jit(solution)/shard_map/ppermute | solution.py:445
  8.5 9.5 %collective-permute-start.2 = (bf16[3,256,128]{2,1,0:T(8,128)(2,1)}, bf16[3,256,128]{2,1,0:T(8,128)(2,1)S(1)}, u32[]{:S(2)}, u32[]{:S(2)}) collective-permute-start(bf16[3,256,128]{2,1,0:T(8,128)(2,1)} %get-tuple-element.98), channel_id=1, source_target_pairs={{0,3},{1,2},{2,1},{3,0},{4,7},{5,6},{6,5},{7,4},{8,11},{9,10},{10,... | collective-permute-start | bytes 589832 | tf_op jit(solution)/shard_map/ppermute | solution.py:445
  8.6 1.1 %copy-start = (bf16[384,768]{1,0:T(8,128)(2,1)S(1)}, bf16[384,768]{1,0:T(8,128)(2,1)}, u32[]{:S(2)}) copy-start(bf16[384,768]{1,0:T(8,128)(2,1)} %w.3) | copy-start | bytes 1769476
  9.6 1.0 copy-start.2
  10.6 0.9 copy-start.3
  18.7 11.3 %collective-permute-start.3 = (bf16[2,384,128]{2,1,0:T(8,128)(2,1)S(1)}, bf16[2,384,128]{2,1,0:T(8,128)(2,1)S(1)}, u32[]{:S(2)}, u32[]{:S(2)}) collective-permute-start(bf16[2,384,128]{2,1,0:T(8,128)(2,1)S(1)} %get-tuple-element.101), channel_id=1, source_target_pairs={{0,4},{1,5},{2,6},{3,7},{4,0},{5,1},{6,2},{7,3},{8,12},{9,13},{10,... | collective-permute-start | bytes 589832 | tf_op jit(solution)/shard_map/ppermute | solution.py:445
  30.0 6.7 %collective-permute-start.4 = (bf16[4,128,128]{2,1,0:T(8,128)(2,1)S(1)}, bf16[4,128,128]{2,1,0:T(8,128)(2,1)S(1)}, u32[]{:S(2)}, u32[]{:S(2)}) collective-permute-start(bf16[4,128,128]{2,1,0:T(8,128)(2,1)S(1)} %shard_map.114), channel_id=1, source_target_pairs={{0,12},{1,13},{2,14},{3,15},{4,8},{5,9},{6,10},{7,11},{8,4},{9,5},... | collective-permute-start | bytes 393224 | tf_op jit(solution)/shard_map/ppermute | solution.py:445
  38.2 8.1 %collective-permute-start.5 = (bf16[512,128]{1,0:T(8,128)(2,1)S(1)}, bf16[512,128]{1,0:T(8,128)(2,1)S(1)}, u32[]{:S(2)}, u32[]{:S(2)}) collective-permute-start(bf16[512,128]{1,0:T(8,128)(2,1)S(1)} %get-tuple-element.122.mx1), channel_id=1, source_target_pairs={{0,1},{1,0},{2,3},{3,2},{4,5},{5,4},{6,7},{7,6},{8,9},{9,8},{10,11... | collective-permute-start | bytes 393224 | tf_op jit(solution)/shard_map/ppermute | solution.py:445
  40.2 8.7 %collective-permute-start.6 = (bf16[512,128]{1,0:T(8,128)(2,1)S(1)}, bf16[512,128]{1,0:T(8,128)(2,1)S(1)}, u32[]{:S(2)}, u32[]{:S(2)}) collective-permute-start(bf16[512,128]{1,0:T(8,128)(2,1)S(1)} %get-tuple-element.123.mx2), channel_id=1, source_target_pairs={{0,2},{1,3},{2,0},{3,1},{4,6},{5,7},{6,4},{7,5},{8,10},{9,11},{10,... | collective-permute-start | bytes 393224 | tf_op jit(solution)/shard_map/ppermute | solution.py:445
  45.8 6.2 %collective-permute-start.7 = (bf16[512,128]{1,0:T(8,128)(2,1)S(1)}, bf16[512,128]{1,0:T(8,128)(2,1)S(1)}, u32[]{:S(2)}, u32[]{:S(2)}) collective-permute-start(bf16[512,128]{1,0:T(8,128)(2,1)S(1)} %get-tuple-element.124.mx3), channel_id=1, source_target_pairs={{0,3},{1,2},{2,1},{3,0},{4,7},{5,6},{6,5},{7,4},{8,11},{9,10},{10,... | collective-permute-start | bytes 393224 | tf_op jit(solution)/shard_map/ppermute | solution.py:445
  53.1 3.5 %collective-permute-start.8 = (bf16[16,72,128]{2,1,0:T(8,128)(2,1)S(1)}, bf16[16,72,128]{2,1,0:T(8,128)(2,1)S(1)}, u32[]{:S(2)}, u32[]{:S(2)}) collective-permute-start(bf16[16,72,128]{2,1,0:T(8,128)(2,1)S(1)} %get-tuple-element.138), channel_id=1, source_target_pairs={{0,16},{16,0},{32,48},{48,32},{64,80},{80,64},{96,112},{112,96},{1... | collective-permute-start | bytes 884744 | tf_op jit(solution)/shard_map/ppermute | solution.py:449
  56.6 7.1 %collective-permute-start.9 = (bf16[288,128]{1,0:T(8,128)(2,1)S(1)}, bf16[288,128]{1,0:T(8,128)(2,1)S(1)}, u32[]{:S(2)}, u32[]{:S(2)}) collective-permute-start(bf16[288,128]{1,0:T(8,128)(2,1)S(1)} %get-tuple-element.141), channel_id=1, source_target_pairs={{0,1},{1,0},{2,3},{3,2},{4,5},{5,4},{6,7},{7,6},{8,9},{9,8},{10,11... | collective-permute-start | bytes 221192 | tf_op jit(solution)/shard_map/ppermute | solution.py:453
  58.2 5.5 %collective-permute-start.10 = (bf16[288,128]{1,0:T(8,128)(2,1)S(1)}, bf16[288,128]{1,0:T(8,128)(2,1)S(1)}, u32[]{:S(2)}, u32[]{:S(2)}) collective-permute-start(bf16[288,128]{1,0:T(8,128)(2,1)S(1)} %get-tuple-element.142), channel_id=1, source_target_pairs={{0,2},{1,3},{2,0},{3,1},{4,6},{5,7},{6,4},{7,5},{8,10},{9,11},{10,... | collective-permute-start | bytes 221192 | tf_op jit(solution)/shard_map/ppermute | solution.py:453
  59.7 5.6 %collective-permute-start.11 = (bf16[288,128]{1,0:T(8,128)(2,1)S(1)}, bf16[288,128]{1,0:T(8,128)(2,1)S(1)}, u32[]{:S(2)}, u32[]{:S(2)}) collective-permute-start(bf16[288,128]{1,0:T(8,128)(2,1)S(1)} %get-tuple-element.143), channel_id=1, source_target_pairs={{0,3},{1,2},{2,1},{3,0},{4,7},{5,6},{6,5},{7,4},{8,11},{9,10},{10,... | collective-permute-start | bytes 221192 | tf_op jit(solution)/shard_map/ppermute | solution.py:453
  65.4 3.8 %collective-permute-start.12 = (bf16[288,128]{1,0:T(8,128)(2,1)S(1)}, bf16[288,128]{1,0:T(8,128)(2,1)S(1)}, u32[]{:S(2)}, u32[]{:S(2)}) collective-permute-start(bf16[288,128]{1,0:T(8,128)(2,1)S(1)} %shard_map.120.a), channel_id=1, source_target_pairs={{0,32},{16,48},{32,0},{48,16},{64,96},{80,112},{96,64},{112,80},{1... | collective-permute-start | bytes 221192 | tf_op jit(solution)/shard_map/ppermute | solution.py:449
  65.7 15.3 %collective-permute-start.16 = (bf16[2,384,128]{2,1,0:T(8,128)(2,1)S(1)}, bf16[2,384,128]{2,1,0:T(8,128)(2,1)S(1)}, u32[]{:S(2)}, u32[]{:S(2)}) collective-permute-start(bf16[2,384,128]{2,1,0:T(8,128)(2,1)S(1)} %get-tuple-element.158), channel_id=1, source_target_pairs={{0,4},{1,5},{2,6},{3,7},{4,0},{5,1},{6,2},{7,3},{8,12},{9,13},{10,... | collective-permute-start | bytes 589832 | tf_op jit(solution)/shard_map/ppermute | solution.py:445
  69.2 6.1 %collective-permute-start.15 = (bf16[288,128]{1,0:T(8,128)(2,1)S(1)}, bf16[288,128]{1,0:T(8,128)(2,1)S(1)}, u32[]{:S(2)}, u32[]{:S(2)}) collective-permute-start(bf16[288,128]{1,0:T(8,128)(2,1)S(1)} %shard_map.122.a), channel_id=1, source_target_pairs={{0,192},{16,208},{32,224},{48,240},{64,128},{80,144},{96,160},{112... | collective-permute-start | bytes 221192 | tf_op jit(solution)/shard_map/ppermute | solution.py:449
  72.0 7.7 %collective-permute-start.14 = (bf16[288,128]{1,0:T(8,128)(2,1)S(1)}, bf16[288,128]{1,0:T(8,128)(2,1)S(1)}, u32[]{:S(2)}, u32[]{:S(2)}) collective-permute-start(bf16[288,128]{1,0:T(8,128)(2,1)S(1)} %shard_map.122.a), channel_id=1, source_target_pairs={{0,128},{16,144},{32,160},{48,176},{64,192},{80,208},{96,224},{112... | collective-permute-start | bytes 221192 | tf_op jit(solution)/shard_map/ppermute | solution.py:449
  72.3 7.3 %collective-permute-start.13 = (bf16[288,128]{1,0:T(8,128)(2,1)S(1)}, bf16[288,128]{1,0:T(8,128)(2,1)S(1)}, u32[]{:S(2)}, u32[]{:S(2)}) collective-permute-start(bf16[288,128]{1,0:T(8,128)(2,1)S(1)} %shard_map.122.a), channel_id=1, source_target_pairs={{0,64},{16,80},{32,96},{48,112},{64,0},{80,16},{96,32},{112,48},{1... | collective-permute-start | bytes 221192 | tf_op jit(solution)/shard_map/ppermute | solution.py:449
  72.7 7.0 %collective-permute-start.17 = (bf16[2,128,128]{2,1,0:T(8,128)(2,1)S(1)}, bf16[2,128,128]{2,1,0:T(8,128)(2,1)S(1)}, u32[]{:S(2)}, u32[]{:S(2)}) collective-permute-start(bf16[2,128,128]{2,1,0:T(8,128)(2,1)S(1)} %get-tuple-element.159), channel_id=1, source_target_pairs={{0,8},{1,9},{2,10},{3,11},{4,12},{5,13},{6,14},{7,15},{8,0},{9,1},... | collective-permute-start | bytes 196616 | tf_op jit(solution)/shard_map/ppermute | solution.py:445
  75.3 5.7 %collective-permute-start.18 = (bf16[2,128,128]{2,1,0:T(8,128)(2,1)S(1)}, bf16[2,128,128]{2,1,0:T(8,128)(2,1)S(1)}, u32[]{:S(2)}, u32[]{:S(2)}) collective-permute-start(bf16[2,128,128]{2,1,0:T(8,128)(2,1)S(1)} %get-tuple-element.160), channel_id=1, source_target_pairs={{0,12},{1,13},{2,14},{3,15},{4,8},{5,9},{6,10},{7,11},{8,4},{9,5},... | collective-permute-start | bytes 196616 | tf_op jit(solution)/shard_map/ppermute | solution.py:445
  79.6 12.6 %copy-start.1 = (bf16[384,768]{1,0:T(8,128)(2,1)S(1)}, bf16[384,768]{1,0:T(8,128)(2,1)}, u32[]{:S(2)}) copy-start(bf16[384,768]{1,0:T(8,128)(2,1)} %w.3) | copy-start | bytes 1769476
  81.9 9.0 %collective-permute-start.19 = (bf16[768,128]{1,0:T(8,128)(2,1)S(1)}, bf16[768,128]{1,0:T(8,128)(2,1)S(1)}, u32[]{:S(2)}, u32[]{:S(2)}) collective-permute-start(bf16[768,128]{1,0:T(8,128)(2,1)S(1)} %get-tuple-element.169), channel_id=1, source_target_pairs={{0,1},{1,0},{2,3},{3,2},{4,5},{5,4},{6,7},{7,6},{8,9},{9,8},{10,11... | collective-permute-start | bytes 589832 | tf_op jit(solution)/shard_map/ppermute | solution.py:445
  84.0 10.1 %collective-permute-start.20 = (bf16[768,128]{1,0:T(8,128)(2,1)S(1)}, bf16[768,128]{1,0:T(8,128)(2,1)S(1)}, u32[]{:S(2)}, u32[]{:S(2)}) collective-permute-start(bf16[768,128]{1,0:T(8,128)(2,1)S(1)} %get-tuple-element.170), channel_id=1, source_target_pairs={{0,2},{1,3},{2,0},{3,1},{4,6},{5,7},{6,4},{7,5},{8,10},{9,11},{10,... | collective-permute-start | bytes 589832 | tf_op jit(solution)/shard_map/ppermute | solution.py:445
  85.8 8.3 %collective-permute-start.21 = (bf16[768,128]{1,0:T(8,128)(2,1)S(1)}, bf16[768,128]{1,0:T(8,128)(2,1)S(1)}, u32[]{:S(2)}, u32[]{:S(2)}) collective-permute-start(bf16[768,128]{1,0:T(8,128)(2,1)S(1)} %get-tuple-element.171), channel_id=1, source_target_pairs={{0,3},{1,2},{2,1},{3,0},{4,7},{5,6},{6,5},{7,4},{8,11},{9,10},{10,... | collective-permute-start | bytes 589832 | tf_op jit(solution)/shard_map/ppermute | solution.py:445
  86.5 9.3 %collective-permute-start.22 = (bf16[72,128]{1,0:T(8,128)(2,1)S(1)}, bf16[72,128]{1,0:T(8,128)(2,1)S(1)}, u32[]{:S(2)}, u32[]{:S(2)}) collective-permute-start(bf16[72,128]{1,0:T(8,128)(2,1)S(1)} %get-tuple-element.180), channel_id=1, source_target_pairs={{0,4},{1,5},{2,6},{3,7},{4,0},{5,1},{6,2},{7,3},{8,12},{9,13},{10,... | collective-permute-start | bytes 55304 | tf_op jit(solution)/shard_map/ppermute | solution.py:453
  88.4 7.3 %collective-permute-start.23 = (bf16[72,128]{1,0:T(8,128)(2,1)S(1)}, bf16[72,128]{1,0:T(8,128)(2,1)S(1)}, u32[]{:S(2)}, u32[]{:S(2)}) collective-permute-start(bf16[72,128]{1,0:T(8,128)(2,1)S(1)} %get-tuple-element.181), channel_id=1, source_target_pairs={{0,8},{1,9},{2,10},{3,11},{4,12},{5,13},{6,14},{7,15},{8,0},{9,1},... | collective-permute-start | bytes 55304 | tf_op jit(solution)/shard_map/ppermute | solution.py:453
  90.9 5.3 %collective-permute-start.24 = (bf16[72,128]{1,0:T(8,128)(2,1)S(1)}, bf16[72,128]{1,0:T(8,128)(2,1)S(1)}, u32[]{:S(2)}, u32[]{:S(2)}) collective-permute-start(bf16[72,128]{1,0:T(8,128)(2,1)S(1)} %get-tuple-element.182), channel_id=1, source_target_pairs={{0,12},{1,13},{2,14},{3,15},{4,8},{5,9},{6,10},{7,11},{8,4},{9,5},... | collective-permute-start | bytes 55304 | tf_op jit(solution)/shard_map/ppermute | solution.py:453
  96.2 7.2 %collective-permute-start.25 = (f32[72,128]{1,0:T(8,128)S(1)}, f32[72,128]{1,0:T(8,128)S(1)}, u32[]{:S(2)}, u32[]{:S(2)}) collective-permute-start(f32[72,128]{1,0:T(8,128)S(1)} %shard_map.128.a), channel_id=1, source_target_pairs={{0,16},{16,0},{32,48},{48,32},{64,80},{80,64},{96,112},{112,96},{1... | collective-permute-start | bytes 110600 | tf_op jit(solution)/shard_map/ppermute | solution.py:449

commit v6 on v5

--- a/solution.py
+++ b/solution.py
@@ -339,11 +339,11 @@
         o[...] = jnp.concatenate(parts, axis=0).astype(o.dtype)
 
 
-def quarters_body(a, b, c, d, own, s4, s8, s12):
-    one = a[...].astype(f32) + b[...].astype(f32)
-    total = one + (c[...].astype(f32) + d[...].astype(f32))
+def halves_body(mine, other, own, s4, s8, s12):
+    a, b = mine[...].astype(f32), other[...].astype(f32)
     for u, o in enumerate((own, s4, s8, s12)):
-        o[...] = total[72 * u : 72 * u + 72].astype(o.dtype)
+        at = slice(72 * u, 72 * u + 72)
+        o[...] = jnp.concatenate([a[at], b[at]], axis=0).astype(o.dtype)
 
 
 def finish_body(info, offsets, counts, acc_in, r4, r8, r12, o0, o1, o2, o3, acc):
@@ -404,11 +404,12 @@
     o[...] = (a[...].astype(f32) + b[...].astype(f32)).astype(o.dtype)
 
 
-def join_body(info, a, b, o):
-    for h, m in enumerate((a, b)):
+def join_body(info, own, a, b, c, o):
+    total = own[...] + a[...].astype(f32) + (b[...].astype(f32) + c[...].astype(f32))
+    for h in (0, 1):
         for t in range(3):
             col = pl.multiple_of((info[2] ^ h) * 384 + t * 128, 128)
-            o[:, pl.ds(col, 128)] = m[24 * t : 24 * t + 24]
+            o[:, pl.ds(col, 128)] = total[72 * h + 24 * t : 72 * h + 24 * t + 24]
 
 
 smem = pl.BlockSpec(memory_space=pltpu.SMEM)
@@ -416,9 +417,8 @@
 hbm = pl.BlockSpec(memory_space=pltpu.HBM)
 
 
-def call(body, scalars, arrays, outs, scratch=(), flops=0, space=vmem, sems=0, limit=12):
+def call(body, scalars, arrays, outs, scratch=(), cost=1000, space=vmem, sems=0, limit=12):
     shapes = [jax.ShapeDtypeStruct(s, t) for s, t in outs]
-    moved = sum(a.size * a.dtype.itemsize for a in arrays) + sum(s.size * s.dtype.itemsize for s in shapes)
     return pl.pallas_call(
         body,
         out_shape=shapes,
@@ -426,7 +426,7 @@
         out_specs=[vmem] * len(shapes),
         scratch_shapes=[pltpu.VMEM(s, t) for s, t in scratch] + [pltpu.SemaphoreType.DMA((sems,))] * (sems > 0),
         compiler_params=pltpu.CompilerParams(vmem_limit_bytes=limit * 1024 * 1024),
-        cost_estimate=pl.CostEstimate(flops=1000, bytes_accessed=1000, transcendentals=0),
+        cost_estimate=pl.CostEstimate(flops=cost, bytes_accessed=1000, transcendentals=0),
     )(*scalars, *arrays)
 
 
@@ -482,7 +482,6 @@
         [out_grad[0], out_weight, msgs[0]],
         [((256, 768), bf16)] + [((256, 128), bf16)] * 4 + [chunk],
         [((256, 384), bf16)],
-        flops=3 * 10**8,
     )
     x, s4, s8 = call(
         collect_body,
@@ -496,7 +495,6 @@
         places,
         [x],
         [(cube, f32)] * 4 + [((512, 128), f32), ((4, 2, 256, 256), bf16), ((2, 512, 512), bf16)],
-        flops=10**9,
     )
     top, r4 = lax.optimization_barrier((top, r4))
     (s12,) = call(relay_body, [], [s8, r4], [((4, 128, 128), bf16)])
@@ -507,7 +505,6 @@
         places,
         [x, r4, top, num, den],
         [(cube, f32)] * 3 + [((256, 128), f32), ((2, 256, 512), bf16)],
-        flops=10**9,
     )
     top, norm, mx0, mx1, mx2, mx3, m4, e4 = call(
         far_body,
@@ -515,7 +512,6 @@
         [x, r4, r12, top, num, den, g0, g1, g2, g3],
         [(cube, f32)] * 2 + [((512, 128), bf16)] * 4 + [((128, 128), f32), ((2, 128, 512), bf16)],
         [(cube, f32)] * 2,
-        flops=10**9,
     )
     mixed = [mx0] + [shift(b, routes(d)) for d, b in ((1, mx1), (2, mx2), (3, mx3))]
     send, keep = call(
@@ -524,7 +520,6 @@
         mixed + [og],
         [((16, *block), bf16), ((16, *block), f32)],
         [((256, 512), bf16), ((384, 768), f32), ((16, *block), f32)],
-        flops=3 * 10**8,
     )
     arrived = dp_step(send, 1)
     keep, *mixed = lax.optimization_barrier([keep] + mixed)
@@ -534,9 +529,12 @@
         [x, r4, r12, top, norm, m3, m4, e3, e4, mx0, mx1, mx2, mx3] + mixed,
         [(cube, bf16), (cube, f32), ((3, *cube), f32)]
         + [((2, 384, 128), bf16), ((2, 128, 128), bf16), ((2, 128, 128), bf16)],
-        flops=10**9,
     )
     state = [x, g, top, norm, delta]
+    (attended,) = call(
+        attended_body, [info], mixed + [out_weight], [((256, 768), bf16)], [((256, 512), bf16)]
+    )
+    attended, keep = lax.optimization_barrier((attended, keep))
     flat = ((288, 128), bf16)
     own, s1, s2, s3 = call(cores_body, [], [keep, arrived], [((288, 128), f32)] + [flat] * 3)
     near = [seq_step(b, d) for d, b in ((1, s1), (2, s2), (3, s3))]
@@ -545,28 +543,27 @@
     (low,) = call(sum_body, [], [own] + near, [flat])
     acc, low = lax.optimization_barrier((acc, low))
     arrived = dp_step(low, 2)
-    (acc,) = call(back_two_body, places, state + [acc, m2, e2], [((3, *cube), f32)], flops=10**9)
+    (acc,) = call(back_two_body, places, state + [acc, m2, e2], [((3, *cube), f32)])
     acc, low = lax.optimization_barrier((acc, low))
     (low,) = call(pair_body, [], [low, arrived], [flat])
     rest = [dp_step(low, d) for d in (4, 8, 12)]
     acc, low = lax.optimization_barrier((acc, low))
-    (acc,) = call(back_one_body, places, state + [acc, m1, e1], [((3, *cube), f32)], flops=10**9)
+    (acc,) = call(back_one_body, places, state + [acc, m1, e1], [((3, *cube), f32)])
     acc, low = lax.optimization_barrier((acc, low))
-    own, s4, s8, s12 = call(quarters_body, [], [low] + rest, [(block, f32)] + [(block, bf16)] * 3)
-    acc, own = lax.optimization_barrier((acc, own))
-    outs = call(finish_body, places, [acc] + far, [((768, 128), bf16)] * 4, [((3, *cube), f32)])
+    (low,) = call(sum_body, [], [low] + rest, [flat])
+    acc, low = lax.optimization_barrier((acc, low))
+    other = dp_step(low, 1)
+    outs = call(
+        finish_body, places, [acc] + far, [((768, 128), bf16)] * 4, [((3, *cube), f32)], cost=2 * 10**9
+    )
+    *outs, other = lax.optimization_barrier([*outs, other])
     home = [outs[0]] + [shift(outs[d], routes(d)) for d in (1, 2, 3)]
+    both = (144, 128)
+    own, s4, s8, s12 = call(halves_body, [], [low, other], [(both, f32)] + [(both, bf16)] * 3)
     quarters = [seq_step(b, d) for d, b in ((4, s4), (8, s8), (12, s12))]
-    first, *mixed = lax.optimization_barrier([outs[0]] + mixed)
-    (attended,) = call(
-        attended_body, [info], mixed + [out_weight], [((256, 768), bf16)], [((256, 512), bf16)], flops=3 * 10**8
-    )
-    first, attended = lax.optimization_barrier((first, attended))
-    grads = call(home_body, [info], [first] + home[1:], [third] * 3, [((3, 256, 512), bf16)])
+    grads = call(home_body, [info], home, [third] * 3, [((3, 256, 512), bf16)])
     *grads, own = lax.optimization_barrier([*grads, own])
-    (own,) = call(sum_body, [], [own] + quarters, [(block, f32)])
-    other = dp_step(own, 1)
-    (grad_weight,) = call(join_body, [info], [own, other], [((24, 768), f32)])
+    (grad_weight,) = call(join_body, [info], [own] + quarters, [((24, 768), f32)])
     return (attended[None], grads[0][None], grads[1][None], grads[2][None], grad_weight)
 
 

time: 105 us -> 103 us (0.981)
  the two profiles are of different devices: /device:TPU:1 before, /device:TPU:24 now
where the time goes in v6:
time: 103 us
  starting transfers between devices  46.9 us (46%)
  waiting for transfers between devices  26.6 us (26%)
  Pallas kernels  25.2 us (24%)
  local copies, waits for them, and re-layouts  2.99 us (3%)
  between operations  1.48 us (1%)
    ppermute x14, starting transfers between devices, shift(): return lax.ppermute(block, ('dp', 'seq'), pairs)  29.7 us
    pallas_call x20, Pallas kernels, call(): pl.pallas_call(body, out_shape=shapes, in_specs=[smem] * len(scalars) + [...  25.2 us
    ppermute x14, waiting for transfers between devices, shift(): return lax.ppermute(block, ('dp', 'seq'), pairs)  23.3 us
    ppermute x6, starting transfers between devices, seq_step(): return lax.ppermute(block, 'seq', [(i, i ^ step) for i in range(16)])  12.1 us
    ppermute x6, starting transfers between devices, dp_step(): return lax.ppermute(block, 'dp', [(i, i ^ step) for i in range(16)])  5.05 us
    ppermute x6, waiting for transfers between devices, seq_step(): return lax.ppermute(block, 'seq', [(i, i ^ step) for i in range(16)])  3.11 us
    unnamed x10, local copies, waits for them, and re-layouts  2.99 us
  transfers between devices with their start and end apart: 26, of which 13 were waited for; matrix products, arithmetic and copies ran while one was open for 0% of the time, Pallas kernels for 18%

profile of v6, /device:TPU:24, one launch (start us, length us, event | category | flops | bytes accessed | tf_op | source)
XLA Modules:
  0.0 103.2 jit_solution(504233931708440093)
XLA Ops:
  0.6 2.5 %shard_map.110 = (bf16[3,256,128]{2,1,0:T(8,128)(2,1)}, bf16[3,256,128]{2,1,0:T(8,128)(2,1)}, bf16[3,256,128]{2,1,0:T(8,128)(2,1)}, bf16[3,256,128]{2,1,0:T(8,128)(2,1)}) custom-call(bf16[256,384]{1,0:T(8,128)(2,1)} %bitcast.13, bf16[256,384]{1,0:T(8,128)(2,1)} %bitcast.14, bf16[256,384]{1,0:T(8,128)(2,1)} %bitcast.15), custom_call_target="tpu_custom_call" | custom-call | flops 1000 | bytes 1000 | tf_op jit(solution)/shard_map/pallas_call | solution.py:422
  3.2 3.1 %collective-permute-start = (bf16[3,256,128]{2,1,0:T(8,128)(2,1)}, bf16[3,256,128]{2,1,0:T(8,128)(2,1)S(1)}, u32[]{:S(2)}, u32[]{:S(2)}) collective-permute-start(bf16[3,256,128]{2,1,0:T(8,128)(2,1)} %get-tuple-element.96), channel_id=1, source_target_pairs={{0,1},{1,0},{2,3},{3,2},{4,5},{5,4},{6,7},{7,6},{8,9},{9,8},{10,11... | collective-permute-start | bytes 589832 | tf_op jit(solution)/shard_map/ppermute | solution.py:445
  6.3 1.9 %collective-permute-start.1 = (bf16[3,256,128]{2,1,0:T(8,128)(2,1)}, bf16[3,256,128]{2,1,0:T(8,128)(2,1)S(1)}, u32[]{:S(2)}, u32[]{:S(2)}) collective-permute-start(bf16[3,256,128]{2,1,0:T(8,128)(2,1)} %get-tuple-element.97), channel_id=1, source_target_pairs={{0,2},{1,3},{2,0},{3,1},{4,6},{5,7},{6,4},{7,5},{8,10},{9,11},{10,... | collective-permute-start | bytes 589832 | tf_op jit(solution)/shard_map/ppermute | solution.py:445
  8.3 1.1 %copy-done = bf16[384,768]{1,0:T(8,128)(2,1)S(1)} copy-done((bf16[384,768]{1,0:T(8,128)(2,1)S(1)}, bf16[384,768]{1,0:T(8,128)(2,1)}, u32[]{:S(2)}) %copy-start) | copy-done | bytes 589848
  9.4 1.0 copy-done.2
  10.4 0.9 copy-done.3
  11.3 1.1 %shard_map.111 = (bf16[256,768]{1,0:T(8,128)(2,1)S(1)}, bf16[256,128]{1,0:T(8,128)(2,1)S(1)}, bf16[256,128]{1,0:T(8,128)(2,1)S(1)}, bf16[256,128]{1,0:T(8,128)(2...) custom-call(s32[3]{0:T(128)S(1)} %pad_add_fusion.info, bf16[256,768]{1,0:T(8,128)(2,1)S(1)} %bitcast.11, ...), custom_call_target="tpu_custom_call" | custom-call | flops 1000 | bytes 1000 | tf_op jit(solution)/shard_map/pallas_call | solution.py:422
  13.1 1.2 %collective-permute-done.1.m2 = bf16[3,256,128]{2,1,0:T(8,128)(2,1)S(1)} collective-permute-done((bf16[3,256,128]{2,1,0:T(8,128)(2,1)}, bf16[3,256,128]{2,1,0:T(8,128)(2,1)S(1)}, u32[]{:S(2)}, u32[]{:S(2)}) %collective-permute-start.1) | collective-permute-done | bytes 196640 | tf_op jit(solution)/shard_map/ppermute | solution.py:445
  14.3 2.9 %collective-permute-done.2.m3 = bf16[3,256,128]{2,1,0:T(8,128)(2,1)S(1)} collective-permute-done((bf16[3,256,128]{2,1,0:T(8,128)(2,1)}, bf16[3,256,128]{2,1,0:T(8,128)(2,1)S(1)}, u32[]{:S(2)}, u32[]{:S(2)}) %collective-permute-start.2) | collective-permute-done | bytes 196640 | tf_op jit(solution)/shard_map/ppermute | solution.py:445
  17.2 0.7 shard_map.112
  17.9 3.4 %collective-permute-start.3 = (bf16[2,384,128]{2,1,0:T(8,128)(2,1)S(1)}, bf16[2,384,128]{2,1,0:T(8,128)(2,1)S(1)}, u32[]{:S(2)}, u32[]{:S(2)}) collective-permute-start(bf16[2,384,128]{2,1,0:T(8,128)(2,1)S(1)} %get-tuple-element.101), channel_id=1, source_target_pairs={{0,4},{1,5},{2,6},{3,7},{4,0},{5,1},{6,2},{7,3},{8,12},{9,13},{10,... | collective-permute-start | bytes 589832 | tf_op jit(solution)/shard_map/ppermute | solution.py:445
  21.2 3.3 %shard_map.113 = (f32[8,128,128]{2,1,0:T(8,128)S(1)}, f32[8,128,128]{2,1,0:T(8,128)S(1)}, f32[8,128,128]{2,1,0:T(8,128)S(1)}, f32[8,128,128]{2,1,0:T(8,128)S(1)}...) custom-call(s32[3]{0:T(128)S(1)} %pad_add_fusion.info, ...), custom_call_target="tpu_custom_call" | custom-call | flops 1000 | bytes 1000 | tf_op jit(solution)/shard_map/pallas_call | solution.py:422
  24.6 4.6 %collective-permute-done.3.r4 = bf16[2,384,128]{2,1,0:T(8,128)(2,1)S(1)} collective-permute-done((bf16[2,384,128]{2,1,0:T(8,128)(2,1)S(1)}, bf16[2,384,128]{2,1,0:T(8,128)(2,1)S(1)}, u32[]{:S(2)}, u32[]{:S(2)}) %collective-permute-start.3) | collective-permute-done | bytes 196640 | tf_op jit(solution)/shard_map/ppermute | solution.py:445
  29.2 4.2 %collective-permute-start.4 = (bf16[4,128,128]{2,1,0:T(8,128)(2,1)S(1)}, bf16[4,128,128]{2,1,0:T(8,128)(2,1)S(1)}, u32[]{:S(2)}, u32[]{:S(2)}) collective-permute-start(bf16[4,128,128]{2,1,0:T(8,128)(2,1)S(1)} %shard_map.114), channel_id=1, source_target_pairs={{0,12},{1,13},{2,14},{3,15},{4,8},{5,9},{6,10},{7,11},{8,4},{9,5},... | collective-permute-start | bytes 393224 | tf_op jit(solution)/shard_map/ppermute | solution.py:445
  33.4 1.7 %shard_map.115 = (f32[8,128,128]{2,1,0:T(8,128)S(1)}, f32[8,128,128]{2,1,0:T(8,128)S(1)}, f32[8,128,128]{2,1,0:T(8,128)S(1)}, f32[256,128]{1,0:T(8,128)S(1)}, bf16[2,256,512]{2,1,0:T(8,128)(2,1)S(1)}) custom-call(s32[3]{0:T(128)S(1)} %pad_add_fusion.info, s32[3,6]{1,0:T(4,128)S(1)} %copy-done.4, s32[1]{0:T(128)S(6)} %copy.12.counts, ...), custom_call_target="tpu_custom_call" | custom-call | flops 1000 | bytes 1000 | tf_op jit(solution)/shard_map/pallas_call | solution.py:422
  35.1 3.6 %collective-permute-done.4.r12 = bf16[4,128,128]{2,1,0:T(8,128)(2,1)S(1)} collective-permute-done((bf16[4,128,128]{2,1,0:T(8,128)(2,1)S(1)}, bf16[4,128,128]{2,1,0:T(8,128)(2,1)S(1)}, u32[]{:S(2)}, u32[]{:S(2)}) %collective-permute-start.4) | collective-permute-done | bytes 131104 | tf_op jit(solution)/shard_map/ppermute | solution.py:445
  38.7 1.5 %shard_map.116 = (f32[8,128,128]{2,1,0:T(8,128)S(1)}, f32[8,128,128]{2,1,0:T(8,128)S(1)}, bf16[512,128]{1,0:T(8,128)(2,1)S(1)}, bf16[512,128]{1,0:T(8,128)(2,1)S...) custom-call(s32[3]{0:T(128)S(1)} %pad_add_fusion.info, ...), custom_call_target="tpu_custom_call" | custom-call | flops 1000 | bytes 1000 | tf_op jit(solution)/shard_map/pallas_call | solution.py:422
  40.2 2.6 %collective-permute-start.5 = (bf16[512,128]{1,0:T(8,128)(2,1)S(1)}, bf16[512,128]{1,0:T(8,128)(2,1)S(1)}, u32[]{:S(2)}, u32[]{:S(2)}) collective-permute-start(bf16[512,128]{1,0:T(8,128)(2,1)S(1)} %get-tuple-element.116.mx1), channel_id=1, source_target_pairs={{0,1},{1,0},{2,3},{3,2},{4,5},{5,4},{6,7},{7,6},{8,9},{9,8},{10,11... | collective-permute-start | bytes 393224 | tf_op jit(solution)/shard_map/ppermute | solution.py:445
  42.8 2.6 %collective-permute-start.6 = (bf16[512,128]{1,0:T(8,128)(2,1)S(1)}, bf16[512,128]{1,0:T(8,128)(2,1)S(1)}, u32[]{:S(2)}, u32[]{:S(2)}) collective-permute-start(bf16[512,128]{1,0:T(8,128)(2,1)S(1)} %get-tuple-element.117.mx2), channel_id=1, source_target_pairs={{0,2},{1,3},{2,0},{3,1},{4,6},{5,7},{6,4},{7,5},{8,10},{9,11},{10,... | collective-permute-start | bytes 393224 | tf_op jit(solution)/shard_map/ppermute | solution.py:445
  45.8 0.9 collective-permute-done.5.m1.in1
  46.7 2.9 %collective-permute-done.6.m2.in2 = bf16[512,128]{1,0:T(8,128)(2,1)S(1)} collective-permute-done((bf16[512,128]{1,0:T(8,128)(2,1)S(1)}, bf16[512,128]{1,0:T(8,128)(2,1)S(1)}, u32[]{:S(2)}, u32[]{:S(2)}) %collective-permute-start.6) | collective-permute-done | bytes 131104 | tf_op jit(solution)/shard_map/ppermute | solution.py:445
  49.6 3.1 %collective-permute-done.7.m3.in3 = bf16[512,128]{1,0:T(8,128)(2,1)S(1)} collective-permute-done((bf16[512,128]{1,0:T(8,128)(2,1)S(1)}, bf16[512,128]{1,0:T(8,128)(2,1)S(1)}, u32[]{:S(2)}, u32[]{:S(2)}) %collective-permute-start.7) | collective-permute-done | bytes 131104 | tf_op jit(solution)/shard_map/ppermute | solution.py:445
  52.7 1.1 %shard_map.117 = (bf16[16,72,128]{2,1,0:T(8,128)(2,1)S(1)}, f32[16,72,128]{2,1,0:T(8,128)S(1)}) custom-call(s32[3]{0:T(128)S(1)} %pad_add_fusion.info, bf16[512,128]{1,0:T(8,128)(2,1)S(1)} %get-tuple-element.121.m0.mx0.in0, bf16[512,128]{1,0:T(8,128)(2,1)S(1)} %collective-permute-done.5.m1.in1, bf16[512,128]{1,0:T(8,128)(2,1)S(1)} %collective-permute-done.6.m2.in2, ...), custom_call_target="tpu_custom_call" | custom-call | flops 1000 | bytes 1000 | tf_op jit(solution)/shard_map/pallas_call | solution.py:422
  53.9 1.9 %shard_map.118 = bf16[256,768]{1,0:T(8,128)(2,1)} custom-call(s32[3]{0:T(128)S(1)} %pad_add_fusion.info, bf16[512,128]{1,0:T(8,128)(2,1)S(1)} %get-tuple-element.121.m0.mx0.in0, bf16[512,128]{1,0:T(8,128)(2,1)S(1)} %collective-permute-done.5.m1.in1, bf16[512,128]{1,0:T(8,128)(2,1)S(1)} %collective-permute-done.6.m2.in2, ...), custom_call_target="tpu_custom_call" | custom-call | flops 1000 | bytes 1000 | tf_op jit(solution)/shard_map/pallas_call | solution.py:422
  55.8 1.9 %collective-permute-start.9 = (bf16[288,128]{1,0:T(8,128)(2,1)S(1)}, bf16[288,128]{1,0:T(8,128)(2,1)S(1)}, u32[]{:S(2)}, u32[]{:S(2)}) collective-permute-start(bf16[288,128]{1,0:T(8,128)(2,1)S(1)} %get-tuple-element.143), channel_id=1, source_target_pairs={{0,1},{1,0},{2,3},{3,2},{4,5},{5,4},{6,7},{7,6},{8,9},{9,8},{10,11... | collective-permute-start | bytes 221192 | tf_op jit(solution)/shard_map/ppermute | solution.py:453
  57.7 1.7 %collective-permute-start.10 = (bf16[288,128]{1,0:T(8,128)(2,1)S(1)}, bf16[288,128]{1,0:T(8,128)(2,1)S(1)}, u32[]{:S(2)}, u32[]{:S(2)}) collective-permute-start(bf16[288,128]{1,0:T(8,128)(2,1)S(1)} %get-tuple-element.144), channel_id=1, source_target_pairs={{0,2},{1,3},{2,0},{3,1},{4,6},{5,7},{6,4},{7,5},{8,10},{9,11},{10,... | collective-permute-start | bytes 221192 | tf_op jit(solution)/shard_map/ppermute | solution.py:453
  59.4 1.4 %collective-permute-start.11 = (bf16[288,128]{1,0:T(8,128)(2,1)S(1)}, bf16[288,128]{1,0:T(8,128)(2,1)S(1)}, u32[]{:S(2)}, u32[]{:S(2)}) collective-permute-start(bf16[288,128]{1,0:T(8,128)(2,1)S(1)} %get-tuple-element.145), channel_id=1, source_target_pairs={{0,3},{1,2},{2,1},{3,0},{4,7},{5,6},{6,5},{7,4},{8,11},{9,10},{10,... | collective-permute-start | bytes 221192 | tf_op jit(solution)/shard_map/ppermute | solution.py:453
  60.9 2.8 %shard_map.119 = (bf16[8,128,128]{2,1,0:T(8,128)(2,1)S(1)}, f32[8,128,128]{2,1,0:T(8,128)S(1)}, f32[3,8,128,128]{3,2,1,0:T(8,128)S(1)}, bf16[2,384,128]{2,1,0:T(...) custom-call(s32[3]{0:T(128)S(1)} %pad_add_fusion.info, s32[3,6]{1,0:T(4,128)S(1)} %copy-done.4, ...), custom_call_target="tpu_custom_call" | custom-call | flops 1000 | bytes 1000 | tf_op jit(solution)/shard_map/pallas_call | solution.py:422
  63.8 2.5 %collective-permute-done.11.d = bf16[288,128]{1,0:T(8,128)(2,1)S(1)} collective-permute-done((bf16[288,128]{1,0:T(8,128)(2,1)S(1)}, bf16[288,128]{1,0:T(8,128)(2,1)S(1)}, u32[]{:S(2)}, u32[]{:S(2)}) %collective-permute-start.11) | collective-permute-done | bytes 73760 | tf_op jit(solution)/shard_map/ppermute | solution.py:453
  66.2 0.7 collective-permute-start.12
  66.9 1.3 %collective-permute-start.16 = (bf16[2,384,128]{2,1,0:T(8,128)(2,1)S(1)}, bf16[2,384,128]{2,1,0:T(8,128)(2,1)S(1)}, u32[]{:S(2)}, u32[]{:S(2)}) collective-permute-start(bf16[2,384,128]{2,1,0:T(8,128)(2,1)S(1)} %get-tuple-element.159), channel_id=1, source_target_pairs={{0,4},{1,5},{2,6},{3,7},{4,0},{5,1},{6,2},{7,3},{8,12},{9,13},{10,... | collective-permute-start | bytes 589832 | tf_op jit(solution)/shard_map/ppermute | solution.py:445
  68.3 2.3 %shard_map.122.acc_in = f32[3,8,128,128]{3,2,1,0:T(8,128)S(1)} custom-call(s32[3]{0:T(128)S(1)} %pad_add_fusion.info, s32[3,6]{1,0:T(4,128)S(1)} %copy-done.4, s32[1]{0:T(128)S(6)} %copy.12.counts, bf16[3,8,128,128]{3,2,1,0:T(8,128)(2,1)S(1)} %get-tuple-element.99.x, bf16[8,128,128]{2,1,0:T(8,128)(2,1)S(1)} %get-tuple-element.133.g, ...), custom_call_target="tpu_custom_call" | custom-call | flops 1000 | bytes 1000 | tf_op jit(solution)/shard_map/pallas_call | solution.py:422
  71.0 2.6 %collective-permute-start.14 = (bf16[288,128]{1,0:T(8,128)(2,1)S(1)}, bf16[288,128]{1,0:T(8,128)(2,1)S(1)}, u32[]{:S(2)}, u32[]{:S(2)}) collective-permute-start(bf16[288,128]{1,0:T(8,128)(2,1)S(1)} %shard_map.123.a), channel_id=1, source_target_pairs={{0,128},{16,144},{32,160},{48,176},{64,192},{80,208},{96,224},{112... | collective-permute-start | bytes 221192 | tf_op jit(solution)/shard_map/ppermute | solution.py:449
  73.6 1.3 %collective-permute-start.13 = (bf16[288,128]{1,0:T(8,128)(2,1)S(1)}, bf16[288,128]{1,0:T(8,128)(2,1)S(1)}, u32[]{:S(2)}, u32[]{:S(2)}) collective-permute-start(bf16[288,128]{1,0:T(8,128)(2,1)S(1)} %shard_map.123.a), channel_id=1, source_target_pairs={{0,64},{16,80},{32,96},{48,112},{64,0},{80,16},{96,32},{112,48},{1... | collective-permute-start | bytes 221192 | tf_op jit(solution)/shard_map/ppermute | solution.py:449
  74.9 2.8 %collective-permute-start.17 = (bf16[2,128,128]{2,1,0:T(8,128)(2,1)S(1)}, bf16[2,128,128]{2,1,0:T(8,128)(2,1)S(1)}, u32[]{:S(2)}, u32[]{:S(2)}) collective-permute-start(bf16[2,128,128]{2,1,0:T(8,128)(2,1)S(1)} %get-tuple-element.160), channel_id=1, source_target_pairs={{0,8},{1,9},{2,10},{3,11},{4,12},{5,13},{6,14},{7,15},{8,0},{9,1},... | collective-permute-start | bytes 196616 | tf_op jit(solution)/shard_map/ppermute | solution.py:445
  77.7 2.3 %collective-permute-start.18 = (bf16[2,128,128]{2,1,0:T(8,128)(2,1)S(1)}, bf16[2,128,128]{2,1,0:T(8,128)(2,1)S(1)}, u32[]{:S(2)}, u32[]{:S(2)}) collective-permute-start(bf16[2,128,128]{2,1,0:T(8,128)(2,1)S(1)} %get-tuple-element.161), channel_id=1, source_target_pairs={{0,12},{1,13},{2,14},{3,15},{4,8},{5,9},{6,10},{7,11},{8,4},{9,5},... | collective-permute-start | bytes 196616 | tf_op jit(solution)/shard_map/ppermute | solution.py:445
  80.0 2.3 %shard_map.124.acc_in = f32[3,8,128,128]{3,2,1,0:T(8,128)S(1)} custom-call(s32[3]{0:T(128)S(1)} %pad_add_fusion.info, s32[3,6]{1,0:T(4,128)S(1)} %copy-done.4, s32[1]{0:T(128)S(6)} %copy.12.counts, bf16[3,8,128,128]{3,2,1,0:T(8,128)(2,1)S(1)} %get-tuple-element.99.x, bf16[8,128,128]{2,1,0:T(8,128)(2,1)S(1)} %get-tuple-element.133.g, ...), custom_call_target="tpu_custom_call" | custom-call | flops 1000 | bytes 1000 | tf_op jit(solution)/shard_map/pallas_call | solution.py:422
  82.5 1.9 %collective-permute-done.17.r8 = bf16[2,128,128]{2,1,0:T(8,128)(2,1)S(1)} collective-permute-done((bf16[2,128,128]{2,1,0:T(8,128)(2,1)S(1)}, bf16[2,128,128]{2,1,0:T(8,128)(2,1)S(1)}, u32[]{:S(2)}, u32[]{:S(2)}) %collective-permute-start.17) | collective-permute-done | bytes 65568 | tf_op jit(solution)/shard_map/ppermute | solution.py:445
  84.4 0.9 shard_map.126
  85.3 2.7 %collective-permute-start.20 = (bf16[768,128]{1,0:T(8,128)(2,1)S(1)}, bf16[768,128]{1,0:T(8,128)(2,1)S(1)}, u32[]{:S(2)}, u32[]{:S(2)}) collective-permute-start(bf16[768,128]{1,0:T(8,128)(2,1)S(1)} %get-tuple-element.168), channel_id=1, source_target_pairs={{0,1},{1,0},{2,3},{3,2},{4,5},{5,4},{6,7},{7,6},{8,9},{9,8},{10,11... | collective-permute-start | bytes 589832 | tf_op jit(solution)/shard_map/ppermute | solution.py:445
  88.0 1.6 %collective-permute-start.21 = (bf16[768,128]{1,0:T(8,128)(2,1)S(1)}, bf16[768,128]{1,0:T(8,128)(2,1)S(1)}, u32[]{:S(2)}, u32[]{:S(2)}) collective-permute-start(bf16[768,128]{1,0:T(8,128)(2,1)S(1)} %get-tuple-element.169), channel_id=1, source_target_pairs={{0,2},{1,3},{2,0},{3,1},{4,6},{5,7},{6,4},{7,5},{8,10},{9,11},{10,... | collective-permute-start | bytes 589832 | tf_op jit(solution)/shard_map/ppermute | solution.py:445
  89.6 0.8 collective-permute-start.22
  90.4 2.0 %collective-permute-start.23 = (bf16[144,128]{1,0:T(8,128)(2,1)S(1)}, bf16[144,128]{1,0:T(8,128)(2,1)S(1)}, u32[]{:S(2)}, u32[]{:S(2)}) collective-permute-start(bf16[144,128]{1,0:T(8,128)(2,1)S(1)} %get-tuple-element.180), channel_id=1, source_target_pairs={{0,4},{1,5},{2,6},{3,7},{4,0},{5,1},{6,2},{7,3},{8,12},{9,13},{10,... | collective-permute-start | bytes 110600 | tf_op jit(solution)/shard_map/ppermute | solution.py:453
  92.5 3.2 %collective-permute-start.24 = (bf16[144,128]{1,0:T(8,128)(2,1)S(1)}, bf16[144,128]{1,0:T(8,128)(2,1)S(1)}, u32[]{:S(2)}, u32[]{:S(2)}) collective-permute-start(bf16[144,128]{1,0:T(8,128)(2,1)S(1)} %get-tuple-element.181), channel_id=1, source_target_pairs={{0,8},{1,9},{2,10},{3,11},{4,12},{5,13},{6,14},{7,15},{8,0},{9,1},... | collective-permute-start | bytes 110600 | tf_op jit(solution)/shard_map/ppermute | solution.py:453
  95.7 1.8 %collective-permute-start.25 = (bf16[144,128]{1,0:T(8,128)(2,1)S(1)}, bf16[144,128]{1,0:T(8,128)(2,1)S(1)}, u32[]{:S(2)}, u32[]{:S(2)}) collective-permute-start(bf16[144,128]{1,0:T(8,128)(2,1)S(1)} %get-tuple-element.182), channel_id=1, source_target_pairs={{0,12},{1,13},{2,14},{3,15},{4,8},{5,9},{6,10},{7,11},{8,4},{9,5},... | collective-permute-start | bytes 110600 | tf_op jit(solution)/shard_map/ppermute | solution.py:453
  97.5 2.2 %collective-permute-done.22.m3 = bf16[768,128]{1,0:T(8,128)(2,1)S(1)} collective-permute-done((bf16[768,128]{1,0:T(8,128)(2,1)S(1)}, bf16[768,128]{1,0:T(8,128)(2,1)S(1)}, u32[]{:S(2)}, u32[]{:S(2)}) %collective-permute-start.22) | collective-permute-done | bytes 196640 | tf_op jit(solution)/shard_map/ppermute | solution.py:445
  99.7 1.7 %shard_map.127 = (bf16[256,384]{1,0:T(8,128)(2,1)}, bf16[256,384]{1,0:T(8,128)(2,1)}, bf16[256,384]{1,0:T(8,128)(2,1)}) custom-call(s32[3]{0:T(128)S(1)} %pad_add_fusion.info, bf16[768,128]{1,0:T(8,128)(2,1)S(1)} %get-tuple-element.167.m0, bf16[768,128]{1,0:T(8,128)(2,1)S(1)} %collective-permute-done.20.m1, bf16[768,128]{1,0:T(8,128)(2,1)S(1)} %collective-permute-done.21.m2, ...), custom_call_target="tpu_custom_call" | custom-call | flops 1000 | bytes 1000 | tf_op jit(solution)/shard_map/pallas_call | solution.py:422
  102.0 1.2 %shard_map.129 = f32[24,768]{1,0:T(8,128)} custom-call(s32[3]{0:T(128)S(1)} %pad_add_fusion.info, f32[144,128]{1,0:T(8,128)S(1)} %get-tuple-element.179.own, bf16[144,128]{1,0:T(8,128)(2,1)S(1)} %collective-permute-done.23.a, bf16[144,128]{1,0:T(8,128)(2,1)S(1)} %collective-permute-done.24.b, bf16[144,128]{1,0:T(8,128)(2,1)S(1)} %collective-permute-done.25.c), custom_call_target="tpu_custom_call" | custom-call | flops 1000 | bytes 1000 | tf_op jit(solution)/shard_map/pallas_call | solution.py:422
  (35 shorter events, 2.1 us)
Async XLA Ops:
  0.6 16.6 %copy-start.4 = (s32[3,6]{1,0:T(4,128)S(1)}, s32[3,6]{1,0:T(4,128)}, u32[]{:S(2)}) copy-start(s32[3,6]{1,0:T(4,128)} %offsets.15) | copy-start | bytes 220
  3.2 9.9 %collective-permute-start = (bf16[3,256,128]{2,1,0:T(8,128)(2,1)}, bf16[3,256,128]{2,1,0:T(8,128)(2,1)S(1)}, u32[]{:S(2)}, u32[]{:S(2)}) collective-permute-start(bf16[3,256,128]{2,1,0:T(8,128)(2,1)} %get-tuple-element.96), channel_id=1, source_target_pairs={{0,1},{1,0},{2,3},{3,2},{4,5},{5,4},{6,7},{7,6},{8,9},{9,8},{10,11... | collective-permute-start | bytes 589832 | tf_op jit(solution)/shard_map/ppermute | solution.py:445
  6.3 8.0 %collective-permute-start.1 = (bf16[3,256,128]{2,1,0:T(8,128)(2,1)}, bf16[3,256,128]{2,1,0:T(8,128)(2,1)S(1)}, u32[]{:S(2)}, u32[]{:S(2)}) collective-permute-start(bf16[3,256,128]{2,1,0:T(8,128)(2,1)} %get-tuple-element.97), channel_id=1, source_target_pairs={{0,2},{1,3},{2,0},{3,1},{4,6},{5,7},{6,4},{7,5},{8,10},{9,11},{10,... | collective-permute-start | bytes 589832 | tf_op jit(solution)/shard_map/ppermute | solution.py:445
  8.2 9.0 %collective-permute-start.2 = (bf16[3,256,128]{2,1,0:T(8,128)(2,1)}, bf16[3,256,128]{2,1,0:T(8,128)(2,1)S(1)}, u32[]{:S(2)}, u32[]{:S(2)}) collective-permute-start(bf16[3,256,128]{2,1,0:T(8,128)(2,1)} %get-tuple-element.98), channel_id=1, source_target_pairs={{0,3},{1,2},{2,1},{3,0},{4,7},{5,6},{6,5},{7,4},{8,11},{9,10},{10,... | collective-permute-start | bytes 589832 | tf_op jit(solution)/shard_map/ppermute | solution.py:445
  8.3 1.1 %copy-start = (bf16[384,768]{1,0:T(8,128)(2,1)S(1)}, bf16[384,768]{1,0:T(8,128)(2,1)}, u32[]{:S(2)}) copy-start(bf16[384,768]{1,0:T(8,128)(2,1)} %w.3) | copy-start | bytes 1769476
  9.4 1.0 copy-start.2
  10.4 0.9 copy-start.3
  17.9 11.3 %collective-permute-start.3 = (bf16[2,384,128]{2,1,0:T(8,128)(2,1)S(1)}, bf16[2,384,128]{2,1,0:T(8,128)(2,1)S(1)}, u32[]{:S(2)}, u32[]{:S(2)}) collective-permute-start(bf16[2,384,128]{2,1,0:T(8,128)(2,1)S(1)} %get-tuple-element.101), channel_id=1, source_target_pairs={{0,4},{1,5},{2,6},{3,7},{4,0},{5,1},{6,2},{7,3},{8,12},{9,13},{10,... | collective-permute-start | bytes 589832 | tf_op jit(solution)/shard_map/ppermute | solution.py:445
  29.2 9.5 %collective-permute-start.4 = (bf16[4,128,128]{2,1,0:T(8,128)(2,1)S(1)}, bf16[4,128,128]{2,1,0:T(8,128)(2,1)S(1)}, u32[]{:S(2)}, u32[]{:S(2)}) collective-permute-start(bf16[4,128,128]{2,1,0:T(8,128)(2,1)S(1)} %shard_map.114), channel_id=1, source_target_pairs={{0,12},{1,13},{2,14},{3,15},{4,8},{5,9},{6,10},{7,11},{8,4},{9,5},... | collective-permute-start | bytes 393224 | tf_op jit(solution)/shard_map/ppermute | solution.py:445
  38.7 15.2 %copy-start.1 = (bf16[384,768]{1,0:T(8,128)(2,1)S(1)}, bf16[384,768]{1,0:T(8,128)(2,1)}, u32[]{:S(2)}) copy-start(bf16[384,768]{1,0:T(8,128)(2,1)} %w.3) | copy-start | bytes 1769476
  40.2 6.6 %collective-permute-start.5 = (bf16[512,128]{1,0:T(8,128)(2,1)S(1)}, bf16[512,128]{1,0:T(8,128)(2,1)S(1)}, u32[]{:S(2)}, u32[]{:S(2)}) collective-permute-start(bf16[512,128]{1,0:T(8,128)(2,1)S(1)} %get-tuple-element.116.mx1), channel_id=1, source_target_pairs={{0,1},{1,0},{2,3},{3,2},{4,5},{5,4},{6,7},{7,6},{8,9},{9,8},{10,11... | collective-permute-start | bytes 393224 | tf_op jit(solution)/shard_map/ppermute | solution.py:445
  42.8 6.8 %collective-permute-start.6 = (bf16[512,128]{1,0:T(8,128)(2,1)S(1)}, bf16[512,128]{1,0:T(8,128)(2,1)S(1)}, u32[]{:S(2)}, u32[]{:S(2)}) collective-permute-start(bf16[512,128]{1,0:T(8,128)(2,1)S(1)} %get-tuple-element.117.mx2), channel_id=1, source_target_pairs={{0,2},{1,3},{2,0},{3,1},{4,6},{5,7},{6,4},{7,5},{8,10},{9,11},{10,... | collective-permute-start | bytes 393224 | tf_op jit(solution)/shard_map/ppermute | solution.py:445
  45.3 7.4 %collective-permute-start.7 = (bf16[512,128]{1,0:T(8,128)(2,1)S(1)}, bf16[512,128]{1,0:T(8,128)(2,1)S(1)}, u32[]{:S(2)}, u32[]{:S(2)}) collective-permute-start(bf16[512,128]{1,0:T(8,128)(2,1)S(1)} %get-tuple-element.118.mx3), channel_id=1, source_target_pairs={{0,3},{1,2},{2,1},{3,0},{4,7},{5,6},{6,5},{7,4},{8,11},{9,10},{10,... | collective-permute-start | bytes 393224 | tf_op jit(solution)/shard_map/ppermute | solution.py:445
  53.8 2.0 %collective-permute-start.8 = (bf16[16,72,128]{2,1,0:T(8,128)(2,1)S(1)}, bf16[16,72,128]{2,1,0:T(8,128)(2,1)S(1)}, u32[]{:S(2)}, u32[]{:S(2)}) collective-permute-start(bf16[16,72,128]{2,1,0:T(8,128)(2,1)S(1)} %get-tuple-element.140), channel_id=1, source_target_pairs={{0,16},{16,0},{32,48},{48,32},{64,80},{80,64},{96,112},{112,96},{1... | collective-permute-start | bytes 884744 | tf_op jit(solution)/shard_map/ppermute | solution.py:449
  55.8 7.9 %collective-permute-start.9 = (bf16[288,128]{1,0:T(8,128)(2,1)S(1)}, bf16[288,128]{1,0:T(8,128)(2,1)S(1)}, u32[]{:S(2)}, u32[]{:S(2)}) collective-permute-start(bf16[288,128]{1,0:T(8,128)(2,1)S(1)} %get-tuple-element.143), channel_id=1, source_target_pairs={{0,1},{1,0},{2,3},{3,2},{4,5},{5,4},{6,7},{7,6},{8,9},{9,8},{10,11... | collective-permute-start | bytes 221192 | tf_op jit(solution)/shard_map/ppermute | solution.py:453
  57.7 6.0 %collective-permute-start.10 = (bf16[288,128]{1,0:T(8,128)(2,1)S(1)}, bf16[288,128]{1,0:T(8,128)(2,1)S(1)}, u32[]{:S(2)}, u32[]{:S(2)}) collective-permute-start(bf16[288,128]{1,0:T(8,128)(2,1)S(1)} %get-tuple-element.144), channel_id=1, source_target_pairs={{0,2},{1,3},{2,0},{3,1},{4,6},{5,7},{6,4},{7,5},{8,10},{9,11},{10,... | collective-permute-start | bytes 221192 | tf_op jit(solution)/shard_map/ppermute | solution.py:453
  59.4 6.8 %collective-permute-start.11 = (bf16[288,128]{1,0:T(8,128)(2,1)S(1)}, bf16[288,128]{1,0:T(8,128)(2,1)S(1)}, u32[]{:S(2)}, u32[]{:S(2)}) collective-permute-start(bf16[288,128]{1,0:T(8,128)(2,1)S(1)} %get-tuple-element.145), channel_id=1, source_target_pairs={{0,3},{1,2},{2,1},{3,0},{4,7},{5,6},{6,5},{7,4},{8,11},{9,10},{10,... | collective-permute-start | bytes 221192 | tf_op jit(solution)/shard_map/ppermute | solution.py:453
  66.2 4.4 %collective-permute-start.12 = (bf16[288,128]{1,0:T(8,128)(2,1)S(1)}, bf16[288,128]{1,0:T(8,128)(2,1)S(1)}, u32[]{:S(2)}, u32[]{:S(2)}) collective-permute-start(bf16[288,128]{1,0:T(8,128)(2,1)S(1)} %shard_map.121.a), channel_id=1, source_target_pairs={{0,32},{16,48},{32,0},{48,16},{64,96},{80,112},{96,64},{112,80},{1... | collective-permute-start | bytes 221192 | tf_op jit(solution)/shard_map/ppermute | solution.py:449
  66.9 17.5 %collective-permute-start.16 = (bf16[2,384,128]{2,1,0:T(8,128)(2,1)S(1)}, bf16[2,384,128]{2,1,0:T(8,128)(2,1)S(1)}, u32[]{:S(2)}, u32[]{:S(2)}) collective-permute-start(bf16[2,384,128]{2,1,0:T(8,128)(2,1)S(1)} %get-tuple-element.159), channel_id=1, source_target_pairs={{0,4},{1,5},{2,6},{3,7},{4,0},{5,1},{6,2},{7,3},{8,12},{9,13},{10,... | collective-permute-start | bytes 589832 | tf_op jit(solution)/shard_map/ppermute | solution.py:445
  70.7 7.0 %collective-permute-start.15 = (bf16[288,128]{1,0:T(8,128)(2,1)S(1)}, bf16[288,128]{1,0:T(8,128)(2,1)S(1)}, u32[]{:S(2)}, u32[]{:S(2)}) collective-permute-start(bf16[288,128]{1,0:T(8,128)(2,1)S(1)} %shard_map.123.a), channel_id=1, source_target_pairs={{0,192},{16,208},{32,224},{48,240},{64,128},{80,144},{96,160},{112... | collective-permute-start | bytes 221192 | tf_op jit(solution)/shard_map/ppermute | solution.py:449
  71.0 11.3 %collective-permute-start.14 = (bf16[288,128]{1,0:T(8,128)(2,1)S(1)}, bf16[288,128]{1,0:T(8,128)(2,1)S(1)}, u32[]{:S(2)}, u32[]{:S(2)}) collective-permute-start(bf16[288,128]{1,0:T(8,128)(2,1)S(1)} %shard_map.123.a), channel_id=1, source_target_pairs={{0,128},{16,144},{32,160},{48,176},{64,192},{80,208},{96,224},{112... | collective-permute-start | bytes 221192 | tf_op jit(solution)/shard_map/ppermute | solution.py:449
  73.6 8.7 %collective-permute-start.13 = (bf16[288,128]{1,0:T(8,128)(2,1)S(1)}, bf16[288,128]{1,0:T(8,128)(2,1)S(1)}, u32[]{:S(2)}, u32[]{:S(2)}) collective-permute-start(bf16[288,128]{1,0:T(8,128)(2,1)S(1)} %shard_map.123.a), channel_id=1, source_target_pairs={{0,64},{16,80},{32,96},{48,112},{64,0},{80,16},{96,32},{112,48},{1... | collective-permute-start | bytes 221192 | tf_op jit(solution)/shard_map/ppermute | solution.py:449
  74.9 9.5 %collective-permute-start.17 = (bf16[2,128,128]{2,1,0:T(8,128)(2,1)S(1)}, bf16[2,128,128]{2,1,0:T(8,128)(2,1)S(1)}, u32[]{:S(2)}, u32[]{:S(2)}) collective-permute-start(bf16[2,128,128]{2,1,0:T(8,128)(2,1)S(1)} %get-tuple-element.160), channel_id=1, source_target_pairs={{0,8},{1,9},{2,10},{3,11},{4,12},{5,13},{6,14},{7,15},{8,0},{9,1},... | collective-permute-start | bytes 196616 | tf_op jit(solution)/shard_map/ppermute | solution.py:445
  77.7 6.7 %collective-permute-start.18 = (bf16[2,128,128]{2,1,0:T(8,128)(2,1)S(1)}, bf16[2,128,128]{2,1,0:T(8,128)(2,1)S(1)}, u32[]{:S(2)}, u32[]{:S(2)}) collective-permute-start(bf16[2,128,128]{2,1,0:T(8,128)(2,1)S(1)} %get-tuple-element.161), channel_id=1, source_target_pairs={{0,12},{1,13},{2,14},{3,15},{4,8},{5,9},{6,10},{7,11},{8,4},{9,5},... | collective-permute-start | bytes 196616 | tf_op jit(solution)/shard_map/ppermute | solution.py:445
  82.4 2.9 %collective-permute-start.19 = (bf16[288,128]{1,0:T(8,128)(2,1)S(1)}, bf16[288,128]{1,0:T(8,128)(2,1)S(1)}, u32[]{:S(2)}, u32[]{:S(2)}) collective-permute-start(bf16[288,128]{1,0:T(8,128)(2,1)S(1)} %shard_map.125.mine), channel_id=1, source_target_pairs={{0,16},{16,0},{32,48},{48,32},{64,80},{80,64},{96,112},{112,96},{1... | collective-permute-start | bytes 221192 | tf_op jit(solution)/shard_map/ppermute | solution.py:449
  85.3 10.4 %collective-permute-start.20 = (bf16[768,128]{1,0:T(8,128)(2,1)S(1)}, bf16[768,128]{1,0:T(8,128)(2,1)S(1)}, u32[]{:S(2)}, u32[]{:S(2)}) collective-permute-start(bf16[768,128]{1,0:T(8,128)(2,1)S(1)} %get-tuple-element.168), channel_id=1, source_target_pairs={{0,1},{1,0},{2,3},{3,2},{4,5},{5,4},{6,7},{7,6},{8,9},{9,8},{10,11... | collective-permute-start | bytes 589832 | tf_op jit(solution)/shard_map/ppermute | solution.py:445
  88.0 9.5 %collective-permute-start.21 = (bf16[768,128]{1,0:T(8,128)(2,1)S(1)}, bf16[768,128]{1,0:T(8,128)(2,1)S(1)}, u32[]{:S(2)}, u32[]{:S(2)}) collective-permute-start(bf16[768,128]{1,0:T(8,128)(2,1)S(1)} %get-tuple-element.169), channel_id=1, source_target_pairs={{0,2},{1,3},{2,0},{3,1},{4,6},{5,7},{6,4},{7,5},{8,10},{9,11},{10,... | collective-permute-start | bytes 589832 | tf_op jit(solution)/shard_map/ppermute | solution.py:445
  89.6 10.1 %collective-permute-start.22 = (bf16[768,128]{1,0:T(8,128)(2,1)S(1)}, bf16[768,128]{1,0:T(8,128)(2,1)S(1)}, u32[]{:S(2)}, u32[]{:S(2)}) collective-permute-start(bf16[768,128]{1,0:T(8,128)(2,1)S(1)} %get-tuple-element.170), channel_id=1, source_target_pairs={{0,3},{1,2},{2,1},{3,0},{4,7},{5,6},{6,5},{7,4},{8,11},{9,10},{10,... | collective-permute-start | bytes 589832 | tf_op jit(solution)/shard_map/ppermute | solution.py:445
  90.4 11.0 %collective-permute-start.23 = (bf16[144,128]{1,0:T(8,128)(2,1)S(1)}, bf16[144,128]{1,0:T(8,128)(2,1)S(1)}, u32[]{:S(2)}, u32[]{:S(2)}) collective-permute-start(bf16[144,128]{1,0:T(8,128)(2,1)S(1)} %get-tuple-element.180), channel_id=1, source_target_pairs={{0,4},{1,5},{2,6},{3,7},{4,0},{5,1},{6,2},{7,3},{8,12},{9,13},{10,... | collective-permute-start | bytes 110600 | tf_op jit(solution)/shard_map/ppermute | solution.py:453
  92.5 9.2 %collective-permute-start.24 = (bf16[144,128]{1,0:T(8,128)(2,1)S(1)}, bf16[144,128]{1,0:T(8,128)(2,1)S(1)}, u32[]{:S(2)}, u32[]{:S(2)}) collective-permute-start(bf16[144,128]{1,0:T(8,128)(2,1)S(1)} %get-tuple-element.181), channel_id=1, source_target_pairs={{0,8},{1,9},{2,10},{3,11},{4,12},{5,13},{6,14},{7,15},{8,0},{9,1},... | collective-permute-start | bytes 110600 | tf_op jit(solution)/shard_map/ppermute | solution.py:453
  95.7 6.4 %collective-permute-start.25 = (bf16[144,128]{1,0:T(8,128)(2,1)S(1)}, bf16[144,128]{1,0:T(8,128)(2,1)S(1)}, u32[]{:S(2)}, u32[]{:S(2)}) collective-permute-start(bf16[144,128]{1,0:T(8,128)(2,1)S(1)} %get-tuple-element.182), channel_id=1, source_target_pairs={{0,12},{1,13},{2,14},{3,15},{4,8},{5,9},{6,10},{7,11},{8,4},{9,5},... | collective-permute-start | bytes 110600 | tf_op jit(solution)/shard_map/ppermute | solution.py:453

commit v7 on v6

--- a/solution.py
+++ b/solution.py
@@ -162,23 +162,21 @@
         o[...] = gx[:, pl.ds(pl.multiple_of(jnp.minimum(info[1] ^ d, 2) * 128, 128), 128)]
 
 
-def collect_body(info, offsets, counts, m0, m1, m2, m3, x, s4, s8):
+def collect_body(info, offsets, counts, m0, m1, m2, m3, x, s3, s8):
     place = Place(info, offsets, counts)
     for slot, m in enumerate((m0, m1, m2, m3)):
         for i in range(3):
             x[i, :, slot * 32 : slot * 32 + 32, :] = m[i].reshape(8, 32, 128)
     o3, o4 = place.offs(1), place.offs(2)
     for i in (0, 1):
-        s4[i, 0:256] = pick(reader(x, i + 1), 1, o3)
-        last = pick(reader(x, i + 1), 2, o4)
-        s4[i, 256:384] = last
-        s8[i] = last
+        s3[i] = pick(reader(x, i + 1), 1, o3)
+        s8[i] = pick(reader(x, i + 1), 2, o4)
 
 
 def relay_body(s8, r4, o):
     for i in (0, 1):
         o[i] = s8[i]
-        o[2 + i] = r4[i, 256:384]
+        o[2 + i] = r4[i]
 
 
 def near_body(
@@ -215,25 +213,25 @@
     put(reader(den), writer(den), d, pair, oo, False)
 
 
-def keys3(place, x, r4):
+def keys3(place, x, r3):
     oo = place.offs(1)
-    return [oo] + [jnp.concatenate([pick(reader(x, i + 1), 1, oo), r4[i, 0:256]], axis=0) for i in (0, 1)]
+    return [oo] + [jnp.concatenate([pick(reader(x, i + 1), 1, oo), r3[i]], axis=0) for i in (0, 1)]
 
 
 def keys4(place, x, r4, r12):
     oo = place.offs(2)
     return [oo] + [
-        jnp.concatenate([pick(reader(x, i + 1), 2, oo), r4[i, 256:384], r12[2 + i], r12[i]], axis=0)
+        jnp.concatenate([pick(reader(x, i + 1), 2, oo), r4[i], r12[2 + i], r12[i]], axis=0)
         for i in (0, 1)
     ]
 
 
-def mid_body(info, offsets, counts, x, r4, top_in, num_in, den_in, top, num, den, m3, e3):
+def mid_body(info, offsets, counts, x, r3, top_in, num_in, den_in, top, num, den, m3, e3):
     place = Place(info, offsets, counts)
     top[...] = top_in[...]
     num[...] = num_in[...]
     den[...] = den_in[...]
-    oo, k2, v2 = keys3(place, x, r4)
+    oo, k2, v2 = keys3(place, x, r3)
     at = [(place.quarter ^ i) * 1024 for i in (0, 1)]
     bias = [jnp.concatenate([place.bias(256, 4, oo[h], b) for b in at], axis=1) for h in (0, 1)]
     es, t, out = attend(pick(reader(x, 0), 1, oo), k2, v2, bias)
@@ -277,7 +275,7 @@
 
 
 def far_back_body(
-    info, offsets, counts, x, r4, r12, top, norm, m3, m4, e3, e4, mx0, mx1, mx2, mx3, in0, in1, in2, in3,
+    info, offsets, counts, x, r3, r4, r12, top, norm, m3, m4, e3, e4, mx0, mx1, mx2, mx3, in0, in1, in2, in3,
     g, delta, acc, d4, d8, d12,
 ):
     place = Place(info, offsets, counts)
@@ -293,7 +291,7 @@
             prod, same, (((1,), (0,)), ((), ())), precision=lax.Precision.HIGHEST, preferred_element_type=f32
         )
         delta[:, sl, :] = sums.reshape(8, 32, 128)
-    o3, k3, v3 = keys3(place, x, r4)
+    o3, k3, v3 = keys3(place, x, r3)
     o4, k4, v4 = keys4(place, x, r4, r12)
     acc[...] = jnp.zeros_like(acc)
     for pair, oo, k2, v2, m, e, parts in (
@@ -483,13 +481,14 @@
         [((256, 768), bf16)] + [((256, 128), bf16)] * 4 + [chunk],
         [((256, 384), bf16)],
     )
-    x, s4, s8 = call(
+    x, s3, s8 = call(
         collect_body,
         places,
         [own] + got,
-        [((3, *cube), bf16), ((2, 384, 128), bf16), ((2, 128, 128), bf16)],
-    )
-    r4 = shift(s4, routes(4))
+        [((3, *cube), bf16), ((2, 256, 128), bf16), ((2, 128, 128), bf16)],
+    )
+    r4 = shift(s8, routes(4))
+    r3 = shift(s3, routes(4))
     top, num, den, m1, m2, e1, e2 = call(
         near_body,
         places,
@@ -503,7 +502,7 @@
     top, num, den, m3, e3 = call(
         mid_body,
         places,
-        [x, r4, top, num, den],
+        [x, r3, top, num, den],
         [(cube, f32)] * 3 + [((256, 128), f32), ((2, 256, 512), bf16)],
     )
     top, norm, mx0, mx1, mx2, mx3, m4, e4 = call(
@@ -526,7 +525,7 @@
     g, delta, acc, d4, d8, d12 = call(
         far_back_body,
         places,
-        [x, r4, r12, top, norm, m3, m4, e3, e4, mx0, mx1, mx2, mx3] + mixed,
+        [x, r3, r4, r12, top, norm, m3, m4, e3, e4, mx0, mx1, mx2, mx3] + mixed,
         [(cube, bf16), (cube, f32), ((3, *cube), f32)]
         + [((2, 384, 128), bf16), ((2, 128, 128), bf16), ((2, 128, 128), bf16)],
     )

time: 103 us -> 100 us (0.971)
  the two profiles are of different devices: /device:TPU:24 before, /device:TPU:1 now
where the time goes in v7:
time: 100 us; the launch traced here: 98.7 us
  starting transfers between devices  51.3 us (51%)
  Pallas kernels  25.2 us (25%)
  waiting for transfers between devices  17.6 us (18%)
  local copies, waits for them, and re-layouts  3 us (3%)
  between operations  1.49 us (1%)
    ppermute x15, starting transfers between devices, shift(): return lax.ppermute(block, ('dp', 'seq'), pairs)  27.2 us
    pallas_call x20, Pallas kernels, call(): pl.pallas_call(body, out_shape=shapes, in_specs=[smem] * len(scalars) + [...  25.2 us
    ppermute x15, waiting for transfers between devices, shift(): return lax.ppermute(block, ('dp', 'seq'), pairs)  15.2 us
    ppermute x6, starting transfers between devices, dp_step(): return lax.ppermute(block, 'dp', [(i, i ^ step) for i in range(16)])  13.9 us
    ppermute x6, starting transfers between devices, seq_step(): return lax.ppermute(block, 'seq', [(i, i ^ step) for i in range(16)])  10.2 us
    unnamed x10, local copies, waits for them, and re-layouts  3 us
    ppermute x6, waiting for transfers between devices, seq_step(): return lax.ppermute(block, 'seq', [(i, i ^ step) for i in range(16)])  2.4 us
  transfers between devices with their start and end apart: 27, of which 8 were waited for; matrix products, arithmetic and copies ran while one was open for 0% of the time, Pallas kernels for 18%

profile of v7, /device:TPU:1, one launch (start us, length us, event | category | flops | bytes accessed | tf_op | source)
XLA Modules:
  0.0 98.7 jit_solution(13010006727304018542)
XLA Ops:
  0.6 2.5 %shard_map.110 = (bf16[3,256,128]{2,1,0:T(8,128)(2,1)}, bf16[3,256,128]{2,1,0:T(8,128)(2,1)}, bf16[3,256,128]{2,1,0:T(8,128)(2,1)}, bf16[3,256,128]{2,1,0:T(8,128)(2,1)}) custom-call(bf16[256,384]{1,0:T(8,128)(2,1)} %bitcast.13, bf16[256,384]{1,0:T(8,128)(2,1)} %bitcast.14, bf16[256,384]{1,0:T(8,128)(2,1)} %bitcast.15), custom_call_target="tpu_custom_call" | custom-call | flops 1000 | bytes 1000 | tf_op jit(solution)/shard_map/pallas_call | solution.py:420
  3.2 3.7 %collective-permute-start = (bf16[3,256,128]{2,1,0:T(8,128)(2,1)}, bf16[3,256,128]{2,1,0:T(8,128)(2,1)S(1)}, u32[]{:S(2)}, u32[]{:S(2)}) collective-permute-start(bf16[3,256,128]{2,1,0:T(8,128)(2,1)} %get-tuple-element.96), channel_id=1, source_target_pairs={{0,1},{1,0},{2,3},{3,2},{4,5},{5,4},{6,7},{7,6},{8,9},{9,8},{10,11... | collective-permute-start | bytes 589832 | tf_op jit(solution)/shard_map/ppermute | solution.py:443
  6.8 1.6 %collective-permute-start.1 = (bf16[3,256,128]{2,1,0:T(8,128)(2,1)}, bf16[3,256,128]{2,1,0:T(8,128)(2,1)S(1)}, u32[]{:S(2)}, u32[]{:S(2)}) collective-permute-start(bf16[3,256,128]{2,1,0:T(8,128)(2,1)} %get-tuple-element.97), channel_id=1, source_target_pairs={{0,2},{1,3},{2,0},{3,1},{4,6},{5,7},{6,4},{7,5},{8,10},{9,11},{10,... | collective-permute-start | bytes 589832 | tf_op jit(solution)/shard_map/ppermute | solution.py:443
  8.6 1.1 %copy-done = bf16[384,768]{1,0:T(8,128)(2,1)S(1)} copy-done((bf16[384,768]{1,0:T(8,128)(2,1)S(1)}, bf16[384,768]{1,0:T(8,128)(2,1)}, u32[]{:S(2)}) %copy-start) | copy-done | bytes 589848
  9.6 1.0 %copy-done.2 = bf16[1,256,768]{2,1,0:T(8,128)(2,1)S(1)} copy-done((bf16[1,256,768]{2,1,0:T(8,128)(2,1)S(1)}, bf16[1,256,768]{2,1,0:T(8,128)(2,1)}, u32[]{:S(2)}) %copy-start.2) | copy-done | bytes 393240
  10.6 0.9 copy-done.3
  11.6 1.1 %shard_map.111 = (bf16[256,768]{1,0:T(8,128)(2,1)S(1)}, bf16[256,128]{1,0:T(8,128)(2,1)S(1)}, bf16[256,128]{1,0:T(8,128)(2,1)S(1)}, bf16[256,128]{1,0:T(8,128)(2...) custom-call(s32[3]{0:T(128)S(1)} %pad_add_fusion.info, bf16[256,768]{1,0:T(8,128)(2,1)S(1)} %bitcast.11, ...), custom_call_target="tpu_custom_call" | custom-call | flops 1000 | bytes 1000 | tf_op jit(solution)/shard_map/pallas_call | solution.py:420
  13.3 4.7 %collective-permute-done.2.m3 = bf16[3,256,128]{2,1,0:T(8,128)(2,1)S(1)} collective-permute-done((bf16[3,256,128]{2,1,0:T(8,128)(2,1)}, bf16[3,256,128]{2,1,0:T(8,128)(2,1)S(1)}, u32[]{:S(2)}, u32[]{:S(2)}) %collective-permute-start.2) | collective-permute-done | bytes 196640 | tf_op jit(solution)/shard_map/ppermute | solution.py:443
  18.0 0.7 shard_map.112
  18.7 1.9 %collective-permute-start.3 = (bf16[2,128,128]{2,1,0:T(8,128)(2,1)S(1)}, bf16[2,128,128]{2,1,0:T(8,128)(2,1)S(1)}, u32[]{:S(2)}, u32[]{:S(2)}) collective-permute-start(bf16[2,128,128]{2,1,0:T(8,128)(2,1)S(1)} %get-tuple-element.101.s8), channel_id=1, source_target_pairs={{0,4},{1,5},{2,6},{3,7},{4,0},{5,1},{6,2},{7,3},{8,12},{9,13},{10,... | collective-permute-start | bytes 196616 | tf_op jit(solution)/shard_map/ppermute | solution.py:443
  20.6 0.5 collective-permute-start.5
  21.1 3.3 %shard_map.113 = (f32[8,128,128]{2,1,0:T(8,128)S(1)}, f32[8,128,128]{2,1,0:T(8,128)S(1)}, f32[8,128,128]{2,1,0:T(8,128)S(1)}, f32[8,128,128]{2,1,0:T(8,128)S(1)}...) custom-call(s32[3]{0:T(128)S(1)} %pad_add_fusion.info, ...), custom_call_target="tpu_custom_call" | custom-call | flops 1000 | bytes 1000 | tf_op jit(solution)/shard_map/pallas_call | solution.py:420
  24.5 5.3 %collective-permute-start.4 = (bf16[4,128,128]{2,1,0:T(8,128)(2,1)S(1)}, bf16[4,128,128]{2,1,0:T(8,128)(2,1)S(1)}, u32[]{:S(2)}, u32[]{:S(2)}) collective-permute-start(bf16[4,128,128]{2,1,0:T(8,128)(2,1)S(1)} %shard_map.114), channel_id=1, source_target_pairs={{0,12},{1,13},{2,14},{3,15},{4,8},{5,9},{6,10},{7,11},{8,4},{9,5},... | collective-permute-start | bytes 393224 | tf_op jit(solution)/shard_map/ppermute | solution.py:443
  29.8 0.5 collective-permute-done.5.r3
  30.3 1.7 %shard_map.115 = (f32[8,128,128]{2,1,0:T(8,128)S(1)}, f32[8,128,128]{2,1,0:T(8,128)S(1)}, f32[8,128,128]{2,1,0:T(8,128)S(1)}, f32[256,128]{1,0:T(8,128)S(1)}, bf16[2,256,512]{2,1,0:T(8,128)(2,1)S(1)}) custom-call(s32[3]{0:T(128)S(1)} %pad_add_fusion.info, s32[3,6]{1,0:T(4,128)S(1)} %copy-done.4, s32[1]{0:T(128)S(6)} %copy.12.counts, ...), custom_call_target="tpu_custom_call" | custom-call | flops 1000 | bytes 1000 | tf_op jit(solution)/shard_map/pallas_call | solution.py:420
  32.0 3.9 %collective-permute-done.4.r12 = bf16[4,128,128]{2,1,0:T(8,128)(2,1)S(1)} collective-permute-done((bf16[4,128,128]{2,1,0:T(8,128)(2,1)S(1)}, bf16[4,128,128]{2,1,0:T(8,128)(2,1)S(1)}, u32[]{:S(2)}, u32[]{:S(2)}) %collective-permute-start.4) | collective-permute-done | bytes 131104 | tf_op jit(solution)/shard_map/ppermute | solution.py:443
  36.0 1.5 %shard_map.116 = (f32[8,128,128]{2,1,0:T(8,128)S(1)}, f32[8,128,128]{2,1,0:T(8,128)S(1)}, bf16[512,128]{1,0:T(8,128)(2,1)S(1)}, bf16[512,128]{1,0:T(8,128)(2,1)S...) custom-call(s32[3]{0:T(128)S(1)} %pad_add_fusion.info, ...), custom_call_target="tpu_custom_call" | custom-call | flops 1000 | bytes 1000 | tf_op jit(solution)/shard_map/pallas_call | solution.py:420
  37.5 1.1 %collective-permute-start.7 = (bf16[512,128]{1,0:T(8,128)(2,1)S(1)}, bf16[512,128]{1,0:T(8,128)(2,1)S(1)}, u32[]{:S(2)}, u32[]{:S(2)}) collective-permute-start(bf16[512,128]{1,0:T(8,128)(2,1)S(1)} %get-tuple-element.117.mx2), channel_id=1, source_target_pairs={{0,2},{1,3},{2,0},{3,1},{4,6},{5,7},{6,4},{7,5},{8,10},{9,11},{10,... | collective-permute-start | bytes 393224 | tf_op jit(solution)/shard_map/ppermute | solution.py:443
  38.7 3.0 %collective-permute-start.8 = (bf16[512,128]{1,0:T(8,128)(2,1)S(1)}, bf16[512,128]{1,0:T(8,128)(2,1)S(1)}, u32[]{:S(2)}, u32[]{:S(2)}) collective-permute-start(bf16[512,128]{1,0:T(8,128)(2,1)S(1)} %get-tuple-element.118.mx3), channel_id=1, source_target_pairs={{0,3},{1,2},{2,1},{3,0},{4,7},{5,6},{6,5},{7,4},{8,11},{9,10},{10,... | collective-permute-start | bytes 393224 | tf_op jit(solution)/shard_map/ppermute | solution.py:443
  41.7 1.2 %collective-permute-done.6.m1.in1 = bf16[512,128]{1,0:T(8,128)(2,1)S(1)} collective-permute-done((bf16[512,128]{1,0:T(8,128)(2,1)S(1)}, bf16[512,128]{1,0:T(8,128)(2,1)S(1)}, u32[]{:S(2)}, u32[]{:S(2)}) %collective-permute-start.6) | collective-permute-done | bytes 131104 | tf_op jit(solution)/shard_map/ppermute | solution.py:443
  42.9 2.7 %collective-permute-done.8.m3.in3 = bf16[512,128]{1,0:T(8,128)(2,1)S(1)} collective-permute-done((bf16[512,128]{1,0:T(8,128)(2,1)S(1)}, bf16[512,128]{1,0:T(8,128)(2,1)S(1)}, u32[]{:S(2)}, u32[]{:S(2)}) %collective-permute-start.8) | collective-permute-done | bytes 131104 | tf_op jit(solution)/shard_map/ppermute | solution.py:443
  45.5 1.1 %shard_map.117 = (bf16[16,72,128]{2,1,0:T(8,128)(2,1)S(1)}, f32[16,72,128]{2,1,0:T(8,128)S(1)}) custom-call(s32[3]{0:T(128)S(1)} %pad_add_fusion.info, bf16[512,128]{1,0:T(8,128)(2,1)S(1)} %get-tuple-element.121.m0.mx0.in0, bf16[512,128]{1,0:T(8,128)(2,1)S(1)} %collective-permute-done.6.m1.in1, bf16[512,128]{1,0:T(8,128)(2,1)S(1)} %collective-permute-done.7.m2.in2, ...), custom_call_target="tpu_custom_call" | custom-call | flops 1000 | bytes 1000 | tf_op jit(solution)/shard_map/pallas_call | solution.py:420
  46.6 5.9 %collective-permute-start.9 = (bf16[16,72,128]{2,1,0:T(8,128)(2,1)S(1)}, bf16[16,72,128]{2,1,0:T(8,128)(2,1)S(1)}, u32[]{:S(2)}, u32[]{:S(2)}) collective-permute-start(bf16[16,72,128]{2,1,0:T(8,128)(2,1)S(1)} %get-tuple-element.140), channel_id=1, source_target_pairs={{0,16},{16,0},{32,48},{48,32},{64,80},{80,64},{96,112},{112,96},{1... | collective-permute-start | bytes 884744 | tf_op jit(solution)/shard_map/ppermute | solution.py:447
  52.6 1.9 %shard_map.118 = bf16[256,768]{1,0:T(8,128)(2,1)} custom-call(s32[3]{0:T(128)S(1)} %pad_add_fusion.info, bf16[512,128]{1,0:T(8,128)(2,1)S(1)} %get-tuple-element.121.m0.mx0.in0, bf16[512,128]{1,0:T(8,128)(2,1)S(1)} %collective-permute-done.6.m1.in1, bf16[512,128]{1,0:T(8,128)(2,1)S(1)} %collective-permute-done.7.m2.in2, ...), custom_call_target="tpu_custom_call" | custom-call | flops 1000 | bytes 1000 | tf_op jit(solution)/shard_map/pallas_call | solution.py:420
  54.5 1.4 %collective-permute-start.10 = (bf16[288,128]{1,0:T(8,128)(2,1)S(1)}, bf16[288,128]{1,0:T(8,128)(2,1)S(1)}, u32[]{:S(2)}, u32[]{:S(2)}) collective-permute-start(bf16[288,128]{1,0:T(8,128)(2,1)S(1)} %get-tuple-element.143), channel_id=1, source_target_pairs={{0,1},{1,0},{2,3},{3,2},{4,5},{5,4},{6,7},{7,6},{8,9},{9,8},{10,11... | collective-permute-start | bytes 221192 | tf_op jit(solution)/shard_map/ppermute | solution.py:451
  56.2 2.7 %collective-permute-start.12 = (bf16[288,128]{1,0:T(8,128)(2,1)S(1)}, bf16[288,128]{1,0:T(8,128)(2,1)S(1)}, u32[]{:S(2)}, u32[]{:S(2)}) collective-permute-start(bf16[288,128]{1,0:T(8,128)(2,1)S(1)} %get-tuple-element.145), channel_id=1, source_target_pairs={{0,3},{1,2},{2,1},{3,0},{4,7},{5,6},{6,5},{7,4},{8,11},{9,10},{10,... | collective-permute-start | bytes 221192 | tf_op jit(solution)/shard_map/ppermute | solution.py:451
  58.9 2.9 %shard_map.119 = (bf16[8,128,128]{2,1,0:T(8,128)(2,1)S(1)}, f32[8,128,128]{2,1,0:T(8,128)S(1)}, f32[3,8,128,128]{3,2,1,0:T(8,128)S(1)}, bf16[2,384,128]{2,1,0:T(...) custom-call(s32[3]{0:T(128)S(1)} %pad_add_fusion.info, s32[3,6]{1,0:T(4,128)S(1)} %copy-done.4, ...), custom_call_target="tpu_custom_call" | custom-call | flops 1000 | bytes 1000 | tf_op jit(solution)/shard_map/pallas_call | solution.py:420
  61.8 0.9 collective-permute-done.12.d
  62.7 0.4 collective-permute-start.13
  63.1 2.1 %collective-permute-start.17 = (bf16[2,384,128]{2,1,0:T(8,128)(2,1)S(1)}, bf16[2,384,128]{2,1,0:T(8,128)(2,1)S(1)}, u32[]{:S(2)}, u32[]{:S(2)}) collective-permute-start(bf16[2,384,128]{2,1,0:T(8,128)(2,1)S(1)} %get-tuple-element.159), channel_id=1, source_target_pairs={{0,4},{1,5},{2,6},{3,7},{4,0},{5,1},{6,2},{7,3},{8,12},{9,13},{10,... | collective-permute-start | bytes 589832 | tf_op jit(solution)/shard_map/ppermute | solution.py:443
  65.2 2.3 %shard_map.122.acc_in = f32[3,8,128,128]{3,2,1,0:T(8,128)S(1)} custom-call(s32[3]{0:T(128)S(1)} %pad_add_fusion.info, s32[3,6]{1,0:T(4,128)S(1)} %copy-done.4, s32[1]{0:T(128)S(6)} %copy.12.counts, bf16[3,8,128,128]{3,2,1,0:T(8,128)(2,1)S(1)} %get-tuple-element.99.x, bf16[8,128,128]{2,1,0:T(8,128)(2,1)S(1)} %get-tuple-element.133.g, ...), custom_call_target="tpu_custom_call" | custom-call | flops 1000 | bytes 1000 | tf_op jit(solution)/shard_map/pallas_call | solution.py:420
  67.6 2.8 %collective-permute-start.16 = (bf16[288,128]{1,0:T(8,128)(2,1)S(1)}, bf16[288,128]{1,0:T(8,128)(2,1)S(1)}, u32[]{:S(2)}, u32[]{:S(2)}) collective-permute-start(bf16[288,128]{1,0:T(8,128)(2,1)S(1)} %shard_map.123.a), channel_id=1, source_target_pairs={{0,192},{16,208},{32,224},{48,240},{64,128},{80,144},{96,160},{112... | collective-permute-start | bytes 221192 | tf_op jit(solution)/shard_map/ppermute | solution.py:447
  70.4 0.4 collective-permute-start.15
  71.1 2.8 %collective-permute-start.18 = (bf16[2,128,128]{2,1,0:T(8,128)(2,1)S(1)}, bf16[2,128,128]{2,1,0:T(8,128)(2,1)S(1)}, u32[]{:S(2)}, u32[]{:S(2)}) collective-permute-start(bf16[2,128,128]{2,1,0:T(8,128)(2,1)S(1)} %get-tuple-element.160), channel_id=1, source_target_pairs={{0,8},{1,9},{2,10},{3,11},{4,12},{5,13},{6,14},{7,15},{8,0},{9,1},... | collective-permute-start | bytes 196616 | tf_op jit(solution)/shard_map/ppermute | solution.py:443
  73.9 0.8 collective-permute-start.19
  74.7 2.3 %shard_map.124.acc_in = f32[3,8,128,128]{3,2,1,0:T(8,128)S(1)} custom-call(s32[3]{0:T(128)S(1)} %pad_add_fusion.info, s32[3,6]{1,0:T(4,128)S(1)} %copy-done.4, s32[1]{0:T(128)S(6)} %copy.12.counts, bf16[3,8,128,128]{3,2,1,0:T(8,128)(2,1)S(1)} %get-tuple-element.99.x, bf16[8,128,128]{2,1,0:T(8,128)(2,1)S(1)} %get-tuple-element.133.g, ...), custom_call_target="tpu_custom_call" | custom-call | flops 1000 | bytes 1000 | tf_op jit(solution)/shard_map/pallas_call | solution.py:420
  77.1 4.1 %collective-permute-start.20 = (bf16[288,128]{1,0:T(8,128)(2,1)S(1)}, bf16[288,128]{1,0:T(8,128)(2,1)S(1)}, u32[]{:S(2)}, u32[]{:S(2)}) collective-permute-start(bf16[288,128]{1,0:T(8,128)(2,1)S(1)} %shard_map.125.mine), channel_id=1, source_target_pairs={{0,16},{16,0},{32,48},{48,32},{64,80},{80,64},{96,112},{112,96},{1... | collective-permute-start | bytes 221192 | tf_op jit(solution)/shard_map/ppermute | solution.py:447
  81.2 0.9 shard_map.126
  82.1 2.3 %collective-permute-start.21 = (bf16[768,128]{1,0:T(8,128)(2,1)S(1)}, bf16[768,128]{1,0:T(8,128)(2,1)S(1)}, u32[]{:S(2)}, u32[]{:S(2)}) collective-permute-start(bf16[768,128]{1,0:T(8,128)(2,1)S(1)} %get-tuple-element.168), channel_id=1, source_target_pairs={{0,1},{1,0},{2,3},{3,2},{4,5},{5,4},{6,7},{7,6},{8,9},{9,8},{10,11... | collective-permute-start | bytes 589832 | tf_op jit(solution)/shard_map/ppermute | solution.py:443
  84.4 0.7 collective-permute-start.22
  85.2 1.2 %collective-permute-start.23 = (bf16[768,128]{1,0:T(8,128)(2,1)S(1)}, bf16[768,128]{1,0:T(8,128)(2,1)S(1)}, u32[]{:S(2)}, u32[]{:S(2)}) collective-permute-start(bf16[768,128]{1,0:T(8,128)(2,1)S(1)} %get-tuple-element.170), channel_id=1, source_target_pairs={{0,3},{1,2},{2,1},{3,0},{4,7},{5,6},{6,5},{7,4},{8,11},{9,10},{10,... | collective-permute-start | bytes 589832 | tf_op jit(solution)/shard_map/ppermute | solution.py:443
  86.4 1.7 %collective-permute-start.24 = (bf16[144,128]{1,0:T(8,128)(2,1)S(1)}, bf16[144,128]{1,0:T(8,128)(2,1)S(1)}, u32[]{:S(2)}, u32[]{:S(2)}) collective-permute-start(bf16[144,128]{1,0:T(8,128)(2,1)S(1)} %get-tuple-element.180), channel_id=1, source_target_pairs={{0,4},{1,5},{2,6},{3,7},{4,0},{5,1},{6,2},{7,3},{8,12},{9,13},{10,... | collective-permute-start | bytes 110600 | tf_op jit(solution)/shard_map/ppermute | solution.py:451
  88.1 2.1 %collective-permute-start.25 = (bf16[144,128]{1,0:T(8,128)(2,1)S(1)}, bf16[144,128]{1,0:T(8,128)(2,1)S(1)}, u32[]{:S(2)}, u32[]{:S(2)}) collective-permute-start(bf16[144,128]{1,0:T(8,128)(2,1)S(1)} %get-tuple-element.181), channel_id=1, source_target_pairs={{0,8},{1,9},{2,10},{3,11},{4,12},{5,13},{6,14},{7,15},{8,0},{9,1},... | collective-permute-start | bytes 110600 | tf_op jit(solution)/shard_map/ppermute | solution.py:451
  90.1 2.0 %collective-permute-start.26 = (bf16[144,128]{1,0:T(8,128)(2,1)S(1)}, bf16[144,128]{1,0:T(8,128)(2,1)S(1)}, u32[]{:S(2)}, u32[]{:S(2)}) collective-permute-start(bf16[144,128]{1,0:T(8,128)(2,1)S(1)} %get-tuple-element.182), channel_id=1, source_target_pairs={{0,12},{1,13},{2,14},{3,15},{4,8},{5,9},{6,10},{7,11},{8,4},{9,5},... | collective-permute-start | bytes 110600 | tf_op jit(solution)/shard_map/ppermute | solution.py:451
  92.1 2.2 %collective-permute-done.23.m3 = bf16[768,128]{1,0:T(8,128)(2,1)S(1)} collective-permute-done((bf16[768,128]{1,0:T(8,128)(2,1)S(1)}, bf16[768,128]{1,0:T(8,128)(2,1)S(1)}, u32[]{:S(2)}, u32[]{:S(2)}) %collective-permute-start.23) | collective-permute-done | bytes 196640 | tf_op jit(solution)/shard_map/ppermute | solution.py:443
  94.3 1.7 %shard_map.127 = (bf16[256,384]{1,0:T(8,128)(2,1)}, bf16[256,384]{1,0:T(8,128)(2,1)}, bf16[256,384]{1,0:T(8,128)(2,1)}) custom-call(s32[3]{0:T(128)S(1)} %pad_add_fusion.info, bf16[768,128]{1,0:T(8,128)(2,1)S(1)} %get-tuple-element.167.m0, bf16[768,128]{1,0:T(8,128)(2,1)S(1)} %collective-permute-done.21.m1, bf16[768,128]{1,0:T(8,128)(2,1)S(1)} %collective-permute-done.22.m2, ...), custom_call_target="tpu_custom_call" | custom-call | flops 1000 | bytes 1000 | tf_op jit(solution)/shard_map/pallas_call | solution.py:420
  96.0 1.5 %collective-permute-done.26.c = bf16[144,128]{1,0:T(8,128)(2,1)S(1)} collective-permute-done((bf16[144,128]{1,0:T(8,128)(2,1)S(1)}, bf16[144,128]{1,0:T(8,128)(2,1)S(1)}, u32[]{:S(2)}, u32[]{:S(2)}) %collective-permute-start.26) | collective-permute-done | bytes 36896 | tf_op jit(solution)/shard_map/ppermute | solution.py:451
  97.5 1.2 %shard_map.129 = f32[24,768]{1,0:T(8,128)} custom-call(s32[3]{0:T(128)S(1)} %pad_add_fusion.info, f32[144,128]{1,0:T(8,128)S(1)} %get-tuple-element.179.own, bf16[144,128]{1,0:T(8,128)(2,1)S(1)} %collective-permute-done.24.a, bf16[144,128]{1,0:T(8,128)(2,1)S(1)} %collective-permute-done.25.b, bf16[144,128]{1,0:T(8,128)(2,1)S(1)} %collective-permute-done.26.c), custom_call_target="tpu_custom_call" | custom-call | flops 1000 | bytes 1000 | tf_op jit(solution)/shard_map/pallas_call | solution.py:420
  (37 shorter events, 1.0 us)
Async XLA Ops:
  0.6 17.4 %copy-start.4 = (s32[3,6]{1,0:T(4,128)S(1)}, s32[3,6]{1,0:T(4,128)}, u32[]{:S(2)}) copy-start(s32[3,6]{1,0:T(4,128)} %offsets.15) | copy-start | bytes 220
  3.2 10.1 %collective-permute-start = (bf16[3,256,128]{2,1,0:T(8,128)(2,1)}, bf16[3,256,128]{2,1,0:T(8,128)(2,1)S(1)}, u32[]{:S(2)}, u32[]{:S(2)}) collective-permute-start(bf16[3,256,128]{2,1,0:T(8,128)(2,1)} %get-tuple-element.96), channel_id=1, source_target_pairs={{0,1},{1,0},{2,3},{3,2},{4,5},{5,4},{6,7},{7,6},{8,9},{9,8},{10,11... | collective-permute-start | bytes 589832 | tf_op jit(solution)/shard_map/ppermute | solution.py:443
  6.8 6.5 %collective-permute-start.1 = (bf16[3,256,128]{2,1,0:T(8,128)(2,1)}, bf16[3,256,128]{2,1,0:T(8,128)(2,1)S(1)}, u32[]{:S(2)}, u32[]{:S(2)}) collective-permute-start(bf16[3,256,128]{2,1,0:T(8,128)(2,1)} %get-tuple-element.97), channel_id=1, source_target_pairs={{0,2},{1,3},{2,0},{3,1},{4,6},{5,7},{6,4},{7,5},{8,10},{9,11},{10,... | collective-permute-start | bytes 589832 | tf_op jit(solution)/shard_map/ppermute | solution.py:443
  8.5 9.5 %collective-permute-start.2 = (bf16[3,256,128]{2,1,0:T(8,128)(2,1)}, bf16[3,256,128]{2,1,0:T(8,128)(2,1)S(1)}, u32[]{:S(2)}, u32[]{:S(2)}) collective-permute-start(bf16[3,256,128]{2,1,0:T(8,128)(2,1)} %get-tuple-element.98), channel_id=1, source_target_pairs={{0,3},{1,2},{2,1},{3,0},{4,7},{5,6},{6,5},{7,4},{8,11},{9,10},{10,... | collective-permute-start | bytes 589832 | tf_op jit(solution)/shard_map/ppermute | solution.py:443
  8.6 1.1 %copy-start = (bf16[384,768]{1,0:T(8,128)(2,1)S(1)}, bf16[384,768]{1,0:T(8,128)(2,1)}, u32[]{:S(2)}) copy-start(bf16[384,768]{1,0:T(8,128)(2,1)} %w.3) | copy-start | bytes 1769476
  9.6 1.0 %copy-start.2 = (bf16[1,256,768]{2,1,0:T(8,128)(2,1)S(1)}, bf16[1,256,768]{2,1,0:T(8,128)(2,1)}, u32[]{:S(2)}) copy-start(bf16[1,256,768]{2,1,0:T(8,128)(2,1)} %param.11) | copy-start | bytes 1179652
  10.6 0.9 copy-start.3
  18.7 5.8 %collective-permute-start.3 = (bf16[2,128,128]{2,1,0:T(8,128)(2,1)S(1)}, bf16[2,128,128]{2,1,0:T(8,128)(2,1)S(1)}, u32[]{:S(2)}, u32[]{:S(2)}) collective-permute-start(bf16[2,128,128]{2,1,0:T(8,128)(2,1)S(1)} %get-tuple-element.101.s8), channel_id=1, source_target_pairs={{0,4},{1,5},{2,6},{3,7},{4,0},{5,1},{6,2},{7,3},{8,12},{9,13},{10,... | collective-permute-start | bytes 196616 | tf_op jit(solution)/shard_map/ppermute | solution.py:443
  20.6 9.7 %collective-permute-start.5 = (bf16[2,256,128]{2,1,0:T(8,128)(2,1)S(1)}, bf16[2,256,128]{2,1,0:T(8,128)(2,1)S(1)}, u32[]{:S(2)}, u32[]{:S(2)}) collective-permute-start(bf16[2,256,128]{2,1,0:T(8,128)(2,1)S(1)} %get-tuple-element.103), channel_id=1, source_target_pairs={{0,4},{1,5},{2,6},{3,7},{4,0},{5,1},{6,2},{7,3},{8,12},{9,13},{10,... | collective-permute-start | bytes 393224 | tf_op jit(solution)/shard_map/ppermute | solution.py:443
  24.5 11.5 %collective-permute-start.4 = (bf16[4,128,128]{2,1,0:T(8,128)(2,1)S(1)}, bf16[4,128,128]{2,1,0:T(8,128)(2,1)S(1)}, u32[]{:S(2)}, u32[]{:S(2)}) collective-permute-start(bf16[4,128,128]{2,1,0:T(8,128)(2,1)S(1)} %shard_map.114), channel_id=1, source_target_pairs={{0,12},{1,13},{2,14},{3,15},{4,8},{5,9},{6,10},{7,11},{8,4},{9,5},... | collective-permute-start | bytes 393224 | tf_op jit(solution)/shard_map/ppermute | solution.py:443
  36.0 16.6 %copy-start.1 = (bf16[384,768]{1,0:T(8,128)(2,1)S(1)}, bf16[384,768]{1,0:T(8,128)(2,1)}, u32[]{:S(2)}) copy-start(bf16[384,768]{1,0:T(8,128)(2,1)} %w.3) | copy-start | bytes 1769476
  37.4 5.4 %collective-permute-start.6 = (bf16[512,128]{1,0:T(8,128)(2,1)S(1)}, bf16[512,128]{1,0:T(8,128)(2,1)S(1)}, u32[]{:S(2)}, u32[]{:S(2)}) collective-permute-start(bf16[512,128]{1,0:T(8,128)(2,1)S(1)} %get-tuple-element.116.mx1), channel_id=1, source_target_pairs={{0,1},{1,0},{2,3},{3,2},{4,5},{5,4},{6,7},{7,6},{8,9},{9,8},{10,11... | collective-permute-start | bytes 393224 | tf_op jit(solution)/shard_map/ppermute | solution.py:443
  37.5 5.3 %collective-permute-start.7 = (bf16[512,128]{1,0:T(8,128)(2,1)S(1)}, bf16[512,128]{1,0:T(8,128)(2,1)S(1)}, u32[]{:S(2)}, u32[]{:S(2)}) collective-permute-start(bf16[512,128]{1,0:T(8,128)(2,1)S(1)} %get-tuple-element.117.mx2), channel_id=1, source_target_pairs={{0,2},{1,3},{2,0},{3,1},{4,6},{5,7},{6,4},{7,5},{8,10},{9,11},{10,... | collective-permute-start | bytes 393224 | tf_op jit(solution)/shard_map/ppermute | solution.py:443
  38.7 6.9 %collective-permute-start.8 = (bf16[512,128]{1,0:T(8,128)(2,1)S(1)}, bf16[512,128]{1,0:T(8,128)(2,1)S(1)}, u32[]{:S(2)}, u32[]{:S(2)}) collective-permute-start(bf16[512,128]{1,0:T(8,128)(2,1)S(1)} %get-tuple-element.118.mx3), channel_id=1, source_target_pairs={{0,3},{1,2},{2,1},{3,0},{4,7},{5,6},{6,5},{7,4},{8,11},{9,10},{10,... | collective-permute-start | bytes 393224 | tf_op jit(solution)/shard_map/ppermute | solution.py:443
  46.6 7.8 %collective-permute-start.9 = (bf16[16,72,128]{2,1,0:T(8,128)(2,1)S(1)}, bf16[16,72,128]{2,1,0:T(8,128)(2,1)S(1)}, u32[]{:S(2)}, u32[]{:S(2)}) collective-permute-start(bf16[16,72,128]{2,1,0:T(8,128)(2,1)S(1)} %get-tuple-element.140), channel_id=1, source_target_pairs={{0,16},{16,0},{32,48},{48,32},{64,80},{80,64},{96,112},{112,96},{1... | collective-permute-start | bytes 884744 | tf_op jit(solution)/shard_map/ppermute | solution.py:447
  54.5 7.3 %collective-permute-start.10 = (bf16[288,128]{1,0:T(8,128)(2,1)S(1)}, bf16[288,128]{1,0:T(8,128)(2,1)S(1)}, u32[]{:S(2)}, u32[]{:S(2)}) collective-permute-start(bf16[288,128]{1,0:T(8,128)(2,1)S(1)} %get-tuple-element.143), channel_id=1, source_target_pairs={{0,1},{1,0},{2,3},{3,2},{4,5},{5,4},{6,7},{7,6},{8,9},{9,8},{10,11... | collective-permute-start | bytes 221192 | tf_op jit(solution)/shard_map/ppermute | solution.py:451
  55.9 5.9 %collective-permute-start.11 = (bf16[288,128]{1,0:T(8,128)(2,1)S(1)}, bf16[288,128]{1,0:T(8,128)(2,1)S(1)}, u32[]{:S(2)}, u32[]{:S(2)}) collective-permute-start(bf16[288,128]{1,0:T(8,128)(2,1)S(1)} %get-tuple-element.144), channel_id=1, source_target_pairs={{0,2},{1,3},{2,0},{3,1},{4,6},{5,7},{6,4},{7,5},{8,10},{9,11},{10,... | collective-permute-start | bytes 221192 | tf_op jit(solution)/shard_map/ppermute | solution.py:451
  56.2 6.5 %collective-permute-start.12 = (bf16[288,128]{1,0:T(8,128)(2,1)S(1)}, bf16[288,128]{1,0:T(8,128)(2,1)S(1)}, u32[]{:S(2)}, u32[]{:S(2)}) collective-permute-start(bf16[288,128]{1,0:T(8,128)(2,1)S(1)} %get-tuple-element.145), channel_id=1, source_target_pairs={{0,3},{1,2},{2,1},{3,0},{4,7},{5,6},{6,5},{7,4},{8,11},{9,10},{10,... | collective-permute-start | bytes 221192 | tf_op jit(solution)/shard_map/ppermute | solution.py:451
  62.7 4.8 %collective-permute-start.13 = (bf16[288,128]{1,0:T(8,128)(2,1)S(1)}, bf16[288,128]{1,0:T(8,128)(2,1)S(1)}, u32[]{:S(2)}, u32[]{:S(2)}) collective-permute-start(bf16[288,128]{1,0:T(8,128)(2,1)S(1)} %shard_map.121.a), channel_id=1, source_target_pairs={{0,32},{16,48},{32,0},{48,16},{64,96},{80,112},{96,64},{112,80},{1... | collective-permute-start | bytes 221192 | tf_op jit(solution)/shard_map/ppermute | solution.py:447
  63.1 18.1 %collective-permute-start.17 = (bf16[2,384,128]{2,1,0:T(8,128)(2,1)S(1)}, bf16[2,384,128]{2,1,0:T(8,128)(2,1)S(1)}, u32[]{:S(2)}, u32[]{:S(2)}) collective-permute-start(bf16[2,384,128]{2,1,0:T(8,128)(2,1)S(1)} %get-tuple-element.159), channel_id=1, source_target_pairs={{0,4},{1,5},{2,6},{3,7},{4,0},{5,1},{6,2},{7,3},{8,12},{9,13},{10,... | collective-permute-start | bytes 589832 | tf_op jit(solution)/shard_map/ppermute | solution.py:443
  67.6 6.3 %collective-permute-start.16 = (bf16[288,128]{1,0:T(8,128)(2,1)S(1)}, bf16[288,128]{1,0:T(8,128)(2,1)S(1)}, u32[]{:S(2)}, u32[]{:S(2)}) collective-permute-start(bf16[288,128]{1,0:T(8,128)(2,1)S(1)} %shard_map.123.a), channel_id=1, source_target_pairs={{0,192},{16,208},{32,224},{48,240},{64,128},{80,144},{96,160},{112... | collective-permute-start | bytes 221192 | tf_op jit(solution)/shard_map/ppermute | solution.py:447
  70.4 6.6 %collective-permute-start.15 = (bf16[288,128]{1,0:T(8,128)(2,1)S(1)}, bf16[288,128]{1,0:T(8,128)(2,1)S(1)}, u32[]{:S(2)}, u32[]{:S(2)}) collective-permute-start(bf16[288,128]{1,0:T(8,128)(2,1)S(1)} %shard_map.123.a), channel_id=1, source_target_pairs={{0,128},{16,144},{32,160},{48,176},{64,192},{80,208},{96,224},{112... | collective-permute-start | bytes 221192 | tf_op jit(solution)/shard_map/ppermute | solution.py:447
  70.8 6.3 %collective-permute-start.14 = (bf16[288,128]{1,0:T(8,128)(2,1)S(1)}, bf16[288,128]{1,0:T(8,128)(2,1)S(1)}, u32[]{:S(2)}, u32[]{:S(2)}) collective-permute-start(bf16[288,128]{1,0:T(8,128)(2,1)S(1)} %shard_map.123.a), channel_id=1, source_target_pairs={{0,64},{16,80},{32,96},{48,112},{64,0},{80,16},{96,32},{112,48},{1... | collective-permute-start | bytes 221192 | tf_op jit(solution)/shard_map/ppermute | solution.py:447
  71.1 10.1 %collective-permute-start.18 = (bf16[2,128,128]{2,1,0:T(8,128)(2,1)S(1)}, bf16[2,128,128]{2,1,0:T(8,128)(2,1)S(1)}, u32[]{:S(2)}, u32[]{:S(2)}) collective-permute-start(bf16[2,128,128]{2,1,0:T(8,128)(2,1)S(1)} %get-tuple-element.160), channel_id=1, source_target_pairs={{0,8},{1,9},{2,10},{3,11},{4,12},{5,13},{6,14},{7,15},{8,0},{9,1},... | collective-permute-start | bytes 196616 | tf_op jit(solution)/shard_map/ppermute | solution.py:443
  73.9 7.3 %collective-permute-start.19 = (bf16[2,128,128]{2,1,0:T(8,128)(2,1)S(1)}, bf16[2,128,128]{2,1,0:T(8,128)(2,1)S(1)}, u32[]{:S(2)}, u32[]{:S(2)}) collective-permute-start(bf16[2,128,128]{2,1,0:T(8,128)(2,1)S(1)} %get-tuple-element.161), channel_id=1, source_target_pairs={{0,12},{1,13},{2,14},{3,15},{4,8},{5,9},{6,10},{7,11},{8,4},{9,5},... | collective-permute-start | bytes 196616 | tf_op jit(solution)/shard_map/ppermute | solution.py:443
  77.1 5.0 %collective-permute-start.20 = (bf16[288,128]{1,0:T(8,128)(2,1)S(1)}, bf16[288,128]{1,0:T(8,128)(2,1)S(1)}, u32[]{:S(2)}, u32[]{:S(2)}) collective-permute-start(bf16[288,128]{1,0:T(8,128)(2,1)S(1)} %shard_map.125.mine), channel_id=1, source_target_pairs={{0,16},{16,0},{32,48},{48,32},{64,80},{80,64},{96,112},{112,96},{1... | collective-permute-start | bytes 221192 | tf_op jit(solution)/shard_map/ppermute | solution.py:447
  82.1 8.0 %collective-permute-start.21 = (bf16[768,128]{1,0:T(8,128)(2,1)S(1)}, bf16[768,128]{1,0:T(8,128)(2,1)S(1)}, u32[]{:S(2)}, u32[]{:S(2)}) collective-permute-start(bf16[768,128]{1,0:T(8,128)(2,1)S(1)} %get-tuple-element.168), channel_id=1, source_target_pairs={{0,1},{1,0},{2,3},{3,2},{4,5},{5,4},{6,7},{7,6},{8,9},{9,8},{10,11... | collective-permute-start | bytes 589832 | tf_op jit(solution)/shard_map/ppermute | solution.py:443
  84.4 7.7 %collective-permute-start.22 = (bf16[768,128]{1,0:T(8,128)(2,1)S(1)}, bf16[768,128]{1,0:T(8,128)(2,1)S(1)}, u32[]{:S(2)}, u32[]{:S(2)}) collective-permute-start(bf16[768,128]{1,0:T(8,128)(2,1)S(1)} %get-tuple-element.169), channel_id=1, source_target_pairs={{0,2},{1,3},{2,0},{3,1},{4,6},{5,7},{6,4},{7,5},{8,10},{9,11},{10,... | collective-permute-start | bytes 589832 | tf_op jit(solution)/shard_map/ppermute | solution.py:443
  85.2 9.2 %collective-permute-start.23 = (bf16[768,128]{1,0:T(8,128)(2,1)S(1)}, bf16[768,128]{1,0:T(8,128)(2,1)S(1)}, u32[]{:S(2)}, u32[]{:S(2)}) collective-permute-start(bf16[768,128]{1,0:T(8,128)(2,1)S(1)} %get-tuple-element.170), channel_id=1, source_target_pairs={{0,3},{1,2},{2,1},{3,0},{4,7},{5,6},{6,5},{7,4},{8,11},{9,10},{10,... | collective-permute-start | bytes 589832 | tf_op jit(solution)/shard_map/ppermute | solution.py:443
  86.4 9.7 %collective-permute-start.24 = (bf16[144,128]{1,0:T(8,128)(2,1)S(1)}, bf16[144,128]{1,0:T(8,128)(2,1)S(1)}, u32[]{:S(2)}, u32[]{:S(2)}) collective-permute-start(bf16[144,128]{1,0:T(8,128)(2,1)S(1)} %get-tuple-element.180), channel_id=1, source_target_pairs={{0,4},{1,5},{2,6},{3,7},{4,0},{5,1},{6,2},{7,3},{8,12},{9,13},{10,... | collective-permute-start | bytes 110600 | tf_op jit(solution)/shard_map/ppermute | solution.py:451
  88.1 8.0 %collective-permute-start.25 = (bf16[144,128]{1,0:T(8,128)(2,1)S(1)}, bf16[144,128]{1,0:T(8,128)(2,1)S(1)}, u32[]{:S(2)}, u32[]{:S(2)}) collective-permute-start(bf16[144,128]{1,0:T(8,128)(2,1)S(1)} %get-tuple-element.181), channel_id=1, source_target_pairs={{0,8},{1,9},{2,10},{3,11},{4,12},{5,13},{6,14},{7,15},{8,0},{9,1},... | collective-permute-start | bytes 110600 | tf_op jit(solution)/shard_map/ppermute | solution.py:451
  90.1 7.4 %collective-permute-start.26 = (bf16[144,128]{1,0:T(8,128)(2,1)S(1)}, bf16[144,128]{1,0:T(8,128)(2,1)S(1)}, u32[]{:S(2)}, u32[]{:S(2)}) collective-permute-start(bf16[144,128]{1,0:T(8,128)(2,1)S(1)} %get-tuple-element.182), channel_id=1, source_target_pairs={{0,12},{1,13},{2,14},{3,15},{4,8},{5,9},{6,10},{7,11},{8,4},{9,5},... | collective-permute-start | bytes 110600 | tf_op jit(solution)/shard_map/ppermute | solution.py:451

commit v8 on v7

--- a/solution.py
+++ b/solution.py
@@ -281,15 +281,15 @@
     place = Place(info, offsets, counts)
     ri = lax.broadcasted_iota(jnp.int32, (128, 128), 0) >> 6
     ci = lax.broadcasted_iota(jnp.int32, (128, 128), 1) >> 6
-    same = jnp.where(ri == ci, 1.0, 0.0)
+    same = jnp.where(ri == ci, 1.0, 0.0).astype(bf16)
     for slot, (mx, got) in enumerate(((mx0, in0), (mx1, in1), (mx2, in2), (mx3, in3))):
         sl = slice(slot * 32, slot * 32 + 32)
         rows = got[256:512]
         g[:, sl, :] = rows.reshape(8, 32, 128)
         prod = rows.astype(f32) * mx[0:256].astype(f32)
-        sums = lax.dot_general(
-            prod, same, (((1,), (0,)), ((), ())), precision=lax.Precision.HIGHEST, preferred_element_type=f32
-        )
+        high = prod.astype(bf16)
+        rest = (prod - high.astype(f32)).astype(bf16)
+        sums = dot_nn(jnp.concatenate([high, rest], axis=1), jnp.concatenate([same, same], axis=0))
         delta[:, sl, :] = sums.reshape(8, 32, 128)
     o3, k3, v3 = keys3(place, x, r3)
     o4, k4, v4 = keys4(place, x, r4, r12)
@@ -538,7 +538,8 @@
     own, s1, s2, s3 = call(cores_body, [], [keep, arrived], [((288, 128), f32)] + [flat] * 3)
     near = [seq_step(b, d) for d, b in ((1, s1), (2, s2), (3, s3))]
     d4, d8, d12, own = lax.optimization_barrier((d4, d8, d12, own))
-    far = [shift(b, routes(d)) for d, b in ((4, d4), (8, d8), (12, d12))]
+    far = [shift(b, routes(d)) for d, b in ((8, d8), (12, d12), (4, d4))]
+    far = [far[2], far[0], far[1]]
     (low,) = call(sum_body, [], [own] + near, [flat])
     acc, low = lax.optimization_barrier((acc, low))
     arrived = dp_step(low, 2)

time: 100 us -> 100 us (level)
  no operation moved by 1% of the time
where the time goes in v8:
time: 100 us; the launch traced here: 98.7 us
  starting transfers between devices  51.4 us (51%)
  Pallas kernels  24.8 us (25%)
  waiting for transfers between devices  17.9 us (18%)
  local copies, waits for them, and re-layouts  3 us (3%)
  between operations  1.51 us (2%)
    ppermute x15, starting transfers between devices, shift(): return lax.ppermute(block, ('dp', 'seq'), pairs)  27.2 us
    pallas_call x20, Pallas kernels, call(): pl.pallas_call(body, out_shape=shapes, in_specs=[smem] * len(scalars) + [...  24.8 us
    ppermute x15, waiting for transfers between devices, shift(): return lax.ppermute(block, ('dp', 'seq'), pairs)  15.1 us
    ppermute x6, starting transfers between devices, dp_step(): return lax.ppermute(block, 'dp', [(i, i ^ step) for i in range(16)])  14 us
    ppermute x6, starting transfers between devices, seq_step(): return lax.ppermute(block, 'seq', [(i, i ^ step) for i in range(16)])  10.2 us
    unnamed x10, local copies, waits for them, and re-layouts  3 us
    ppermute x6, waiting for transfers between devices, seq_step(): return lax.ppermute(block, 'seq', [(i, i ^ step) for i in range(16)])  2.78 us
  transfers between devices with their start and end apart: 27, of which 8 were waited for; matrix products, arithmetic and copies ran while one was open for 0% of the time, Pallas kernels for 18%

profile of v8, /device:TPU:1, one launch (start us, length us, event | category | flops | bytes accessed | tf_op | source)
XLA Modules:
  0.0 98.7 jit_solution(8559498115480027701)
XLA Ops:
  0.6 2.5 %shard_map.110 = (bf16[3,256,128]{2,1,0:T(8,128)(2,1)}, bf16[3,256,128]{2,1,0:T(8,128)(2,1)}, bf16[3,256,128]{2,1,0:T(8,128)(2,1)}, bf16[3,256,128]{2,1,0:T(8,128)(2,1)}) custom-call(bf16[256,384]{1,0:T(8,128)(2,1)} %bitcast.13, bf16[256,384]{1,0:T(8,128)(2,1)} %bitcast.14, bf16[256,384]{1,0:T(8,128)(2,1)} %bitcast.15), custom_call_target="tpu_custom_call" | custom-call | flops 1000 | bytes 1000 | tf_op jit(solution)/shard_map/pallas_call | solution.py:420
  3.2 3.7 %collective-permute-start = (bf16[3,256,128]{2,1,0:T(8,128)(2,1)}, bf16[3,256,128]{2,1,0:T(8,128)(2,1)S(1)}, u32[]{:S(2)}, u32[]{:S(2)}) collective-permute-start(bf16[3,256,128]{2,1,0:T(8,128)(2,1)} %get-tuple-element.96), channel_id=1, source_target_pairs={{0,1},{1,0},{2,3},{3,2},{4,5},{5,4},{6,7},{7,6},{8,9},{9,8},{10,11... | collective-permute-start | bytes 589832 | tf_op jit(solution)/shard_map/ppermute | solution.py:443
  6.8 1.6 %collective-permute-start.1 = (bf16[3,256,128]{2,1,0:T(8,128)(2,1)}, bf16[3,256,128]{2,1,0:T(8,128)(2,1)S(1)}, u32[]{:S(2)}, u32[]{:S(2)}) collective-permute-start(bf16[3,256,128]{2,1,0:T(8,128)(2,1)} %get-tuple-element.97), channel_id=1, source_target_pairs={{0,2},{1,3},{2,0},{3,1},{4,6},{5,7},{6,4},{7,5},{8,10},{9,11},{10,... | collective-permute-start | bytes 589832 | tf_op jit(solution)/shard_map/ppermute | solution.py:443
  8.6 1.1 %copy-done = bf16[384,768]{1,0:T(8,128)(2,1)S(1)} copy-done((bf16[384,768]{1,0:T(8,128)(2,1)S(1)}, bf16[384,768]{1,0:T(8,128)(2,1)}, u32[]{:S(2)}) %copy-start) | copy-done | bytes 589848
  9.6 1.0 %copy-done.2 = bf16[1,256,768]{2,1,0:T(8,128)(2,1)S(1)} copy-done((bf16[1,256,768]{2,1,0:T(8,128)(2,1)S(1)}, bf16[1,256,768]{2,1,0:T(8,128)(2,1)}, u32[]{:S(2)}) %copy-start.2) | copy-done | bytes 393240
  10.6 0.9 copy-done.3
  11.6 1.1 %shard_map.111 = (bf16[256,768]{1,0:T(8,128)(2,1)S(1)}, bf16[256,128]{1,0:T(8,128)(2,1)S(1)}, bf16[256,128]{1,0:T(8,128)(2,1)S(1)}, bf16[256,128]{1,0:T(8,128)(2...) custom-call(s32[3]{0:T(128)S(1)} %pad_add_fusion.info, bf16[256,768]{1,0:T(8,128)(2,1)S(1)} %bitcast.11, ...), custom_call_target="tpu_custom_call" | custom-call | flops 1000 | bytes 1000 | tf_op jit(solution)/shard_map/pallas_call | solution.py:420
  13.3 4.7 %collective-permute-done.2.m3 = bf16[3,256,128]{2,1,0:T(8,128)(2,1)S(1)} collective-permute-done((bf16[3,256,128]{2,1,0:T(8,128)(2,1)}, bf16[3,256,128]{2,1,0:T(8,128)(2,1)S(1)}, u32[]{:S(2)}, u32[]{:S(2)}) %collective-permute-start.2) | collective-permute-done | bytes 196640 | tf_op jit(solution)/shard_map/ppermute | solution.py:443
  18.0 0.7 shard_map.112
  18.7 1.9 %collective-permute-start.3 = (bf16[2,128,128]{2,1,0:T(8,128)(2,1)S(1)}, bf16[2,128,128]{2,1,0:T(8,128)(2,1)S(1)}, u32[]{:S(2)}, u32[]{:S(2)}) collective-permute-start(bf16[2,128,128]{2,1,0:T(8,128)(2,1)S(1)} %get-tuple-element.101.s8), channel_id=1, source_target_pairs={{0,4},{1,5},{2,6},{3,7},{4,0},{5,1},{6,2},{7,3},{8,12},{9,13},{10,... | collective-permute-start | bytes 196616 | tf_op jit(solution)/shard_map/ppermute | solution.py:443
  20.6 0.5 collective-permute-start.5
  21.1 3.3 %shard_map.113 = (f32[8,128,128]{2,1,0:T(8,128)S(1)}, f32[8,128,128]{2,1,0:T(8,128)S(1)}, f32[8,128,128]{2,1,0:T(8,128)S(1)}, f32[8,128,128]{2,1,0:T(8,128)S(1)}...) custom-call(s32[3]{0:T(128)S(1)} %pad_add_fusion.info, ...), custom_call_target="tpu_custom_call" | custom-call | flops 1000 | bytes 1000 | tf_op jit(solution)/shard_map/pallas_call | solution.py:420
  24.4 5.3 %collective-permute-start.4 = (bf16[4,128,128]{2,1,0:T(8,128)(2,1)S(1)}, bf16[4,128,128]{2,1,0:T(8,128)(2,1)S(1)}, u32[]{:S(2)}, u32[]{:S(2)}) collective-permute-start(bf16[4,128,128]{2,1,0:T(8,128)(2,1)S(1)} %shard_map.114), channel_id=1, source_target_pairs={{0,12},{1,13},{2,14},{3,15},{4,8},{5,9},{6,10},{7,11},{8,4},{9,5},... | collective-permute-start | bytes 393224 | tf_op jit(solution)/shard_map/ppermute | solution.py:443
  29.7 0.6 collective-permute-done.5.r3
  30.3 1.7 %shard_map.115 = (f32[8,128,128]{2,1,0:T(8,128)S(1)}, f32[8,128,128]{2,1,0:T(8,128)S(1)}, f32[8,128,128]{2,1,0:T(8,128)S(1)}, f32[256,128]{1,0:T(8,128)S(1)}, bf16[2,256,512]{2,1,0:T(8,128)(2,1)S(1)}) custom-call(s32[3]{0:T(128)S(1)} %pad_add_fusion.info, s32[3,6]{1,0:T(4,128)S(1)} %copy-done.4, s32[1]{0:T(128)S(6)} %copy.12.counts, ...), custom_call_target="tpu_custom_call" | custom-call | flops 1000 | bytes 1000 | tf_op jit(solution)/shard_map/pallas_call | solution.py:420
  32.0 3.8 %collective-permute-done.4.r12 = bf16[4,128,128]{2,1,0:T(8,128)(2,1)S(1)} collective-permute-done((bf16[4,128,128]{2,1,0:T(8,128)(2,1)S(1)}, bf16[4,128,128]{2,1,0:T(8,128)(2,1)S(1)}, u32[]{:S(2)}, u32[]{:S(2)}) %collective-permute-start.4) | collective-permute-done | bytes 131104 | tf_op jit(solution)/shard_map/ppermute | solution.py:443
  35.9 1.5 %shard_map.116 = (f32[8,128,128]{2,1,0:T(8,128)S(1)}, f32[8,128,128]{2,1,0:T(8,128)S(1)}, bf16[512,128]{1,0:T(8,128)(2,1)S(1)}, bf16[512,128]{1,0:T(8,128)(2,1)S...) custom-call(s32[3]{0:T(128)S(1)} %pad_add_fusion.info, ...), custom_call_target="tpu_custom_call" | custom-call | flops 1000 | bytes 1000 | tf_op jit(solution)/shard_map/pallas_call | solution.py:420
  37.4 1.2 %collective-permute-start.7 = (bf16[512,128]{1,0:T(8,128)(2,1)S(1)}, bf16[512,128]{1,0:T(8,128)(2,1)S(1)}, u32[]{:S(2)}, u32[]{:S(2)}) collective-permute-start(bf16[512,128]{1,0:T(8,128)(2,1)S(1)} %get-tuple-element.117.mx2), channel_id=1, source_target_pairs={{0,2},{1,3},{2,0},{3,1},{4,6},{5,7},{6,4},{7,5},{8,10},{9,11},{10,... | collective-permute-start | bytes 393224 | tf_op jit(solution)/shard_map/ppermute | solution.py:443
  38.7 2.9 %collective-permute-start.8 = (bf16[512,128]{1,0:T(8,128)(2,1)S(1)}, bf16[512,128]{1,0:T(8,128)(2,1)S(1)}, u32[]{:S(2)}, u32[]{:S(2)}) collective-permute-start(bf16[512,128]{1,0:T(8,128)(2,1)S(1)} %get-tuple-element.118.mx3), channel_id=1, source_target_pairs={{0,3},{1,2},{2,1},{3,0},{4,7},{5,6},{6,5},{7,4},{8,11},{9,10},{10,... | collective-permute-start | bytes 393224 | tf_op jit(solution)/shard_map/ppermute | solution.py:443
  41.6 1.2 %collective-permute-done.6.m1.in1 = bf16[512,128]{1,0:T(8,128)(2,1)S(1)} collective-permute-done((bf16[512,128]{1,0:T(8,128)(2,1)S(1)}, bf16[512,128]{1,0:T(8,128)(2,1)S(1)}, u32[]{:S(2)}, u32[]{:S(2)}) %collective-permute-start.6) | collective-permute-done | bytes 131104 | tf_op jit(solution)/shard_map/ppermute | solution.py:443
  42.8 2.7 %collective-permute-done.8.m3.in3 = bf16[512,128]{1,0:T(8,128)(2,1)S(1)} collective-permute-done((bf16[512,128]{1,0:T(8,128)(2,1)S(1)}, bf16[512,128]{1,0:T(8,128)(2,1)S(1)}, u32[]{:S(2)}, u32[]{:S(2)}) %collective-permute-start.8) | collective-permute-done | bytes 131104 | tf_op jit(solution)/shard_map/ppermute | solution.py:443
  45.4 1.1 %shard_map.117 = (bf16[16,72,128]{2,1,0:T(8,128)(2,1)S(1)}, f32[16,72,128]{2,1,0:T(8,128)S(1)}) custom-call(s32[3]{0:T(128)S(1)} %pad_add_fusion.info, bf16[512,128]{1,0:T(8,128)(2,1)S(1)} %get-tuple-element.121.m0.mx0.in0, bf16[512,128]{1,0:T(8,128)(2,1)S(1)} %collective-permute-done.6.m1.in1, bf16[512,128]{1,0:T(8,128)(2,1)S(1)} %collective-permute-done.7.m2.in2, ...), custom_call_target="tpu_custom_call" | custom-call | flops 1000 | bytes 1000 | tf_op jit(solution)/shard_map/pallas_call | solution.py:420
  46.5 6.0 %collective-permute-start.9 = (bf16[16,72,128]{2,1,0:T(8,128)(2,1)S(1)}, bf16[16,72,128]{2,1,0:T(8,128)(2,1)S(1)}, u32[]{:S(2)}, u32[]{:S(2)}) collective-permute-start(bf16[16,72,128]{2,1,0:T(8,128)(2,1)S(1)} %get-tuple-element.140), channel_id=1, source_target_pairs={{0,16},{16,0},{32,48},{48,32},{64,80},{80,64},{96,112},{112,96},{1... | collective-permute-start | bytes 884744 | tf_op jit(solution)/shard_map/ppermute | solution.py:447
  52.6 1.9 %shard_map.118 = bf16[256,768]{1,0:T(8,128)(2,1)} custom-call(s32[3]{0:T(128)S(1)} %pad_add_fusion.info, bf16[512,128]{1,0:T(8,128)(2,1)S(1)} %get-tuple-element.121.m0.mx0.in0, bf16[512,128]{1,0:T(8,128)(2,1)S(1)} %collective-permute-done.6.m1.in1, bf16[512,128]{1,0:T(8,128)(2,1)S(1)} %collective-permute-done.7.m2.in2, ...), custom_call_target="tpu_custom_call" | custom-call | flops 1000 | bytes 1000 | tf_op jit(solution)/shard_map/pallas_call | solution.py:420
  54.5 1.4 %collective-permute-start.10 = (bf16[288,128]{1,0:T(8,128)(2,1)S(1)}, bf16[288,128]{1,0:T(8,128)(2,1)S(1)}, u32[]{:S(2)}, u32[]{:S(2)}) collective-permute-start(bf16[288,128]{1,0:T(8,128)(2,1)S(1)} %get-tuple-element.143), channel_id=1, source_target_pairs={{0,1},{1,0},{2,3},{3,2},{4,5},{5,4},{6,7},{7,6},{8,9},{9,8},{10,11... | collective-permute-start | bytes 221192 | tf_op jit(solution)/shard_map/ppermute | solution.py:451
  56.2 2.8 %collective-permute-start.12 = (bf16[288,128]{1,0:T(8,128)(2,1)S(1)}, bf16[288,128]{1,0:T(8,128)(2,1)S(1)}, u32[]{:S(2)}, u32[]{:S(2)}) collective-permute-start(bf16[288,128]{1,0:T(8,128)(2,1)S(1)} %get-tuple-element.145), channel_id=1, source_target_pairs={{0,3},{1,2},{2,1},{3,0},{4,7},{5,6},{6,5},{7,4},{8,11},{9,10},{10,... | collective-permute-start | bytes 221192 | tf_op jit(solution)/shard_map/ppermute | solution.py:451
  58.9 2.5 %shard_map.119 = (bf16[8,128,128]{2,1,0:T(8,128)(2,1)S(1)}, f32[8,128,128]{2,1,0:T(8,128)S(1)}, f32[3,8,128,128]{3,2,1,0:T(8,128)S(1)}, bf16[2,384,128]{2,1,0:T(...) custom-call(s32[3]{0:T(128)S(1)} %pad_add_fusion.info, s32[3,6]{1,0:T(4,128)S(1)} %copy-done.4, ...), custom_call_target="tpu_custom_call" | custom-call | flops 1000 | bytes 1000 | tf_op jit(solution)/shard_map/pallas_call | solution.py:420
  61.4 1.3 %collective-permute-done.12.d = bf16[288,128]{1,0:T(8,128)(2,1)S(1)} collective-permute-done((bf16[288,128]{1,0:T(8,128)(2,1)S(1)}, bf16[288,128]{1,0:T(8,128)(2,1)S(1)}, u32[]{:S(2)}, u32[]{:S(2)}) %collective-permute-start.12) | collective-permute-done | bytes 73760 | tf_op jit(solution)/shard_map/ppermute | solution.py:451
  62.8 0.4 collective-permute-start.13
  63.1 2.1 %collective-permute-start.17 = (bf16[2,384,128]{2,1,0:T(8,128)(2,1)S(1)}, bf16[2,384,128]{2,1,0:T(8,128)(2,1)S(1)}, u32[]{:S(2)}, u32[]{:S(2)}) collective-permute-start(bf16[2,384,128]{2,1,0:T(8,128)(2,1)S(1)} %get-tuple-element.159), channel_id=1, source_target_pairs={{0,4},{1,5},{2,6},{3,7},{4,0},{5,1},{6,2},{7,3},{8,12},{9,13},{10,... | collective-permute-start | bytes 589832 | tf_op jit(solution)/shard_map/ppermute | solution.py:443
  65.2 2.3 %shard_map.122.acc_in = f32[3,8,128,128]{3,2,1,0:T(8,128)S(1)} custom-call(s32[3]{0:T(128)S(1)} %pad_add_fusion.info, s32[3,6]{1,0:T(4,128)S(1)} %copy-done.4, s32[1]{0:T(128)S(6)} %copy.12.counts, bf16[3,8,128,128]{3,2,1,0:T(8,128)(2,1)S(1)} %get-tuple-element.99.x, bf16[8,128,128]{2,1,0:T(8,128)(2,1)S(1)} %get-tuple-element.133.g, ...), custom_call_target="tpu_custom_call" | custom-call | flops 1000 | bytes 1000 | tf_op jit(solution)/shard_map/pallas_call | solution.py:420
  67.6 2.8 %collective-permute-start.16 = (bf16[288,128]{1,0:T(8,128)(2,1)S(1)}, bf16[288,128]{1,0:T(8,128)(2,1)S(1)}, u32[]{:S(2)}, u32[]{:S(2)}) collective-permute-start(bf16[288,128]{1,0:T(8,128)(2,1)S(1)} %shard_map.123.a), channel_id=1, source_target_pairs={{0,192},{16,208},{32,224},{48,240},{64,128},{80,144},{96,160},{112... | collective-permute-start | bytes 221192 | tf_op jit(solution)/shard_map/ppermute | solution.py:447
  70.4 0.4 collective-permute-start.15
  71.1 2.8 %collective-permute-start.18 = (bf16[2,128,128]{2,1,0:T(8,128)(2,1)S(1)}, bf16[2,128,128]{2,1,0:T(8,128)(2,1)S(1)}, u32[]{:S(2)}, u32[]{:S(2)}) collective-permute-start(bf16[2,128,128]{2,1,0:T(8,128)(2,1)S(1)} %get-tuple-element.160), channel_id=1, source_target_pairs={{0,8},{1,9},{2,10},{3,11},{4,12},{5,13},{6,14},{7,15},{8,0},{9,1},... | collective-permute-start | bytes 196616 | tf_op jit(solution)/shard_map/ppermute | solution.py:443
  73.9 0.8 collective-permute-start.19
  74.7 2.3 %shard_map.124.acc_in = f32[3,8,128,128]{3,2,1,0:T(8,128)S(1)} custom-call(s32[3]{0:T(128)S(1)} %pad_add_fusion.info, s32[3,6]{1,0:T(4,128)S(1)} %copy-done.4, s32[1]{0:T(128)S(6)} %copy.12.counts, bf16[3,8,128,128]{3,2,1,0:T(8,128)(2,1)S(1)} %get-tuple-element.99.x, bf16[8,128,128]{2,1,0:T(8,128)(2,1)S(1)} %get-tuple-element.133.g, ...), custom_call_target="tpu_custom_call" | custom-call | flops 1000 | bytes 1000 | tf_op jit(solution)/shard_map/pallas_call | solution.py:420
  77.1 4.1 %collective-permute-start.20 = (bf16[288,128]{1,0:T(8,128)(2,1)S(1)}, bf16[288,128]{1,0:T(8,128)(2,1)S(1)}, u32[]{:S(2)}, u32[]{:S(2)}) collective-permute-start(bf16[288,128]{1,0:T(8,128)(2,1)S(1)} %shard_map.125.mine), channel_id=1, source_target_pairs={{0,16},{16,0},{32,48},{48,32},{64,80},{80,64},{96,112},{112,96},{1... | collective-permute-start | bytes 221192 | tf_op jit(solution)/shard_map/ppermute | solution.py:447
  81.2 0.9 shard_map.126
  82.1 2.3 %collective-permute-start.21 = (bf16[768,128]{1,0:T(8,128)(2,1)S(1)}, bf16[768,128]{1,0:T(8,128)(2,1)S(1)}, u32[]{:S(2)}, u32[]{:S(2)}) collective-permute-start(bf16[768,128]{1,0:T(8,128)(2,1)S(1)} %get-tuple-element.168), channel_id=1, source_target_pairs={{0,1},{1,0},{2,3},{3,2},{4,5},{5,4},{6,7},{7,6},{8,9},{9,8},{10,11... | collective-permute-start | bytes 589832 | tf_op jit(solution)/shard_map/ppermute | solution.py:443
  84.4 0.7 collective-permute-start.22
  85.1 1.2 %collective-permute-start.23 = (bf16[768,128]{1,0:T(8,128)(2,1)S(1)}, bf16[768,128]{1,0:T(8,128)(2,1)S(1)}, u32[]{:S(2)}, u32[]{:S(2)}) collective-permute-start(bf16[768,128]{1,0:T(8,128)(2,1)S(1)} %get-tuple-element.170), channel_id=1, source_target_pairs={{0,3},{1,2},{2,1},{3,0},{4,7},{5,6},{6,5},{7,4},{8,11},{9,10},{10,... | collective-permute-start | bytes 589832 | tf_op jit(solution)/shard_map/ppermute | solution.py:443
  86.4 1.7 %collective-permute-start.24 = (bf16[144,128]{1,0:T(8,128)(2,1)S(1)}, bf16[144,128]{1,0:T(8,128)(2,1)S(1)}, u32[]{:S(2)}, u32[]{:S(2)}) collective-permute-start(bf16[144,128]{1,0:T(8,128)(2,1)S(1)} %get-tuple-element.180), channel_id=1, source_target_pairs={{0,4},{1,5},{2,6},{3,7},{4,0},{5,1},{6,2},{7,3},{8,12},{9,13},{10,... | collective-permute-start | bytes 110600 | tf_op jit(solution)/shard_map/ppermute | solution.py:451
  88.1 2.1 %collective-permute-start.25 = (bf16[144,128]{1,0:T(8,128)(2,1)S(1)}, bf16[144,128]{1,0:T(8,128)(2,1)S(1)}, u32[]{:S(2)}, u32[]{:S(2)}) collective-permute-start(bf16[144,128]{1,0:T(8,128)(2,1)S(1)} %get-tuple-element.181), channel_id=1, source_target_pairs={{0,8},{1,9},{2,10},{3,11},{4,12},{5,13},{6,14},{7,15},{8,0},{9,1},... | collective-permute-start | bytes 110600 | tf_op jit(solution)/shard_map/ppermute | solution.py:451
  90.1 2.0 %collective-permute-start.26 = (bf16[144,128]{1,0:T(8,128)(2,1)S(1)}, bf16[144,128]{1,0:T(8,128)(2,1)S(1)}, u32[]{:S(2)}, u32[]{:S(2)}) collective-permute-start(bf16[144,128]{1,0:T(8,128)(2,1)S(1)} %get-tuple-element.182), channel_id=1, source_target_pairs={{0,12},{1,13},{2,14},{3,15},{4,8},{5,9},{6,10},{7,11},{8,4},{9,5},... | collective-permute-start | bytes 110600 | tf_op jit(solution)/shard_map/ppermute | solution.py:451
  92.1 2.2 %collective-permute-done.23.m3 = bf16[768,128]{1,0:T(8,128)(2,1)S(1)} collective-permute-done((bf16[768,128]{1,0:T(8,128)(2,1)S(1)}, bf16[768,128]{1,0:T(8,128)(2,1)S(1)}, u32[]{:S(2)}, u32[]{:S(2)}) %collective-permute-start.23) | collective-permute-done | bytes 196640 | tf_op jit(solution)/shard_map/ppermute | solution.py:443
  94.3 1.7 %shard_map.127 = (bf16[256,384]{1,0:T(8,128)(2,1)}, bf16[256,384]{1,0:T(8,128)(2,1)}, bf16[256,384]{1,0:T(8,128)(2,1)}) custom-call(s32[3]{0:T(128)S(1)} %pad_add_fusion.info, bf16[768,128]{1,0:T(8,128)(2,1)S(1)} %get-tuple-element.167.m0, bf16[768,128]{1,0:T(8,128)(2,1)S(1)} %collective-permute-done.21.m1, bf16[768,128]{1,0:T(8,128)(2,1)S(1)} %collective-permute-done.22.m2, ...), custom_call_target="tpu_custom_call" | custom-call | flops 1000 | bytes 1000 | tf_op jit(solution)/shard_map/pallas_call | solution.py:420
  96.0 1.5 %collective-permute-done.26.c = bf16[144,128]{1,0:T(8,128)(2,1)S(1)} collective-permute-done((bf16[144,128]{1,0:T(8,128)(2,1)S(1)}, bf16[144,128]{1,0:T(8,128)(2,1)S(1)}, u32[]{:S(2)}, u32[]{:S(2)}) %collective-permute-start.26) | collective-permute-done | bytes 36896 | tf_op jit(solution)/shard_map/ppermute | solution.py:451
  97.5 1.2 %shard_map.129 = f32[24,768]{1,0:T(8,128)} custom-call(s32[3]{0:T(128)S(1)} %pad_add_fusion.info, f32[144,128]{1,0:T(8,128)S(1)} %get-tuple-element.179.own, bf16[144,128]{1,0:T(8,128)(2,1)S(1)} %collective-permute-done.24.a, bf16[144,128]{1,0:T(8,128)(2,1)S(1)} %collective-permute-done.25.b, bf16[144,128]{1,0:T(8,128)(2,1)S(1)} %collective-permute-done.26.c), custom_call_target="tpu_custom_call" | custom-call | flops 1000 | bytes 1000 | tf_op jit(solution)/shard_map/pallas_call | solution.py:420
  (37 shorter events, 1.0 us)
Async XLA Ops:
  0.6 17.4 %copy-start.4 = (s32[3,6]{1,0:T(4,128)S(1)}, s32[3,6]{1,0:T(4,128)}, u32[]{:S(2)}) copy-start(s32[3,6]{1,0:T(4,128)} %offsets.15) | copy-start | bytes 220
  3.2 10.1 %collective-permute-start = (bf16[3,256,128]{2,1,0:T(8,128)(2,1)}, bf16[3,256,128]{2,1,0:T(8,128)(2,1)S(1)}, u32[]{:S(2)}, u32[]{:S(2)}) collective-permute-start(bf16[3,256,128]{2,1,0:T(8,128)(2,1)} %get-tuple-element.96), channel_id=1, source_target_pairs={{0,1},{1,0},{2,3},{3,2},{4,5},{5,4},{6,7},{7,6},{8,9},{9,8},{10,11... | collective-permute-start | bytes 589832 | tf_op jit(solution)/shard_map/ppermute | solution.py:443
  6.8 6.5 %collective-permute-start.1 = (bf16[3,256,128]{2,1,0:T(8,128)(2,1)}, bf16[3,256,128]{2,1,0:T(8,128)(2,1)S(1)}, u32[]{:S(2)}, u32[]{:S(2)}) collective-permute-start(bf16[3,256,128]{2,1,0:T(8,128)(2,1)} %get-tuple-element.97), channel_id=1, source_target_pairs={{0,2},{1,3},{2,0},{3,1},{4,6},{5,7},{6,4},{7,5},{8,10},{9,11},{10,... | collective-permute-start | bytes 589832 | tf_op jit(solution)/shard_map/ppermute | solution.py:443
  8.5 9.5 %collective-permute-start.2 = (bf16[3,256,128]{2,1,0:T(8,128)(2,1)}, bf16[3,256,128]{2,1,0:T(8,128)(2,1)S(1)}, u32[]{:S(2)}, u32[]{:S(2)}) collective-permute-start(bf16[3,256,128]{2,1,0:T(8,128)(2,1)} %get-tuple-element.98), channel_id=1, source_target_pairs={{0,3},{1,2},{2,1},{3,0},{4,7},{5,6},{6,5},{7,4},{8,11},{9,10},{10,... | collective-permute-start | bytes 589832 | tf_op jit(solution)/shard_map/ppermute | solution.py:443
  8.6 1.1 %copy-start = (bf16[384,768]{1,0:T(8,128)(2,1)S(1)}, bf16[384,768]{1,0:T(8,128)(2,1)}, u32[]{:S(2)}) copy-start(bf16[384,768]{1,0:T(8,128)(2,1)} %w.3) | copy-start | bytes 1769476
  9.6 1.0 %copy-start.2 = (bf16[1,256,768]{2,1,0:T(8,128)(2,1)S(1)}, bf16[1,256,768]{2,1,0:T(8,128)(2,1)}, u32[]{:S(2)}) copy-start(bf16[1,256,768]{2,1,0:T(8,128)(2,1)} %param.11) | copy-start | bytes 1179652
  10.6 0.9 copy-start.3
  18.7 5.7 %collective-permute-start.3 = (bf16[2,128,128]{2,1,0:T(8,128)(2,1)S(1)}, bf16[2,128,128]{2,1,0:T(8,128)(2,1)S(1)}, u32[]{:S(2)}, u32[]{:S(2)}) collective-permute-start(bf16[2,128,128]{2,1,0:T(8,128)(2,1)S(1)} %get-tuple-element.101.s8), channel_id=1, source_target_pairs={{0,4},{1,5},{2,6},{3,7},{4,0},{5,1},{6,2},{7,3},{8,12},{9,13},{10,... | collective-permute-start | bytes 196616 | tf_op jit(solution)/shard_map/ppermute | solution.py:443
  20.6 9.7 %collective-permute-start.5 = (bf16[2,256,128]{2,1,0:T(8,128)(2,1)S(1)}, bf16[2,256,128]{2,1,0:T(8,128)(2,1)S(1)}, u32[]{:S(2)}, u32[]{:S(2)}) collective-permute-start(bf16[2,256,128]{2,1,0:T(8,128)(2,1)S(1)} %get-tuple-element.103), channel_id=1, source_target_pairs={{0,4},{1,5},{2,6},{3,7},{4,0},{5,1},{6,2},{7,3},{8,12},{9,13},{10,... | collective-permute-start | bytes 393224 | tf_op jit(solution)/shard_map/ppermute | solution.py:443
  24.4 11.4 %collective-permute-start.4 = (bf16[4,128,128]{2,1,0:T(8,128)(2,1)S(1)}, bf16[4,128,128]{2,1,0:T(8,128)(2,1)S(1)}, u32[]{:S(2)}, u32[]{:S(2)}) collective-permute-start(bf16[4,128,128]{2,1,0:T(8,128)(2,1)S(1)} %shard_map.114), channel_id=1, source_target_pairs={{0,12},{1,13},{2,14},{3,15},{4,8},{5,9},{6,10},{7,11},{8,4},{9,5},... | collective-permute-start | bytes 393224 | tf_op jit(solution)/shard_map/ppermute | solution.py:443
  35.9 16.7 %copy-start.1 = (bf16[384,768]{1,0:T(8,128)(2,1)S(1)}, bf16[384,768]{1,0:T(8,128)(2,1)}, u32[]{:S(2)}) copy-start(bf16[384,768]{1,0:T(8,128)(2,1)} %w.3) | copy-start | bytes 1769476
  37.3 5.4 %collective-permute-start.6 = (bf16[512,128]{1,0:T(8,128)(2,1)S(1)}, bf16[512,128]{1,0:T(8,128)(2,1)S(1)}, u32[]{:S(2)}, u32[]{:S(2)}) collective-permute-start(bf16[512,128]{1,0:T(8,128)(2,1)S(1)} %get-tuple-element.116.mx1), channel_id=1, source_target_pairs={{0,1},{1,0},{2,3},{3,2},{4,5},{5,4},{6,7},{7,6},{8,9},{9,8},{10,11... | collective-permute-start | bytes 393224 | tf_op jit(solution)/shard_map/ppermute | solution.py:443
  37.4 5.3 %collective-permute-start.7 = (bf16[512,128]{1,0:T(8,128)(2,1)S(1)}, bf16[512,128]{1,0:T(8,128)(2,1)S(1)}, u32[]{:S(2)}, u32[]{:S(2)}) collective-permute-start(bf16[512,128]{1,0:T(8,128)(2,1)S(1)} %get-tuple-element.117.mx2), channel_id=1, source_target_pairs={{0,2},{1,3},{2,0},{3,1},{4,6},{5,7},{6,4},{7,5},{8,10},{9,11},{10,... | collective-permute-start | bytes 393224 | tf_op jit(solution)/shard_map/ppermute | solution.py:443
  38.7 6.8 %collective-permute-start.8 = (bf16[512,128]{1,0:T(8,128)(2,1)S(1)}, bf16[512,128]{1,0:T(8,128)(2,1)S(1)}, u32[]{:S(2)}, u32[]{:S(2)}) collective-permute-start(bf16[512,128]{1,0:T(8,128)(2,1)S(1)} %get-tuple-element.118.mx3), channel_id=1, source_target_pairs={{0,3},{1,2},{2,1},{3,0},{4,7},{5,6},{6,5},{7,4},{8,11},{9,10},{10,... | collective-permute-start | bytes 393224 | tf_op jit(solution)/shard_map/ppermute | solution.py:443
  46.5 7.9 %collective-permute-start.9 = (bf16[16,72,128]{2,1,0:T(8,128)(2,1)S(1)}, bf16[16,72,128]{2,1,0:T(8,128)(2,1)S(1)}, u32[]{:S(2)}, u32[]{:S(2)}) collective-permute-start(bf16[16,72,128]{2,1,0:T(8,128)(2,1)S(1)} %get-tuple-element.140), channel_id=1, source_target_pairs={{0,16},{16,0},{32,48},{48,32},{64,80},{80,64},{96,112},{112,96},{1... | collective-permute-start | bytes 884744 | tf_op jit(solution)/shard_map/ppermute | solution.py:447
  54.5 6.9 %collective-permute-start.10 = (bf16[288,128]{1,0:T(8,128)(2,1)S(1)}, bf16[288,128]{1,0:T(8,128)(2,1)S(1)}, u32[]{:S(2)}, u32[]{:S(2)}) collective-permute-start(bf16[288,128]{1,0:T(8,128)(2,1)S(1)} %get-tuple-element.143), channel_id=1, source_target_pairs={{0,1},{1,0},{2,3},{3,2},{4,5},{5,4},{6,7},{7,6},{8,9},{9,8},{10,11... | collective-permute-start | bytes 221192 | tf_op jit(solution)/shard_map/ppermute | solution.py:451
  55.9 5.5 %collective-permute-start.11 = (bf16[288,128]{1,0:T(8,128)(2,1)S(1)}, bf16[288,128]{1,0:T(8,128)(2,1)S(1)}, u32[]{:S(2)}, u32[]{:S(2)}) collective-permute-start(bf16[288,128]{1,0:T(8,128)(2,1)S(1)} %get-tuple-element.144), channel_id=1, source_target_pairs={{0,2},{1,3},{2,0},{3,1},{4,6},{5,7},{6,4},{7,5},{8,10},{9,11},{10,... | collective-permute-start | bytes 221192 | tf_op jit(solution)/shard_map/ppermute | solution.py:451
  56.2 6.6 %collective-permute-start.12 = (bf16[288,128]{1,0:T(8,128)(2,1)S(1)}, bf16[288,128]{1,0:T(8,128)(2,1)S(1)}, u32[]{:S(2)}, u32[]{:S(2)}) collective-permute-start(bf16[288,128]{1,0:T(8,128)(2,1)S(1)} %get-tuple-element.145), channel_id=1, source_target_pairs={{0,3},{1,2},{2,1},{3,0},{4,7},{5,6},{6,5},{7,4},{8,11},{9,10},{10,... | collective-permute-start | bytes 221192 | tf_op jit(solution)/shard_map/ppermute | solution.py:451
  62.8 4.8 %collective-permute-start.13 = (bf16[288,128]{1,0:T(8,128)(2,1)S(1)}, bf16[288,128]{1,0:T(8,128)(2,1)S(1)}, u32[]{:S(2)}, u32[]{:S(2)}) collective-permute-start(bf16[288,128]{1,0:T(8,128)(2,1)S(1)} %shard_map.121.a), channel_id=1, source_target_pairs={{0,32},{16,48},{32,0},{48,16},{64,96},{80,112},{96,64},{112,80},{1... | collective-permute-start | bytes 221192 | tf_op jit(solution)/shard_map/ppermute | solution.py:447
  63.1 18.1 %collective-permute-start.17 = (bf16[2,384,128]{2,1,0:T(8,128)(2,1)S(1)}, bf16[2,384,128]{2,1,0:T(8,128)(2,1)S(1)}, u32[]{:S(2)}, u32[]{:S(2)}) collective-permute-start(bf16[2,384,128]{2,1,0:T(8,128)(2,1)S(1)} %get-tuple-element.159), channel_id=1, source_target_pairs={{0,4},{1,5},{2,6},{3,7},{4,0},{5,1},{6,2},{7,3},{8,12},{9,13},{10,... | collective-permute-start | bytes 589832 | tf_op jit(solution)/shard_map/ppermute | solution.py:443
  67.6 6.3 %collective-permute-start.16 = (bf16[288,128]{1,0:T(8,128)(2,1)S(1)}, bf16[288,128]{1,0:T(8,128)(2,1)S(1)}, u32[]{:S(2)}, u32[]{:S(2)}) collective-permute-start(bf16[288,128]{1,0:T(8,128)(2,1)S(1)} %shard_map.123.a), channel_id=1, source_target_pairs={{0,192},{16,208},{32,224},{48,240},{64,128},{80,144},{96,160},{112... | collective-permute-start | bytes 221192 | tf_op jit(solution)/shard_map/ppermute | solution.py:447
  70.4 6.6 %collective-permute-start.15 = (bf16[288,128]{1,0:T(8,128)(2,1)S(1)}, bf16[288,128]{1,0:T(8,128)(2,1)S(1)}, u32[]{:S(2)}, u32[]{:S(2)}) collective-permute-start(bf16[288,128]{1,0:T(8,128)(2,1)S(1)} %shard_map.123.a), channel_id=1, source_target_pairs={{0,128},{16,144},{32,160},{48,176},{64,192},{80,208},{96,224},{112... | collective-permute-start | bytes 221192 | tf_op jit(solution)/shard_map/ppermute | solution.py:447
  70.8 6.2 %collective-permute-start.14 = (bf16[288,128]{1,0:T(8,128)(2,1)S(1)}, bf16[288,128]{1,0:T(8,128)(2,1)S(1)}, u32[]{:S(2)}, u32[]{:S(2)}) collective-permute-start(bf16[288,128]{1,0:T(8,128)(2,1)S(1)} %shard_map.123.a), channel_id=1, source_target_pairs={{0,64},{16,80},{32,96},{48,112},{64,0},{80,16},{96,32},{112,48},{1... | collective-permute-start | bytes 221192 | tf_op jit(solution)/shard_map/ppermute | solution.py:447
  71.1 10.1 %collective-permute-start.18 = (bf16[2,128,128]{2,1,0:T(8,128)(2,1)S(1)}, bf16[2,128,128]{2,1,0:T(8,128)(2,1)S(1)}, u32[]{:S(2)}, u32[]{:S(2)}) collective-permute-start(bf16[2,128,128]{2,1,0:T(8,128)(2,1)S(1)} %get-tuple-element.160), channel_id=1, source_target_pairs={{0,8},{1,9},{2,10},{3,11},{4,12},{5,13},{6,14},{7,15},{8,0},{9,1},... | collective-permute-start | bytes 196616 | tf_op jit(solution)/shard_map/ppermute | solution.py:443
  73.9 7.3 %collective-permute-start.19 = (bf16[2,128,128]{2,1,0:T(8,128)(2,1)S(1)}, bf16[2,128,128]{2,1,0:T(8,128)(2,1)S(1)}, u32[]{:S(2)}, u32[]{:S(2)}) collective-permute-start(bf16[2,128,128]{2,1,0:T(8,128)(2,1)S(1)} %get-tuple-element.161), channel_id=1, source_target_pairs={{0,12},{1,13},{2,14},{3,15},{4,8},{5,9},{6,10},{7,11},{8,4},{9,5},... | collective-permute-start | bytes 196616 | tf_op jit(solution)/shard_map/ppermute | solution.py:443
  77.1 5.0 %collective-permute-start.20 = (bf16[288,128]{1,0:T(8,128)(2,1)S(1)}, bf16[288,128]{1,0:T(8,128)(2,1)S(1)}, u32[]{:S(2)}, u32[]{:S(2)}) collective-permute-start(bf16[288,128]{1,0:T(8,128)(2,1)S(1)} %shard_map.125.mine), channel_id=1, source_target_pairs={{0,16},{16,0},{32,48},{48,32},{64,80},{80,64},{96,112},{112,96},{1... | collective-permute-start | bytes 221192 | tf_op jit(solution)/shard_map/ppermute | solution.py:447
  82.1 8.0 %collective-permute-start.21 = (bf16[768,128]{1,0:T(8,128)(2,1)S(1)}, bf16[768,128]{1,0:T(8,128)(2,1)S(1)}, u32[]{:S(2)}, u32[]{:S(2)}) collective-permute-start(bf16[768,128]{1,0:T(8,128)(2,1)S(1)} %get-tuple-element.168), channel_id=1, source_target_pairs={{0,1},{1,0},{2,3},{3,2},{4,5},{5,4},{6,7},{7,6},{8,9},{9,8},{10,11... | collective-permute-start | bytes 589832 | tf_op jit(solution)/shard_map/ppermute | solution.py:443
  84.4 7.7 %collective-permute-start.22 = (bf16[768,128]{1,0:T(8,128)(2,1)S(1)}, bf16[768,128]{1,0:T(8,128)(2,1)S(1)}, u32[]{:S(2)}, u32[]{:S(2)}) collective-permute-start(bf16[768,128]{1,0:T(8,128)(2,1)S(1)} %get-tuple-element.169), channel_id=1, source_target_pairs={{0,2},{1,3},{2,0},{3,1},{4,6},{5,7},{6,4},{7,5},{8,10},{9,11},{10,... | collective-permute-start | bytes 589832 | tf_op jit(solution)/shard_map/ppermute | solution.py:443
  85.1 9.2 %collective-permute-start.23 = (bf16[768,128]{1,0:T(8,128)(2,1)S(1)}, bf16[768,128]{1,0:T(8,128)(2,1)S(1)}, u32[]{:S(2)}, u32[]{:S(2)}) collective-permute-start(bf16[768,128]{1,0:T(8,128)(2,1)S(1)} %get-tuple-element.170), channel_id=1, source_target_pairs={{0,3},{1,2},{2,1},{3,0},{4,7},{5,6},{6,5},{7,4},{8,11},{9,10},{10,... | collective-permute-start | bytes 589832 | tf_op jit(solution)/shard_map/ppermute | solution.py:443
  86.4 9.6 %collective-permute-start.24 = (bf16[144,128]{1,0:T(8,128)(2,1)S(1)}, bf16[144,128]{1,0:T(8,128)(2,1)S(1)}, u32[]{:S(2)}, u32[]{:S(2)}) collective-permute-start(bf16[144,128]{1,0:T(8,128)(2,1)S(1)} %get-tuple-element.180), channel_id=1, source_target_pairs={{0,4},{1,5},{2,6},{3,7},{4,0},{5,1},{6,2},{7,3},{8,12},{9,13},{10,... | collective-permute-start | bytes 110600 | tf_op jit(solution)/shard_map/ppermute | solution.py:451
  88.1 8.0 %collective-permute-start.25 = (bf16[144,128]{1,0:T(8,128)(2,1)S(1)}, bf16[144,128]{1,0:T(8,128)(2,1)S(1)}, u32[]{:S(2)}, u32[]{:S(2)}) collective-permute-start(bf16[144,128]{1,0:T(8,128)(2,1)S(1)} %get-tuple-element.181), channel_id=1, source_target_pairs={{0,8},{1,9},{2,10},{3,11},{4,12},{5,13},{6,14},{7,15},{8,0},{9,1},... | collective-permute-start | bytes 110600 | tf_op jit(solution)/shard_map/ppermute | solution.py:451
  90.1 7.3 %collective-permute-start.26 = (bf16[144,128]{1,0:T(8,128)(2,1)S(1)}, bf16[144,128]{1,0:T(8,128)(2,1)S(1)}, u32[]{:S(2)}, u32[]{:S(2)}) collective-permute-start(bf16[144,128]{1,0:T(8,128)(2,1)S(1)} %get-tuple-element.182), channel_id=1, source_target_pairs={{0,12},{1,13},{2,14},{3,15},{4,8},{5,9},{6,10},{7,11},{8,4},{9,5},... | collective-permute-start | bytes 110600 | tf_op jit(solution)/shard_map/ppermute | solution.py:451
